TPU v7x, 32 devices: a whole 2x2x4 slice. The times are simulated.
32 devices in a mesh: sub: 8 (over z, core), row: 4 (over y, x).
Axes of the slice: x: 2, y: 2, z: 4, core: 2. Of those that a mesh axis runs over, the one named last changes fastest.
Arguments:
- modes: float32 [24576, 64], P(('sub', 'row')), may hold values from -6 to 6
- search: float32 [24576, 64], P(('sub', 'row')), may hold values from -6 to 6
- precond: float32 [24576], P(('sub', 'row')), may hold values from 0.05 to 0.25
- in_row: int32 [8, 4, 96], P('sub', 'row'), may hold values from 0 to 11, as said below
- in_col: int32 [8, 4, 96], P('sub', 'row'), may hold values from 0 to 47, as said below
- in_val: bfloat16 [8, 4, 96, 64, 64], P('sub', 'row'), as said below
- bnd_rows: int32 [8, 4, 3], P('sub', 'row'), may hold values from 0 to 11, as said below
- if_row: int32 [8, 4, 12], P('sub', 'row'), may hold values from 0 to 11, as said below
- if_src: int32 [8, 4, 12], P('sub', 'row'), may hold values from 0 to 23, as said below
- if_val: bfloat16 [8, 4, 12, 64, 64], P('sub', 'row')
Outputs:
- modes_out: float32 [24576, 64], P(('sub', 'row'))
- search_out: float32 [24576, 64], P(('sub', 'row'))
Inputs may be any that keep to these rules, and one draw needn't show every extreme that they name: `in_row`: entry k < 12 is k; each later group of 12 entries names each of the device's block-rows once. `in_col`: entry k < 12 is r * 12 + k on device (s, r); in each later group of 12 entries the devices of a subdomain together name each of its 48 block-rows once, and no entry names its own block-row. `in_val`: the first 12 blocks of every device are symmetric; the operator A is symmetric positive definite. `bnd_rows`: distinct within a device. `if_row`: each of the device's 12 block-rows once. `if_src`: t * 3 + q with t never the device's own subdomain; among the devices with one index of row, each boundary slot of each subdomain is named exactly 4 times.
All inputs are finite; a program needn't handle non-finite values.
Results may differ from a plain program's by a relative error of at most 0.0006.
Values may be sent and summed in bfloat16 or wider, within the bound.
No kernel may reach another device: no remote copies, remote signals or barrier semaphores. Data moves between devices by JAX's collectives and lax.ppermute only.
A program may use at most 128 MiB of HBM per device.

v0:
```python
import jax
import jax.numpy as jnp
from jax import lax
from jax.sharding import PartitionSpec as P

KB = 64
LB = 12
ITERS = 2
IFR = 3


precise_mode = lax.Precision.HIGHEST


def gram_product(left, right):
    return jnp.dot(left.T, right, precision=precise_mode, preferred_element_type=jnp.float32)


def full_dot(left, right):
    return jnp.dot(left, right, precision=precise_mode, preferred_element_type=jnp.float32)


def chol_solve(matrix, rhs):
    factor = jnp.linalg.cholesky(matrix)
    halfway = lax.linalg.triangular_solve(factor, rhs, left_side=True, lower=True)
    return lax.linalg.triangular_solve(
        factor, halfway, left_side=True, lower=True, transpose_a=True
    )


def rescale(factor, moved):
    return lax.linalg.triangular_solve(factor, moved, left_side=False, lower=True, transpose_a=True)


def project(current, image_x):
    return lax.psum(
        (gram_product(current, current), gram_product(current, image_x)), ("sub", "row")
    )


def apply_blocks(vector, blocks):
    rows_here, cols_here, vals_here, bnd_here, face_rows, face_src, face_vals = blocks
    width = vector.shape[1]
    mine = vector.reshape(LB, KB, width)
    local_ids = jnp.arange(LB, dtype=jnp.int32)
    position = lax.axis_index("row")
    group = lax.all_gather(vector, "row", axis=0, tiled=True).reshape(-1, KB, width)
    forward = jnp.einsum("kij,kjw->kiw", vals_here, group[cols_here], precision=precise_mode)
    select = (rows_here[:, None] == local_ids[None, :]).astype(jnp.float32)
    result = jnp.einsum("ka,kiw->aiw", select, forward, precision=precise_mode)
    backward = jnp.einsum("kji,kjw->kiw", vals_here, mine[rows_here], precision=precise_mode)
    keeper = (cols_here != position * LB + rows_here).astype(jnp.float32)
    backward = backward * keeper[:, None, None]
    wanted = jnp.arange(LB * KB * lax.axis_size("row") // KB, dtype=jnp.int32)
    chosen = (cols_here[None, :] == wanted[:, None]).astype(jnp.float32)
    returned = lax.psum_scatter(
        jnp.einsum("bk,kiw->biw", chosen, backward, precision=precise_mode).reshape(
            LB * KB * lax.axis_size("row"), width
        ),
        "row",
        scatter_dimension=0,
        tiled=True,
    )
    result = result + returned.reshape(LB, KB, width)
    boundary = mine[bnd_here].reshape(-1, width)
    remote = lax.all_gather(boundary, "sub", axis=0, tiled=True).reshape(-1, KB, width)
    forward = jnp.einsum("kij,kjw->kiw", face_vals, remote[face_src], precision=precise_mode)
    face_select = (face_rows[:, None] == local_ids[None, :]).astype(jnp.float32)
    result = result + jnp.einsum("ka,kiw->aiw", face_select, forward, precision=precise_mode)
    backward = jnp.einsum("kji,kjw->kiw", face_vals, mine[face_rows], precision=precise_mode)
    wanted = jnp.arange(IFR * KB * lax.axis_size("sub") // KB, dtype=jnp.int32)
    chosen = (face_src[None, :] == wanted[:, None]).astype(jnp.float32)
    landed = lax.psum_scatter(
        jnp.einsum("bk,kiw->biw", chosen, backward, precision=precise_mode).reshape(
            IFR * KB * lax.axis_size("sub"), width
        ),
        "sub",
        scatter_dimension=0,
        tiled=True,
    ).reshape(IFR, KB, width)
    placed = (bnd_here[:, None] == local_ids[None, :]).astype(jnp.float32)
    result = result + jnp.einsum("qa,qiw->aiw", placed, landed, precision=precise_mode)
    return result.reshape(LB * KB, width)


def local(modes, search, precond, in_row, in_col, in_val, bnd_rows, if_row, if_src, if_val):
    blocks = (
        in_row[0, 0],
        in_col[0, 0],
        in_val[0, 0].astype(jnp.float32),
        bnd_rows[0, 0],
        if_row[0, 0],
        if_src[0, 0],
        if_val[0, 0].astype(jnp.float32),
    )
    total_rows = modes.shape[0] * lax.axis_size("sub") * lax.axis_size("row")
    nmode = modes.shape[1]
    images = apply_blocks(jnp.concatenate([modes, search], 1), blocks)
    current, direction = (modes, search)
    image_x, image_p = (images[:, :nmode], images[:, nmode:])
    for sweep in range(ITERS):
        correlation, energy = project(current, image_x)
        ritz = chol_solve(correlation, energy)
        residue = image_x - full_dot(current, ritz)
        update = precond[:, None] * residue
        image_w = apply_blocks(update, blocks)
        basis = jnp.concatenate([update, direction], 1)
        image_b = jnp.concatenate([image_w, image_p], 1)
        coupled, driving = lax.psum(
            (gram_product(basis, image_b), gram_product(basis, image_x)), ("sub", "row")
        )
        coeffs = -chol_solve(coupled, driving)
        step_x = full_dot(basis, coeffs)
        step_a = full_dot(image_b, coeffs)
        moved = current + step_x
        moved_image = image_x + step_a
        lengths = lax.psum(gram_product(moved, moved), ("sub", "row"))
        factor = jnp.linalg.cholesky(lengths / total_rows)
        current = rescale(factor, moved)
        image_x = rescale(factor, moved_image)
        direction = rescale(factor, step_x)
        image_p = rescale(factor, step_a)
    return (current, direction)


def solution(mesh):
    return jax.shard_map(
        local,
        mesh=mesh,
        in_specs=(
            P(("sub", "row"), None),
            P(("sub", "row"), None),
            P(("sub", "row")),
            P("sub", "row", None),
            P("sub", "row", None),
            P("sub", "row", None, None, None),
            P("sub", "row", None),
            P("sub", "row", None),
            P("sub", "row", None),
            P("sub", "row", None, None, None),
        ),
        out_specs=(P(("sub", "row"), None), P(("sub", "row"), None)),
        check_vma=False,
    )
```

profile of v0, /device:TPU:0, one launch (start us, length us, event | category | flops | bytes accessed | tf_op | source)
XLA Modules:
  0.0 761.1 jit_solution(15770148787730468204)
XLA Ops:
  15.0 1.7 gather_fusion.1
  16.8 4.8 copy.144
  21.5 3.3 multiply_bitcast_fusion.2
  24.8 3.1 fusion.4
  28.0 1.6 copy.146
  29.7 2.4 copy.142
  32.1 1.5 gather_fusion.2
  33.7 19.4 %all_gather.19 = f32[1536,128]{1,0:T(8,128)S(1)} all-gather(f32[192,128]{1,0:T(8,128)S(1)} %bitcast.313), channel_id=1, replica_groups=mesh['sub'=8,'row'=4] {'sub'}, dimensions={0}, use_global_device_ids=true | all-gather | bytes 884736 | tf_op jit(solution)/shard_map/all_gather | solution.py:66
  54.4 2.2 fusion.44
  56.6 4.1 gather_fusion
  60.7 5.4 convolution_bitcast_fusion.2
  66.1 16.0 %reduce-scatter.11.cloned.1.call-done = f32[768,128]{1,0:T(8,128)} async-done(((f32[3072,128]{1,0:T(8,128)}), f32[768,128]{1,0:T(8,128)}) %reduce-scatter.11.cloned.1.call-update) | async-done | bytes 393232 | tf_op jit(solution)/shard_map/reduce_scatter | solution.py:56
  82.0 4.8 fusion.11
  89.4 39.9 %all-reduce.1 = (f32[64,64]{0,1:T(8,128)S(1)}, f32[64,64]{0,1:T(8,128)S(1)}) all-reduce(f32[64,64]{0,1:T(8,128)S(1)} %convolution_bitcast_fusion.16, f32[64,64]{0,1:T(8,128)S(1)} %fusion.134), channel_id=1, replica_groups=mesh['sub'=8,'row'=4] {'sub','row'}, use_global_device_ids=true, to_apply=%region_5.0 | all-reduce | flops 8192 | bytes 65536 | tf_op jit(solution)/shard_map/psum | solution.py:36
  129.5 5.8 cholesky.116
  136.7 4.9 custom-call.29
  146.6 2.5 gather_fusion.6
  149.1 4.9 multiply_bitcast_fusion.1
  154.1 4.3 fusion.2
  158.3 2.7 reshape.293
  162.3 12.8 %all_gather.20 = f32[3072,64]{0,1:T(8,128)} all-gather(f32[768,64]{0,1:T(8,128)S(1)} %fusion.16), channel_id=1, replica_groups=mesh['sub'=8,'row'=4] {'row'}, dimensions={0}, use_global_device_ids=true | all-gather | bytes 983040 | tf_op jit(solution)/shard_map/all_gather | solution.py:47
  175.1 1.6 copy.237
  176.7 2.6 gather_fusion.5
  179.3 6.2 convolution_bitcast_fusion.1
  185.5 4.8 copy.160
  190.5 14.9 %all-gather = f32[8,192,64]{1,2,0:T(8,128)S(1)} all-gather(f32[1,192,64]{1,2,0:T(8,128)S(1)} %copy.168), channel_id=1, replica_groups=mesh['sub'=8,'row'=4] {'sub'}, dimensions={0}, use_global_device_ids=true | all-gather | bytes 442368 | tf_op jit(solution)/shard_map/all_gather | solution.py:66
  205.7 1.4 gather_fusion.8
  207.1 1.5 convolution_bitcast_fusion.6
  209.7 2.2 fusion.42
  214.1 4.4 convolution_add_fusion.4
  219.1 1.6 fusion.32
  222.1 38.9 %psum.73 = f32[128,64]{0,1:T(8,128)S(1)} all-reduce(f32[128,64]{0,1:T(8,128)} %fusion.31), channel_id=1, replica_groups=mesh['sub'=8,'row'=4] {'sub','row'}, use_global_device_ids=true, to_apply=%region_11.16 | all-reduce | flops 8192 | bytes 65536 | tf_op jit(solution)/shard_map/psum | solution.py:109
  261.0 76.2 %all-reduce.5.cloned.1.call-done = f32[128,128]{0,1:T(8,128)} async-done(((f32[128,128]{0,1:T(8,128)}), f32[128,128]{0,1:T(8,128)}) %all-reduce.5.cloned.1.call-update) | async-done | bytes 65552 | tf_op jit(solution)/shard_map/psum | solution.py:109
  339.0 11.7 %cholesky.127 = f32[128,128]{1,0:T(8,128)S(1)} custom-call(f32[128,128]{1,0:T(8,128)S(1)} %fusion.56), custom_call_target="Cholesky" | custom-call | tf_op jit(solution)/shard_map/jit(cholesky)/cholesky | solution.py:24
  352.0 9.8 %custom-call.31 = f32[1,128,128]{1,2,0:T(8,128)S(1)} custom-call(f32[1,128,128]{2,1,0:T(8,128)S(1)} %fusion.47), custom_call_target="InvertDiagBlocksLowerTriangular" | custom-call | tf_op jit(solution)/shard_map/triangular_solve/custom-call.5 | solution.py:26
  364.9 41.1 %psum.74 = f32[64,64]{0,1:T(8,128)S(1)} all-reduce(f32[64,64]{0,1:T(8,128)S(1)} %fusion.135), channel_id=1, replica_groups=mesh['sub'=8,'row'=4] {'sub','row'}, use_global_device_ids=true, to_apply=%region_12.19 | all-reduce | flops 4096 | bytes 32768 | tf_op jit(solution)/shard_map/psum | solution.py:117
  406.1 5.8 cholesky.138
  413.2 4.9 custom-call.32
  420.5 39.7 %all-reduce = (f32[64,64]{1,0:T(8,128)S(1)}, f32[64,64]{0,1:T(8,128)S(1)}) all-reduce(f32[64,64]{1,0:T(8,128)S(1)} %fusion.137, f32[64,64]{0,1:T(8,128)S(1)} %fusion.136), channel_id=1, replica_groups=mesh['sub'=8,'row'=4] {'sub','row'}, use_global_device_ids=true, to_apply=%region_14.22 | all-reduce | flops 8192 | bytes 65536 | tf_op jit(solution)/shard_map/psum | solution.py:36
  460.2 5.8 cholesky.149
  467.4 4.9 custom-call.35
  476.5 2.5 gather_fusion.11
  479.0 4.9 multiply_bitcast_fusion
  484.0 4.3 fusion
  488.2 2.7 reshape.302
  491.0 12.8 %all_gather.22 = f32[3072,64]{0,1:T(8,128)} all-gather(f32[768,64]{0,1:T(8,128)S(1)} %fusion.14), channel_id=1, replica_groups=mesh['sub'=8,'row'=4] {'row'}, dimensions={0}, use_global_device_ids=true | all-gather | bytes 983040 | tf_op jit(solution)/shard_map/all_gather | solution.py:47
  505.2 1.6 copy.242
  506.8 2.5 gather_fusion.10
  509.3 6.3 convolution_bitcast_fusion
  515.6 4.0 copy.190
  520.3 15.4 %all-gather.1 = f32[8,192,64]{1,2,0:T(8,128)S(1)} all-gather(f32[1,192,64]{1,2,0:T(8,128)} %copy.198), channel_id=1, replica_groups=mesh['sub'=8,'row'=4] {'sub'}, dimensions={0}, use_global_device_ids=true | all-gather | bytes 442368 | tf_op jit(solution)/shard_map/all_gather | solution.py:66
  536.9 2.6 gather_fusion.13
  539.4 1.5 convolution_bitcast_fusion.4
  543.4 2.2 fusion.40
  545.7 1.9 reshape.303
  547.5 2.2 copy.196
  549.7 3.7 convolution_add_fusion.3
  556.0 38.6 %psum.78 = f32[128,64]{0,1:T(8,128)S(1)} all-reduce(f32[128,64]{0,1:T(8,128)S(1)} %fusion.29), channel_id=1, replica_groups=mesh['sub'=8,'row'=4] {'sub','row'}, use_global_device_ids=true, to_apply=%region_18.26 | all-reduce | flops 8192 | bytes 65536 | tf_op jit(solution)/shard_map/psum | solution.py:109
  594.7 77.2 %all-reduce.7.cloned.1.call-done = f32[128,128]{0,1:T(8,128)} async-done(((f32[128,128]{0,1:T(8,128)}), f32[128,128]{0,1:T(8,128)}) %all-reduce.7.cloned.1.call-update) | async-done | bytes 65552 | tf_op jit(solution)/shard_map/psum | solution.py:109
  673.7 11.7 %cholesky.160 = f32[128,128]{1,0:T(8,128)S(1)} custom-call(f32[128,128]{1,0:T(8,128)S(1)} %fusion.52), custom_call_target="Cholesky" | custom-call | tf_op jit(solution)/shard_map/jit(cholesky)/cholesky | solution.py:24
  686.7 9.8 %custom-call.39 = f32[1,128,128]{1,2,0:T(8,128)S(1)} custom-call(f32[1,128,128]{2,1,0:T(8,128)S(1)} %fusion.48), custom_call_target="InvertDiagBlocksLowerTriangular" | custom-call | tf_op jit(solution)/shard_map/triangular_solve/custom-call.5 | solution.py:26
  697.6 41.1 %psum.79 = f32[64,64]{0,1:T(8,128)S(1)} all-reduce(f32[64,64]{0,1:T(8,128)S(1)} %fusion.138), channel_id=1, replica_groups=mesh['sub'=8,'row'=4] {'sub','row'}, use_global_device_ids=true, to_apply=%region_19.27 | all-reduce | flops 4096 | bytes 32768 | tf_op jit(solution)/shard_map/psum | solution.py:117
  738.9 5.8 cholesky.171
  746.1 4.9 custom-call.40
  (223 shorter events, 55.1 us)
Async XLA Ops:
  8.0 4.1 copy-start
  8.0 4.5 copy-start.36
  8.0 46.3 %reduce-scatter.13.cloned.1.call-start = ((), (), s32[]{:S(2)}) async-start(), calls=%async_computation.8 | async-start | bytes 884736 | tf_op jit(solution)/shard_map/reduce_scatter | solution.py:73
  11.0 0.6 copy-start.34
  11.2 3.2 copy-start.1
  11.2 3.8 copy-start.30
  14.3 42.3 %all-gather.4.cloned.1.call-start = ((), (), s32[]{:S(2)}) async-start(), calls=%async_computation.6 | async-start | bytes 1966080 | tf_op jit(solution)/shard_map/all_gather | solution.py:47
  14.9 67.1 %reduce-scatter.11.cloned.1.call-start = ((), (), s32[]{:S(2)}) async-start(), calls=%async_computation.7 | async-start | bytes 1966080 | tf_op jit(solution)/shard_map/reduce_scatter | solution.py:56
  15.0 1.8 copy-start.31
  15.0 6.5 copy-start.29
  28.0 1.7 copy-start.9
  28.0 4.1 copy-start.42
  29.6 24.1 %copy-start.4 = (f32[768,64]{0,1:T(8,128)S(1)}, f32[768,64]{0,1:T(8,128)}, u32[]{:S(2)}) copy-start(f32[768,64]{0,1:T(8,128)} %param.22) | copy-start | bytes 589828
  29.6 180.0 %reduce-scatter.19.cloned.1.call-start = ((), (), s32[]{:S(2)}) async-start(), calls=%async_computation.13 | async-start | bytes 884736 | tf_op jit(solution)/shard_map/reduce_scatter | solution.py:73
  32.1 129.0 %copy-start.32 = (s32[1024]{0:T(1024)}, s32[1024]{0:T(1024)S(1)}, u32[]{:S(2)}) copy-start(s32[1024]{0:T(1024)S(1)} %pad_clamp_fusion.2) | copy-start | bytes 12292
  33.7 20.0 %copy-start.35 = (s32[1024]{0:T(1024)}, s32[1024]{0:T(1024)S(1)}, u32[]{:S(2)}) copy-start(s32[1024]{0:T(1024)S(1)} %pad_clamp_fusion.1) | copy-start | bytes 12292
  53.7 7.0 copy-start.33
  66.1 20.8 %copy-start.39 = (s32[1,1,12]{2,1,0:T(1,128)S(1)}, s32[1,1,12]{2,1,0:T(1,128)}, u32[]{:S(2)}) copy-start(s32[1,1,12]{2,1,0:T(1,128)} %param.29) | copy-start | bytes 148
  82.0 4.8 copy-start.16
  86.9 56.0 %copy-start.28 = (f32[768]{0:T(1024)S(1)}, f32[768]{0:T(1024)}, u32[]{:S(2)}) copy-start(f32[768]{0:T(1024)} %param.24) | copy-start | bytes 9220
  87.7 0.8 copy-start.2
  87.7 56.9 %copy-start.37 = (s32[1,1,12]{2,1,0:T(1,128)S(1)}, s32[1,1,12]{2,1,0:T(1,128)}, u32[]{:S(2)}) copy-start(s32[1,1,12]{2,1,0:T(1,128)} %param.30) | copy-start | bytes 148
  142.1 0.7 copy-start.19
  143.2 19.1 %copy-start.5 = (f32[768,64]{0,1:T(8,128)}, f32[768,64]{0,1:T(8,128)S(1)}, u32[]{:S(2)}) copy-start(f32[768,64]{0,1:T(8,128)S(1)} %fusion.16) | copy-start | bytes 589828
  146.5 65.4 %reduce-scatter.15.cloned.1.call-start = ((), (), s32[]{:S(2)}) async-start(), calls=%async_computation.9 | async-start | bytes 983040 | tf_op jit(solution)/shard_map/reduce_scatter | solution.py:56
  161.1 176.1 %all-reduce.5.cloned.1.call-start = ((), (), s32[]{:S(2)}) async-start(), calls=%async_computation.10 | async-start | bytes 131072 | tf_op jit(solution)/shard_map/psum | solution.py:109
  185.5 4.8 copy-start.27
  190.4 19.3 %copy-start.43 = (s32[1,1,3]{2,1,0:T(1,128)S(1)}, s32[1,1,3]{2,1,0:T(1,128)}, u32[]{:S(2)}) copy-start(s32[1,1,3]{2,1,0:T(1,128)} %param.28) | copy-start | bytes 40
  208.6 9.9 %copy-start.40 = (s32[1,1,12]{2,1,0:T(1,128)S(1)}, s32[1,1,12]{2,1,0:T(1,128)}, u32[]{:S(2)}) copy-start(s32[1,1,12]{2,1,0:T(1,128)} %param.29) | copy-start | bytes 148
  214.1 4.4 copy-start.15
  214.1 4.4 copy-start.17
  214.1 5.0 copy-start.6
  214.1 5.0 copy-start.10
  214.1 5.0 copy-start.13
  214.1 6.6 copy-start.3
  220.7 322.7 %reduce-scatter.21.cloned.1.call-start = ((), (), s32[]{:S(2)}) async-start(), calls=%async_computation.14 | async-start | bytes 884736 | tf_op jit(solution)/shard_map/reduce_scatter | solution.py:73
  222.1 196.4 %copy-start.20 = (f32[768,64]{0,1:T(8,128)S(1)}, f32[768,64]{0,1:T(8,128)}, u32[]{:S(2)}) copy-start(f32[768,64]{0,1:T(8,128)} %copy-done.19) | copy-start | bytes 589828
  364.6 109.9 %copy-start.38 = (s32[1,1,12]{2,1,0:T(1,128)S(1)}, s32[1,1,12]{2,1,0:T(1,128)}, u32[]{:S(2)}) copy-start(s32[1,1,12]{2,1,0:T(1,128)} %param.30) | copy-start | bytes 148
  418.1 54.4 %copy-start.24 = (f32[1,64,64]{1,2,0:T(8,128)}, f32[1,64,64]{1,2,0:T(8,128)S(1)}, u32[]{:S(2)}) copy-start(f32[1,64,64]{1,2,0:T(8,128)S(1)} %custom-call.32) | copy-start | bytes 49156
  419.8 52.9 %copy-start.11 = (f32[768,64]{0,1:T(8,128)}, f32[768,64]{0,1:T(8,128)S(1)}, u32[]{:S(2)}) copy-start(f32[768,64]{0,1:T(8,128)S(1)} %convolution_bitcast_fusion.13) | copy-start | bytes 589828
  473.1 17.9 %copy-start.7 = (f32[768,64]{0,1:T(8,128)}, f32[768,64]{0,1:T(8,128)S(1)}, u32[]{:S(2)}) copy-start(f32[768,64]{0,1:T(8,128)S(1)} %fusion.14) | copy-start | bytes 589828
  476.4 69.2 %reduce-scatter.17.cloned.1.call-start = ((), (), s32[]{:S(2)}) async-start(), calls=%async_computation.11 | async-start | bytes 983040 | tf_op jit(solution)/shard_map/reduce_scatter | solution.py:56
  491.0 180.9 %all-reduce.7.cloned.1.call-start = ((), (), s32[]{:S(2)}) async-start(), calls=%async_computation.12 | async-start | bytes 131072 | tf_op jit(solution)/shard_map/psum | solution.py:109
  515.6 4.1 copy-start.26
  519.6 22.4 %copy-start.21 = (f32[768,64]{0,1:T(8,128)S(1)}, f32[768,64]{0,1:T(8,128)}, u32[]{:S(2)}) copy-start(f32[768,64]{0,1:T(8,128)} %fusion.46) | copy-start | bytes 589828
  519.6 22.4 %copy-start.25 = (f32[1,64,64]{1,2,0:T(8,128)S(1)}, f32[1,64,64]{1,2,0:T(8,128)}, u32[]{:S(2)}) copy-start(f32[1,64,64]{1,2,0:T(8,128)} %copy-done.24) | copy-start | bytes 49156
  519.6 23.4 %copy-start.22 = (f32[768,64]{0,1:T(8,128)S(1)}, f32[768,64]{0,1:T(8,128)}, u32[]{:S(2)}) copy-start(f32[768,64]{0,1:T(8,128)} %get-tuple-element.16) | copy-start | bytes 589828
  519.6 23.8 %copy-start.44 = (s32[1,1,3]{2,1,0:T(1,128)S(1)}, s32[1,1,3]{2,1,0:T(1,128)}, u32[]{:S(2)}) copy-start(s32[1,1,3]{2,1,0:T(1,128)} %param.28) | copy-start | bytes 40
  542.0 11.4 %copy-start.41 = (s32[1,1,12]{2,1,0:T(1,128)S(1)}, s32[1,1,12]{2,1,0:T(1,128)}, u32[]{:S(2)}) copy-start(s32[1,1,12]{2,1,0:T(1,128)} %param.29) | copy-start | bytes 148
  549.7 3.7 copy-start.14
  549.7 3.7 copy-start.18
  549.7 4.6 copy-start.8
  549.7 4.6 copy-start.23
  553.4 2.1 copy-start.12
Sparse Core Ops, SparseCore 0:
  14.4 35.0 reduce-scatter.12
  52.8 29.1 reduce-scatter.10
  146.7 32.2 reduce-scatter.18
  181.7 24.2 reduce-scatter.14
  476.6 32.2 reduce-scatter.20
  511.9 24.2 reduce-scatter.16
Sparse Core Ops, SparseCore 1:
  16.8 33.5 all-gather.3
  220.7 116.4 all-reduce.4
  555.6 116.2 all-reduce.6
where the time goes:
time: 770 us; the launch traced here: 761 us
  blocking collectives  315 us (41%)
  waiting for transfers between devices  170 us (22%)
  other arithmetic  96.5 us (13%)
  matrix products  87.6 us (11%)
  local copies, waits for them, and re-layouts  74.5 us (10%)
  between operations  17.4 us (2%)
    psum x2, waiting for transfers between devices, local(): lax.psum((gram_product(basis, image_b), gram_product(basis, image_x)), ('...  153 us
    psum x2, blocking collectives, local(): lengths = lax.psum(gram_product(moved, moved), ('sub', 'row'))  82.2 us
    psum x2, blocking collectives, project(): lax.psum((gram_product(current, current), gram_product(current, image_x))...  79.6 us
    psum x2, blocking collectives, local(): lax.psum((gram_product(basis, image_b), gram_product(basis, image_x)), ('...  77.5 us
    all_gather x3, blocking collectives, apply_blocks(): lax.all_gather(boundary, 'sub', axis=0, tiled=True).reshape(-1, KB, width)  49.7 us
    another operation x12, other arithmetic, chol_solve(): factor = jnp.linalg.cholesky(matrix)  37.8 us
    another operation x8, other arithmetic, chol_solve(): lax.linalg.triangular_solve(factor, halfway, left_side=True, lower=True,...  32 us
    all_gather x2, blocking collectives, apply_blocks(): lax.all_gather(vector, 'row', axis=0, tiled=True).reshape(-1, KB, width)  25.6 us
  transfers between devices with their start and end apart: 9, of which 3 were waited for; matrix products, arithmetic and copies ran while one was open for 15% of the time, Pallas kernels for 0%

commit v1 on v0

v1 whole, which is shorter than its diff:
```python
import functools

import jax
import jax.numpy as jnp
from jax import lax
from jax.experimental import pallas as pl
from jax.experimental.pallas import tpu as pltpu
from jax.sharding import PartitionSpec as P

f32 = jnp.float32
bf16 = jnp.bfloat16
precise_mode = lax.Precision.HIGHEST
VMEM = pltpu.VMEM
SMEM = pltpu.SMEM


def nn(a, b):
    return lax.dot_general(a, b, (((1,), (0,)), ((), ())), precision=precise_mode, preferred_element_type=f32)


def nt(a, b):
    return lax.dot_general(a, b, (((1,), (1,)), ((), ())), precision=precise_mode, preferred_element_type=f32)


def two_parts(block):
    high = block.astype(bf16).astype(f32)
    return jnp.concatenate([high, block - high], axis=1).astype(bf16)


def write_wire(vector, bnd, wire, edge):
    blocks, kb = wire.shape[0], wire.shape[2] // 2
    for i in range(blocks):
        wire[i] = two_parts(vector[:, i * kb : (i + 1) * kb])
    for q in range(edge.shape[0]):
        edge[q] = wire[bnd[q]]


def loop(count, body):
    def step(i, carry):
        body(i)
        return carry

    lax.fori_loop(0, count, step, 0)


def fill_halo(wires, edges, pos, halo):
    n_row, n_z = len(wires), len(edges)
    lb, ifr = wires[0][2], edges[0][0][2]
    for k, (wire, offset, count) in enumerate(wires):
        start = (pos[0] ^ k) * lb

        def copy(i, wire=wire, offset=offset, start=start):
            halo[start + i] = wire[offset + i]

        loop(count, copy)
    for k, pair in enumerate(edges):
        for other, (edge, offset, count) in enumerate(pair):
            start = n_row * lb + (((pos[1] // 2) ^ k) * 2 + ((pos[1] % 2) ^ other)) * ifr
            for q in range(count):
                halo[start + q] = edge[offset + q]


def write_halves(table, pos, keep, send):
    height = keep.shape[0]
    core = pos[1] % 2
    keep[...] = table[pl.ds(pl.multiple_of(core * height, 8), height), :]
    send[...] = table[pl.ds(pl.multiple_of((1 - core) * height, 8), height), :]


def read_halves(mine, other, pos, table):
    height = mine.shape[0]
    core = pos[1] % 2
    table[pl.ds(pl.multiple_of(core * height, 8), height), :] = mine[...]
    table[pl.ds(pl.multiple_of((1 - core) * height, 8), height), :] = other[...]


def forward(halo, wire, stored, diagonal, where, out, diag_out):
    lb, kb = wire.shape[0], wire.shape[2] // 2
    groups = stored.shape[2] // (2 * kb)
    for i in range(0, lb, 2):
        sums, diags = [], []
        for m in (i, i + 1):
            row = jnp.concatenate([halo[where[m * groups + g]] for g in range(groups)], axis=1)
            sums.append(lax.dot_general(row, stored[m], (((1,), (1,)), ((), ())), preferred_element_type=f32))
            diags.append(lax.dot_general(wire[m], diagonal[m], (((1,), (1,)), ((), ())), preferred_element_type=f32))
        out[:, i * kb : (i + 2) * kb] = jnp.concatenate(sums, axis=1)
        diag_out[:, i * kb : (i + 2) * kb] = jnp.concatenate(diags, axis=1)


def returned(index, own, rows, edge_own, edges, bnd, back):
    lb, kb = back.shape[0], back.shape[2]
    ifr = bnd.shape[0]
    for i in range(lb):
        total = rows[0][index * lb + i].astype(f32)
        for row in rows[1:]:
            total = total + row[index * lb + i].astype(f32)
        back[i] = own[index * lb + i] + (total[:, :kb] + total[:, kb:])
    for q in range(ifr):
        total = edges[0][index * ifr + q].astype(f32)
        for edge in edges[1:]:
            total = total + edge[index * ifr + q].astype(f32)
        back[bnd[q]] = back[bnd[q]] + edge_own[index * ifr + q] + (total[:, :kb] + total[:, kb:])


def add_returned(back, target):
    lb, kb = back.shape[0], back.shape[2]
    for i in range(0, lb, 2):
        span = slice(i * kb, (i + 2) * kb)
        target[:, span] = target[:, span] + jnp.concatenate([back[i], back[i + 1]], axis=1)


def eliminate(table, full):
    order = table.shape[0]
    rows = lax.broadcasted_iota(jnp.int32, table.shape, 0)
    for j in range(0, order, 2):
        one, two = table[j : j + 1, :], table[j + 1 : j + 2, :]
        a, b = one[:, j : j + 1], one[:, j + 1 : j + 2]
        c, d = two[:, j : j + 1], two[:, j + 1 : j + 2]
        scale = 1.0 / (a * d - b * c)
        first = (d * scale) * one - (b * scale) * two
        second = (a * scale) * two - (c * scale) * one
        moved = table - table[:, j : j + 1] * first - table[:, j + 1 : j + 2] * second
        if full:
            table = jnp.where(rows == j, first, jnp.where(rows == j + 1, second, moved))
        else:
            table = jnp.where(rows > j + 1, moved, jnp.where(rows == j + 1, two - (c / a) * one, table))
    return table


def unit(order):
    return (
        lax.broadcasted_iota(jnp.int32, (order, order), 0) == lax.broadcasted_iota(jnp.int32, (order, order), 1)
    ).astype(f32)


def inverse(matrix):
    order = matrix.shape[0]
    return eliminate(jnp.concatenate([matrix, unit(order)], axis=1), True)[:, order:]


def cholesky_inverse(matrix):
    order = matrix.shape[0]
    done = eliminate(jnp.concatenate([matrix, unit(order)], axis=1), False)
    pivots = jnp.sum(done[:, :order] * unit(order), axis=1, keepdims=True)
    return done[:, order:] * (1.0 / jnp.sqrt(pivots))


def coefficients(table, gram, xp, pp, pax, pap_inverse, total_rows):
    n = gram.shape[0]
    waw, wap = table[0:n, :n], table[0:n, n:]
    wax, wx = table[n : 2 * n, :n], table[n : 2 * n, n:]
    wp, ww = table[2 * n : 3 * n, :n], table[2 * n : 3 * n, n:]
    waw = waw + waw.T
    first = nn(pap_inverse, wap.T)
    if pax is None:
        rhs = -wax
    else:
        second = nn(pap_inverse, pax)
        rhs = nn(wap, second) - wax
    schur = waw - nn(wap, first)
    zw = eliminate(jnp.concatenate([schur, rhs], axis=1), True)[:, n:]
    zp = -nn(first, zw)
    if pax is not None:
        zp = zp - second
    cross = nn(wx.T, zw) + nn(xp, zp)
    zwt, zpt = zw.T, zp.T
    inner = nn(zwt, nn(ww, zw) + nn(wp, zp)) + nn(zpt, nn(wp.T, zw) + nn(pp, zp))
    lengths = (gram + cross + cross.T + inner) / total_rows
    return zw, zp, zwt, zpt, cross, inner, wax, cholesky_inverse(lengths)


def prepare_kernel(groups, base, vals, faces, rows, cols, face_rows, face_src, stored, joined, diagonal, where):
    lb, kb = faces.shape[0], faces.shape[1]
    for k in range(lb):
        diagonal[k] = vals[k]
    for g in range(groups):
        half = (g % 2) * kb
        for m in range(lb):
            if g < groups - 1:
                k = (g + 1) * lb + m
                i, target, block = rows[k], cols[k], vals[k]
            else:
                i, target, block = face_rows[m], base + face_src[m], faces[m]
            stored[i, :, 2 * kb * g : 2 * kb * (g + 1)] = block
            joined[i, :, kb * g : kb * (g + 1)] = block[:, half : half + kb]
            where[i * groups + g] = target


def wire_kernel(vector, bnd, wire, edge):
    write_wire(vector, bnd, wire, edge)


def partial_kernel(n_row, n_z, count, extra, *refs):
    refs = list(refs)
    take = lambda number: [refs.pop(0) for _ in range(number)]
    wires = take(count)
    joined, where, pos = take(3)
    more_wire, more_edge = take(2) if extra else (None, None)
    own, core_keep, core_send = take(3)
    row_outs, acc = refs[:-1], refs[-1]
    lb, kb = wires[0].shape[0], wires[0].shape[2] // 2
    ifr = core_keep.shape[0] // (count * n_z)
    groups = joined.shape[2] // kb
    low = lax.broadcasted_iota(jnp.int32, (kb, 2 * kb), 1) < kb
    core = pos[1] % 2
    for v, wire in enumerate(wires):
        acc[...] = jnp.zeros(acc.shape, f32)

        def step(i):
            blocks = jnp.concatenate([joined[i], joined[i]], axis=0)
            out = jnp.dot(wire[i], blocks, preferred_element_type=f32)
            for t in range(groups // 2):
                tile = out[:, 2 * kb * t : 2 * kb * (t + 1)]
                one = where[i * groups + 2 * t]
                two = where[i * groups + 2 * t + 1]
                acc[one] = acc[one] + jnp.where(low, tile, 0.0)
                acc[two] = acc[two] + jnp.where(low, 0.0, tile)

        loop(lb, step)

        def folded(index):
            block = acc[index]
            return block[:, :kb] + block[:, kb:]

        for k in range(n_row):
            start = (pos[0] ^ k) * lb

            def emit(i, k=k, start=start):
                if k == 0:
                    own[v * lb + i] = folded(start + i)
                else:
                    row_outs[k - 1][v * lb + i] = two_parts(folded(start + i))

            loop(lb, emit)

        def emit_edge(z):
            for q in range(ifr):
                spot = (v * n_z + z) * ifr + q
                core_keep[spot] = folded(n_row * lb + (z * 2 + core) * ifr + q)
                core_send[spot] = two_parts(folded(n_row * lb + (z * 2 + 1 - core) * ifr + q))

        loop(n_z, emit_edge)
    if extra:
        for k in range(1, n_row):
            row_outs[k - 1][pl.ds(count * lb, lb)] = more_wire[...]
        core_send[pl.ds(count * n_z * ifr, ifr)] = more_edge[...]


def pair_kernel(n_z, count, extra, keep, got, pos, *refs):
    refs = list(refs)
    more_edge = refs.pop(0) if extra else None
    own, outs = refs[0], refs[1:]
    ifr, kb = own.shape[0] // count, own.shape[2]
    for k in range(n_z):
        z = (pos[1] // 2) ^ k
        for v in range(count):
            for q in range(ifr):
                spot = (v * n_z + z) * ifr + q
                there = got[spot].astype(f32)
                total = keep[spot] + (there[:, :kb] + there[:, kb:])
                if k == 0:
                    own[v * ifr + q] = total
                else:
                    outs[k - 1][v * ifr + q] = two_parts(total)
        if extra and k > 0:
            outs[k - 1][pl.ds(count * ifr, ifr)] = more_edge[...]
            outs[k - 1][pl.ds((count + 1) * ifr, ifr)] = got[pl.ds(count * n_z * ifr, ifr)]


def split_halo(refs, n_row, n_z):
    wires = [refs.pop(0) for _ in range(n_row)]
    same, other = refs.pop(0), refs.pop(0)
    lb, ifr = wires[0].shape[0], same.shape[0] // n_z
    return [(wire, 0, lb) for wire in wires], [((same, k * ifr, ifr), (other, k * ifr, ifr)) for k in range(n_z)]


def x_image_kernel(n_row, n_z, *refs):
    refs = list(refs)
    wires, edges = split_halo(refs, n_row, n_z)
    stored, diagonal, where, pos, x, half, diag, table, halo = refs
    n = x.shape[0]
    fill_halo(wires, edges, pos, halo)
    forward(halo, wires[0][0], stored, diagonal, where, half, diag)
    half[...] = half[...] + 0.5 * diag[...]
    table[...] = nt(x[...], jnp.concatenate([half[...], x[...]], axis=0))


def p_image_kernel(n_row, n_z, ifr, *refs):
    refs = list(refs)
    wire, edge, core_got = refs[:3]
    rows, edges = refs[3 : 2 + n_row], refs[2 + n_row : 1 + n_row + n_z]
    stored, diagonal, where, pos, half, diag, halo = refs[1 + n_row + n_z :]
    lb = wire.shape[0]
    wires = [(wire, 0, lb)] + [(row, lb, lb) for row in rows]
    pairs = [((edge, 0, ifr), (core_got, n_z * ifr, ifr))]
    pairs += [((got, ifr, ifr), (got, 2 * ifr, ifr)) for got in edges]
    fill_halo(wires, pairs, pos, halo)
    forward(halo, wire, stored, diagonal, where, half, diag)
    half[...] = half[...] + 0.5 * diag[...]


def take_returned(refs, n_row, n_z):
    own = refs.pop(0)
    rows = [refs.pop(0) for _ in range(n_row - 1)]
    edge_own = refs.pop(0)
    return own, rows, edge_own, [refs.pop(0) for _ in range(n_z - 1)]


def update_kernel(n_row, n_z, *refs):
    refs = list(refs)
    back_parts = take_returned(refs, n_row, n_z)
    bnd, table, x, half, diag, precond, ax, energy, w, wire, edge, back = refs
    n = x.shape[0]
    returned(0, *back_parts, bnd, back)
    ax[...] = half[...] + 0.5 * diag[...]
    add_returned(back, ax)
    stored, gram = table[:, 0:n], table[:, n:]
    total = stored + stored.T
    energy[...] = total
    ritz = nn(total, inverse(0.5 * (gram + gram.T)))
    w[...] = precond[...] * (ax[...] - nn(ritz, x[...]))
    write_wire(w, bnd, wire, edge)


def update_image_kernel(n_row, n_z, first, *refs):
    refs = list(refs)
    wires, edges = split_halo(refs, n_row, n_z)
    stored, diagonal, where, pos, w, x, p, ax, ap, half, diag, keep, send, halo, table = refs
    n = w.shape[0]
    fill_halo(wires, edges, pos, halo)
    forward(halo, wires[0][0], stored, diagonal, where, half, diag)
    half[...] = half[...] + 0.5 * diag[...]
    here = w[...]
    table[0:n, :] = nt(here, jnp.concatenate([half[...], ap[...]], axis=0))
    table[n : 2 * n, :] = nt(here, jnp.concatenate([ax[...], x[...]], axis=0))
    table[2 * n : 3 * n, :] = nt(here, jnp.concatenate([p[...], here], axis=0))
    if first:
        table[0:n, n:] = table[0:n, n:] + nt(half[...], p[...])
        table[3 * n : 4 * n, :] = nt(p[...], jnp.concatenate([ax[...], ap[...]], axis=0))
        table[4 * n : 5 * n, :] = nt(p[...], jnp.concatenate([x[...], p[...]], axis=0))
    write_halves(table, pos, keep, send)


def move_kernel(n_row, n_z, total_rows, *refs):
    refs = list(refs)
    back_parts = take_returned(refs, n_row, n_z)
    mine, other, pos, bnd, gram, energy, x, p, ax, ap, ap_diag, w, aw, aw_diag, precond = refs[:15]
    x_out, ax_out, w_out, wire, edge, step_x, step_a, small, table, back = refs[15:]
    n = x.shape[0]
    read_halves(mine, other, pos, table)
    gram_here = gram[:, n:]
    pax, pap = table[3 * n : 4 * n, 0:n], table[3 * n : 4 * n, n:]
    px, pp = table[4 * n : 5 * n, 0:n], table[4 * n : 5 * n, n:]
    zw, zp, zwt, zpt, cross, inner, wax, scale = coefficients(
        table, 0.5 * (gram_here + gram_here.T), px.T, pp, pax, inverse(pap + pap.T), total_rows
    )
    step_a[...] = nn(zpt, ap[...] + 0.5 * ap_diag[...]) + nn(zwt, aw[...] + 0.5 * aw_diag[...])
    returned(0, *back_parts, bnd, back)
    for i in range(0, back.shape[0], 2):
        pair = jnp.concatenate([back[i], back[i + 1]], axis=1)
        span = slice(i * back.shape[2], (i + 2) * back.shape[2])
        step_a[:, span] = step_a[:, span] + nn(zpt, pair)
    returned(1, *back_parts, bnd, back)
    for i in range(0, back.shape[0], 2):
        pair = jnp.concatenate([back[i], back[i + 1]], axis=1)
        span = slice(i * back.shape[2], (i + 2) * back.shape[2])
        step_a[:, span] = step_a[:, span] + nn(zwt, pair)
    step_x[...] = nn(zwt, w[...]) + nn(zpt, p[...])
    x_out[...] = nn(scale, x[...] + step_x[...])
    ax_out[...] = nn(scale, ax[...] + step_a[...])
    gain = nn(wax.T, zw) + nn(pax.T, zp)
    gain = 0.5 * (gain + gain.T)
    ritz = nn(scale, nn(energy[...] + gain, scale.T)) / total_rows
    w_out[...] = precond[...] * (ax_out[...] - nn(ritz, x_out[...]))
    write_wire(w_out, bnd, wire, edge)
    small[0:n, :] = -gain
    small[n : 2 * n, :] = cross + inner
    small[2 * n : 3 * n, :] = inner
    small[3 * n : 4 * n, :] = scale


def settle_kernel(small, step_x, step_a, p_out, ap_out, state):
    n = small.shape[1]
    scale = small[3 * n : 4 * n, :]
    scale_t = scale.T
    p_out[...] = nn(scale, step_x[...])
    ap_out[...] = nn(scale, step_a[...])
    state[0:n, :] = inverse(nn(scale, nn(small[0:n, :], scale_t)))
    state[n : 2 * n, :] = nn(scale, nn(small[n : 2 * n, :], scale_t))
    state[2 * n : 3 * n, :] = nn(scale, nn(small[2 * n : 3 * n, :], scale_t))


def finish_kernel(total_rows, mine, other, pos, state, x, p, w, x_out, p_out, table):
    n = x.shape[0]
    read_halves(mine, other, pos, table)
    zw, zp, zwt, zpt, _, _, _, scale = coefficients(
        table,
        unit(n) * total_rows,
        state[n : 2 * n, :],
        state[2 * n : 3 * n, :],
        None,
        state[0:n, :],
        total_rows,
    )
    step = nn(zwt, w[...]) + nn(zpt, p[...])
    x_out[...] = nn(scale, x[...] + step)
    p_out[...] = nn(scale, step)


def run(kernel, name, outs, ins, scratch=(), smem=(), smem_outs=(), flops=1000000):
    in_specs = [pl.BlockSpec(memory_space=SMEM if i in smem else VMEM) for i in range(len(ins))]
    out_specs = [pl.BlockSpec(memory_space=SMEM if i in smem_outs else VMEM) for i in range(len(outs))]
    moved = sum(a.size * a.dtype.itemsize for a in ins) + sum(o.size * o.dtype.itemsize for o in outs)
    return pl.pallas_call(
        kernel,
        name=name,
        out_shape=outs,
        in_specs=in_specs,
        out_specs=out_specs,
        scratch_shapes=list(scratch),
        compiler_params=pltpu.CompilerParams(vmem_limit_bytes=48 * 1024 * 1024),
        cost_estimate=pl.CostEstimate(flops=flops, bytes_accessed=moved, transcendentals=0),
    )(*ins)


def shaped(*shape, dtype=f32):
    return jax.ShapeDtypeStruct(shape, dtype)


def local(n_sub, n_row, modes, search, precond, in_row, in_col, in_val, bnd_rows, if_row, if_src, if_val):
    nin, kb = in_val.shape[2], in_val.shape[3]
    rows, n = modes.shape
    lb = rows // kb
    ifr = bnd_rows.shape[2]
    groups = nin // lb
    n_z = n_sub // 2
    total_rows = float(rows * n_sub * n_row)
    halo_blocks = n_row * lb + n_sub * ifr
    bnd = bnd_rows[0, 0]
    me_row, me_sub = lax.axis_index("row"), lax.axis_index("sub")
    pos = jnp.stack([me_row, me_sub]).astype(jnp.int32)
    after = lax.optimization_barrier

    def row_send(value, k):
        return lax.ppermute(value, "row", [(r, r ^ k) for r in range(n_row)])

    def sub_send(value, k):
        return lax.ppermute(value, "sub", [(s, s ^ k) for s in range(n_sub)])

    def wire(*shape):
        return shaped(*shape, n, 2 * kb, dtype=bf16)

    def halo_of(own, edge):
        rows_got = [row_send(own, k) for k in range(1, n_row)]
        same = jnp.concatenate([edge] + [sub_send(edge, 2 * k) for k in range(1, n_z)], axis=0)
        return [own] + rows_got + [same, sub_send(same, 1)]

    def doubled(value):
        k = 1
        while k < n_row:
            value = value + row_send(value, k)
            k *= 2
        k = 2
        while k < n_sub:
            value = value + sub_send(value, k)
            k *= 2
        return value

    def sum_halves(keep, send):
        mine = doubled(keep + sub_send(send, 1))
        return [mine, sub_send(mine, 1)]

    def partials(wires, more):
        m, e = len(wires), 1 if more else 0
        outs = [shaped(m * lb, n, kb), shaped(m * n_z * ifr, n, kb), wire((m * n_z + e) * ifr)]
        outs += [wire((m + e) * lb)] * (n_row - 1)
        return run(
            functools.partial(partial_kernel, n_row, n_z, m, e > 0),
            "partials",
            outs,
            wires + [joined, where, pos] + more,
            [VMEM((halo_blocks, n, 2 * kb), f32)],
            smem=(m + 1, m + 2),
        )

    def send_partials(parts, m, more):
        own, keep, send, *row_parts = parts
        e = 1 if more else 0
        rows_got = [row_send(row_parts[k - 1], k) for k in range(1, n_row)]
        got = sub_send(send, 1)
        edge_own, *outs = run(
            functools.partial(pair_kernel, n_z, m, e > 0),
            "pair",
            [shaped(m * ifr, n, kb)] + [wire((m + 2 * e) * ifr)] * (n_z - 1),
            [keep, got, pos] + more,
            smem=(2,),
        )
        edges_got = [sub_send(outs[k - 1], 2 * k) for k in range(1, n_z)]
        return [own] + rows_got + [edge_own] + edges_got, got

    x, p = modes.T, search.T
    scaling = precond.reshape(1, rows)
    wire_shapes = [wire(lb), wire(ifr)]
    x_wire, x_edge = run(wire_kernel, "wire", wire_shapes, [x, bnd], smem=(1,))
    x_halo = halo_of(x_wire, x_edge)
    p_wire, p_edge = run(wire_kernel, "wire", wire_shapes, [p, bnd], smem=(1,))
    twice = jnp.concatenate([in_val[0, 0], in_val[0, 0]], axis=-1)
    twice_face = jnp.concatenate([if_val[0, 0], if_val[0, 0]], axis=-1)
    stored, joined, diagonal, where = run(
        functools.partial(prepare_kernel, groups, n_row * lb),
        "prepare",
        [
            shaped(lb, kb, groups * 2 * kb, dtype=bf16),
            shaped(lb, kb, groups * kb, dtype=bf16),
            shaped(lb, kb, 2 * kb, dtype=bf16),
            shaped(lb * groups, dtype=jnp.int32),
        ],
        [twice, twice_face, in_row[0, 0], in_col[0, 0], if_row[0, 0], if_src[0, 0]],
        smem=(2, 3, 4, 5),
        smem_outs=(3,),
    )
    x_parts = partials([x_wire], [p_wire, p_edge])
    blocks = [stored, diagonal, where, pos]
    halo_scratch = VMEM((halo_blocks, n, 2 * kb), bf16)
    back_scratch = VMEM((lb, n, kb), f32)
    whole = shaped(n, rows)

    count = len(x_halo)
    half_x, diag_x, table = run(
        functools.partial(x_image_kernel, n_row, n_z),
        "x_image",
        [whole, whole, shaped(n, 2 * n)],
        x_halo + blocks + [x],
        [halo_scratch],
        smem=(count + 2, count + 3),
    )
    table, x_parts = after((table, x_parts))
    table = doubled(table)
    table = table + sub_send(table, 1)
    x_back, core_got = send_partials(x_parts, 1, [p_edge])
    p_rows, p_edges = x_back[1:n_row], x_back[n_row + 1 :]
    count = len(x_back)
    ax, energy, w, w_wire, w_edge = run(
        functools.partial(update_kernel, n_row, n_z),
        "update",
        [whole, shaped(n, n), whole] + wire_shapes,
        x_back + [bnd, table, x, half_x, diag_x, scaling],
        [back_scratch],
        smem=(count,),
    )
    w_halo = halo_of(w_wire, w_edge)
    count = 1 + n_row + n_z
    half_p, diag_p = run(
        functools.partial(p_image_kernel, n_row, n_z, ifr),
        "p_image",
        [whole, whole],
        [p_wire, p_edge, core_got] + p_rows + p_edges + blocks,
        [halo_scratch],
        smem=(count + 2, count + 3),
    )
    w_parts = partials([p_wire, w_wire], [])

    def update_image(first, halo, w, x, p, ax, ap):
        count = len(halo)
        height = (5 if first else 3) * n
        return run(
            functools.partial(update_image_kernel, n_row, n_z, first),
            "update_image",
            [whole, whole, shaped(height // 2, 2 * n), shaped(height // 2, 2 * n)],
            halo + blocks + [w, x, p, ax, ap],
            [halo_scratch, VMEM((height, 2 * n), f32)],
            smem=(count + 2, count + 3),
        )

    half_w, diag_w, keep, send = update_image(True, w_halo, w, x, p, ax, half_p)
    keep, send, w_parts = after((keep, send, w_parts))
    halves = sum_halves(keep, send)
    w_back, _ = send_partials(w_parts, 2, [])
    count = len(w_back)
    x, ax, w, w_wire, w_edge, step_x, step_a, small = run(
        functools.partial(move_kernel, n_row, n_z, total_rows),
        "move",
        [whole] * 3 + wire_shapes + [whole, whole, shaped(4 * n, n)],
        w_back + halves + [pos, bnd, table, energy, x, p, ax, half_p, diag_p, w, half_w, diag_w, scaling],
        [VMEM((5 * n, 2 * n), f32), back_scratch],
        smem=(count + 2, count + 3),
    )
    w_halo = halo_of(w_wire, w_edge)
    p, ap, state = run(settle_kernel, "settle", [whole, whole, shaped(3 * n, n)], [small, step_x, step_a])
    _, _, keep, send = update_image(False, w_halo, w, x, p, ax, ap)
    halves = sum_halves(keep, send)
    x, p = run(
        functools.partial(finish_kernel, total_rows),
        "finish",
        [whole, whole],
        halves + [pos, state, x, p, w],
        [VMEM((3 * n, 2 * n), f32)],
        smem=(2,),
    )
    return (x.T, p.T)


def solution(mesh):
    return jax.shard_map(
        functools.partial(local, mesh.shape["sub"], mesh.shape["row"]),
        mesh=mesh,
        in_specs=(
            P(("sub", "row"), None),
            P(("sub", "row"), None),
            P(("sub", "row")),
            P("sub", "row", None),
            P("sub", "row", None),
            P("sub", "row", None, None, None),
            P("sub", "row", None),
            P("sub", "row", None),
            P("sub", "row", None),
            P("sub", "row", None, None, None),
        ),
        out_specs=(P(("sub", "row"), None), P(("sub", "row"), None)),
        check_vma=False,
    )
```

time: 770 us -> 270 us (0.35); the launches traced: 761 us -> 270 us
  blocking collectives: 315 us -> 0 us
  Pallas kernels: 0 us -> 120 us
  other arithmetic: 96.5 us -> 3.16 us
  waiting for transfers between devices: 170 us -> 77.2 us
  matrix products: 87.6 us -> 0 us
  local copies, waits for them, and re-layouts: 74.5 us -> 5.84 us
  starting transfers between devices: 0.38 us -> 62.2 us
  between operations: 17.4 us -> 1.17 us
    psum x6 -> x0, blocking collectives: 239 us -> none  [the longest x2 82.2 us: local(): lengths = lax.psum(gram_product(moved, moved), ('sub', 'row'))]
    psum x2 -> x0, waiting for transfers between devices: 153 us -> none  [local(): lax.psum((gram_product(basis, image_b), gram_product(basis, image_x)), ('...]
    pallas_call x0 -> x15, Pallas kernels: none -> 120 us  [run(): pl.pallas_call(kernel, name=name, out_shape=outs, in_specs=in_specs, out_...]
    another operation x30 -> x1, other arithmetic: 93.9 us -> 0.08 us  [local(): pos = jnp.stack([me_row, me_sub]).astype(jnp.int32)]
    dot_general x42 -> x0, matrix products: 80.8 us -> none  [the longest x3 17.9 us: apply_blocks(): jnp.einsum('kij,kjw->kiw', vals_here, group[cols_here], precision=precise...]
    ppermute x0 -> x52, waiting for transfers between devices: none -> 77.2 us  [the longest x21 42.7 us: row_send(): return lax.ppermute(value, 'row', [(r, r ^ k) for r in range(n_row)])]
    all_gather x5 -> x0, blocking collectives: 75.3 us -> none  [the longest x3 49.7 us: apply_blocks(): lax.all_gather(boundary, 'sub', axis=0, tiled=True).reshape(-1, KB, width)]
    ppermute x0 -> x52, starting transfers between devices: none -> 62.2 us  [the longest x31 37.2 us: sub_send(): return lax.ppermute(value, 'sub', [(s, s ^ k) for s in range(n_sub)])]
  transfers between devices with their start and end apart: 9 -> 52, of which waited for: 3 -> 20; matrix products, arithmetic and copies ran while one was open for 15% -> 3% of each run, Pallas kernels for 0% -> 17%
where the time goes in v1:
time: 270 us
  Pallas kernels  120 us (44%)
  waiting for transfers between devices  77.2 us (29%)
  starting transfers between devices  62.2 us (23%)
  local copies, waits for them, and re-layouts  5.84 us (2%)
  other arithmetic  3.16 us (1%)
    pallas_call x15, Pallas kernels, run(): pl.pallas_call(kernel, name=name, out_shape=outs, in_specs=in_specs, out_...  120 us
    ppermute x21, waiting for transfers between devices, row_send(): return lax.ppermute(value, 'row', [(r, r ^ k) for r in range(n_row)])  42.7 us
    ppermute x31, starting transfers between devices, sub_send(): return lax.ppermute(value, 'sub', [(s, s ^ k) for s in range(n_sub)])  37.2 us
    ppermute x31, waiting for transfers between devices, sub_send(): return lax.ppermute(value, 'sub', [(s, s ^ k) for s in range(n_sub)])  34.5 us
    ppermute x21, starting transfers between devices, row_send(): return lax.ppermute(value, 'row', [(r, r ^ k) for r in range(n_row)])  25 us
    unnamed x32, local copies, waits for them, and re-layouts  5.8 us
  transfers between devices with their start and end apart: 52, of which 20 were waited for; matrix products, arithmetic and copies ran while one was open for 3% of the time, Pallas kernels for 17%

profile of v1, /device:TPU:0, one launch (start us, length us, event | category | flops | bytes accessed | tf_op | source)
XLA Modules:
  0.0 270.0 jit_solution(2369796162496960919)
XLA Ops:
  0.6 0.9 copy-done
  1.6 0.7 copy-done.3
  2.2 0.7 wire.2
  2.9 5.1 %collective-permute-start.5 = (bf16[3,64,128]{2,1,0:T(8,128)(2,1)S(1)}, bf16[3,64,128]{2,1,0:T(8,128)(2,1)S(1)}, u32[]{:S(2)}, u32[]{:S(2)}) collective-permute-start(bf16[3,64,128]{2,1,0:T(8,128)(2,1)S(1)} %get-tuple-element.75), channel_id=1, source_target_pairs={{0,24},{4,28},{8,16},{12,20},{16,8},{20,12},{24,0},{28,4},{1,25},{... | collective-permute-start | bytes 147464 | tf_op jit(solution)/shard_map/ppermute | solution.py:448
  8.6 2.6 collective-permute-start.2
  11.7 4.1 %copy.12 = bf16[1,1,96,64,64]{4,3,2,1,0:T(8,128)(2,1)} copy(bf16[1,1,96,64,64]{2,4,3,1,0:T(8,128)(2,1)} %param.15) | data formatting | bytes 1572864 | tf_op args[5]
  15.9 2.8 %pad_maximum_fusion.vals = bf16[96,64,128]{2,1,0:T(8,128)(2,1)S(1)} fusion(bf16[96,64,64]{2,1,0:T(8,128)(2,1)} %bitcast.29), kind=kLoop, calls=%fused_computation | loop fusion | flops 3145728 | bytes 2359296 | tf_op jit(solution)/shard_map/concatenate | solution.py:507
  18.8 0.7 wire.3
  20.3 1.8 prepare.1
  22.1 9.9 %partials.2 = (f32[12,64,64]{2,1,0:T(8,128)S(1)}, f32[12,64,64]{2,1,0:T(8,128)S(1)}, bf16[15,64,128]{2,1,0:T(8,128)(2,1)S(1)}, bf16[24,64,128]{2,1,0:T(8,128)(2,...) custom-call(bf16[12,64,128]{2,1,0:T(8,128)(2,1)S(1)} %get-tuple-element.74.refs_0_, ...), custom_call_target="tpu_custom_call" | custom-call | flops 1000000 | bytes 3047816 | tf_op jit(solution)/shard_map/partials/pallas_call | solution.py:414
  32.1 2.0 x_image.1
  34.1 1.7 collective-permute-start.7
  36.0 1.5 collective-permute-start.8
  37.9 1.6 collective-permute-start.14
  39.5 15.3 %collective-permute-done.14 = f32[64,128]{1,0:T(8,128)S(1)} collective-permute-done((f32[64,128]{1,0:T(8,128)S(1)}, f32[64,128]{1,0:T(8,128)S(1)}, u32[]{:S(2)}, u32[]{:S(2)}) %collective-permute-start.14) | collective-permute-done | bytes 32800 | tf_op jit(solution)/shard_map/ppermute | solution.py:445
  54.9 1.7 collective-permute-start.15
  56.6 2.2 collective-permute-done.15
  58.8 1.4 collective-permute-start.16
  60.2 2.5 collective-permute-done.16
  62.7 2.3 collective-permute-start.17
  65.0 2.5 collective-permute-done.17
  67.6 0.8 pair.2
  68.4 1.5 collective-permute-start.11
  69.9 2.9 %collective-permute-start.12 = (bf16[9,64,128]{2,1,0:T(8,128)(2,1)S(1)}, bf16[9,64,128]{2,1,0:T(8,128)(2,1)S(1)}, u32[]{:S(2)}, u32[]{:S(2)}) collective-permute-start(bf16[9,64,128]{2,1,0:T(8,128)(2,1)S(1)} %get-tuple-element.97), channel_id=1, source_target_pairs={{0,16},{4,20},{8,24},{12,28},{16,0},{20,4},{24,8},{28,12},{1,17},{... | collective-permute-start | bytes 442376 | tf_op jit(solution)/shard_map/ppermute | solution.py:448
  72.9 4.7 %collective-permute-done.11.refs_5_.refs_6_ = bf16[9,64,128]{2,1,0:T(8,128)(2,1)S(1)} collective-permute-done((bf16[9,64,128]{2,1,0:T(8,128)(2,1)S(1)}, bf16[9,64,128]{2,1,0:T(8,128)(2,1)S(1)}, u32[]{:S(2)}, u32[]{:S(2)}) %collective-permute-start.11) | collective-permute-done | bytes 147488 | tf_op jit(solution)/shard_map/ppermute | solution.py:448
  77.6 6.2 %collective-permute-done.12.refs_6_.refs_7_ = bf16[9,64,128]{2,1,0:T(8,128)(2,1)S(1)} collective-permute-done((bf16[9,64,128]{2,1,0:T(8,128)(2,1)S(1)}, bf16[9,64,128]{2,1,0:T(8,128)(2,1)S(1)}, u32[]{:S(2)}, u32[]{:S(2)}) %collective-permute-start.12) | collective-permute-done | bytes 147488 | tf_op jit(solution)/shard_map/ppermute | solution.py:448
  83.8 11.0 %update.1 = (f32[64,768]{1,0:T(8,128)S(1)}, f32[64,64]{1,0:T(8,128)S(1)}, f32[64,768]{1,0:T(8,128)S(1)}, bf16[12,64,128]{2,1,0:T(8,128)(2,1)S(1)}, bf16[3,64,128]{2,1,0:T(8,128)(2,1)S(1)}) custom-call(f32[12,64,64]{2,1,0:T(8,128)S(1)} %get-tuple-element.89.refs_0_, bf16[24,64,128]{2,1,0:T(8,128)(2,1)S(1)} %collective-permute-done.7.refs_1_.refs_3_, ...), custom_call_target="tpu_custom_call" | custom-call | flops 1000000 | bytes 3148812 | tf_op jit(solution)/shard_map/update/pallas_call | solution.py:414
  94.7 2.7 %collective-permute-start.24 = (bf16[3,64,128]{2,1,0:T(8,128)(2,1)S(1)}, bf16[3,64,128]{2,1,0:T(8,128)(2,1)S(1)}, u32[]{:S(2)}, u32[]{:S(2)}) collective-permute-start(bf16[3,64,128]{2,1,0:T(8,128)(2,1)S(1)} %get-tuple-element.103), channel_id=1, source_target_pairs={{0,24},{4,28},{8,16},{12,20},{16,8},{20,12},{24,0},{28,4},{1,25},{... | collective-permute-start | bytes 147464 | tf_op jit(solution)/shard_map/ppermute | solution.py:448
  97.5 2.1 collective-permute-start.23
  99.7 2.4 collective-permute-start.21
  102.6 1.0 collective-permute-done.22
  103.7 1.5 collective-permute-start.19
  105.3 19.1 %partials.3 = (f32[24,64,64]{2,1,0:T(8,128)S(1)}, f32[24,64,64]{2,1,0:T(8,128)S(1)}, bf16[24,64,128]{2,1,0:T(8,128)(2,1)S(1)}, bf16[24,64,128]{2,1,0:T(8,128)(2,...) custom-call(bf16[12,64,128]{2,1,0:T(8,128)(2,1)S(1)} %get-tuple-element.81.refs_4_.refs_0_, ...), custom_call_target="tpu_custom_call" | custom-call | flops 1000000 | bytes 3539336 | tf_op jit(solution)/shard_map/partials/pallas_call | solution.py:414
  124.4 1.6 p_image.1
  126.1 3.9 %update_image.2 = (f32[64,768]{1,0:T(8,128)S(1)}, f32[64,768]{1,0:T(8,128)S(1)}, f32[160,128]{1,0:T(8,128)S(1)}, f32[160,128]{1,0:T(8,128)S(1)}) custom-call(bf16[12,64,128]{2,1,0:T(8,128)(2,1)S(1)} %get-tuple-element.102.refs_0_.refs_1_, bf16[12,64,128]{2,1,0:T(8,128)(2,1)S(1)} %collective-permute-done.19.refs_1_, ...), custom_call_target="tpu_custom_call" | custom-call | flops 1000000 | bytes 4489608 | tf_op jit(solution)/shard_map/update_image/pallas_call | solution.py:414
  131.2 1.5 collective-permute-start.27
  132.7 1.5 collective-permute-start.34
  134.8 9.6 %collective-permute-done.34 = f32[160,128]{1,0:T(8,128)S(1)} collective-permute-done((f32[160,128]{1,0:T(8,128)S(1)}, f32[160,128]{1,0:T(8,128)S(1)}, u32[]{:S(2)}, u32[]{:S(2)}) %collective-permute-start.34) | collective-permute-done | bytes 81952 | tf_op jit(solution)/shard_map/ppermute | solution.py:445
  144.3 1.5 collective-permute-start.35
  145.9 9.1 %collective-permute-done.35 = f32[160,128]{1,0:T(8,128)S(1)} collective-permute-done((f32[160,128]{1,0:T(8,128)S(1)}, f32[160,128]{1,0:T(8,128)S(1)}, u32[]{:S(2)}, u32[]{:S(2)}) %collective-permute-start.35) | collective-permute-done | bytes 81952 | tf_op jit(solution)/shard_map/ppermute | solution.py:445
  155.6 3.9 %collective-permute-done.36 = f32[160,128]{1,0:T(8,128)S(1)} collective-permute-done((f32[160,128]{1,0:T(8,128)S(1)}, f32[160,128]{1,0:T(8,128)S(1)}, u32[]{:S(2)}, u32[]{:S(2)}) %collective-permute-start.36) | collective-permute-done | bytes 81952 | tf_op jit(solution)/shard_map/ppermute | solution.py:448
  159.5 1.6 collective-permute-start.37
  161.1 1.4 pair.3
  162.5 1.7 collective-permute-start.30
  164.5 1.3 collective-permute-done.37
  165.7 4.3 %collective-permute-start.32 = (bf16[6,64,128]{2,1,0:T(8,128)(2,1)S(1)}, bf16[6,64,128]{2,1,0:T(8,128)(2,1)S(1)}, u32[]{:S(2)}, u32[]{:S(2)}) collective-permute-start(bf16[6,64,128]{2,1,0:T(8,128)(2,1)S(1)} %get-tuple-element.124), channel_id=1, source_target_pairs={{0,24},{4,28},{8,16},{12,20},{16,8},{20,12},{24,0},{28,4},{1,25},{... | collective-permute-start | bytes 294920 | tf_op jit(solution)/shard_map/ppermute | solution.py:448
  170.2 3.1 %collective-permute-done.31.refs_6_ = bf16[6,64,128]{2,1,0:T(8,128)(2,1)S(1)} collective-permute-done((bf16[6,64,128]{2,1,0:T(8,128)(2,1)S(1)}, bf16[6,64,128]{2,1,0:T(8,128)(2,1)S(1)}, u32[]{:S(2)}, u32[]{:S(2)}) %collective-permute-start.31) | collective-permute-done | bytes 98336 | tf_op jit(solution)/shard_map/ppermute | solution.py:448
  173.3 32.2 %move.1 = (f32[64,768]{1,0:T(8,128)S(1)}, f32[64,768]{1,0:T(8,128)S(1)}, f32[64,768]{1,0:T(8,128)S(1)}, bf16[12,64,128]{2,1,0:T(8,128)(2,1)S(1)}, bf16[3,64,128]...) custom-call(f32[24,64,64]{2,1,0:T(8,128)S(1)} %get-tuple-element.115.refs_0_, ...), custom_call_target="tpu_custom_call" | custom-call | flops 1000000 | bytes 5049364 | tf_op jit(solution)/shard_map/move/pallas_call | solution.py:414
  205.4 3.4 %collective-permute-start.44 = (bf16[3,64,128]{2,1,0:T(8,128)(2,1)S(1)}, bf16[3,64,128]{2,1,0:T(8,128)(2,1)S(1)}, u32[]{:S(2)}, u32[]{:S(2)}) collective-permute-start(bf16[3,64,128]{2,1,0:T(8,128)(2,1)S(1)} %get-tuple-element.132), channel_id=1, source_target_pairs={{0,24},{4,28},{8,16},{12,20},{16,8},{20,12},{24,0},{28,4},{1,25},{... | collective-permute-start | bytes 147464 | tf_op jit(solution)/shard_map/ppermute | solution.py:448
  208.8 1.1 collective-permute-start.42
  210.5 1.5 collective-permute-start.40
  212.1 0.9 collective-permute-done.42
  213.9 10.4 %settle.1 = (f32[64,768]{1,0:T(8,128)S(1)}, f32[64,768]{1,0:T(8,128)S(1)}, f32[192,64]{1,0:T(8,128)S(1)}) custom-call(f32[256,64]{1,0:T(8,128)S(1)} %get-tuple-element.135.small, f32[64,768]{1,0:T(8,128)S(1)} %get-tuple-element.136.step_x, f32[64,768]{1,0:T(8,128)S(1)} %get-tuple-element.137.step_a), custom_call_target="tpu_custom_call" | custom-call | flops 1000000 | bytes 901120 | tf_op jit(solution)/shard_map/settle/pallas_call | solution.py:414
  224.4 3.2 %update_image.3 = (f32[64,768]{1,0:T(8,128)}, f32[64,768]{1,0:T(8,128)}, f32[96,128]{1,0:T(8,128)S(1)}, f32[96,128]{1,0:T(8,128)S(1)}) custom-call(bf16[12,64,128]{2,1,0:T(8,128)(2,1)S(1)} %get-tuple-element.131.refs_0_, bf16[12,64,128]{2,1,0:T(8,128)(2,1)S(1)} %collective-permute-done.39.refs_1_, bf16[12,64,128]{2,1,0:T(8,128)(2,1)S(1)} %collective-permute-done.40.refs_2_, ...), custom_call_target="tpu_custom_call" | custom-call | flops 1000000 | bytes 4424072 | tf_op jit(solution)/shard_map/update_image/pallas_call | solution.py:414
  228.1 0.9 collective-permute-done.46
  229.0 1.2 collective-permute-start.47
  230.2 2.9 %collective-permute-done.47 = f32[96,128]{1,0:T(8,128)S(1)} collective-permute-done((f32[96,128]{1,0:T(8,128)S(1)}, f32[96,128]{1,0:T(8,128)S(1)}, u32[]{:S(2)}, u32[]{:S(2)}) %collective-permute-start.47) | collective-permute-done | bytes 49184 | tf_op jit(solution)/shard_map/ppermute | solution.py:445
  233.7 3.5 %collective-permute-done.48 = f32[96,128]{1,0:T(8,128)S(1)} collective-permute-done((f32[96,128]{1,0:T(8,128)S(1)}, f32[96,128]{1,0:T(8,128)S(1)}, u32[]{:S(2)}, u32[]{:S(2)}) %collective-permute-start.48) | collective-permute-done | bytes 49184 | tf_op jit(solution)/shard_map/ppermute | solution.py:445
  237.3 1.0 collective-permute-start.49
  238.2 3.2 %collective-permute-done.49 = f32[96,128]{1,0:T(8,128)S(1)} collective-permute-done((f32[96,128]{1,0:T(8,128)S(1)}, f32[96,128]{1,0:T(8,128)S(1)}, u32[]{:S(2)}, u32[]{:S(2)}) %collective-permute-start.49) | collective-permute-done | bytes 49184 | tf_op jit(solution)/shard_map/ppermute | solution.py:448
  241.4 2.7 %collective-permute-start.50 = (f32[96,128]{1,0:T(8,128)S(1)}, f32[96,128]{1,0:T(8,128)S(1)}, u32[]{:S(2)}, u32[]{:S(2)}) collective-permute-start(f32[96,128]{1,0:T(8,128)S(1)} %add.58), channel_id=1, source_target_pairs={{0,16},{4,20},{8,24},{12,28},{16,0},{20,4},{24,8},{28,12},{1,17},{... | collective-permute-start | bytes 147464 | tf_op jit(solution)/shard_map/ppermute | solution.py:448
  244.2 2.8 %collective-permute-done.50 = f32[96,128]{1,0:T(8,128)S(1)} collective-permute-done((f32[96,128]{1,0:T(8,128)S(1)}, f32[96,128]{1,0:T(8,128)S(1)}, u32[]{:S(2)}, u32[]{:S(2)}) %collective-permute-start.50) | collective-permute-done | bytes 49184 | tf_op jit(solution)/shard_map/ppermute | solution.py:448
  247.1 1.2 collective-permute-done.51.other
  248.3 21.7 %finish.1 = (f32[64,768]{1,0:T(8,128)}, f32[64,768]{1,0:T(8,128)}) custom-call(f32[96,128]{1,0:T(8,128)S(1)} %add.59.mine, f32[96,128]{1,0:T(8,128)S(1)} %collective-permute-done.51.other, s32[2]{0:T(128)S(1)} %pad_add_fusion.refs_9_.refs_3_.pos.refs_12_.refs_4_.refs_10_, f32[192,64]{1,0:T(8,128)S(1)} %get-tuple-element.143.state, ...), custom_call_target="tpu_custom_call" | custom-call | flops 1000000 | bytes 1130504 | tf_op jit(solution)/shard_map/finish/pallas_call | solution.py:414
  (109 shorter events, 9.0 us)
Async XLA Ops:
  0.6 0.9 copy-start
  1.6 0.7 copy-start.3
  2.9 17.1 %collective-permute-start.5 = (bf16[3,64,128]{2,1,0:T(8,128)(2,1)S(1)}, bf16[3,64,128]{2,1,0:T(8,128)(2,1)S(1)}, u32[]{:S(2)}, u32[]{:S(2)}) collective-permute-start(bf16[3,64,128]{2,1,0:T(8,128)(2,1)S(1)} %get-tuple-element.75), channel_id=1, source_target_pairs={{0,24},{4,28},{8,16},{12,20},{16,8},{20,12},{24,0},{28,4},{1,25},{... | collective-permute-start | bytes 147464 | tf_op jit(solution)/shard_map/ppermute | solution.py:448
  8.0 11.9 %collective-permute-start.4 = (bf16[3,64,128]{2,1,0:T(8,128)(2,1)S(1)}, bf16[3,64,128]{2,1,0:T(8,128)(2,1)S(1)}, u32[]{:S(2)}, u32[]{:S(2)}) collective-permute-start(bf16[3,64,128]{2,1,0:T(8,128)(2,1)S(1)} %get-tuple-element.75), channel_id=1, source_target_pairs={{0,16},{4,20},{8,24},{12,28},{16,0},{20,4},{24,8},{28,12},{1,17},{... | collective-permute-start | bytes 147464 | tf_op jit(solution)/shard_map/ppermute | solution.py:448
  8.0 11.4 %collective-permute-start.3 = (bf16[3,64,128]{2,1,0:T(8,128)(2,1)S(1)}, bf16[3,64,128]{2,1,0:T(8,128)(2,1)S(1)}, u32[]{:S(2)}, u32[]{:S(2)}) collective-permute-start(bf16[3,64,128]{2,1,0:T(8,128)(2,1)S(1)} %get-tuple-element.75), channel_id=1, source_target_pairs={{0,8},{4,12},{8,0},{12,4},{16,24},{20,28},{24,16},{28,20},{1,9},{5... | collective-permute-start | bytes 147464 | tf_op jit(solution)/shard_map/ppermute | solution.py:448
  8.6 23.4 %collective-permute-start.2 = (bf16[12,64,128]{2,1,0:T(8,128)(2,1)S(1)}, bf16[12,64,128]{2,1,0:T(8,128)(2,1)S(1)}, u32[]{:S(2)}, u32[]{:S(2)}) collective-permute-start(bf16[12,64,128]{2,1,0:T(8,128)(2,1)S(1)} %get-tuple-element.74.refs_0_), channel_id=1, source_target_pairs={{0,3},{1,2},{2,1},{3,0},{4,7},{5,6},{6,5},{7,4},{8,11},{9,10},{10,... | collective-permute-start | bytes 589832 | tf_op jit(solution)/shard_map/ppermute | solution.py:445
  11.2 20.8 %collective-permute-start.1 = (bf16[12,64,128]{2,1,0:T(8,128)(2,1)S(1)}, bf16[12,64,128]{2,1,0:T(8,128)(2,1)S(1)}, u32[]{:S(2)}, u32[]{:S(2)}) collective-permute-start(bf16[12,64,128]{2,1,0:T(8,128)(2,1)S(1)} %get-tuple-element.74.refs_0_), channel_id=1, source_target_pairs={{0,2},{1,3},{2,0},{3,1},{4,6},{5,7},{6,4},{7,5},{8,10},{9,11},{10,... | collective-permute-start | bytes 589832 | tf_op jit(solution)/shard_map/ppermute | solution.py:445
  15.8 2.9 %copy-start.2 = (f32[768,64]{0,1:T(8,128)S(1)}, f32[768,64]{0,1:T(8,128)}, u32[]{:S(2)}) copy-start(f32[768,64]{0,1:T(8,128)} %param.11) | copy-start | bytes 589828
  15.8 2.9 %copy-start.4 = (s32[1,1,3]{2,1,0:T(1,128)S(1)}, s32[1,1,3]{2,1,0:T(1,128)}, u32[]{:S(2)}) copy-start(s32[1,1,3]{2,1,0:T(1,128)} %param.16) | copy-start | bytes 40
  15.8 4.2 %copy-start.9 = (bf16[1,1,12,64,64]{4,3,2,1,0:T(8,128)(2,1)S(1)}, bf16[1,1,12,64,64]{4,3,2,1,0:T(8,128)(2,1)}, u32[]{:S(2)}) copy-start(bf16[1,1,12,64,64]{4,3,2,1,0:T(8,128)(2,1)} %param.19) | copy-start | bytes 294916
  15.8 4.4 %copy-start.5 = (s32[1,1,96]{2,1,0:T(1,128)S(1)}, s32[1,1,96]{2,1,0:T(1,128)}, u32[]{:S(2)}) copy-start(s32[1,1,96]{2,1,0:T(1,128)} %param.13) | copy-start | bytes 1156
  15.9 4.4 %copy-start.6 = (s32[1,1,96]{2,1,0:T(1,128)S(1)}, s32[1,1,96]{2,1,0:T(1,128)}, u32[]{:S(2)}) copy-start(s32[1,1,96]{2,1,0:T(1,128)} %param.14) | copy-start | bytes 1156
  15.9 4.4 %copy-start.7 = (s32[1,1,12]{2,1,0:T(1,128)S(1)}, s32[1,1,12]{2,1,0:T(1,128)}, u32[]{:S(2)}) copy-start(s32[1,1,12]{2,1,0:T(1,128)} %param.17) | copy-start | bytes 148
  15.9 4.4 %copy-start.8 = (s32[1,1,12]{2,1,0:T(1,128)S(1)}, s32[1,1,12]{2,1,0:T(1,128)}, u32[]{:S(2)}) copy-start(s32[1,1,12]{2,1,0:T(1,128)} %param.18) | copy-start | bytes 148
  19.4 12.6 %collective-permute-start = (bf16[12,64,128]{2,1,0:T(8,128)(2,1)S(1)}, bf16[12,64,128]{2,1,0:T(8,128)(2,1)S(1)}, u32[]{:S(2)}, u32[]{:S(2)}) collective-permute-start(bf16[12,64,128]{2,1,0:T(8,128)(2,1)S(1)} %get-tuple-element.74.refs_0_), channel_id=1, source_target_pairs={{0,1},{1,0},{2,3},{3,2},{4,5},{5,4},{6,7},{7,6},{8,9},{9,8},{10,11... | collective-permute-start | bytes 589832 | tf_op jit(solution)/shard_map/ppermute | solution.py:445
  20.0 12.1 %collective-permute-start.6 = (bf16[12,64,128]{2,1,0:T(8,128)(2,1)S(1)}, bf16[12,64,128]{2,1,0:T(8,128)(2,1)S(1)}, u32[]{:S(2)}, u32[]{:S(2)}) collective-permute-start(bf16[12,64,128]{2,1,0:T(8,128)(2,1)S(1)} %constant_dynamic-update-slice_fusion.refs_4_), channel_id=1, source_target_pairs={{0,4},{4,0},{8,12},{12,8},{16,20},{20,16},{24,28},{28,24},{1,5},{5... | collective-permute-start | bytes 589832 | tf_op jit(solution)/shard_map/ppermute | solution.py:448
  20.2 11.9 %copy-start.1 = (f32[768,64]{0,1:T(8,128)S(1)}, f32[768,64]{0,1:T(8,128)}, u32[]{:S(2)}) copy-start(f32[768,64]{0,1:T(8,128)} %param.10) | copy-start | bytes 589828
  32.1 40.8 %copy-start.10 = (f32[768]{0:T(1024)S(1)}, f32[768]{0:T(1024)}, u32[]{:S(2)}) copy-start(f32[768]{0:T(1024)} %param.12) | copy-start | bytes 9220
  34.1 38.7 %collective-permute-start.7 = (bf16[24,64,128]{2,1,0:T(8,128)(2,1)S(1)}, bf16[24,64,128]{2,1,0:T(8,128)(2,1)S(1)}, u32[]{:S(2)}, u32[]{:S(2)}) collective-permute-start(bf16[24,64,128]{2,1,0:T(8,128)(2,1)S(1)} %get-tuple-element.90), channel_id=1, source_target_pairs={{0,1},{1,0},{2,3},{3,2},{4,5},{5,4},{6,7},{7,6},{8,9},{9,8},{10,11... | collective-permute-start | bytes 1179656 | tf_op jit(solution)/shard_map/ppermute | solution.py:445
  35.8 31.7 %collective-permute-start.10 = (bf16[15,64,128]{2,1,0:T(8,128)(2,1)S(1)}, bf16[15,64,128]{2,1,0:T(8,128)(2,1)S(1)}, u32[]{:S(2)}, u32[]{:S(2)}) collective-permute-start(bf16[15,64,128]{2,1,0:T(8,128)(2,1)S(1)} %get-tuple-element.94), channel_id=1, source_target_pairs={{0,4},{4,0},{8,12},{12,8},{16,20},{20,16},{24,28},{28,24},{1,5},{5... | collective-permute-start | bytes 737288 | tf_op jit(solution)/shard_map/ppermute | solution.py:448
  36.0 36.8 %collective-permute-start.8 = (bf16[24,64,128]{2,1,0:T(8,128)(2,1)S(1)}, bf16[24,64,128]{2,1,0:T(8,128)(2,1)S(1)}, u32[]{:S(2)}, u32[]{:S(2)}) collective-permute-start(bf16[24,64,128]{2,1,0:T(8,128)(2,1)S(1)} %get-tuple-element.91), channel_id=1, source_target_pairs={{0,2},{1,3},{2,0},{3,1},{4,6},{5,7},{6,4},{7,5},{8,10},{9,11},{10,... | collective-permute-start | bytes 1179656 | tf_op jit(solution)/shard_map/ppermute | solution.py:445
  37.6 35.3 %collective-permute-start.9 = (bf16[24,64,128]{2,1,0:T(8,128)(2,1)S(1)}, bf16[24,64,128]{2,1,0:T(8,128)(2,1)S(1)}, u32[]{:S(2)}, u32[]{:S(2)}) collective-permute-start(bf16[24,64,128]{2,1,0:T(8,128)(2,1)S(1)} %get-tuple-element.92), channel_id=1, source_target_pairs={{0,3},{1,2},{2,1},{3,0},{4,7},{5,6},{6,5},{7,4},{8,11},{9,10},{10,... | collective-permute-start | bytes 1179656 | tf_op jit(solution)/shard_map/ppermute | solution.py:445
  37.9 17.0 %collective-permute-start.14 = (f32[64,128]{1,0:T(8,128)S(1)}, f32[64,128]{1,0:T(8,128)S(1)}, u32[]{:S(2)}, u32[]{:S(2)}) collective-permute-start(f32[64,128]{1,0:T(8,128)S(1)} %get-tuple-element.99), channel_id=1, source_target_pairs={{0,1},{1,0},{2,3},{3,2},{4,5},{5,4},{6,7},{7,6},{8,9},{9,8},{10,11... | collective-permute-start | bytes 98312 | tf_op jit(solution)/shard_map/ppermute | solution.py:445
  54.9 3.9 %collective-permute-start.15 = (f32[64,128]{1,0:T(8,128)S(1)}, f32[64,128]{1,0:T(8,128)S(1)}, u32[]{:S(2)}, u32[]{:S(2)}) collective-permute-start(f32[64,128]{1,0:T(8,128)S(1)} %add.45), channel_id=1, source_target_pairs={{0,2},{1,3},{2,0},{3,1},{4,6},{5,7},{6,4},{7,5},{8,10},{9,11},{10,... | collective-permute-start | bytes 98312 | tf_op jit(solution)/shard_map/ppermute | solution.py:445
  58.8 3.9 %collective-permute-start.16 = (f32[64,128]{1,0:T(8,128)S(1)}, f32[64,128]{1,0:T(8,128)S(1)}, u32[]{:S(2)}, u32[]{:S(2)}) collective-permute-start(f32[64,128]{1,0:T(8,128)S(1)} %add.46), channel_id=1, source_target_pairs={{0,8},{4,12},{8,0},{12,4},{16,24},{20,28},{24,16},{28,20},{1,9},{5... | collective-permute-start | bytes 98312 | tf_op jit(solution)/shard_map/ppermute | solution.py:448
  62.7 4.8 %collective-permute-start.17 = (f32[64,128]{1,0:T(8,128)S(1)}, f32[64,128]{1,0:T(8,128)S(1)}, u32[]{:S(2)}, u32[]{:S(2)}) collective-permute-start(f32[64,128]{1,0:T(8,128)S(1)} %add.47), channel_id=1, source_target_pairs={{0,16},{4,20},{8,24},{12,28},{16,0},{20,4},{24,8},{28,12},{1,17},{... | collective-permute-start | bytes 98312 | tf_op jit(solution)/shard_map/ppermute | solution.py:448
  67.5 2.3 collective-permute-start.18
  68.4 9.2 %collective-permute-start.11 = (bf16[9,64,128]{2,1,0:T(8,128)(2,1)S(1)}, bf16[9,64,128]{2,1,0:T(8,128)(2,1)S(1)}, u32[]{:S(2)}, u32[]{:S(2)}) collective-permute-start(bf16[9,64,128]{2,1,0:T(8,128)(2,1)S(1)} %get-tuple-element.96), channel_id=1, source_target_pairs={{0,8},{4,12},{8,0},{12,4},{16,24},{20,28},{24,16},{28,20},{1,9},{5... | collective-permute-start | bytes 442376 | tf_op jit(solution)/shard_map/ppermute | solution.py:448
  69.9 13.9 %collective-permute-start.12 = (bf16[9,64,128]{2,1,0:T(8,128)(2,1)S(1)}, bf16[9,64,128]{2,1,0:T(8,128)(2,1)S(1)}, u32[]{:S(2)}, u32[]{:S(2)}) collective-permute-start(bf16[9,64,128]{2,1,0:T(8,128)(2,1)S(1)} %get-tuple-element.97), channel_id=1, source_target_pairs={{0,16},{4,20},{8,24},{12,28},{16,0},{20,4},{24,8},{28,12},{1,17},{... | collective-permute-start | bytes 442376 | tf_op jit(solution)/shard_map/ppermute | solution.py:448
  72.8 11.0 %collective-permute-start.13 = (bf16[9,64,128]{2,1,0:T(8,128)(2,1)S(1)}, bf16[9,64,128]{2,1,0:T(8,128)(2,1)S(1)}, u32[]{:S(2)}, u32[]{:S(2)}) collective-permute-start(bf16[9,64,128]{2,1,0:T(8,128)(2,1)S(1)} %get-tuple-element.98), channel_id=1, source_target_pairs={{0,24},{4,28},{8,16},{12,20},{16,8},{20,12},{24,0},{28,4},{1,25},{... | collective-permute-start | bytes 442376 | tf_op jit(solution)/shard_map/ppermute | solution.py:448
  94.7 10.5 %collective-permute-start.24 = (bf16[3,64,128]{2,1,0:T(8,128)(2,1)S(1)}, bf16[3,64,128]{2,1,0:T(8,128)(2,1)S(1)}, u32[]{:S(2)}, u32[]{:S(2)}) collective-permute-start(bf16[3,64,128]{2,1,0:T(8,128)(2,1)S(1)} %get-tuple-element.103), channel_id=1, source_target_pairs={{0,24},{4,28},{8,16},{12,20},{16,8},{20,12},{24,0},{28,4},{1,25},{... | collective-permute-start | bytes 147464 | tf_op jit(solution)/shard_map/ppermute | solution.py:448
  97.5 7.7 %collective-permute-start.23 = (bf16[3,64,128]{2,1,0:T(8,128)(2,1)S(1)}, bf16[3,64,128]{2,1,0:T(8,128)(2,1)S(1)}, u32[]{:S(2)}, u32[]{:S(2)}) collective-permute-start(bf16[3,64,128]{2,1,0:T(8,128)(2,1)S(1)} %get-tuple-element.103), channel_id=1, source_target_pairs={{0,16},{4,20},{8,24},{12,28},{16,0},{20,4},{24,8},{28,12},{1,17},{... | collective-permute-start | bytes 147464 | tf_op jit(solution)/shard_map/ppermute | solution.py:448
  99.6 4.1 %collective-permute-start.22 = (bf16[3,64,128]{2,1,0:T(8,128)(2,1)S(1)}, bf16[3,64,128]{2,1,0:T(8,128)(2,1)S(1)}, u32[]{:S(2)}, u32[]{:S(2)}) collective-permute-start(bf16[3,64,128]{2,1,0:T(8,128)(2,1)S(1)} %get-tuple-element.103), channel_id=1, source_target_pairs={{0,8},{4,12},{8,0},{12,4},{16,24},{20,28},{24,16},{28,20},{1,9},{5... | collective-permute-start | bytes 147464 | tf_op jit(solution)/shard_map/ppermute | solution.py:448
  99.7 26.4 %collective-permute-start.21 = (bf16[12,64,128]{2,1,0:T(8,128)(2,1)S(1)}, bf16[12,64,128]{2,1,0:T(8,128)(2,1)S(1)}, u32[]{:S(2)}, u32[]{:S(2)}) collective-permute-start(bf16[12,64,128]{2,1,0:T(8,128)(2,1)S(1)} %get-tuple-element.102.refs_0_.refs_1_), channel_id=1, source_target_pairs={{0,3},{1,2},{2,1},{3,0},{4,7},{5,6},{6,5},{7,4},{8,11},{9,10},{10,... | collective-permute-start | bytes 589832 | tf_op jit(solution)/shard_map/ppermute | solution.py:445
  102.1 24.0 %collective-permute-start.20 = (bf16[12,64,128]{2,1,0:T(8,128)(2,1)S(1)}, bf16[12,64,128]{2,1,0:T(8,128)(2,1)S(1)}, u32[]{:S(2)}, u32[]{:S(2)}) collective-permute-start(bf16[12,64,128]{2,1,0:T(8,128)(2,1)S(1)} %get-tuple-element.102.refs_0_.refs_1_), channel_id=1, source_target_pairs={{0,2},{1,3},{2,0},{3,1},{4,6},{5,7},{6,4},{7,5},{8,10},{9,11},{10,... | collective-permute-start | bytes 589832 | tf_op jit(solution)/shard_map/ppermute | solution.py:445
  103.7 22.4 %collective-permute-start.19 = (bf16[12,64,128]{2,1,0:T(8,128)(2,1)S(1)}, bf16[12,64,128]{2,1,0:T(8,128)(2,1)S(1)}, u32[]{:S(2)}, u32[]{:S(2)}) collective-permute-start(bf16[12,64,128]{2,1,0:T(8,128)(2,1)S(1)} %get-tuple-element.102.refs_0_.refs_1_), channel_id=1, source_target_pairs={{0,1},{1,0},{2,3},{3,2},{4,5},{5,4},{6,7},{7,6},{8,9},{9,8},{10,11... | collective-permute-start | bytes 589832 | tf_op jit(solution)/shard_map/ppermute | solution.py:445
  105.2 20.9 %collective-permute-start.25 = (bf16[12,64,128]{2,1,0:T(8,128)(2,1)S(1)}, bf16[12,64,128]{2,1,0:T(8,128)(2,1)S(1)}, u32[]{:S(2)}, u32[]{:S(2)}) collective-permute-start(bf16[12,64,128]{2,1,0:T(8,128)(2,1)S(1)} %constant_dynamic-update-slice_fusion.4.refs_4_), channel_id=1, source_target_pairs={{0,4},{4,0},{8,12},{12,8},{16,20},{20,16},{24,28},{28,24},{1,5},{5... | collective-permute-start | bytes 589832 | tf_op jit(solution)/shard_map/ppermute | solution.py:448
  130.0 2.7 collective-permute-start.33
  130.6 30.5 %collective-permute-start.29 = (bf16[24,64,128]{2,1,0:T(8,128)(2,1)S(1)}, bf16[24,64,128]{2,1,0:T(8,128)(2,1)S(1)}, u32[]{:S(2)}, u32[]{:S(2)}) collective-permute-start(bf16[24,64,128]{2,1,0:T(8,128)(2,1)S(1)} %get-tuple-element.120), channel_id=1, source_target_pairs={{0,4},{4,0},{8,12},{12,8},{16,20},{20,16},{24,28},{28,24},{1,5},{5... | collective-permute-start | bytes 1179656 | tf_op jit(solution)/shard_map/ppermute | solution.py:448
  130.7 33.6 %collective-permute-start.26 = (bf16[24,64,128]{2,1,0:T(8,128)(2,1)S(1)}, bf16[24,64,128]{2,1,0:T(8,128)(2,1)S(1)}, u32[]{:S(2)}, u32[]{:S(2)}) collective-permute-start(bf16[24,64,128]{2,1,0:T(8,128)(2,1)S(1)} %get-tuple-element.116), channel_id=1, source_target_pairs={{0,1},{1,0},{2,3},{3,2},{4,5},{5,4},{6,7},{7,6},{8,9},{9,8},{10,11... | collective-permute-start | bytes 1179656 | tf_op jit(solution)/shard_map/ppermute | solution.py:445
  131.2 38.9 %collective-permute-start.27 = (bf16[24,64,128]{2,1,0:T(8,128)(2,1)S(1)}, bf16[24,64,128]{2,1,0:T(8,128)(2,1)S(1)}, u32[]{:S(2)}, u32[]{:S(2)}) collective-permute-start(bf16[24,64,128]{2,1,0:T(8,128)(2,1)S(1)} %get-tuple-element.117), channel_id=1, source_target_pairs={{0,2},{1,3},{2,0},{3,1},{4,6},{5,7},{6,4},{7,5},{8,10},{9,11},{10,... | collective-permute-start | bytes 1179656 | tf_op jit(solution)/shard_map/ppermute | solution.py:445
  132.7 11.6 %collective-permute-start.34 = (f32[160,128]{1,0:T(8,128)S(1)}, f32[160,128]{1,0:T(8,128)S(1)}, u32[]{:S(2)}, u32[]{:S(2)}) collective-permute-start(f32[160,128]{1,0:T(8,128)S(1)} %add.50), channel_id=1, source_target_pairs={{0,1},{1,0},{2,3},{3,2},{4,5},{5,4},{6,7},{7,6},{8,9},{9,8},{10,11... | collective-permute-start | bytes 245768 | tf_op jit(solution)/shard_map/ppermute | solution.py:445
  134.2 35.9 %collective-permute-start.28 = (bf16[24,64,128]{2,1,0:T(8,128)(2,1)S(1)}, bf16[24,64,128]{2,1,0:T(8,128)(2,1)S(1)}, u32[]{:S(2)}, u32[]{:S(2)}) collective-permute-start(bf16[24,64,128]{2,1,0:T(8,128)(2,1)S(1)} %get-tuple-element.118), channel_id=1, source_target_pairs={{0,3},{1,2},{2,1},{3,0},{4,7},{5,6},{6,5},{7,4},{8,11},{9,10},{10,... | collective-permute-start | bytes 1179656 | tf_op jit(solution)/shard_map/ppermute | solution.py:445
  144.3 10.6 %collective-permute-start.35 = (f32[160,128]{1,0:T(8,128)S(1)}, f32[160,128]{1,0:T(8,128)S(1)}, u32[]{:S(2)}, u32[]{:S(2)}) collective-permute-start(f32[160,128]{1,0:T(8,128)S(1)} %add.51), channel_id=1, source_target_pairs={{0,2},{1,3},{2,0},{3,1},{4,6},{5,7},{6,4},{7,5},{8,10},{9,11},{10,... | collective-permute-start | bytes 245768 | tf_op jit(solution)/shard_map/ppermute | solution.py:445
  155.0 4.5 %collective-permute-start.36 = (f32[160,128]{1,0:T(8,128)S(1)}, f32[160,128]{1,0:T(8,128)S(1)}, u32[]{:S(2)}, u32[]{:S(2)}) collective-permute-start(f32[160,128]{1,0:T(8,128)S(1)} %add.52), channel_id=1, source_target_pairs={{0,8},{4,12},{8,0},{12,4},{16,24},{20,28},{24,16},{28,20},{1,9},{5... | collective-permute-start | bytes 245768 | tf_op jit(solution)/shard_map/ppermute | solution.py:448
  159.5 6.2 %collective-permute-start.37 = (f32[160,128]{1,0:T(8,128)S(1)}, f32[160,128]{1,0:T(8,128)S(1)}, u32[]{:S(2)}, u32[]{:S(2)}) collective-permute-start(f32[160,128]{1,0:T(8,128)S(1)} %add.53), channel_id=1, source_target_pairs={{0,16},{4,20},{8,24},{12,28},{16,0},{20,4},{24,8},{28,12},{1,17},{... | collective-permute-start | bytes 245768 | tf_op jit(solution)/shard_map/ppermute | solution.py:448
  162.5 7.7 %collective-permute-start.30 = (bf16[6,64,128]{2,1,0:T(8,128)(2,1)S(1)}, bf16[6,64,128]{2,1,0:T(8,128)(2,1)S(1)}, u32[]{:S(2)}, u32[]{:S(2)}) collective-permute-start(bf16[6,64,128]{2,1,0:T(8,128)(2,1)S(1)} %get-tuple-element.122), channel_id=1, source_target_pairs={{0,8},{4,12},{8,0},{12,4},{16,24},{20,28},{24,16},{28,20},{1,9},{5... | collective-permute-start | bytes 294920 | tf_op jit(solution)/shard_map/ppermute | solution.py:448
  164.2 9.1 %collective-permute-start.31 = (bf16[6,64,128]{2,1,0:T(8,128)(2,1)S(1)}, bf16[6,64,128]{2,1,0:T(8,128)(2,1)S(1)}, u32[]{:S(2)}, u32[]{:S(2)}) collective-permute-start(bf16[6,64,128]{2,1,0:T(8,128)(2,1)S(1)} %get-tuple-element.123), channel_id=1, source_target_pairs={{0,16},{4,20},{8,24},{12,28},{16,0},{20,4},{24,8},{28,12},{1,17},{... | collective-permute-start | bytes 294920 | tf_op jit(solution)/shard_map/ppermute | solution.py:448
  165.7 7.6 %collective-permute-start.32 = (bf16[6,64,128]{2,1,0:T(8,128)(2,1)S(1)}, bf16[6,64,128]{2,1,0:T(8,128)(2,1)S(1)}, u32[]{:S(2)}, u32[]{:S(2)}) collective-permute-start(bf16[6,64,128]{2,1,0:T(8,128)(2,1)S(1)} %get-tuple-element.124), channel_id=1, source_target_pairs={{0,24},{4,28},{8,16},{12,20},{16,8},{20,12},{24,0},{28,4},{1,25},{... | collective-permute-start | bytes 294920 | tf_op jit(solution)/shard_map/ppermute | solution.py:448
  170.1 3.2 %collective-permute-start.38 = (f32[160,128]{1,0:T(8,128)S(1)}, f32[160,128]{1,0:T(8,128)S(1)}, u32[]{:S(2)}, u32[]{:S(2)}) collective-permute-start(f32[160,128]{1,0:T(8,128)S(1)} %add.54.refs_8_), channel_id=1, source_target_pairs={{0,4},{4,0},{8,12},{12,8},{16,20},{20,16},{24,28},{28,24},{1,5},{5... | collective-permute-start | bytes 245768 | tf_op jit(solution)/shard_map/ppermute | solution.py:448
  205.4 8.4 %collective-permute-start.44 = (bf16[3,64,128]{2,1,0:T(8,128)(2,1)S(1)}, bf16[3,64,128]{2,1,0:T(8,128)(2,1)S(1)}, u32[]{:S(2)}, u32[]{:S(2)}) collective-permute-start(bf16[3,64,128]{2,1,0:T(8,128)(2,1)S(1)} %get-tuple-element.132), channel_id=1, source_target_pairs={{0,24},{4,28},{8,16},{12,20},{16,8},{20,12},{24,0},{28,4},{1,25},{... | collective-permute-start | bytes 147464 | tf_op jit(solution)/shard_map/ppermute | solution.py:448
  208.8 5.0 %collective-permute-start.43 = (bf16[3,64,128]{2,1,0:T(8,128)(2,1)S(1)}, bf16[3,64,128]{2,1,0:T(8,128)(2,1)S(1)}, u32[]{:S(2)}, u32[]{:S(2)}) collective-permute-start(bf16[3,64,128]{2,1,0:T(8,128)(2,1)S(1)} %get-tuple-element.132), channel_id=1, source_target_pairs={{0,16},{4,20},{8,24},{12,28},{16,0},{20,4},{24,8},{28,12},{1,17},{... | collective-permute-start | bytes 147464 | tf_op jit(solution)/shard_map/ppermute | solution.py:448
  208.8 4.1 %collective-permute-start.42 = (bf16[3,64,128]{2,1,0:T(8,128)(2,1)S(1)}, bf16[3,64,128]{2,1,0:T(8,128)(2,1)S(1)}, u32[]{:S(2)}, u32[]{:S(2)}) collective-permute-start(bf16[3,64,128]{2,1,0:T(8,128)(2,1)S(1)} %get-tuple-element.132), channel_id=1, source_target_pairs={{0,8},{4,12},{8,0},{12,4},{16,24},{20,28},{24,16},{28,20},{1,9},{5... | collective-permute-start | bytes 147464 | tf_op jit(solution)/shard_map/ppermute | solution.py:448
  209.9 14.5 %collective-permute-start.41 = (bf16[12,64,128]{2,1,0:T(8,128)(2,1)S(1)}, bf16[12,64,128]{2,1,0:T(8,128)(2,1)S(1)}, u32[]{:S(2)}, u32[]{:S(2)}) collective-permute-start(bf16[12,64,128]{2,1,0:T(8,128)(2,1)S(1)} %get-tuple-element.131.refs_0_), channel_id=1, source_target_pairs={{0,3},{1,2},{2,1},{3,0},{4,7},{5,6},{6,5},{7,4},{8,11},{9,10},{10,... | collective-permute-start | bytes 589832 | tf_op jit(solution)/shard_map/ppermute | solution.py:445
  210.5 13.8 %collective-permute-start.40 = (bf16[12,64,128]{2,1,0:T(8,128)(2,1)S(1)}, bf16[12,64,128]{2,1,0:T(8,128)(2,1)S(1)}, u32[]{:S(2)}, u32[]{:S(2)}) collective-permute-start(bf16[12,64,128]{2,1,0:T(8,128)(2,1)S(1)} %get-tuple-element.131.refs_0_), channel_id=1, source_target_pairs={{0,2},{1,3},{2,0},{3,1},{4,6},{5,7},{6,4},{7,5},{8,10},{9,11},{10,... | collective-permute-start | bytes 589832 | tf_op jit(solution)/shard_map/ppermute | solution.py:445
  212.9 11.5 %collective-permute-start.39 = (bf16[12,64,128]{2,1,0:T(8,128)(2,1)S(1)}, bf16[12,64,128]{2,1,0:T(8,128)(2,1)S(1)}, u32[]{:S(2)}, u32[]{:S(2)}) collective-permute-start(bf16[12,64,128]{2,1,0:T(8,128)(2,1)S(1)} %get-tuple-element.131.refs_0_), channel_id=1, source_target_pairs={{0,1},{1,0},{2,3},{3,2},{4,5},{5,4},{6,7},{7,6},{8,9},{9,8},{10,11... | collective-permute-start | bytes 589832 | tf_op jit(solution)/shard_map/ppermute | solution.py:445
  213.8 10.5 %collective-permute-start.45 = (bf16[12,64,128]{2,1,0:T(8,128)(2,1)S(1)}, bf16[12,64,128]{2,1,0:T(8,128)(2,1)S(1)}, u32[]{:S(2)}, u32[]{:S(2)}) collective-permute-start(bf16[12,64,128]{2,1,0:T(8,128)(2,1)S(1)} %constant_dynamic-update-slice_fusion.8.refs_4_), channel_id=1, source_target_pairs={{0,4},{4,0},{8,12},{12,8},{16,20},{20,16},{24,28},{28,24},{1,5},{5... | collective-permute-start | bytes 589832 | tf_op jit(solution)/shard_map/ppermute | solution.py:448
  227.6 1.4 collective-permute-start.46
  229.0 4.1 %collective-permute-start.47 = (f32[96,128]{1,0:T(8,128)S(1)}, f32[96,128]{1,0:T(8,128)S(1)}, u32[]{:S(2)}, u32[]{:S(2)}) collective-permute-start(f32[96,128]{1,0:T(8,128)S(1)} %add.55), channel_id=1, source_target_pairs={{0,1},{1,0},{2,3},{3,2},{4,5},{5,4},{6,7},{7,6},{8,9},{9,8},{10,11... | collective-permute-start | bytes 147464 | tf_op jit(solution)/shard_map/ppermute | solution.py:445
  233.1 4.2 %collective-permute-start.48 = (f32[96,128]{1,0:T(8,128)S(1)}, f32[96,128]{1,0:T(8,128)S(1)}, u32[]{:S(2)}, u32[]{:S(2)}) collective-permute-start(f32[96,128]{1,0:T(8,128)S(1)} %add.56), channel_id=1, source_target_pairs={{0,2},{1,3},{2,0},{3,1},{4,6},{5,7},{6,4},{7,5},{8,10},{9,11},{10,... | collective-permute-start | bytes 147464 | tf_op jit(solution)/shard_map/ppermute | solution.py:445
  237.3 4.2 %collective-permute-start.49 = (f32[96,128]{1,0:T(8,128)S(1)}, f32[96,128]{1,0:T(8,128)S(1)}, u32[]{:S(2)}, u32[]{:S(2)}) collective-permute-start(f32[96,128]{1,0:T(8,128)S(1)} %add.57), channel_id=1, source_target_pairs={{0,8},{4,12},{8,0},{12,4},{16,24},{20,28},{24,16},{28,20},{1,9},{5... | collective-permute-start | bytes 147464 | tf_op jit(solution)/shard_map/ppermute | solution.py:448
  241.4 5.6 %collective-permute-start.50 = (f32[96,128]{1,0:T(8,128)S(1)}, f32[96,128]{1,0:T(8,128)S(1)}, u32[]{:S(2)}, u32[]{:S(2)}) collective-permute-start(f32[96,128]{1,0:T(8,128)S(1)} %add.58), channel_id=1, source_target_pairs={{0,16},{4,20},{8,24},{12,28},{16,0},{20,4},{24,8},{28,12},{1,17},{... | collective-permute-start | bytes 147464 | tf_op jit(solution)/shard_map/ppermute | solution.py:448
  247.0 1.3 collective-permute-start.51

commit v2 on v1

--- a/solution.py
+++ b/solution.py
@@ -35,27 +35,16 @@
         edge[q] = wire[bnd[q]]
 
 
-def loop(count, body):
-    def step(i, carry):
-        body(i)
-        return carry
-
-    lax.fori_loop(0, count, step, 0)
-
-
 def fill_halo(wires, edges, pos, halo):
-    n_row, n_z = len(wires), len(edges)
-    lb, ifr = wires[0][2], edges[0][0][2]
-    for k, (wire, offset, count) in enumerate(wires):
+    n_row = len(wires)
+    lb = wires[0].shape[0]
+    for k, wire in enumerate(wires):
         start = (pos[0] ^ k) * lb
-
-        def copy(i, wire=wire, offset=offset, start=start):
-            halo[start + i] = wire[offset + i]
-
-        loop(count, copy)
+        for i in range(lb):
+            halo[start + i] = wire[i]
     for k, pair in enumerate(edges):
         for other, (edge, offset, count) in enumerate(pair):
-            start = n_row * lb + (((pos[1] // 2) ^ k) * 2 + ((pos[1] % 2) ^ other)) * ifr
+            start = n_row * lb + (((pos[1] // 2) ^ k) * 2 + ((pos[1] % 2) ^ other)) * count
             for q in range(count):
                 halo[start + q] = edge[offset + q]
 
@@ -113,17 +102,20 @@
     order = table.shape[0]
     rows = lax.broadcasted_iota(jnp.int32, table.shape, 0)
     for j in range(0, order, 2):
+        left = jnp.broadcast_to(table[:, j : j + 1], table.shape)
+        right = jnp.broadcast_to(table[:, j + 1 : j + 2], table.shape)
         one, two = table[j : j + 1, :], table[j + 1 : j + 2, :]
-        a, b = one[:, j : j + 1], one[:, j + 1 : j + 2]
-        c, d = two[:, j : j + 1], two[:, j + 1 : j + 2]
-        scale = 1.0 / (a * d - b * c)
-        first = (d * scale) * one - (b * scale) * two
-        second = (a * scale) * two - (c * scale) * one
-        moved = table - table[:, j : j + 1] * first - table[:, j + 1 : j + 2] * second
+        over = 1.0 / left[j : j + 1, :]
+        ratio = left[j + 1 : j + 2, :] * over
+        beside = right[j : j + 1, :]
+        two = two - ratio * one
+        second = two * (1.0 / (right[j + 1 : j + 2, :] - ratio * beside))
+        first = (one - beside * second) * over
+        moved = table - left * first - right * second
         if full:
             table = jnp.where(rows == j, first, jnp.where(rows == j + 1, second, moved))
         else:
-            table = jnp.where(rows > j + 1, moved, jnp.where(rows == j + 1, two - (c / a) * one, table))
+            table = jnp.where(rows > j + 1, moved, jnp.where(rows == j + 1, two, table))
     return table
 
 
@@ -171,16 +163,21 @@
 
 def prepare_kernel(groups, base, vals, faces, rows, cols, face_rows, face_src, stored, joined, diagonal, where):
     lb, kb = faces.shape[0], faces.shape[1]
+
+    def twice(block):
+        wide = block.astype(f32)
+        return jnp.concatenate([wide, wide], axis=1).astype(bf16)
+
     for k in range(lb):
-        diagonal[k] = vals[k]
+        diagonal[k] = twice(vals[k])
     for g in range(groups):
         half = (g % 2) * kb
         for m in range(lb):
             if g < groups - 1:
                 k = (g + 1) * lb + m
-                i, target, block = rows[k], cols[k], vals[k]
+                i, target, block = rows[k], cols[k], twice(vals[k])
             else:
-                i, target, block = face_rows[m], base + face_src[m], faces[m]
+                i, target, block = face_rows[m], base + face_src[m], twice(faces[m])
             stored[i, :, 2 * kb * g : 2 * kb * (g + 1)] = block
             joined[i, :, kb * g : kb * (g + 1)] = block[:, half : half + kb]
             where[i * groups + g] = target
@@ -190,12 +187,11 @@
     write_wire(vector, bnd, wire, edge)
 
 
-def partial_kernel(n_row, n_z, count, extra, *refs):
+def partial_kernel(n_row, n_z, count, *refs):
     refs = list(refs)
     take = lambda number: [refs.pop(0) for _ in range(number)]
     wires = take(count)
     joined, where, pos = take(3)
-    more_wire, more_edge = take(2) if extra else (None, None)
     own, core_keep, core_send = take(3)
     row_outs, acc = refs[:-1], refs[-1]
     lb, kb = wires[0].shape[0], wires[0].shape[2] // 2
@@ -205,8 +201,7 @@
     core = pos[1] % 2
     for v, wire in enumerate(wires):
         acc[...] = jnp.zeros(acc.shape, f32)
-
-        def step(i):
+        for i in range(lb):
             blocks = jnp.concatenate([joined[i], joined[i]], axis=0)
             out = jnp.dot(wire[i], blocks, preferred_element_type=f32)
             for t in range(groups // 2):
@@ -216,40 +211,25 @@
                 acc[one] = acc[one] + jnp.where(low, tile, 0.0)
                 acc[two] = acc[two] + jnp.where(low, 0.0, tile)
 
-        loop(lb, step)
-
         def folded(index):
             block = acc[index]
             return block[:, :kb] + block[:, kb:]
 
         for k in range(n_row):
             start = (pos[0] ^ k) * lb
-
-            def emit(i, k=k, start=start):
+            for i in range(lb):
                 if k == 0:
                     own[v * lb + i] = folded(start + i)
                 else:
                     row_outs[k - 1][v * lb + i] = two_parts(folded(start + i))
-
-            loop(lb, emit)
-
-        def emit_edge(z):
+        for z in range(n_z):
             for q in range(ifr):
                 spot = (v * n_z + z) * ifr + q
                 core_keep[spot] = folded(n_row * lb + (z * 2 + core) * ifr + q)
                 core_send[spot] = two_parts(folded(n_row * lb + (z * 2 + 1 - core) * ifr + q))
 
-        loop(n_z, emit_edge)
-    if extra:
-        for k in range(1, n_row):
-            row_outs[k - 1][pl.ds(count * lb, lb)] = more_wire[...]
-        core_send[pl.ds(count * n_z * ifr, ifr)] = more_edge[...]
-
-
-def pair_kernel(n_z, count, extra, keep, got, pos, *refs):
-    refs = list(refs)
-    more_edge = refs.pop(0) if extra else None
-    own, outs = refs[0], refs[1:]
+
+def pair_kernel(n_z, count, keep, got, pos, own, *outs):
     ifr, kb = own.shape[0] // count, own.shape[2]
     for k in range(n_z):
         z = (pos[1] // 2) ^ k
@@ -262,41 +242,39 @@
                     own[v * ifr + q] = total
                 else:
                     outs[k - 1][v * ifr + q] = two_parts(total)
-        if extra and k > 0:
-            outs[k - 1][pl.ds(count * ifr, ifr)] = more_edge[...]
-            outs[k - 1][pl.ds((count + 1) * ifr, ifr)] = got[pl.ds(count * n_z * ifr, ifr)]
 
 
 def split_halo(refs, n_row, n_z):
     wires = [refs.pop(0) for _ in range(n_row)]
     same, other = refs.pop(0), refs.pop(0)
-    lb, ifr = wires[0].shape[0], same.shape[0] // n_z
-    return [(wire, 0, lb) for wire in wires], [((same, k * ifr, ifr), (other, k * ifr, ifr)) for k in range(n_z)]
+    ifr = same.shape[0] // n_z
+    return wires, [((same, k * ifr, ifr), (other, k * ifr, ifr)) for k in range(n_z)]
 
 
 def x_image_kernel(n_row, n_z, *refs):
     refs = list(refs)
     wires, edges = split_halo(refs, n_row, n_z)
-    stored, diagonal, where, pos, x, half, diag, table, halo = refs
+    stored, diagonal, where, pos, x, p, half, diag, table, halo = refs
     n = x.shape[0]
     fill_halo(wires, edges, pos, halo)
-    forward(halo, wires[0][0], stored, diagonal, where, half, diag)
+    forward(halo, wires[0], stored, diagonal, where, half, diag)
     half[...] = half[...] + 0.5 * diag[...]
-    table[...] = nt(x[...], jnp.concatenate([half[...], x[...]], axis=0))
-
-
-def p_image_kernel(n_row, n_z, ifr, *refs):
+    table[0:n, :] = nt(x[...], jnp.concatenate([half[...], x[...]], axis=0))
+    table[n : 2 * n, :] = nt(p[...], jnp.concatenate([x[...], p[...]], axis=0))
+
+
+def p_image_kernel(n_row, n_z, *refs):
     refs = list(refs)
-    wire, edge, core_got = refs[:3]
-    rows, edges = refs[3 : 2 + n_row], refs[2 + n_row : 1 + n_row + n_z]
-    stored, diagonal, where, pos, half, diag, halo = refs[1 + n_row + n_z :]
-    lb = wire.shape[0]
-    wires = [(wire, 0, lb)] + [(row, lb, lb) for row in rows]
-    pairs = [((edge, 0, ifr), (core_got, n_z * ifr, ifr))]
-    pairs += [((got, ifr, ifr), (got, 2 * ifr, ifr)) for got in edges]
-    fill_halo(wires, pairs, pos, halo)
-    forward(halo, wire, stored, diagonal, where, half, diag)
+    wires, edges = split_halo(refs, n_row, n_z)
+    stored, diagonal, where, pos, x, half_x, p, before, half, diag, keep, send, halo, table = refs
+    n = x.shape[0]
+    fill_halo(wires, edges, pos, halo)
+    forward(halo, wires[0], stored, diagonal, where, half, diag)
     half[...] = half[...] + 0.5 * diag[...]
+    table[0 : 2 * n, :] = before[...]
+    table[2 * n : 3 * n, :] = nt(p[...], jnp.concatenate([half[...], half_x[...]], axis=0))
+    table[2 * n : 3 * n, n:] = table[2 * n : 3 * n, n:] + nt(half[...], x[...])
+    write_halves(table, pos, keep, send)
 
 
 def take_returned(refs, n_row, n_z):
@@ -309,17 +287,24 @@
 def update_kernel(n_row, n_z, *refs):
     refs = list(refs)
     back_parts = take_returned(refs, n_row, n_z)
-    bnd, table, x, half, diag, precond, ax, energy, w, wire, edge, back = refs
+    mine, other, pos, bnd, x, half, diag, precond, table, ax, energy, w, wire, edge, back = refs
     n = x.shape[0]
+    read_halves(mine, other, pos, table)
     returned(0, *back_parts, bnd, back)
     ax[...] = half[...] + 0.5 * diag[...]
     add_returned(back, ax)
-    stored, gram = table[:, 0:n], table[:, n:]
+    stored, gram = table[0:n, 0:n], table[0:n, n:]
     total = stored + stored.T
     energy[...] = total
     ritz = nn(total, inverse(0.5 * (gram + gram.T)))
     w[...] = precond[...] * (ax[...] - nn(ritz, x[...]))
     write_wire(w, bnd, wire, edge)
+
+
+def inverse_kernel(table, solved):
+    n = solved.shape[0]
+    stored = table[2 * n : 3 * n, 0:n]
+    solved[...] = inverse(stored + stored.T)
 
 
 def update_image_kernel(n_row, n_z, first, *refs):
@@ -328,7 +313,7 @@
     stored, diagonal, where, pos, w, x, p, ax, ap, half, diag, keep, send, halo, table = refs
     n = w.shape[0]
     fill_halo(wires, edges, pos, halo)
-    forward(halo, wires[0][0], stored, diagonal, where, half, diag)
+    forward(halo, wires[0], stored, diagonal, where, half, diag)
     half[...] = half[...] + 0.5 * diag[...]
     here = w[...]
     table[0:n, :] = nt(here, jnp.concatenate([half[...], ap[...]], axis=0))
@@ -336,23 +321,21 @@
     table[2 * n : 3 * n, :] = nt(here, jnp.concatenate([p[...], here], axis=0))
     if first:
         table[0:n, n:] = table[0:n, n:] + nt(half[...], p[...])
-        table[3 * n : 4 * n, :] = nt(p[...], jnp.concatenate([ax[...], ap[...]], axis=0))
-        table[4 * n : 5 * n, :] = nt(p[...], jnp.concatenate([x[...], p[...]], axis=0))
     write_halves(table, pos, keep, send)
 
 
 def move_kernel(n_row, n_z, total_rows, *refs):
     refs = list(refs)
     back_parts = take_returned(refs, n_row, n_z)
-    mine, other, pos, bnd, gram, energy, x, p, ax, ap, ap_diag, w, aw, aw_diag, precond = refs[:15]
-    x_out, ax_out, w_out, wire, edge, step_x, step_a, small, table, back = refs[15:]
+    mine, other, pos, bnd, start, energy, pap_inverse, x, p, ax, ap, ap_diag, w, aw, aw_diag, precond = refs[:16]
+    x_out, ax_out, w_out, wire, edge, step_x, step_a, small, table, back = refs[16:]
     n = x.shape[0]
     read_halves(mine, other, pos, table)
-    gram_here = gram[:, n:]
-    pax, pap = table[3 * n : 4 * n, 0:n], table[3 * n : 4 * n, n:]
-    px, pp = table[4 * n : 5 * n, 0:n], table[4 * n : 5 * n, n:]
+    gram = start[0:n, n:]
+    px, pp = start[n : 2 * n, 0:n], start[n : 2 * n, n:]
+    pax = start[2 * n : 3 * n, n:]
     zw, zp, zwt, zpt, cross, inner, wax, scale = coefficients(
-        table, 0.5 * (gram_here + gram_here.T), px.T, pp, pax, inverse(pap + pap.T), total_rows
+        table, 0.5 * (gram + gram.T), px.T, pp, pax, pap_inverse[...], total_rows
     )
     step_a[...] = nn(zpt, ap[...] + 0.5 * ap_diag[...]) + nn(zwt, aw[...] + 0.5 * aw_diag[...])
     returned(0, *back_parts, bnd, back)
@@ -455,48 +438,54 @@
         same = jnp.concatenate([edge] + [sub_send(edge, 2 * k) for k in range(1, n_z)], axis=0)
         return [own] + rows_got + [same, sub_send(same, 1)]
 
-    def doubled(value):
+    def sum_halves(keep, send):
+        total = keep + sub_send(send, 1)
         k = 1
         while k < n_row:
-            value = value + row_send(value, k)
+            total = total + row_send(total, k)
             k *= 2
         k = 2
         while k < n_sub:
-            value = value + sub_send(value, k)
+            total = total + sub_send(total, k)
             k *= 2
-        return value
-
-    def sum_halves(keep, send):
-        mine = doubled(keep + sub_send(send, 1))
-        return [mine, sub_send(mine, 1)]
-
-    def partials(wires, more):
-        m, e = len(wires), 1 if more else 0
-        outs = [shaped(m * lb, n, kb), shaped(m * n_z * ifr, n, kb), wire((m * n_z + e) * ifr)]
-        outs += [wire((m + e) * lb)] * (n_row - 1)
+        return [total, sub_send(total, 1)]
+
+    def partials(wires):
+        m = len(wires)
+        outs = [shaped(m * lb, n, kb), shaped(m * n_z * ifr, n, kb), wire(m * n_z * ifr)]
+        outs += [wire(m * lb)] * (n_row - 1)
         return run(
-            functools.partial(partial_kernel, n_row, n_z, m, e > 0),
+            functools.partial(partial_kernel, n_row, n_z, m),
             "partials",
             outs,
-            wires + [joined, where, pos] + more,
+            wires + [joined, where, pos],
             [VMEM((halo_blocks, n, 2 * kb), f32)],
             smem=(m + 1, m + 2),
         )
 
-    def send_partials(parts, m, more):
-        own, keep, send, *row_parts = parts
-        e = 1 if more else 0
+    def sum_with_partials(keep, send, parts, m):
+        own, edge_keep, edge_send, *row_parts = parts
+        total = keep + sub_send(send, 1)
+        edge_got = sub_send(edge_send, 1)
         rows_got = [row_send(row_parts[k - 1], k) for k in range(1, n_row)]
-        got = sub_send(send, 1)
         edge_own, *outs = run(
-            functools.partial(pair_kernel, n_z, m, e > 0),
+            functools.partial(pair_kernel, n_z, m),
             "pair",
-            [shaped(m * ifr, n, kb)] + [wire((m + 2 * e) * ifr)] * (n_z - 1),
-            [keep, got, pos] + more,
+            [shaped(m * ifr, n, kb)] + [wire(m * ifr)] * (n_z - 1),
+            [edge_keep, edge_got, pos],
             smem=(2,),
         )
+        k = 2
+        while k < n_sub:
+            total = total + sub_send(total, k)
+            k *= 2
+        total, *outs = after((total, *outs))
         edges_got = [sub_send(outs[k - 1], 2 * k) for k in range(1, n_z)]
-        return [own] + rows_got + [edge_own] + edges_got, got
+        k = 1
+        while k < n_row:
+            total = total + row_send(total, k)
+            k *= 2
+        return [total, sub_send(total, 1)], [own] + rows_got + [edge_own] + edges_got
 
     x, p = modes.T, search.T
     scaling = precond.reshape(1, rows)
@@ -504,8 +493,6 @@
     x_wire, x_edge = run(wire_kernel, "wire", wire_shapes, [x, bnd], smem=(1,))
     x_halo = halo_of(x_wire, x_edge)
     p_wire, p_edge = run(wire_kernel, "wire", wire_shapes, [p, bnd], smem=(1,))
-    twice = jnp.concatenate([in_val[0, 0], in_val[0, 0]], axis=-1)
-    twice_face = jnp.concatenate([if_val[0, 0], if_val[0, 0]], axis=-1)
     stored, joined, diagonal, where = run(
         functools.partial(prepare_kernel, groups, n_row * lb),
         "prepare",
@@ -515,11 +502,14 @@
             shaped(lb, kb, 2 * kb, dtype=bf16),
             shaped(lb * groups, dtype=jnp.int32),
         ],
-        [twice, twice_face, in_row[0, 0], in_col[0, 0], if_row[0, 0], if_src[0, 0]],
+        [in_val[0, 0], if_val[0, 0], in_row[0, 0], in_col[0, 0], if_row[0, 0], if_src[0, 0]],
         smem=(2, 3, 4, 5),
         smem_outs=(3,),
     )
-    x_parts = partials([x_wire], [p_wire, p_edge])
+    p_wire, p_edge, *x_got = after((p_wire, p_edge, *x_halo[1:]))
+    x_halo = [x_wire] + x_got
+    p_halo = halo_of(p_wire, p_edge)
+    x_parts = partials([x_wire])
     blocks = [stored, diagonal, where, pos]
     halo_scratch = VMEM((halo_blocks, n, 2 * kb), bf16)
     back_scratch = VMEM((lb, n, kb), f32)
@@ -529,60 +519,58 @@
     half_x, diag_x, table = run(
         functools.partial(x_image_kernel, n_row, n_z),
         "x_image",
-        [whole, whole, shaped(n, 2 * n)],
-        x_halo + blocks + [x],
+        [whole, whole, shaped(2 * n, 2 * n)],
+        x_halo + blocks + [x, p],
         [halo_scratch],
         smem=(count + 2, count + 3),
     )
-    table, x_parts = after((table, x_parts))
-    table = doubled(table)
-    table = table + sub_send(table, 1)
-    x_back, core_got = send_partials(x_parts, 1, [p_edge])
-    p_rows, p_edges = x_back[1:n_row], x_back[n_row + 1 :]
+    table_shape = shaped(3 * n, 2 * n)
+    halves_shape = [shaped(3 * n // 2, 2 * n)] * 2
+    table_scratch = VMEM((3 * n, 2 * n), f32)
+    half_p, diag_p, keep, send = run(
+        functools.partial(p_image_kernel, n_row, n_z),
+        "p_image",
+        [whole, whole] + halves_shape,
+        p_halo + blocks + [x, half_x, p, table],
+        [halo_scratch, table_scratch],
+        smem=(count + 2, count + 3),
+    )
+    keep, send, x_parts = after((keep, send, x_parts))
+    halves, x_back = sum_with_partials(keep, send, x_parts, 1)
     count = len(x_back)
-    ax, energy, w, w_wire, w_edge = run(
+    table, ax, energy, w, w_wire, w_edge = run(
         functools.partial(update_kernel, n_row, n_z),
         "update",
-        [whole, shaped(n, n), whole] + wire_shapes,
-        x_back + [bnd, table, x, half_x, diag_x, scaling],
+        [table_shape, whole, shaped(n, n), whole] + wire_shapes,
+        x_back + halves + [pos, bnd, x, half_x, diag_x, scaling],
         [back_scratch],
-        smem=(count,),
+        smem=(count + 2, count + 3),
     )
     w_halo = halo_of(w_wire, w_edge)
-    count = 1 + n_row + n_z
-    half_p, diag_p = run(
-        functools.partial(p_image_kernel, n_row, n_z, ifr),
-        "p_image",
-        [whole, whole],
-        [p_wire, p_edge, core_got] + p_rows + p_edges + blocks,
-        [halo_scratch],
-        smem=(count + 2, count + 3),
-    )
-    w_parts = partials([p_wire, w_wire], [])
+    (pap_inverse,) = run(inverse_kernel, "pap_inverse", [shaped(n, n)], [table])
+    w_parts = partials([p_wire, w_wire])
 
     def update_image(first, halo, w, x, p, ax, ap):
         count = len(halo)
-        height = (5 if first else 3) * n
         return run(
             functools.partial(update_image_kernel, n_row, n_z, first),
             "update_image",
-            [whole, whole, shaped(height // 2, 2 * n), shaped(height // 2, 2 * n)],
+            [whole, whole] + halves_shape,
             halo + blocks + [w, x, p, ax, ap],
-            [halo_scratch, VMEM((height, 2 * n), f32)],
+            [halo_scratch, table_scratch],
             smem=(count + 2, count + 3),
         )
 
     half_w, diag_w, keep, send = update_image(True, w_halo, w, x, p, ax, half_p)
     keep, send, w_parts = after((keep, send, w_parts))
-    halves = sum_halves(keep, send)
-    w_back, _ = send_partials(w_parts, 2, [])
+    halves, w_back = sum_with_partials(keep, send, w_parts, 2)
     count = len(w_back)
     x, ax, w, w_wire, w_edge, step_x, step_a, small = run(
         functools.partial(move_kernel, n_row, n_z, total_rows),
         "move",
         [whole] * 3 + wire_shapes + [whole, whole, shaped(4 * n, n)],
-        w_back + halves + [pos, bnd, table, energy, x, p, ax, half_p, diag_p, w, half_w, diag_w, scaling],
-        [VMEM((5 * n, 2 * n), f32), back_scratch],
+        w_back + halves + [pos, bnd, table, energy, pap_inverse, x, p, ax, half_p, diag_p, w, half_w, diag_w, scaling],
+        [table_scratch, back_scratch],
         smem=(count + 2, count + 3),
     )
     w_halo = halo_of(w_wire, w_edge)
@@ -594,7 +582,7 @@
         "finish",
         [whole, whole],
         halves + [pos, state, x, p, w],
-        [VMEM((3 * n, 2 * n), f32)],
+        [table_scratch],
         smem=(2,),
     )
     return (x.T, p.T)

time: 270 us -> 184 us (0.68)
  Pallas kernels: 120 us -> 58.9 us
  waiting for transfers between devices: 77.2 us -> 59 us
  starting transfers between devices: 62.2 us -> 57.5 us
  other arithmetic: 3.16 us -> 0.19 us
    pallas_call x15 -> x16, Pallas kernels: 120 us -> 58.9 us  [run(): pl.pallas_call(kernel, name=name, out_shape=outs, in_specs=in_specs, out_...]
    ppermute x21 -> x24, waiting for transfers between devices: 42.7 us -> 21.4 us  [row_send(): return lax.ppermute(value, 'row', [(r, r ^ k) for r in range(n_row)])]
    ppermute x31 -> x36, starting transfers between devices: 37.2 us -> 28.9 us  [sub_send(): return lax.ppermute(value, 'sub', [(s, s ^ k) for s in range(n_sub)])]
    ppermute x21 -> x24, starting transfers between devices: 25 us -> 28.6 us  [row_send(): return lax.ppermute(value, 'row', [(r, r ^ k) for r in range(n_row)])]
    ppermute x31 -> x36, waiting for transfers between devices: 34.5 us -> 37.6 us  [sub_send(): return lax.ppermute(value, 'sub', [(s, s ^ k) for s in range(n_sub)])]
    concatenate x2 -> x0, other arithmetic: 2.96 us -> none  [the longest x1 2.83 us: local(): twice = jnp.concatenate([in_val[0, 0], in_val[0, 0]], axis=-1)]
    unnamed x32 -> x39, local copies, waits for them, and re-layouts: 5.8 us -> 6.79 us
  transfers between devices with their start and end apart: 52 -> 60, of which waited for: 20 -> 25; matrix products, arithmetic and copies ran while one was open for 3% -> 2% of each run, Pallas kernels for 17% -> 13%
where the time goes in v2:
time: 184 us
  waiting for transfers between devices  59 us (32%)
  Pallas kernels  58.9 us (32%)
  starting transfers between devices  57.5 us (31%)
  local copies, waits for them, and re-layouts  6.84 us (4%)
    pallas_call x16, Pallas kernels, run(): pl.pallas_call(kernel, name=name, out_shape=outs, in_specs=in_specs, out_...  58.9 us
    ppermute x36, waiting for transfers between devices, sub_send(): return lax.ppermute(value, 'sub', [(s, s ^ k) for s in range(n_sub)])  37.6 us
    ppermute x36, starting transfers between devices, sub_send(): return lax.ppermute(value, 'sub', [(s, s ^ k) for s in range(n_sub)])  28.9 us
    ppermute x24, starting transfers between devices, row_send(): return lax.ppermute(value, 'row', [(r, r ^ k) for r in range(n_row)])  28.6 us
    ppermute x24, waiting for transfers between devices, row_send(): return lax.ppermute(value, 'row', [(r, r ^ k) for r in range(n_row)])  21.4 us
    unnamed x39, local copies, waits for them, and re-layouts  6.79 us
  transfers between devices with their start and end apart: 60, of which 25 were waited for; matrix products, arithmetic and copies ran while one was open for 2% of the time, Pallas kernels for 13%

profile of v2, /device:TPU:0, one launch (start us, length us, event | category | flops | bytes accessed | tf_op | source)
XLA Modules:
  0.0 183.6 jit_solution(5475405097020094176)
XLA Ops:
  2.9 3.1 %collective-permute-start.3 = (bf16[3,64,128]{2,1,0:T(8,128)(2,1)S(1)}, bf16[3,64,128]{2,1,0:T(8,128)(2,1)S(1)}, u32[]{:S(2)}, u32[]{:S(2)}) collective-permute-start(bf16[3,64,128]{2,1,0:T(8,128)(2,1)S(1)} %get-tuple-element.96), channel_id=1, source_target_pairs={{0,8},{4,12},{8,0},{12,4},{16,24},{20,28},{24,16},{28,20},{1,9},{5... | collective-permute-start | bytes 147464 | tf_op jit(solution)/shard_map/ppermute | solution.py:431
  6.0 2.6 %collective-permute-start.4 = (bf16[3,64,128]{2,1,0:T(8,128)(2,1)S(1)}, bf16[3,64,128]{2,1,0:T(8,128)(2,1)S(1)}, u32[]{:S(2)}, u32[]{:S(2)}) collective-permute-start(bf16[3,64,128]{2,1,0:T(8,128)(2,1)S(1)} %get-tuple-element.96), channel_id=1, source_target_pairs={{0,16},{4,20},{8,24},{12,28},{16,0},{20,4},{24,8},{28,12},{1,17},{... | collective-permute-start | bytes 147464 | tf_op jit(solution)/shard_map/ppermute | solution.py:431
  8.6 1.7 collective-permute-start
  10.3 1.5 collective-permute-start.1
  12.2 2.3 %collective-permute-done.5 = bf16[3,64,128]{2,1,0:T(8,128)(2,1)S(1)} collective-permute-done((bf16[3,64,128]{2,1,0:T(8,128)(2,1)S(1)}, bf16[3,64,128]{2,1,0:T(8,128)(2,1)S(1)}, u32[]{:S(2)}, u32[]{:S(2)}) %collective-permute-start.5) | collective-permute-done | bytes 49184 | tf_op jit(solution)/shard_map/ppermute | solution.py:431
  16.8 3.3 %collective-permute-done.1.refs_2_ = bf16[12,64,128]{2,1,0:T(8,128)(2,1)S(1)} collective-permute-done((bf16[12,64,128]{2,1,0:T(8,128)(2,1)S(1)}, bf16[12,64,128]{2,1,0:T(8,128)(2,1)S(1)}, u32[]{:S(2)}, u32[]{:S(2)}) %collective-permute-start.1) | collective-permute-done | bytes 196640 | tf_op jit(solution)/shard_map/ppermute | solution.py:428
  20.8 3.5 %collective-permute-start.11 = (bf16[3,64,128]{2,1,0:T(8,128)(2,1)S(1)}, bf16[3,64,128]{2,1,0:T(8,128)(2,1)S(1)}, u32[]{:S(2)}, u32[]{:S(2)}) collective-permute-start(bf16[3,64,128]{2,1,0:T(8,128)(2,1)S(1)} %get-tuple-element.98), channel_id=1, source_target_pairs={{0,16},{4,20},{8,24},{12,28},{16,0},{20,4},{24,8},{28,12},{1,17},{... | collective-permute-start | bytes 147464 | tf_op jit(solution)/shard_map/ppermute | solution.py:431
  24.6 1.1 collective-permute-start.7
  26.5 1.5 collective-permute-start.9
  28.1 2.1 %collective-permute-done.12 = bf16[3,64,128]{2,1,0:T(8,128)(2,1)S(1)} collective-permute-done((bf16[3,64,128]{2,1,0:T(8,128)(2,1)S(1)}, bf16[3,64,128]{2,1,0:T(8,128)(2,1)S(1)}, u32[]{:S(2)}, u32[]{:S(2)}) %collective-permute-start.12) | collective-permute-done | bytes 49184 | tf_op jit(solution)/shard_map/ppermute | solution.py:431
  30.3 3.5 %copy.12 = bf16[1,1,96,64,64]{4,3,2,1,0:T(8,128)(2,1)S(1)} copy(bf16[1,1,96,64,64]{2,4,3,1,0:T(8,128)(2,1)} %param.15) | data formatting | bytes 1572864 | tf_op args[5]
  33.8 2.2 %prepare.1 = (bf16[12,64,1024]{2,1,0:T(8,128)(2,1)S(1)}, bf16[12,64,512]{2,1,0:T(8,128)(2,1)S(1)}, bf16[12,64,128]{2,1,0:T(8,128)(2,1)S(1)}, s32[96]{0:T(128)S(1)}) custom-call(bf16[96,64,64]{2,1,0:T(8,128)(2,1)S(1)} %bitcast.19, bf16[12,64,64]{2,1,0:T(8,128)(2,1)S(1)} %bitcast.25, s32[96]{0:T(128)S(1)} %bitcast.30, s32[96]{0:T(128)S(1)} %bitcast.31, ...), custom_call_target="tpu_custom_call" | custom-call | flops 1000000 | bytes 3441888 | tf_op jit(solution)/shard_map/prepare/pallas_call | solution.py:397
  36.1 2.4 %partials.2 = (f32[12,64,64]{2,1,0:T(8,128)S(1)}, f32[12,64,64]{2,1,0:T(8,128)S(1)}, bf16[12,64,128]{2,1,0:T(8,128)(2,1)S(1)}, bf16[12,64,128]{2,1,0:T(8,128)(2,...) custom-call(bf16[12,64,128]{2,1,0:T(8,128)(2,1)S(1)} %get-tuple-element.95.refs_0_, ...), custom_call_target="tpu_custom_call" | custom-call | flops 1000000 | bytes 2163080 | tf_op jit(solution)/shard_map/partials/pallas_call | solution.py:397
  38.6 2.1 %x_image.1 = (f32[64,768]{1,0:T(8,128)S(1)}, f32[64,768]{1,0:T(8,128)S(1)}, f32[128,128]{1,0:T(8,128)S(1)}) custom-call(bf16[12,64,128]{2,1,0:T(8,128)(2,1)S(1)} %get-tuple-element.95.refs_0_, bf16[12,64,128]{2,1,0:T(8,128)(2,1)S(1)} %collective-permute-done.refs_1_, bf16[12,64,128]{2,1,0:T(8,128)(2,1)S(1)} %collective-permute-done.1.refs_2_, ...), custom_call_target="tpu_custom_call" | custom-call | flops 1000000 | bytes 3801480 | tf_op jit(solution)/shard_map/x_image/pallas_call | solution.py:397
  40.8 2.5 %p_image.1 = (f32[64,768]{1,0:T(8,128)S(1)}, f32[64,768]{1,0:T(8,128)S(1)}, f32[96,128]{1,0:T(8,128)S(1)}, f32[96,128]{1,0:T(8,128)S(1)}) custom-call(bf16[12,64,128]{2,1,0:T(8,128)(2,1)S(1)} %get-tuple-element.97.refs_0_, bf16[12,64,128]{2,1,0:T(8,128)(2,1)S(1)} %collective-permute-done.7.refs_1_, bf16[12,64,128]{2,1,0:T(8,128)(2,1)} %collective-permute-done.8.refs_2_, ...), custom_call_target="tpu_custom_call" | custom-call | flops 1000000 | bytes 4096392 | tf_op jit(solution)/shard_map/p_image/pallas_call | solution.py:397
  43.9 1.2 collective-permute-done.18
  45.1 1.2 collective-permute-start.14
  47.1 2.1 %collective-permute-done.19 = f32[96,128]{1,0:T(8,128)S(1)} collective-permute-done((f32[96,128]{1,0:T(8,128)S(1)}, f32[96,128]{1,0:T(8,128)S(1)}, u32[]{:S(2)}, u32[]{:S(2)}) %collective-permute-start.19) | collective-permute-done | bytes 49184 | tf_op jit(solution)/shard_map/ppermute | solution.py:431
  49.4 1.4 collective-permute-start.16
  50.8 3.5 %collective-permute-done.20 = f32[96,128]{1,0:T(8,128)S(1)} collective-permute-done((f32[96,128]{1,0:T(8,128)S(1)}, f32[96,128]{1,0:T(8,128)S(1)}, u32[]{:S(2)}, u32[]{:S(2)}) %collective-permute-start.20) | collective-permute-done | bytes 49184 | tf_op jit(solution)/shard_map/ppermute | solution.py:431
  55.2 1.3 collective-permute-start.24
  56.5 2.8 %collective-permute-done.24 = f32[96,128]{1,0:T(8,128)S(1)} collective-permute-done((f32[96,128]{1,0:T(8,128)S(1)}, f32[96,128]{1,0:T(8,128)S(1)}, u32[]{:S(2)}, u32[]{:S(2)}) %collective-permute-start.24) | collective-permute-done | bytes 49184 | tf_op jit(solution)/shard_map/ppermute | solution.py:428
  59.4 1.5 collective-permute-start.25
  60.9 2.6 %collective-permute-done.25 = f32[96,128]{1,0:T(8,128)S(1)} collective-permute-done((f32[96,128]{1,0:T(8,128)S(1)}, f32[96,128]{1,0:T(8,128)S(1)}, u32[]{:S(2)}, u32[]{:S(2)}) %collective-permute-start.25) | collective-permute-done | bytes 49184 | tf_op jit(solution)/shard_map/ppermute | solution.py:428
  64.0 2.0 %collective-permute-start.23 = (bf16[3,64,128]{2,1,0:T(8,128)(2,1)S(1)}, bf16[3,64,128]{2,1,0:T(8,128)(2,1)S(1)}, u32[]{:S(2)}, u32[]{:S(2)}) collective-permute-start(bf16[3,64,128]{2,1,0:T(8,128)(2,1)S(1)} %get-tuple-element.132), channel_id=1, source_target_pairs={{0,24},{4,28},{8,16},{12,20},{16,8},{20,12},{24,0},{28,4},{1,25},{... | collective-permute-start | bytes 147464 | tf_op jit(solution)/shard_map/ppermute | solution.py:431
  66.0 2.5 %collective-permute-done.22.refs_6_ = bf16[3,64,128]{2,1,0:T(8,128)(2,1)S(1)} collective-permute-done((bf16[3,64,128]{2,1,0:T(8,128)(2,1)S(1)}, bf16[3,64,128]{2,1,0:T(8,128)(2,1)S(1)}, u32[]{:S(2)}, u32[]{:S(2)}) %collective-permute-start.22) | collective-permute-done | bytes 49184 | tf_op jit(solution)/shard_map/ppermute | solution.py:431
  68.5 1.4 collective-permute-done.23.refs_7_
  69.9 5.2 %update.1 = (f32[192,128]{1,0:T(8,128)S(1)}, f32[64,768]{1,0:T(8,128)S(1)}, f32[64,64]{1,0:T(8,128)S(1)}, f32[64,768]{1,0:T(8,128)S(1)}, bf16[12,64,128]{2,1,0:T...) custom-call(f32[12,64,64]{2,1,0:T(8,128)S(1)} %get-tuple-element.118.refs_0_, ...), custom_call_target="tpu_custom_call" | custom-call | flops 1000000 | bytes 2427924 | tf_op jit(solution)/shard_map/update/pallas_call | solution.py:397
  75.2 2.6 %collective-permute-start.31 = (bf16[3,64,128]{2,1,0:T(8,128)(2,1)S(1)}, bf16[3,64,128]{2,1,0:T(8,128)(2,1)S(1)}, u32[]{:S(2)}, u32[]{:S(2)}) collective-permute-start(bf16[3,64,128]{2,1,0:T(8,128)(2,1)S(1)} %get-tuple-element.136), channel_id=1, source_target_pairs={{0,16},{4,20},{8,24},{12,28},{16,0},{20,4},{24,8},{28,12},{1,17},{... | collective-permute-start | bytes 147464 | tf_op jit(solution)/shard_map/ppermute | solution.py:431
  77.8 1.7 collective-permute-start.32
  79.5 1.0 collective-permute-start.27
  81.3 1.8 collective-permute-start.29
  83.8 5.3 %partials.3 = (f32[24,64,64]{2,1,0:T(8,128)S(1)}, f32[24,64,64]{2,1,0:T(8,128)S(1)}, bf16[24,64,128]{2,1,0:T(8,128)(2,1)S(1)}, bf16[24,64,128]{2,1,0:T(8,128)(2,...) custom-call(bf16[12,64,128]{2,1,0:T(8,128)(2,1)S(1)} %get-tuple-element.97.refs_0_, ...), custom_call_target="tpu_custom_call" | custom-call | flops 1000000 | bytes 3539336 | tf_op jit(solution)/shard_map/partials/pallas_call | solution.py:397
  89.1 3.0 %update_image.2 = (f32[64,768]{1,0:T(8,128)S(1)}, f32[64,768]{1,0:T(8,128)S(1)}, f32[96,128]{1,0:T(8,128)S(1)}, f32[96,128]{1,0:T(8,128)S(1)}) custom-call(bf16[12,64,128]{2,1,0:T(8,128)(2,1)S(1)} %get-tuple-element.135.refs_0_.refs_1_, bf16[12,64,128]{2,1,0:T(8,128)(2,1)S(1)} %collective-permute-done.27.refs_1_, ...), custom_call_target="tpu_custom_call" | custom-call | flops 1000000 | bytes 4424072 | tf_op jit(solution)/shard_map/update_image/pallas_call | solution.py:397
  92.7 1.3 collective-permute-start.34
  94.6 1.6 collective-permute-start.36
  96.2 1.2 collective-permute-done.38
  97.5 4.1 %collective-permute-done.39 = f32[96,128]{1,0:T(8,128)S(1)} collective-permute-done((f32[96,128]{1,0:T(8,128)S(1)}, f32[96,128]{1,0:T(8,128)S(1)}, u32[]{:S(2)}, u32[]{:S(2)}) %collective-permute-start.39) | collective-permute-done | bytes 49184 | tf_op jit(solution)/shard_map/ppermute | solution.py:431
  101.9 4.7 %collective-permute-done.40 = f32[96,128]{1,0:T(8,128)S(1)} collective-permute-done((f32[96,128]{1,0:T(8,128)S(1)}, f32[96,128]{1,0:T(8,128)S(1)}, u32[]{:S(2)}, u32[]{:S(2)}) %collective-permute-start.40) | collective-permute-done | bytes 49184 | tf_op jit(solution)/shard_map/ppermute | solution.py:431
  106.6 1.4 pair.3
  108.0 1.4 collective-permute-start.44
  109.4 3.9 %collective-permute-done.44 = f32[96,128]{1,0:T(8,128)S(1)} collective-permute-done((f32[96,128]{1,0:T(8,128)S(1)}, f32[96,128]{1,0:T(8,128)S(1)}, u32[]{:S(2)}, u32[]{:S(2)}) %collective-permute-start.44) | collective-permute-done | bytes 49184 | tf_op jit(solution)/shard_map/ppermute | solution.py:428
  113.3 1.5 collective-permute-start.45
  114.8 2.0 %collective-permute-start.42 = (bf16[6,64,128]{2,1,0:T(8,128)(2,1)S(1)}, bf16[6,64,128]{2,1,0:T(8,128)(2,1)S(1)}, u32[]{:S(2)}, u32[]{:S(2)}) collective-permute-start(bf16[6,64,128]{2,1,0:T(8,128)(2,1)S(1)} %get-tuple-element.161), channel_id=1, source_target_pairs={{0,16},{4,20},{8,24},{12,28},{16,0},{20,4},{24,8},{28,12},{1,17},{... | collective-permute-start | bytes 294920 | tf_op jit(solution)/shard_map/ppermute | solution.py:431
  117.5 1.7 collective-permute-start.43
  119.3 3.8 %pap_inverse.1.refs_14_ = f32[64,64]{1,0:T(8,128)S(1)} custom-call(f32[192,128]{1,0:T(8,128)S(1)} %get-tuple-element.164.table.refs_12_), custom_call_target="tpu_custom_call" | custom-call | flops 1000000 | bytes 114688 | tf_op jit(solution)/shard_map/pap_inverse/pallas_call | solution.py:397
  123.2 1.5 collective-permute-done.42.refs_6_
  124.7 11.0 %move.1 = (f32[64,768]{1,0:T(8,128)S(1)}, f32[64,768]{1,0:T(8,128)S(1)}, f32[64,768]{1,0:T(8,128)S(1)}, bf16[12,64,128]{2,1,0:T(8,128)(2,1)S(1)}, bf16[3,64,128]...) custom-call(f32[24,64,64]{2,1,0:T(8,128)S(1)} %get-tuple-element.148.refs_0_, ...), custom_call_target="tpu_custom_call" | custom-call | flops 1000000 | bytes 5065748 | tf_op jit(solution)/shard_map/move/pallas_call | solution.py:397
  135.7 1.7 collective-permute-start.50
  137.8 2.3 %collective-permute-start.52 = (bf16[3,64,128]{2,1,0:T(8,128)(2,1)S(1)}, bf16[3,64,128]{2,1,0:T(8,128)(2,1)S(1)}, u32[]{:S(2)}, u32[]{:S(2)}) collective-permute-start(bf16[3,64,128]{2,1,0:T(8,128)(2,1)S(1)} %get-tuple-element.170), channel_id=1, source_target_pairs={{0,24},{4,28},{8,16},{12,20},{16,8},{20,12},{24,0},{28,4},{1,25},{... | collective-permute-start | bytes 147464 | tf_op jit(solution)/shard_map/ppermute | solution.py:431
  140.7 1.3 collective-permute-start.48
  142.0 1.6 collective-permute-start.49
  143.9 4.4 %settle.1 = (f32[64,768]{1,0:T(8,128)S(1)}, f32[64,768]{1,0:T(8,128)S(1)}, f32[192,64]{1,0:T(8,128)S(1)}) custom-call(f32[256,64]{1,0:T(8,128)S(1)} %get-tuple-element.173.small, f32[64,768]{1,0:T(8,128)S(1)} %get-tuple-element.174.step_x, f32[64,768]{1,0:T(8,128)S(1)} %get-tuple-element.175.step_a), custom_call_target="tpu_custom_call" | custom-call | flops 1000000 | bytes 901120 | tf_op jit(solution)/shard_map/settle/pallas_call | solution.py:397
  148.4 1.7 collective-permute-done.48.refs_2_
  150.1 3.2 %update_image.3 = (f32[64,768]{1,0:T(8,128)}, f32[64,768]{1,0:T(8,128)}, f32[96,128]{1,0:T(8,128)S(1)}, f32[96,128]{1,0:T(8,128)S(1)}) custom-call(bf16[12,64,128]{2,1,0:T(8,128)(2,1)S(1)} %get-tuple-element.169.refs_0_, bf16[12,64,128]{2,1,0:T(8,128)(2,1)S(1)} %collective-permute-done.47.refs_1_, bf16[12,64,128]{2,1,0:T(8,128)(2,1)S(1)} %collective-permute-done.48.refs_2_, ...), custom_call_target="tpu_custom_call" | custom-call | flops 1000000 | bytes 4424072 | tf_op jit(solution)/shard_map/update_image/pallas_call | solution.py:397
  153.3 1.2 collective-permute-done.54
  154.5 1.1 collective-permute-start.55
  155.6 3.1 %collective-permute-done.55 = f32[96,128]{1,0:T(8,128)S(1)} collective-permute-done((f32[96,128]{1,0:T(8,128)S(1)}, f32[96,128]{1,0:T(8,128)S(1)}, u32[]{:S(2)}, u32[]{:S(2)}) %collective-permute-start.55) | collective-permute-done | bytes 49184 | tf_op jit(solution)/shard_map/ppermute | solution.py:428
  159.7 3.2 %collective-permute-done.56 = f32[96,128]{1,0:T(8,128)S(1)} collective-permute-done((f32[96,128]{1,0:T(8,128)S(1)}, f32[96,128]{1,0:T(8,128)S(1)}, u32[]{:S(2)}, u32[]{:S(2)}) %collective-permute-start.56) | collective-permute-done | bytes 49184 | tf_op jit(solution)/shard_map/ppermute | solution.py:428
  162.9 4.1 %collective-permute-done.57 = f32[96,128]{1,0:T(8,128)S(1)} collective-permute-done((f32[96,128]{1,0:T(8,128)S(1)}, f32[96,128]{1,0:T(8,128)S(1)}, u32[]{:S(2)}, u32[]{:S(2)}) %collective-permute-start.57) | collective-permute-done | bytes 49184 | tf_op jit(solution)/shard_map/ppermute | solution.py:431
  167.0 1.3 collective-permute-start.58
  168.3 3.7 %collective-permute-done.58 = f32[96,128]{1,0:T(8,128)S(1)} collective-permute-done((f32[96,128]{1,0:T(8,128)S(1)}, f32[96,128]{1,0:T(8,128)S(1)}, u32[]{:S(2)}, u32[]{:S(2)}) %collective-permute-start.58) | collective-permute-done | bytes 49184 | tf_op jit(solution)/shard_map/ppermute | solution.py:431
  172.1 1.2 collective-permute-done.59.other
  173.4 10.2 %finish.1 = (f32[64,768]{1,0:T(8,128)}, f32[64,768]{1,0:T(8,128)}) custom-call(f32[96,128]{1,0:T(8,128)S(1)} %add.59.mine, f32[96,128]{1,0:T(8,128)S(1)} %collective-permute-done.59.other, s32[2]{0:T(128)S(1)} %pad_add_fusion.refs_9_.refs_3_.pos.refs_10_.refs_4_, f32[192,64]{1,0:T(8,128)S(1)} %get-tuple-element.181.state, ...), custom_call_target="tpu_custom_call" | custom-call | flops 1000000 | bytes 1130504 | tf_op jit(solution)/shard_map/finish/pallas_call | solution.py:397
  (132 shorter events, 16.4 us)
Async XLA Ops:
  2.9 8.9 %collective-permute-start.3 = (bf16[3,64,128]{2,1,0:T(8,128)(2,1)S(1)}, bf16[3,64,128]{2,1,0:T(8,128)(2,1)S(1)}, u32[]{:S(2)}, u32[]{:S(2)}) collective-permute-start(bf16[3,64,128]{2,1,0:T(8,128)(2,1)S(1)} %get-tuple-element.96), channel_id=1, source_target_pairs={{0,8},{4,12},{8,0},{12,4},{16,24},{20,28},{24,16},{28,20},{1,9},{5... | collective-permute-start | bytes 147464 | tf_op jit(solution)/shard_map/ppermute | solution.py:431
  6.0 6.2 %collective-permute-start.4 = (bf16[3,64,128]{2,1,0:T(8,128)(2,1)S(1)}, bf16[3,64,128]{2,1,0:T(8,128)(2,1)S(1)}, u32[]{:S(2)}, u32[]{:S(2)}) collective-permute-start(bf16[3,64,128]{2,1,0:T(8,128)(2,1)S(1)} %get-tuple-element.96), channel_id=1, source_target_pairs={{0,16},{4,20},{8,24},{12,28},{16,0},{20,4},{24,8},{28,12},{1,17},{... | collective-permute-start | bytes 147464 | tf_op jit(solution)/shard_map/ppermute | solution.py:431
  8.6 5.9 %collective-permute-start.5 = (bf16[3,64,128]{2,1,0:T(8,128)(2,1)S(1)}, bf16[3,64,128]{2,1,0:T(8,128)(2,1)S(1)}, u32[]{:S(2)}, u32[]{:S(2)}) collective-permute-start(bf16[3,64,128]{2,1,0:T(8,128)(2,1)S(1)} %get-tuple-element.96), channel_id=1, source_target_pairs={{0,24},{4,28},{8,16},{12,20},{16,8},{20,12},{24,0},{28,4},{1,25},{... | collective-permute-start | bytes 147464 | tf_op jit(solution)/shard_map/ppermute | solution.py:431
  8.6 8.3 %collective-permute-start = (bf16[12,64,128]{2,1,0:T(8,128)(2,1)S(1)}, bf16[12,64,128]{2,1,0:T(8,128)(2,1)S(1)}, u32[]{:S(2)}, u32[]{:S(2)}) collective-permute-start(bf16[12,64,128]{2,1,0:T(8,128)(2,1)S(1)} %get-tuple-element.95.refs_0_), channel_id=1, source_target_pairs={{0,1},{1,0},{2,3},{3,2},{4,5},{5,4},{6,7},{7,6},{8,9},{9,8},{10,11... | collective-permute-start | bytes 589832 | tf_op jit(solution)/shard_map/ppermute | solution.py:428
  10.3 9.9 %collective-permute-start.1 = (bf16[12,64,128]{2,1,0:T(8,128)(2,1)S(1)}, bf16[12,64,128]{2,1,0:T(8,128)(2,1)S(1)}, u32[]{:S(2)}, u32[]{:S(2)}) collective-permute-start(bf16[12,64,128]{2,1,0:T(8,128)(2,1)S(1)} %get-tuple-element.95.refs_0_), channel_id=1, source_target_pairs={{0,2},{1,3},{2,0},{3,1},{4,6},{5,7},{6,4},{7,5},{8,10},{9,11},{10,... | collective-permute-start | bytes 589832 | tf_op jit(solution)/shard_map/ppermute | solution.py:428
  11.8 8.4 %collective-permute-start.2 = (bf16[12,64,128]{2,1,0:T(8,128)(2,1)S(1)}, bf16[12,64,128]{2,1,0:T(8,128)(2,1)S(1)}, u32[]{:S(2)}, u32[]{:S(2)}) collective-permute-start(bf16[12,64,128]{2,1,0:T(8,128)(2,1)S(1)} %get-tuple-element.95.refs_0_), channel_id=1, source_target_pairs={{0,3},{1,2},{2,1},{3,0},{4,7},{5,6},{6,5},{7,4},{8,11},{9,10},{10,... | collective-permute-start | bytes 589832 | tf_op jit(solution)/shard_map/ppermute | solution.py:428
  14.5 5.7 %collective-permute-start.6 = (bf16[12,64,128]{2,1,0:T(8,128)(2,1)S(1)}, bf16[12,64,128]{2,1,0:T(8,128)(2,1)S(1)}, u32[]{:S(2)}, u32[]{:S(2)}) collective-permute-start(bf16[12,64,128]{2,1,0:T(8,128)(2,1)S(1)} %constant_dynamic-update-slice_fusion.refs_4_), channel_id=1, source_target_pairs={{0,4},{4,0},{8,12},{12,8},{16,20},{20,16},{24,28},{28,24},{1,5},{5... | collective-permute-start | bytes 589832 | tf_op jit(solution)/shard_map/ppermute | solution.py:431
  16.1 17.7 %copy-start.10 = (s32[1,1,12]{2,1,0:T(1,128)S(1)}, s32[1,1,12]{2,1,0:T(1,128)}, u32[]{:S(2)}) copy-start(s32[1,1,12]{2,1,0:T(1,128)} %param.17) | copy-start | bytes 148
  16.1 17.7 %copy-start.11 = (s32[1,1,12]{2,1,0:T(1,128)S(1)}, s32[1,1,12]{2,1,0:T(1,128)}, u32[]{:S(2)}) copy-start(s32[1,1,12]{2,1,0:T(1,128)} %param.18) | copy-start | bytes 148
  20.2 6.4 %collective-permute-start.10 = (bf16[3,64,128]{2,1,0:T(8,128)(2,1)S(1)}, bf16[3,64,128]{2,1,0:T(8,128)(2,1)S(1)}, u32[]{:S(2)}, u32[]{:S(2)}) collective-permute-start(bf16[3,64,128]{2,1,0:T(8,128)(2,1)S(1)} %get-tuple-element.98), channel_id=1, source_target_pairs={{0,8},{4,12},{8,0},{12,4},{16,24},{20,28},{24,16},{28,20},{1,9},{5... | collective-permute-start | bytes 147464 | tf_op jit(solution)/shard_map/ppermute | solution.py:431
  20.8 7.3 %collective-permute-start.11 = (bf16[3,64,128]{2,1,0:T(8,128)(2,1)S(1)}, bf16[3,64,128]{2,1,0:T(8,128)(2,1)S(1)}, u32[]{:S(2)}, u32[]{:S(2)}) collective-permute-start(bf16[3,64,128]{2,1,0:T(8,128)(2,1)S(1)} %get-tuple-element.98), channel_id=1, source_target_pairs={{0,16},{4,20},{8,24},{12,28},{16,0},{20,4},{24,8},{28,12},{1,17},{... | collective-permute-start | bytes 147464 | tf_op jit(solution)/shard_map/ppermute | solution.py:431
  24.3 5.9 %collective-permute-start.12 = (bf16[3,64,128]{2,1,0:T(8,128)(2,1)S(1)}, bf16[3,64,128]{2,1,0:T(8,128)(2,1)S(1)}, u32[]{:S(2)}, u32[]{:S(2)}) collective-permute-start(bf16[3,64,128]{2,1,0:T(8,128)(2,1)S(1)} %get-tuple-element.98), channel_id=1, source_target_pairs={{0,24},{4,28},{8,16},{12,20},{16,8},{20,12},{24,0},{28,4},{1,25},{... | collective-permute-start | bytes 147464 | tf_op jit(solution)/shard_map/ppermute | solution.py:431
  24.6 16.1 %collective-permute-start.7 = (bf16[12,64,128]{2,1,0:T(8,128)(2,1)S(1)}, bf16[12,64,128]{2,1,0:T(8,128)(2,1)S(1)}, u32[]{:S(2)}, u32[]{:S(2)}) collective-permute-start(bf16[12,64,128]{2,1,0:T(8,128)(2,1)S(1)} %get-tuple-element.97.refs_0_), channel_id=1, source_target_pairs={{0,1},{1,0},{2,3},{3,2},{4,5},{5,4},{6,7},{7,6},{8,9},{9,8},{10,11... | collective-permute-start | bytes 589832 | tf_op jit(solution)/shard_map/ppermute | solution.py:428
  25.7 15.0 %collective-permute-start.8 = (bf16[12,64,128]{2,1,0:T(8,128)(2,1)S(1)}, bf16[12,64,128]{2,1,0:T(8,128)(2,1)}, u32[]{:S(2)}, u32[]{:S(2)}) collective-permute-start(bf16[12,64,128]{2,1,0:T(8,128)(2,1)S(1)} %get-tuple-element.97.refs_0_), channel_id=1, source_target_pairs={{0,2},{1,3},{2,0},{3,1},{4,6},{5,7},{6,4},{7,5},{8,10},{9,11},{10,... | collective-permute-start | bytes 589832 | tf_op jit(solution)/shard_map/ppermute | solution.py:428
  26.5 14.2 %collective-permute-start.9 = (bf16[12,64,128]{2,1,0:T(8,128)(2,1)S(1)}, bf16[12,64,128]{2,1,0:T(8,128)(2,1)}, u32[]{:S(2)}, u32[]{:S(2)}) collective-permute-start(bf16[12,64,128]{2,1,0:T(8,128)(2,1)S(1)} %get-tuple-element.97.refs_0_), channel_id=1, source_target_pairs={{0,3},{1,2},{2,1},{3,0},{4,7},{5,6},{6,5},{7,4},{8,11},{9,10},{10,... | collective-permute-start | bytes 589832 | tf_op jit(solution)/shard_map/ppermute | solution.py:428
  30.2 10.5 %collective-permute-start.13 = (bf16[12,64,128]{2,1,0:T(8,128)(2,1)S(1)}, bf16[12,64,128]{2,1,0:T(8,128)(2,1)}, u32[]{:S(2)}, u32[]{:S(2)}) collective-permute-start(bf16[12,64,128]{2,1,0:T(8,128)(2,1)S(1)} %constant_dynamic-update-slice_fusion.4.refs_4_), channel_id=1, source_target_pairs={{0,4},{4,0},{8,12},{12,8},{16,20},{20,16},{24,28},{28,24},{1,5},{5... | collective-permute-start | bytes 589832 | tf_op jit(solution)/shard_map/ppermute | solution.py:431
  40.7 25.3 %copy-start.12 = (f32[768]{0:T(1024)S(1)}, f32[768]{0:T(1024)}, u32[]{:S(2)}) copy-start(f32[768]{0:T(1024)} %param.12) | copy-start | bytes 9220
  40.7 29.2 %copy-start.7 = (s32[1,1,3]{2,1,0:T(1,128)S(1)}, s32[1,1,3]{2,1,0:T(1,128)}, u32[]{:S(2)}) copy-start(s32[1,1,3]{2,1,0:T(1,128)} %param.16) | copy-start | bytes 40
  43.3 11.1 %collective-permute-start.17 = (bf16[12,64,128]{2,1,0:T(8,128)(2,1)S(1)}, bf16[12,64,128]{2,1,0:T(8,128)(2,1)S(1)}, u32[]{:S(2)}, u32[]{:S(2)}) collective-permute-start(bf16[12,64,128]{2,1,0:T(8,128)(2,1)S(1)} %get-tuple-element.123), channel_id=1, source_target_pairs={{0,4},{4,0},{8,12},{12,8},{16,20},{20,16},{24,28},{28,24},{1,5},{5... | collective-permute-start | bytes 589832 | tf_op jit(solution)/shard_map/ppermute | solution.py:431
  43.8 1.2 collective-permute-start.18
  45.1 4.2 %collective-permute-start.19 = (f32[96,128]{1,0:T(8,128)S(1)}, f32[96,128]{1,0:T(8,128)S(1)}, u32[]{:S(2)}, u32[]{:S(2)}) collective-permute-start(f32[96,128]{1,0:T(8,128)S(1)} %add.45), channel_id=1, source_target_pairs={{0,8},{4,12},{8,0},{12,4},{16,24},{20,28},{24,16},{28,20},{1,9},{5... | collective-permute-start | bytes 147464 | tf_op jit(solution)/shard_map/ppermute | solution.py:431
  45.1 18.8 %collective-permute-start.14 = (bf16[12,64,128]{2,1,0:T(8,128)(2,1)S(1)}, bf16[12,64,128]{2,1,0:T(8,128)(2,1)S(1)}, u32[]{:S(2)}, u32[]{:S(2)}) collective-permute-start(bf16[12,64,128]{2,1,0:T(8,128)(2,1)S(1)} %get-tuple-element.119), channel_id=1, source_target_pairs={{0,1},{1,0},{2,3},{3,2},{4,5},{5,4},{6,7},{7,6},{8,9},{9,8},{10,11... | collective-permute-start | bytes 589832 | tf_op jit(solution)/shard_map/ppermute | solution.py:428
  46.3 19.7 %collective-permute-start.15 = (bf16[12,64,128]{2,1,0:T(8,128)(2,1)S(1)}, bf16[12,64,128]{2,1,0:T(8,128)(2,1)S(1)}, u32[]{:S(2)}, u32[]{:S(2)}) collective-permute-start(bf16[12,64,128]{2,1,0:T(8,128)(2,1)S(1)} %get-tuple-element.120), channel_id=1, source_target_pairs={{0,2},{1,3},{2,0},{3,1},{4,6},{5,7},{6,4},{7,5},{8,10},{9,11},{10,... | collective-permute-start | bytes 589832 | tf_op jit(solution)/shard_map/ppermute | solution.py:428
  49.2 5.1 %collective-permute-start.20 = (f32[96,128]{1,0:T(8,128)S(1)}, f32[96,128]{1,0:T(8,128)S(1)}, u32[]{:S(2)}, u32[]{:S(2)}) collective-permute-start(f32[96,128]{1,0:T(8,128)S(1)} %add.46), channel_id=1, source_target_pairs={{0,16},{4,20},{8,24},{12,28},{16,0},{20,4},{24,8},{28,12},{1,17},{... | collective-permute-start | bytes 147464 | tf_op jit(solution)/shard_map/ppermute | solution.py:431
  49.4 16.6 %collective-permute-start.16 = (bf16[12,64,128]{2,1,0:T(8,128)(2,1)S(1)}, bf16[12,64,128]{2,1,0:T(8,128)(2,1)S(1)}, u32[]{:S(2)}, u32[]{:S(2)}) collective-permute-start(bf16[12,64,128]{2,1,0:T(8,128)(2,1)S(1)} %get-tuple-element.121), channel_id=1, source_target_pairs={{0,3},{1,2},{2,1},{3,0},{4,7},{5,6},{6,5},{7,4},{8,11},{9,10},{10,... | collective-permute-start | bytes 589832 | tf_op jit(solution)/shard_map/ppermute | solution.py:428
  55.2 4.2 %collective-permute-start.24 = (f32[96,128]{1,0:T(8,128)S(1)}, f32[96,128]{1,0:T(8,128)S(1)}, u32[]{:S(2)}, u32[]{:S(2)}) collective-permute-start(f32[96,128]{1,0:T(8,128)S(1)} %add.47), channel_id=1, source_target_pairs={{0,1},{1,0},{2,3},{3,2},{4,5},{5,4},{6,7},{7,6},{8,9},{9,8},{10,11... | collective-permute-start | bytes 147464 | tf_op jit(solution)/shard_map/ppermute | solution.py:428
  59.4 4.2 %collective-permute-start.25 = (f32[96,128]{1,0:T(8,128)S(1)}, f32[96,128]{1,0:T(8,128)S(1)}, u32[]{:S(2)}, u32[]{:S(2)}) collective-permute-start(f32[96,128]{1,0:T(8,128)S(1)} %add.48), channel_id=1, source_target_pairs={{0,2},{1,3},{2,0},{3,1},{4,6},{5,7},{6,4},{7,5},{8,10},{9,11},{10,... | collective-permute-start | bytes 147464 | tf_op jit(solution)/shard_map/ppermute | solution.py:428
  60.9 5.2 %collective-permute-start.21 = (bf16[3,64,128]{2,1,0:T(8,128)(2,1)S(1)}, bf16[3,64,128]{2,1,0:T(8,128)(2,1)S(1)}, u32[]{:S(2)}, u32[]{:S(2)}) collective-permute-start(bf16[3,64,128]{2,1,0:T(8,128)(2,1)S(1)} %get-tuple-element.130), channel_id=1, source_target_pairs={{0,8},{4,12},{8,0},{12,4},{16,24},{20,28},{24,16},{28,20},{1,9},{5... | collective-permute-start | bytes 147464 | tf_op jit(solution)/shard_map/ppermute | solution.py:431
  63.5 5.0 %collective-permute-start.22 = (bf16[3,64,128]{2,1,0:T(8,128)(2,1)S(1)}, bf16[3,64,128]{2,1,0:T(8,128)(2,1)S(1)}, u32[]{:S(2)}, u32[]{:S(2)}) collective-permute-start(bf16[3,64,128]{2,1,0:T(8,128)(2,1)S(1)} %get-tuple-element.131), channel_id=1, source_target_pairs={{0,16},{4,20},{8,24},{12,28},{16,0},{20,4},{24,8},{28,12},{1,17},{... | collective-permute-start | bytes 147464 | tf_op jit(solution)/shard_map/ppermute | solution.py:431
  64.0 6.0 %collective-permute-start.23 = (bf16[3,64,128]{2,1,0:T(8,128)(2,1)S(1)}, bf16[3,64,128]{2,1,0:T(8,128)(2,1)S(1)}, u32[]{:S(2)}, u32[]{:S(2)}) collective-permute-start(bf16[3,64,128]{2,1,0:T(8,128)(2,1)S(1)} %get-tuple-element.132), channel_id=1, source_target_pairs={{0,24},{4,28},{8,16},{12,20},{16,8},{20,12},{24,0},{28,4},{1,25},{... | collective-permute-start | bytes 147464 | tf_op jit(solution)/shard_map/ppermute | solution.py:431
  66.0 3.9 %collective-permute-start.26 = (f32[96,128]{1,0:T(8,128)S(1)}, f32[96,128]{1,0:T(8,128)S(1)}, u32[]{:S(2)}, u32[]{:S(2)}) collective-permute-start(f32[96,128]{1,0:T(8,128)S(1)} %add.49.refs_8_), channel_id=1, source_target_pairs={{0,4},{4,0},{8,12},{12,8},{16,20},{20,16},{24,28},{28,24},{1,5},{5... | collective-permute-start | bytes 147464 | tf_op jit(solution)/shard_map/ppermute | solution.py:431
  75.1 6.2 %collective-permute-start.30 = (bf16[3,64,128]{2,1,0:T(8,128)(2,1)S(1)}, bf16[3,64,128]{2,1,0:T(8,128)(2,1)S(1)}, u32[]{:S(2)}, u32[]{:S(2)}) collective-permute-start(bf16[3,64,128]{2,1,0:T(8,128)(2,1)S(1)} %get-tuple-element.136), channel_id=1, source_target_pairs={{0,8},{4,12},{8,0},{12,4},{16,24},{20,28},{24,16},{28,20},{1,9},{5... | collective-permute-start | bytes 147464 | tf_op jit(solution)/shard_map/ppermute | solution.py:431
  75.2 7.9 %collective-permute-start.31 = (bf16[3,64,128]{2,1,0:T(8,128)(2,1)S(1)}, bf16[3,64,128]{2,1,0:T(8,128)(2,1)S(1)}, u32[]{:S(2)}, u32[]{:S(2)}) collective-permute-start(bf16[3,64,128]{2,1,0:T(8,128)(2,1)S(1)} %get-tuple-element.136), channel_id=1, source_target_pairs={{0,16},{4,20},{8,24},{12,28},{16,0},{20,4},{24,8},{28,12},{1,17},{... | collective-permute-start | bytes 147464 | tf_op jit(solution)/shard_map/ppermute | solution.py:431
  77.8 5.9 %collective-permute-start.32 = (bf16[3,64,128]{2,1,0:T(8,128)(2,1)S(1)}, bf16[3,64,128]{2,1,0:T(8,128)(2,1)S(1)}, u32[]{:S(2)}, u32[]{:S(2)}) collective-permute-start(bf16[3,64,128]{2,1,0:T(8,128)(2,1)S(1)} %get-tuple-element.136), channel_id=1, source_target_pairs={{0,24},{4,28},{8,16},{12,20},{16,8},{20,12},{24,0},{28,4},{1,25},{... | collective-permute-start | bytes 147464 | tf_op jit(solution)/shard_map/ppermute | solution.py:431
  79.5 9.5 %collective-permute-start.27 = (bf16[12,64,128]{2,1,0:T(8,128)(2,1)S(1)}, bf16[12,64,128]{2,1,0:T(8,128)(2,1)S(1)}, u32[]{:S(2)}, u32[]{:S(2)}) collective-permute-start(bf16[12,64,128]{2,1,0:T(8,128)(2,1)S(1)} %get-tuple-element.135.refs_0_.refs_1_), channel_id=1, source_target_pairs={{0,1},{1,0},{2,3},{3,2},{4,5},{5,4},{6,7},{7,6},{8,9},{9,8},{10,11... | collective-permute-start | bytes 589832 | tf_op jit(solution)/shard_map/ppermute | solution.py:428
  80.6 8.6 %collective-permute-start.28 = (bf16[12,64,128]{2,1,0:T(8,128)(2,1)S(1)}, bf16[12,64,128]{2,1,0:T(8,128)(2,1)S(1)}, u32[]{:S(2)}, u32[]{:S(2)}) collective-permute-start(bf16[12,64,128]{2,1,0:T(8,128)(2,1)S(1)} %get-tuple-element.135.refs_0_.refs_1_), channel_id=1, source_target_pairs={{0,2},{1,3},{2,0},{3,1},{4,6},{5,7},{6,4},{7,5},{8,10},{9,11},{10,... | collective-permute-start | bytes 589832 | tf_op jit(solution)/shard_map/ppermute | solution.py:428
  81.3 7.8 %collective-permute-start.29 = (bf16[12,64,128]{2,1,0:T(8,128)(2,1)S(1)}, bf16[12,64,128]{2,1,0:T(8,128)(2,1)S(1)}, u32[]{:S(2)}, u32[]{:S(2)}) collective-permute-start(bf16[12,64,128]{2,1,0:T(8,128)(2,1)S(1)} %get-tuple-element.135.refs_0_.refs_1_), channel_id=1, source_target_pairs={{0,3},{1,2},{2,1},{3,0},{4,7},{5,6},{6,5},{7,4},{8,11},{9,10},{10,... | collective-permute-start | bytes 589832 | tf_op jit(solution)/shard_map/ppermute | solution.py:428
  83.7 5.4 %collective-permute-start.33 = (bf16[12,64,128]{2,1,0:T(8,128)(2,1)S(1)}, bf16[12,64,128]{2,1,0:T(8,128)(2,1)S(1)}, u32[]{:S(2)}, u32[]{:S(2)}) collective-permute-start(bf16[12,64,128]{2,1,0:T(8,128)(2,1)S(1)} %constant_dynamic-update-slice_fusion.8.refs_4_), channel_id=1, source_target_pairs={{0,4},{4,0},{8,12},{12,8},{16,20},{20,16},{24,28},{28,24},{1,5},{5... | collective-permute-start | bytes 589832 | tf_op jit(solution)/shard_map/ppermute | solution.py:431
  92.1 14.5 %collective-permute-start.37 = (bf16[24,64,128]{2,1,0:T(8,128)(2,1)S(1)}, bf16[24,64,128]{2,1,0:T(8,128)(2,1)S(1)}, u32[]{:S(2)}, u32[]{:S(2)}) collective-permute-start(bf16[24,64,128]{2,1,0:T(8,128)(2,1)S(1)} %get-tuple-element.153), channel_id=1, source_target_pairs={{0,4},{4,0},{8,12},{12,8},{16,20},{20,16},{24,28},{28,24},{1,5},{5... | collective-permute-start | bytes 1179656 | tf_op jit(solution)/shard_map/ppermute | solution.py:431
  92.7 22.1 %collective-permute-start.34 = (bf16[24,64,128]{2,1,0:T(8,128)(2,1)S(1)}, bf16[24,64,128]{2,1,0:T(8,128)(2,1)S(1)}, u32[]{:S(2)}, u32[]{:S(2)}) collective-permute-start(bf16[24,64,128]{2,1,0:T(8,128)(2,1)S(1)} %get-tuple-element.149), channel_id=1, source_target_pairs={{0,1},{1,0},{2,3},{3,2},{4,5},{5,4},{6,7},{7,6},{8,9},{9,8},{10,11... | collective-permute-start | bytes 1179656 | tf_op jit(solution)/shard_map/ppermute | solution.py:428
  94.0 25.2 %collective-permute-start.35 = (bf16[24,64,128]{2,1,0:T(8,128)(2,1)S(1)}, bf16[24,64,128]{2,1,0:T(8,128)(2,1)S(1)}, u32[]{:S(2)}, u32[]{:S(2)}) collective-permute-start(bf16[24,64,128]{2,1,0:T(8,128)(2,1)S(1)} %get-tuple-element.150), channel_id=1, source_target_pairs={{0,2},{1,3},{2,0},{3,1},{4,6},{5,7},{6,4},{7,5},{8,10},{9,11},{10,... | collective-permute-start | bytes 1179656 | tf_op jit(solution)/shard_map/ppermute | solution.py:428
  94.6 28.5 %collective-permute-start.36 = (bf16[24,64,128]{2,1,0:T(8,128)(2,1)S(1)}, bf16[24,64,128]{2,1,0:T(8,128)(2,1)S(1)}, u32[]{:S(2)}, u32[]{:S(2)}) collective-permute-start(bf16[24,64,128]{2,1,0:T(8,128)(2,1)S(1)} %get-tuple-element.151), channel_id=1, source_target_pairs={{0,3},{1,2},{2,1},{3,0},{4,7},{5,6},{6,5},{7,4},{8,11},{9,10},{10,... | collective-permute-start | bytes 1179656 | tf_op jit(solution)/shard_map/ppermute | solution.py:428
  96.2 1.2 collective-permute-start.38
  97.4 4.1 %collective-permute-start.39 = (f32[96,128]{1,0:T(8,128)S(1)}, f32[96,128]{1,0:T(8,128)S(1)}, u32[]{:S(2)}, u32[]{:S(2)}) collective-permute-start(f32[96,128]{1,0:T(8,128)S(1)} %add.50), channel_id=1, source_target_pairs={{0,8},{4,12},{8,0},{12,4},{16,24},{20,28},{24,16},{28,20},{1,9},{5... | collective-permute-start | bytes 147464 | tf_op jit(solution)/shard_map/ppermute | solution.py:431
  101.6 5.0 %collective-permute-start.40 = (f32[96,128]{1,0:T(8,128)S(1)}, f32[96,128]{1,0:T(8,128)S(1)}, u32[]{:S(2)}, u32[]{:S(2)}) collective-permute-start(f32[96,128]{1,0:T(8,128)S(1)} %add.51), channel_id=1, source_target_pairs={{0,16},{4,20},{8,24},{12,28},{16,0},{20,4},{24,8},{28,12},{1,17},{... | collective-permute-start | bytes 147464 | tf_op jit(solution)/shard_map/ppermute | solution.py:431
  108.0 5.3 %collective-permute-start.44 = (f32[96,128]{1,0:T(8,128)S(1)}, f32[96,128]{1,0:T(8,128)S(1)}, u32[]{:S(2)}, u32[]{:S(2)}) collective-permute-start(f32[96,128]{1,0:T(8,128)S(1)} %add.52), channel_id=1, source_target_pairs={{0,1},{1,0},{2,3},{3,2},{4,5},{5,4},{6,7},{7,6},{8,9},{9,8},{10,11... | collective-permute-start | bytes 147464 | tf_op jit(solution)/shard_map/ppermute | solution.py:428
  113.3 4.2 %collective-permute-start.45 = (f32[96,128]{1,0:T(8,128)S(1)}, f32[96,128]{1,0:T(8,128)S(1)}, u32[]{:S(2)}, u32[]{:S(2)}) collective-permute-start(f32[96,128]{1,0:T(8,128)S(1)} %add.53), channel_id=1, source_target_pairs={{0,2},{1,3},{2,0},{3,1},{4,6},{5,7},{6,4},{7,5},{8,10},{9,11},{10,... | collective-permute-start | bytes 147464 | tf_op jit(solution)/shard_map/ppermute | solution.py:428
  114.8 8.3 %collective-permute-start.41 = (bf16[6,64,128]{2,1,0:T(8,128)(2,1)S(1)}, bf16[6,64,128]{2,1,0:T(8,128)(2,1)S(1)}, u32[]{:S(2)}, u32[]{:S(2)}) collective-permute-start(bf16[6,64,128]{2,1,0:T(8,128)(2,1)S(1)} %get-tuple-element.160), channel_id=1, source_target_pairs={{0,8},{4,12},{8,0},{12,4},{16,24},{20,28},{24,16},{28,20},{1,9},{5... | collective-permute-start | bytes 294920 | tf_op jit(solution)/shard_map/ppermute | solution.py:431
  114.8 9.9 %collective-permute-start.42 = (bf16[6,64,128]{2,1,0:T(8,128)(2,1)S(1)}, bf16[6,64,128]{2,1,0:T(8,128)(2,1)S(1)}, u32[]{:S(2)}, u32[]{:S(2)}) collective-permute-start(bf16[6,64,128]{2,1,0:T(8,128)(2,1)S(1)} %get-tuple-element.161), channel_id=1, source_target_pairs={{0,16},{4,20},{8,24},{12,28},{16,0},{20,4},{24,8},{28,12},{1,17},{... | collective-permute-start | bytes 294920 | tf_op jit(solution)/shard_map/ppermute | solution.py:431
  117.5 7.2 %collective-permute-start.43 = (bf16[6,64,128]{2,1,0:T(8,128)(2,1)S(1)}, bf16[6,64,128]{2,1,0:T(8,128)(2,1)S(1)}, u32[]{:S(2)}, u32[]{:S(2)}) collective-permute-start(bf16[6,64,128]{2,1,0:T(8,128)(2,1)S(1)} %get-tuple-element.162), channel_id=1, source_target_pairs={{0,24},{4,28},{8,16},{12,20},{16,8},{20,12},{24,0},{28,4},{1,25},{... | collective-permute-start | bytes 294920 | tf_op jit(solution)/shard_map/ppermute | solution.py:431
  119.2 5.5 %collective-permute-start.46 = (f32[96,128]{1,0:T(8,128)S(1)}, f32[96,128]{1,0:T(8,128)S(1)}, u32[]{:S(2)}, u32[]{:S(2)}) collective-permute-start(f32[96,128]{1,0:T(8,128)S(1)} %add.54.refs_8_), channel_id=1, source_target_pairs={{0,4},{4,0},{8,12},{12,8},{16,20},{20,16},{24,28},{28,24},{1,5},{5... | collective-permute-start | bytes 147464 | tf_op jit(solution)/shard_map/ppermute | solution.py:431
  135.7 6.4 %collective-permute-start.50 = (bf16[3,64,128]{2,1,0:T(8,128)(2,1)S(1)}, bf16[3,64,128]{2,1,0:T(8,128)(2,1)S(1)}, u32[]{:S(2)}, u32[]{:S(2)}) collective-permute-start(bf16[3,64,128]{2,1,0:T(8,128)(2,1)S(1)} %get-tuple-element.170), channel_id=1, source_target_pairs={{0,8},{4,12},{8,0},{12,4},{16,24},{20,28},{24,16},{28,20},{1,9},{5... | collective-permute-start | bytes 147464 | tf_op jit(solution)/shard_map/ppermute | solution.py:431
  137.4 6.3 %collective-permute-start.51 = (bf16[3,64,128]{2,1,0:T(8,128)(2,1)S(1)}, bf16[3,64,128]{2,1,0:T(8,128)(2,1)S(1)}, u32[]{:S(2)}, u32[]{:S(2)}) collective-permute-start(bf16[3,64,128]{2,1,0:T(8,128)(2,1)S(1)} %get-tuple-element.170), channel_id=1, source_target_pairs={{0,16},{4,20},{8,24},{12,28},{16,0},{20,4},{24,8},{28,12},{1,17},{... | collective-permute-start | bytes 147464 | tf_op jit(solution)/shard_map/ppermute | solution.py:431
  137.8 6.0 %collective-permute-start.52 = (bf16[3,64,128]{2,1,0:T(8,128)(2,1)S(1)}, bf16[3,64,128]{2,1,0:T(8,128)(2,1)S(1)}, u32[]{:S(2)}, u32[]{:S(2)}) collective-permute-start(bf16[3,64,128]{2,1,0:T(8,128)(2,1)S(1)} %get-tuple-element.170), channel_id=1, source_target_pairs={{0,24},{4,28},{8,16},{12,20},{16,8},{20,12},{24,0},{28,4},{1,25},{... | collective-permute-start | bytes 147464 | tf_op jit(solution)/shard_map/ppermute | solution.py:431
  140.1 8.2 %collective-permute-start.47 = (bf16[12,64,128]{2,1,0:T(8,128)(2,1)S(1)}, bf16[12,64,128]{2,1,0:T(8,128)(2,1)S(1)}, u32[]{:S(2)}, u32[]{:S(2)}) collective-permute-start(bf16[12,64,128]{2,1,0:T(8,128)(2,1)S(1)} %get-tuple-element.169.refs_0_), channel_id=1, source_target_pairs={{0,1},{1,0},{2,3},{3,2},{4,5},{5,4},{6,7},{7,6},{8,9},{9,8},{10,11... | collective-permute-start | bytes 589832 | tf_op jit(solution)/shard_map/ppermute | solution.py:428
  140.7 9.4 %collective-permute-start.48 = (bf16[12,64,128]{2,1,0:T(8,128)(2,1)S(1)}, bf16[12,64,128]{2,1,0:T(8,128)(2,1)S(1)}, u32[]{:S(2)}, u32[]{:S(2)}) collective-permute-start(bf16[12,64,128]{2,1,0:T(8,128)(2,1)S(1)} %get-tuple-element.169.refs_0_), channel_id=1, source_target_pairs={{0,2},{1,3},{2,0},{3,1},{4,6},{5,7},{6,4},{7,5},{8,10},{9,11},{10,... | collective-permute-start | bytes 589832 | tf_op jit(solution)/shard_map/ppermute | solution.py:428
  142.0 8.1 %collective-permute-start.49 = (bf16[12,64,128]{2,1,0:T(8,128)(2,1)S(1)}, bf16[12,64,128]{2,1,0:T(8,128)(2,1)S(1)}, u32[]{:S(2)}, u32[]{:S(2)}) collective-permute-start(bf16[12,64,128]{2,1,0:T(8,128)(2,1)S(1)} %get-tuple-element.169.refs_0_), channel_id=1, source_target_pairs={{0,3},{1,2},{2,1},{3,0},{4,7},{5,6},{6,5},{7,4},{8,11},{9,10},{10,... | collective-permute-start | bytes 589832 | tf_op jit(solution)/shard_map/ppermute | solution.py:428
  143.8 6.3 %collective-permute-start.53 = (bf16[12,64,128]{2,1,0:T(8,128)(2,1)S(1)}, bf16[12,64,128]{2,1,0:T(8,128)(2,1)S(1)}, u32[]{:S(2)}, u32[]{:S(2)}) collective-permute-start(bf16[12,64,128]{2,1,0:T(8,128)(2,1)S(1)} %constant_dynamic-update-slice_fusion.12.refs_4_), channel_id=1, source_target_pairs={{0,4},{4,0},{8,12},{12,8},{16,20},{20,16},{24,28},{28,24},{1,5},{5... | collective-permute-start | bytes 589832 | tf_op jit(solution)/shard_map/ppermute | solution.py:431
  153.3 1.2 collective-permute-start.54
  154.5 4.2 %collective-permute-start.55 = (f32[96,128]{1,0:T(8,128)S(1)}, f32[96,128]{1,0:T(8,128)S(1)}, u32[]{:S(2)}, u32[]{:S(2)}) collective-permute-start(f32[96,128]{1,0:T(8,128)S(1)} %add.55), channel_id=1, source_target_pairs={{0,1},{1,0},{2,3},{3,2},{4,5},{5,4},{6,7},{7,6},{8,9},{9,8},{10,11... | collective-permute-start | bytes 147464 | tf_op jit(solution)/shard_map/ppermute | solution.py:428
  158.7 4.2 %collective-permute-start.56 = (f32[96,128]{1,0:T(8,128)S(1)}, f32[96,128]{1,0:T(8,128)S(1)}, u32[]{:S(2)}, u32[]{:S(2)}) collective-permute-start(f32[96,128]{1,0:T(8,128)S(1)} %add.56), channel_id=1, source_target_pairs={{0,2},{1,3},{2,0},{3,1},{4,6},{5,7},{6,4},{7,5},{8,10},{9,11},{10,... | collective-permute-start | bytes 147464 | tf_op jit(solution)/shard_map/ppermute | solution.py:428
  162.9 4.2 %collective-permute-start.57 = (f32[96,128]{1,0:T(8,128)S(1)}, f32[96,128]{1,0:T(8,128)S(1)}, u32[]{:S(2)}, u32[]{:S(2)}) collective-permute-start(f32[96,128]{1,0:T(8,128)S(1)} %add.57), channel_id=1, source_target_pairs={{0,8},{4,12},{8,0},{12,4},{16,24},{20,28},{24,16},{28,20},{1,9},{5... | collective-permute-start | bytes 147464 | tf_op jit(solution)/shard_map/ppermute | solution.py:431
  167.0 5.0 %collective-permute-start.58 = (f32[96,128]{1,0:T(8,128)S(1)}, f32[96,128]{1,0:T(8,128)S(1)}, u32[]{:S(2)}, u32[]{:S(2)}) collective-permute-start(f32[96,128]{1,0:T(8,128)S(1)} %add.58), channel_id=1, source_target_pairs={{0,16},{4,20},{8,24},{12,28},{16,0},{20,4},{24,8},{28,12},{1,17},{... | collective-permute-start | bytes 147464 | tf_op jit(solution)/shard_map/ppermute | solution.py:431
  172.1 1.3 collective-permute-start.59
  (9 other events, 65.8 us)

commit v3 on v2

--- a/solution.py
+++ b/solution.py
@@ -187,46 +187,48 @@
     write_wire(vector, bnd, wire, edge)
 
 
-def partial_kernel(n_row, n_z, count, *refs):
+def partial_kernel(n_row, n_z, merge, wire, joined, where, pos, *refs):
     refs = list(refs)
-    take = lambda number: [refs.pop(0) for _ in range(number)]
-    wires = take(count)
-    joined, where, pos = take(3)
-    own, core_keep, core_send = take(3)
-    row_outs, acc = refs[:-1], refs[-1]
-    lb, kb = wires[0].shape[0], wires[0].shape[2] // 2
-    ifr = core_keep.shape[0] // (count * n_z)
+    parts = n_row + 2
+    earlier = [refs.pop(0) for _ in range(parts)] if merge else []
+    outs, acc = refs[:-1], refs[-1]
+    own, core_keep, core_send, *row_outs = outs
+    lb, kb = wire.shape[0], wire.shape[2] // 2
+    ifr = core_keep.shape[0] // (n_z * (2 if merge else 1))
     groups = joined.shape[2] // kb
     low = lax.broadcasted_iota(jnp.int32, (kb, 2 * kb), 1) < kb
     core = pos[1] % 2
-    for v, wire in enumerate(wires):
-        acc[...] = jnp.zeros(acc.shape, f32)
+    for source, target in zip(earlier, outs):
+        target[pl.ds(0, source.shape[0])] = source[...]
+    row_base = lb if merge else 0
+    edge_base = n_z * ifr if merge else 0
+    acc[...] = jnp.zeros(acc.shape, f32)
+    for i in range(lb):
+        blocks = jnp.concatenate([joined[i], joined[i]], axis=0)
+        out = jnp.dot(wire[i], blocks, preferred_element_type=f32)
+        for t in range(groups // 2):
+            tile = out[:, 2 * kb * t : 2 * kb * (t + 1)]
+            one = where[i * groups + 2 * t]
+            two = where[i * groups + 2 * t + 1]
+            acc[one] = acc[one] + jnp.where(low, tile, 0.0)
+            acc[two] = acc[two] + jnp.where(low, 0.0, tile)
+
+    def folded(index):
+        block = acc[index]
+        return block[:, :kb] + block[:, kb:]
+
+    for k in range(n_row):
+        start = (pos[0] ^ k) * lb
         for i in range(lb):
-            blocks = jnp.concatenate([joined[i], joined[i]], axis=0)
-            out = jnp.dot(wire[i], blocks, preferred_element_type=f32)
-            for t in range(groups // 2):
-                tile = out[:, 2 * kb * t : 2 * kb * (t + 1)]
-                one = where[i * groups + 2 * t]
-                two = where[i * groups + 2 * t + 1]
-                acc[one] = acc[one] + jnp.where(low, tile, 0.0)
-                acc[two] = acc[two] + jnp.where(low, 0.0, tile)
-
-        def folded(index):
-            block = acc[index]
-            return block[:, :kb] + block[:, kb:]
-
-        for k in range(n_row):
-            start = (pos[0] ^ k) * lb
-            for i in range(lb):
-                if k == 0:
-                    own[v * lb + i] = folded(start + i)
-                else:
-                    row_outs[k - 1][v * lb + i] = two_parts(folded(start + i))
-        for z in range(n_z):
-            for q in range(ifr):
-                spot = (v * n_z + z) * ifr + q
-                core_keep[spot] = folded(n_row * lb + (z * 2 + core) * ifr + q)
-                core_send[spot] = two_parts(folded(n_row * lb + (z * 2 + 1 - core) * ifr + q))
+            if k == 0:
+                own[row_base + i] = folded(start + i)
+            else:
+                row_outs[k - 1][row_base + i] = two_parts(folded(start + i))
+    for z in range(n_z):
+        for q in range(ifr):
+            spot = edge_base + z * ifr + q
+            core_keep[spot] = folded(n_row * lb + (z * 2 + core) * ifr + q)
+            core_send[spot] = two_parts(folded(n_row * lb + (z * 2 + 1 - core) * ifr + q))
 
 
 def pair_kernel(n_z, count, keep, got, pos, own, *outs):
@@ -433,37 +435,50 @@
     def wire(*shape):
         return shaped(*shape, n, 2 * kb, dtype=bf16)
 
+    def halo_start(own, edge):
+        rows_got = [row_send(own, k) for k in range(1, n_row)]
+        return rows_got, [sub_send(edge, 2 * k) for k in range(1, n_z)]
+
+    def halo_end(own, edge, rows_got, edges_got):
+        same = jnp.concatenate([edge] + edges_got, axis=0)
+        return [own] + rows_got + [same, sub_send(same, 1)]
+
     def halo_of(own, edge):
-        rows_got = [row_send(own, k) for k in range(1, n_row)]
-        same = jnp.concatenate([edge] + [sub_send(edge, 2 * k) for k in range(1, n_z)], axis=0)
-        return [own] + rows_got + [same, sub_send(same, 1)]
+        return halo_end(own, edge, *halo_start(own, edge))
+
+    def groups_of_four(value, size, send):
+        base = 1
+        while base < size:
+            got = [value] + [send(value, base * m) for m in range(1, min(4, size // base))]
+            while len(got) > 1:
+                got = [got[i] + got[i + 1] for i in range(0, len(got), 2)]
+            value = got[0]
+            base *= 4
+        return value
+
+    def z_send(value, k):
+        return sub_send(value, 2 * k)
 
     def sum_halves(keep, send):
         total = keep + sub_send(send, 1)
-        k = 1
-        while k < n_row:
-            total = total + row_send(total, k)
-            k *= 2
-        k = 2
-        while k < n_sub:
-            total = total + sub_send(total, k)
-            k *= 2
+        total = groups_of_four(total, n_z, z_send)
+        total = groups_of_four(total, n_row, row_send)
         return [total, sub_send(total, 1)]
 
-    def partials(wires):
-        m = len(wires)
+    def partials(source, earlier=()):
+        m = 2 if earlier else 1
         outs = [shaped(m * lb, n, kb), shaped(m * n_z * ifr, n, kb), wire(m * n_z * ifr)]
         outs += [wire(m * lb)] * (n_row - 1)
         return run(
-            functools.partial(partial_kernel, n_row, n_z, m),
+            functools.partial(partial_kernel, n_row, n_z, m > 1),
             "partials",
             outs,
-            wires + [joined, where, pos],
+            [source, joined, where, pos] + list(earlier),
             [VMEM((halo_blocks, n, 2 * kb), f32)],
-            smem=(m + 1, m + 2),
+            smem=(2, 3),
         )
 
-    def sum_with_partials(keep, send, parts, m):
+    def sum_with_partials(keep, send, parts, m, meanwhile=()):
         own, edge_keep, edge_send, *row_parts = parts
         total = keep + sub_send(send, 1)
         edge_got = sub_send(edge_send, 1)
@@ -475,23 +490,19 @@
             [edge_keep, edge_got, pos],
             smem=(2,),
         )
-        k = 2
-        while k < n_sub:
-            total = total + sub_send(total, k)
-            k *= 2
         total, *outs = after((total, *outs))
-        edges_got = [sub_send(outs[k - 1], 2 * k) for k in range(1, n_z)]
-        k = 1
-        while k < n_row:
-            total = total + row_send(total, k)
-            k *= 2
-        return [total, sub_send(total, 1)], [own] + rows_got + [edge_own] + edges_got
+        edges_got = [z_send(outs[k - 1], k) for k in range(1, n_z)]
+        total = groups_of_four(total, n_z, z_send)
+        total, rows_got, edges_got, meanwhile = after((total, rows_got, edges_got, list(meanwhile)))
+        total = groups_of_four(total, n_row, row_send)
+        return [total, sub_send(total, 1)], [own] + rows_got + [edge_own] + edges_got, meanwhile
 
     x, p = modes.T, search.T
     scaling = precond.reshape(1, rows)
     wire_shapes = [wire(lb), wire(ifr)]
     x_wire, x_edge = run(wire_kernel, "wire", wire_shapes, [x, bnd], smem=(1,))
-    x_halo = halo_of(x_wire, x_edge)
+    x_rows, x_edges = halo_start(x_wire, x_edge)
+    in_val, if_val, p, x_edges[0] = after((in_val, if_val, p, x_edges[0]))
     p_wire, p_edge = run(wire_kernel, "wire", wire_shapes, [p, bnd], smem=(1,))
     stored, joined, diagonal, where = run(
         functools.partial(prepare_kernel, groups, n_row * lb),
@@ -506,10 +517,12 @@
         smem=(2, 3, 4, 5),
         smem_outs=(3,),
     )
-    p_wire, p_edge, *x_got = after((p_wire, p_edge, *x_halo[1:]))
-    x_halo = [x_wire] + x_got
+    stored, *x_edges = after((stored, *x_edges))
+    x_halo = halo_end(x_wire, x_edge, x_rows, x_edges)
+    x_parts = partials(x_wire)
+    p_wire, p_edge, *x_parts = after((p_wire, p_edge, *x_parts))
     p_halo = halo_of(p_wire, p_edge)
-    x_parts = partials([x_wire])
+    p_parts = partials(p_wire)
     blocks = [stored, diagonal, where, pos]
     halo_scratch = VMEM((halo_blocks, n, 2 * kb), bf16)
     back_scratch = VMEM((lb, n, kb), f32)
@@ -535,8 +548,8 @@
         [halo_scratch, table_scratch],
         smem=(count + 2, count + 3),
     )
-    keep, send, x_parts = after((keep, send, x_parts))
-    halves, x_back = sum_with_partials(keep, send, x_parts, 1)
+    keep, send, x_parts, p_parts = after((keep, send, x_parts, p_parts))
+    halves, x_back, _ = sum_with_partials(keep, send, x_parts, 1)
     count = len(x_back)
     table, ax, energy, w, w_wire, w_edge = run(
         functools.partial(update_kernel, n_row, n_z),
@@ -548,7 +561,7 @@
     )
     w_halo = halo_of(w_wire, w_edge)
     (pap_inverse,) = run(inverse_kernel, "pap_inverse", [shaped(n, n)], [table])
-    w_parts = partials([p_wire, w_wire])
+    w_parts = partials(w_wire, p_parts)
 
     def update_image(first, halo, w, x, p, ax, ap):
         count = len(halo)
@@ -563,7 +576,7 @@
 
     half_w, diag_w, keep, send = update_image(True, w_halo, w, x, p, ax, half_p)
     keep, send, w_parts = after((keep, send, w_parts))
-    halves, w_back = sum_with_partials(keep, send, w_parts, 2)
+    halves, w_back, (pap_inverse,) = sum_with_partials(keep, send, w_parts, 2, [pap_inverse])
     count = len(w_back)
     x, ax, w, w_wire, w_edge, step_x, step_a, small = run(
         functools.partial(move_kernel, n_row, n_z, total_rows),

time: 184 us -> 189 us (1.027)
  starting transfers between devices: 57.5 us -> 76.4 us
  waiting for transfers between devices: 59 us -> 47.9 us
    ppermute x36 -> x39, waiting for transfers between devices: 37.6 us -> 21.5 us  [sub_send(): return lax.ppermute(value, 'sub', [(s, s ^ k) for s in range(n_sub)])]
    ppermute x36 -> x39, starting transfers between devices: 28.9 us -> 44.7 us  [sub_send(): return lax.ppermute(value, 'sub', [(s, s ^ k) for s in range(n_sub)])]
    unnamed x39 -> x34, local copies, waits for them, and re-layouts: 6.79 us -> 1.73 us
    ppermute x24 -> x27, waiting for transfers between devices: 21.4 us -> 26.4 us  [row_send(): return lax.ppermute(value, 'row', [(r, r ^ k) for r in range(n_row)])]
    optimization_barrier x0 -> x1, local copies, waits for them, and re-layouts: none -> 3.3 us  [local(): in_val, if_val, p, x_edges[0] = after((in_val, if_val, p, x_edges[0]))]
    ppermute x24 -> x27, starting transfers between devices: 28.6 us -> 31.7 us  [row_send(): return lax.ppermute(value, 'row', [(r, r ^ k) for r in range(n_row)])]
    pallas_call x16 -> x17, Pallas kernels: 58.9 us -> 58 us  [run(): pl.pallas_call(kernel, name=name, out_shape=outs, in_specs=in_specs, out_...]
  transfers between devices with their start and end apart: 60 -> 66, of which waited for: 25 -> 30; matrix products, arithmetic and copies ran while one was open for 2% -> 2% of each run, Pallas kernels for 13% -> 12%
where the time goes in v3:
time: 189 us
  starting transfers between devices  76.4 us (40%)
  Pallas kernels  58 us (31%)
  waiting for transfers between devices  47.9 us (25%)
  local copies, waits for them, and re-layouts  5.07 us (3%)
    pallas_call x17, Pallas kernels, run(): pl.pallas_call(kernel, name=name, out_shape=outs, in_specs=in_specs, out_...  58 us
    ppermute x39, starting transfers between devices, sub_send(): return lax.ppermute(value, 'sub', [(s, s ^ k) for s in range(n_sub)])  44.7 us
    ppermute x27, starting transfers between devices, row_send(): return lax.ppermute(value, 'row', [(r, r ^ k) for r in range(n_row)])  31.7 us
    ppermute x27, waiting for transfers between devices, row_send(): return lax.ppermute(value, 'row', [(r, r ^ k) for r in range(n_row)])  26.4 us
    ppermute x39, waiting for transfers between devices, sub_send(): return lax.ppermute(value, 'sub', [(s, s ^ k) for s in range(n_sub)])  21.5 us
  transfers between devices with their start and end apart: 66, of which 30 were waited for; matrix products, arithmetic and copies ran while one was open for 2% of the time, Pallas kernels for 12%

profile of v3, /device:TPU:0, one launch (start us, length us, event | category | flops | bytes accessed | tf_op | source)
XLA Modules:
  0.0 188.6 jit_solution(1748688262023427658)
XLA Ops:
  2.9 3.1 %collective-permute-start = (bf16[3,64,128]{2,1,0:T(8,128)(2,1)S(1)}, bf16[3,64,128]{2,1,0:T(8,128)(2,1)S(1)}, u32[]{:S(2)}, u32[]{:S(2)}) collective-permute-start(bf16[3,64,128]{2,1,0:T(8,128)(2,1)S(1)} %get-tuple-element.129), channel_id=1, source_target_pairs={{0,8},{4,12},{8,0},{12,4},{16,24},{20,28},{24,16},{28,20},{1,9},{5... | collective-permute-start | bytes 147464 | tf_op jit(solution)/shard_map/ppermute | solution.py:433
  6.0 2.6 %collective-permute-start.8 = (bf16[3,64,128]{2,1,0:T(8,128)(2,1)S(1)}, bf16[3,64,128]{2,1,0:T(8,128)(2,1)S(1)}, u32[]{:S(2)}, u32[]{:S(2)}) collective-permute-start(bf16[3,64,128]{2,1,0:T(8,128)(2,1)S(1)} %get-tuple-element.129), channel_id=1, source_target_pairs={{0,16},{4,20},{8,24},{12,28},{16,0},{20,4},{24,8},{28,12},{1,17},{... | collective-permute-start | bytes 147464 | tf_op jit(solution)/shard_map/ppermute | solution.py:433
  8.6 1.7 collective-permute-start.10
  10.3 1.5 collective-permute-start.11
  12.2 3.3 %copy.12 = bf16[1,1,96,64,64]{4,3,2,1,0:T(8,128)(2,1)S(1)} copy(bf16[1,1,96,64,64]{2,4,3,1,0:T(8,128)(2,1)} %param.15) | data formatting | bytes 1572864 | tf_op jit(solution)/shard_map/optimization_barrier | solution.py:505
  16.2 2.2 %prepare.1 = (bf16[12,64,1024]{2,1,0:T(8,128)(2,1)S(1)}, bf16[12,64,512]{2,1,0:T(8,128)(2,1)S(1)}, bf16[12,64,128]{2,1,0:T(8,128)(2,1)S(1)}, s32[96]{0:T(128)S(1)}) custom-call(bf16[96,64,64]{2,1,0:T(8,128)(2,1)S(1)} %bitcast.19, bf16[12,64,64]{2,1,0:T(8,128)(2,1)S(1)} %bitcast.25, s32[96]{0:T(128)S(1)} %bitcast.30, s32[96]{0:T(128)S(1)} %bitcast.31, ...), custom_call_target="tpu_custom_call" | custom-call | flops 1000000 | bytes 3441888 | tf_op jit(solution)/shard_map/prepare/pallas_call | solution.py:399
  18.5 2.4 %partials.3 = (f32[12,64,64]{2,1,0:T(8,128)S(1)}, f32[12,64,64]{2,1,0:T(8,128)S(1)}, bf16[12,64,128]{2,1,0:T(8,128)(2,1)S(1)}, bf16[12,64,128]{2,1,0:T(8,128)(2,...) custom-call(bf16[12,64,128]{2,1,0:T(8,128)(2,1)S(1)} %get-tuple-element.133.wire.refs_0_, ...), custom_call_target="tpu_custom_call" | custom-call | flops 1000000 | bytes 2163080 | tf_op jit(solution)/shard_map/partials/pallas_call | solution.py:399
  21.9 3.5 %collective-permute-start.5 = (bf16[3,64,128]{2,1,0:T(8,128)(2,1)S(1)}, bf16[3,64,128]{2,1,0:T(8,128)(2,1)S(1)}, u32[]{:S(2)}, u32[]{:S(2)}) collective-permute-start(bf16[3,64,128]{2,1,0:T(8,128)(2,1)S(1)} %get-tuple-element.145), channel_id=1, source_target_pairs={{0,16},{4,20},{8,24},{12,28},{16,0},{20,4},{24,8},{28,12},{1,17},{... | collective-permute-start | bytes 147464 | tf_op jit(solution)/shard_map/ppermute | solution.py:433
  25.5 3.5 %collective-permute-start.6 = (bf16[3,64,128]{2,1,0:T(8,128)(2,1)S(1)}, bf16[3,64,128]{2,1,0:T(8,128)(2,1)S(1)}, u32[]{:S(2)}, u32[]{:S(2)}) collective-permute-start(bf16[3,64,128]{2,1,0:T(8,128)(2,1)S(1)} %get-tuple-element.145), channel_id=1, source_target_pairs={{0,24},{4,28},{8,16},{12,20},{16,8},{20,12},{24,0},{28,4},{1,25},{... | collective-permute-start | bytes 147464 | tf_op jit(solution)/shard_map/ppermute | solution.py:433
  29.0 2.4 %collective-permute-done.6 = bf16[3,64,128]{2,1,0:T(8,128)(2,1)S(1)} collective-permute-done((bf16[3,64,128]{2,1,0:T(8,128)(2,1)S(1)}, bf16[3,64,128]{2,1,0:T(8,128)(2,1)S(1)}, u32[]{:S(2)}, u32[]{:S(2)}) %collective-permute-start.6) | collective-permute-done | bytes 49184 | tf_op jit(solution)/shard_map/ppermute | solution.py:433
  31.4 1.5 collective-permute-start.1
  32.9 1.6 collective-permute-start.2
  35.0 2.5 %partials.4 = (f32[12,64,64]{2,1,0:T(8,128)S(1)}, f32[12,64,64]{2,1,0:T(8,128)S(1)}, bf16[12,64,128]{2,1,0:T(8,128)(2,1)S(1)}, bf16[12,64,128]{2,1,0:T(8,128)(2,...) custom-call(bf16[12,64,128]{2,1,0:T(8,128)(2,1)S(1)} %get-tuple-element.144.refs_0_.wire, ...), custom_call_target="tpu_custom_call" | custom-call | flops 1000000 | bytes 2163080 | tf_op jit(solution)/shard_map/partials/pallas_call | solution.py:399
  37.5 2.1 %x_image.1 = (f32[64,768]{1,0:T(8,128)S(1)}, f32[64,768]{1,0:T(8,128)S(1)}, f32[128,128]{1,0:T(8,128)S(1)}) custom-call(bf16[12,64,128]{2,1,0:T(8,128)(2,1)S(1)} %get-tuple-element.133.wire.refs_0_, bf16[12,64,128]{2,1,0:T(8,128)(2,1)S(1)} %collective-permute-done.10.refs_1_, bf16[12,64,128]{2,1,0:T(8,128)(2,1)S(1)} %collective-permute-done.11.refs_2_, ...), custom_call_target="tpu_custom_call" | custom-call | flops 1000000 | bytes 3801480 | tf_op jit(solution)/shard_map/x_image/pallas_call | solution.py:399
  39.6 2.7 %collective-permute-done.2.refs_2_ = bf16[12,64,128]{2,1,0:T(8,128)(2,1)S(1)} collective-permute-done((bf16[12,64,128]{2,1,0:T(8,128)(2,1)S(1)}, bf16[12,64,128]{2,1,0:T(8,128)(2,1)S(1)}, u32[]{:S(2)}, u32[]{:S(2)}) %collective-permute-start.2) | collective-permute-done | bytes 196640 | tf_op jit(solution)/shard_map/ppermute | solution.py:430
  42.3 1.9 p_image.1
  47.3 2.5 %collective-permute-start.17 = (f32[96,128]{1,0:T(8,128)S(1)}, f32[96,128]{1,0:T(8,128)S(1)}, u32[]{:S(2)}, u32[]{:S(2)}) collective-permute-start(f32[96,128]{1,0:T(8,128)S(1)} %add.63), channel_id=1, source_target_pairs={{0,16},{4,20},{8,24},{12,28},{16,0},{20,4},{24,8},{28,12},{1,17},{... | collective-permute-start | bytes 147464 | tf_op jit(solution)/shard_map/ppermute | solution.py:433
  49.8 1.9 collective-permute-start.18
  52.6 1.8 collective-permute-start.21
  54.4 2.8 %collective-permute-start.23 = (bf16[3,64,128]{2,1,0:T(8,128)(2,1)S(1)}, bf16[3,64,128]{2,1,0:T(8,128)(2,1)S(1)}, u32[]{:S(2)}, u32[]{:S(2)}) collective-permute-start(bf16[3,64,128]{2,1,0:T(8,128)(2,1)S(1)} %get-tuple-element.182), channel_id=1, source_target_pairs={{0,16},{4,20},{8,24},{12,28},{16,0},{20,4},{24,8},{28,12},{1,17},{... | collective-permute-start | bytes 147464 | tf_op jit(solution)/shard_map/ppermute | solution.py:433
  57.1 1.6 collective-permute-start.24
  58.8 3.2 %collective-permute-done.20.refs_2_ = bf16[12,64,128]{2,1,0:T(8,128)(2,1)S(1)} collective-permute-done((bf16[12,64,128]{2,1,0:T(8,128)(2,1)S(1)}, bf16[12,64,128]{2,1,0:T(8,128)(2,1)S(1)}, u32[]{:S(2)}, u32[]{:S(2)}) %collective-permute-start.20) | collective-permute-done | bytes 196640 | tf_op jit(solution)/shard_map/ppermute | solution.py:430
  63.6 1.4 collective-permute-start.26
  65.0 1.5 collective-permute-start.27
  67.6 2.3 %collective-permute-done.27 = f32[96,128]{1,0:T(8,128)S(1)} collective-permute-done((f32[96,128]{1,0:T(8,128)S(1)}, f32[96,128]{1,0:T(8,128)S(1)}, u32[]{:S(2)}, u32[]{:S(2)}) %collective-permute-start.27) | collective-permute-done | bytes 49184 | tf_op jit(solution)/shard_map/ppermute | solution.py:430
  70.1 1.2 collective-permute-done.28.refs_9_
  71.3 5.2 %update.1 = (f32[192,128]{1,0:T(8,128)S(1)}, f32[64,768]{1,0:T(8,128)S(1)}, f32[64,64]{1,0:T(8,128)S(1)}, f32[64,768]{1,0:T(8,128)S(1)}, bf16[12,64,128]{2,1,0:T...) custom-call(f32[12,64,64]{2,1,0:T(8,128)S(1)} %get-tuple-element.169.refs_0_, ...), custom_call_target="tpu_custom_call" | custom-call | flops 1000000 | bytes 2427924 | tf_op jit(solution)/shard_map/update/pallas_call | solution.py:399
  76.5 2.3 %collective-permute-start.33 = (bf16[3,64,128]{2,1,0:T(8,128)(2,1)S(1)}, bf16[3,64,128]{2,1,0:T(8,128)(2,1)S(1)}, u32[]{:S(2)}, u32[]{:S(2)}) collective-permute-start(bf16[3,64,128]{2,1,0:T(8,128)(2,1)S(1)} %get-tuple-element.194), channel_id=1, source_target_pairs={{0,16},{4,20},{8,24},{12,28},{16,0},{20,4},{24,8},{28,12},{1,17},{... | collective-permute-start | bytes 147464 | tf_op jit(solution)/shard_map/ppermute | solution.py:433
  78.8 2.1 %collective-permute-start.34 = (bf16[3,64,128]{2,1,0:T(8,128)(2,1)S(1)}, bf16[3,64,128]{2,1,0:T(8,128)(2,1)S(1)}, u32[]{:S(2)}, u32[]{:S(2)}) collective-permute-start(bf16[3,64,128]{2,1,0:T(8,128)(2,1)S(1)} %get-tuple-element.194), channel_id=1, source_target_pairs={{0,24},{4,28},{8,16},{12,20},{16,8},{20,12},{24,0},{28,4},{1,25},{... | collective-permute-start | bytes 147464 | tf_op jit(solution)/shard_map/ppermute | solution.py:433
  80.9 1.3 collective-permute-start.29
  83.0 1.4 collective-permute-start.31
  84.8 2.8 %partials.5 = (f32[24,64,64]{2,1,0:T(8,128)S(1)}, f32[24,64,64]{2,1,0:T(8,128)S(1)}, bf16[24,64,128]{2,1,0:T(8,128)(2,1)S(1)}, bf16[24,64,128]{2,1,0:T(8,128)(2,...) custom-call(bf16[12,64,128]{2,1,0:T(8,128)(2,1)S(1)} %get-tuple-element.193.refs_0_.wire, ...), custom_call_target="tpu_custom_call" | custom-call | flops 1000000 | bytes 4522376 | tf_op jit(solution)/shard_map/partials/pallas_call | solution.py:399
  88.7 3.5 %collective-permute-done.30.refs_2_ = bf16[12,64,128]{2,1,0:T(8,128)(2,1)S(1)} collective-permute-done((bf16[12,64,128]{2,1,0:T(8,128)(2,1)S(1)}, bf16[12,64,128]{2,1,0:T(8,128)(2,1)S(1)}, u32[]{:S(2)}, u32[]{:S(2)}) %collective-permute-start.30) | collective-permute-done | bytes 196640 | tf_op jit(solution)/shard_map/ppermute | solution.py:430
  92.2 2.7 %update_image.2 = (f32[64,768]{1,0:T(8,128)S(1)}, f32[64,768]{1,0:T(8,128)S(1)}, f32[96,128]{1,0:T(8,128)S(1)}, f32[96,128]{1,0:T(8,128)S(1)}) custom-call(bf16[12,64,128]{2,1,0:T(8,128)(2,1)S(1)} %get-tuple-element.193.refs_0_.wire, bf16[12,64,128]{2,1,0:T(8,128)(2,1)S(1)} %collective-permute-done.29.refs_1_, ...), custom_call_target="tpu_custom_call" | custom-call | flops 1000000 | bytes 4424072 | tf_op jit(solution)/shard_map/update_image/pallas_call | solution.py:399
  96.8 1.7 collective-permute-start.43
  98.6 1.2 collective-permute-done.36
  99.8 1.4 pair.3
  101.3 2.1 %collective-permute-start.39 = (f32[96,128]{1,0:T(8,128)S(1)}, f32[96,128]{1,0:T(8,128)S(1)}, u32[]{:S(2)}, u32[]{:S(2)}) collective-permute-start(f32[96,128]{1,0:T(8,128)S(1)} %add.70), channel_id=1, source_target_pairs={{0,16},{4,20},{8,24},{12,28},{16,0},{20,4},{24,8},{28,12},{1,17},{... | collective-permute-start | bytes 147464 | tf_op jit(solution)/shard_map/ppermute | solution.py:433
  103.4 3.6 %collective-permute-done.41.refs_1_ = bf16[24,64,128]{2,1,0:T(8,128)(2,1)S(1)} collective-permute-done((bf16[24,64,128]{2,1,0:T(8,128)(2,1)S(1)}, bf16[24,64,128]{2,1,0:T(8,128)(2,1)S(1)}, u32[]{:S(2)}, u32[]{:S(2)}) %collective-permute-start.41) | collective-permute-done | bytes 393248 | tf_op jit(solution)/shard_map/ppermute | solution.py:430
  107.0 1.6 collective-permute-start.40
  108.6 3.8 %pap_inverse.1.refs_14_ = f32[64,64]{1,0:T(8,128)S(1)} custom-call(f32[192,128]{1,0:T(8,128)S(1)} %get-tuple-element.227.table.refs_12_), custom_call_target="tpu_custom_call" | custom-call | flops 1000000 | bytes 114688 | tf_op jit(solution)/shard_map/pap_inverse/pallas_call | solution.py:399
  112.5 2.8 %collective-permute-start.45 = (bf16[6,64,128]{2,1,0:T(8,128)(2,1)S(1)}, bf16[6,64,128]{2,1,0:T(8,128)(2,1)S(1)}, u32[]{:S(2)}, u32[]{:S(2)}) collective-permute-start(bf16[6,64,128]{2,1,0:T(8,128)(2,1)S(1)} %get-tuple-element.225), channel_id=1, source_target_pairs={{0,16},{4,20},{8,24},{12,28},{16,0},{20,4},{24,8},{28,12},{1,17},{... | collective-permute-start | bytes 294920 | tf_op jit(solution)/shard_map/ppermute | solution.py:433
  115.3 1.6 collective-permute-start.46
  117.2 5.2 %collective-permute-done.45.refs_6_ = bf16[6,64,128]{2,1,0:T(8,128)(2,1)S(1)} collective-permute-done((bf16[6,64,128]{2,1,0:T(8,128)(2,1)S(1)}, bf16[6,64,128]{2,1,0:T(8,128)(2,1)S(1)}, u32[]{:S(2)}, u32[]{:S(2)}) %collective-permute-start.45) | collective-permute-done | bytes 98336 | tf_op jit(solution)/shard_map/ppermute | solution.py:433
  124.1 1.7 collective-permute-start.49
  127.4 1.7 collective-permute-done.49
  129.2 1.2 collective-permute-done.50.refs_9_
  130.4 11.0 %move.1 = (f32[64,768]{1,0:T(8,128)S(1)}, f32[64,768]{1,0:T(8,128)S(1)}, f32[64,768]{1,0:T(8,128)S(1)}, bf16[12,64,128]{2,1,0:T(8,128)(2,1)S(1)}, bf16[3,64,128]...) custom-call(f32[24,64,64]{2,1,0:T(8,128)S(1)} %get-tuple-element.212.refs_0_, ...), custom_call_target="tpu_custom_call" | custom-call | flops 1000000 | bytes 5065748 | tf_op jit(solution)/shard_map/move/pallas_call | solution.py:399
  141.4 1.7 collective-permute-start.54
  143.1 1.2 collective-permute-start.55
  144.3 1.6 collective-permute-start.56
  147.0 1.2 collective-permute-start.52
  148.2 1.2 collective-permute-start.53
  150.4 4.6 %settle.1 = (f32[64,768]{1,0:T(8,128)S(1)}, f32[64,768]{1,0:T(8,128)S(1)}, f32[192,64]{1,0:T(8,128)S(1)}) custom-call(f32[256,64]{1,0:T(8,128)S(1)} %get-tuple-element.245.small, f32[64,768]{1,0:T(8,128)S(1)} %get-tuple-element.246.step_x, f32[64,768]{1,0:T(8,128)S(1)} %get-tuple-element.247.step_a), custom_call_target="tpu_custom_call" | custom-call | flops 1000000 | bytes 901120 | tf_op jit(solution)/shard_map/settle/pallas_call | solution.py:399
  155.0 2.1 %collective-permute-done.52.refs_2_ = bf16[12,64,128]{2,1,0:T(8,128)(2,1)S(1)} collective-permute-done((bf16[12,64,128]{2,1,0:T(8,128)(2,1)S(1)}, bf16[12,64,128]{2,1,0:T(8,128)(2,1)S(1)}, u32[]{:S(2)}, u32[]{:S(2)}) %collective-permute-start.52) | collective-permute-done | bytes 196640 | tf_op jit(solution)/shard_map/ppermute | solution.py:430
  157.1 3.0 %update_image.3 = (f32[64,768]{1,0:T(8,128)}, f32[64,768]{1,0:T(8,128)}, f32[96,128]{1,0:T(8,128)S(1)}, f32[96,128]{1,0:T(8,128)S(1)}) custom-call(bf16[12,64,128]{2,1,0:T(8,128)(2,1)S(1)} %get-tuple-element.241.refs_0_, bf16[12,64,128]{2,1,0:T(8,128)(2,1)S(1)} %collective-permute-done.51.refs_1_, bf16[12,64,128]{2,1,0:T(8,128)(2,1)S(1)} %collective-permute-done.52.refs_2_, ...), custom_call_target="tpu_custom_call" | custom-call | flops 1000000 | bytes 4424072 | tf_op jit(solution)/shard_map/update_image/pallas_call | solution.py:399
  160.0 1.2 collective-permute-done.58
  162.0 2.0 %collective-permute-start.60 = (f32[96,128]{1,0:T(8,128)S(1)}, f32[96,128]{1,0:T(8,128)S(1)}, u32[]{:S(2)}, u32[]{:S(2)}) collective-permute-start(f32[96,128]{1,0:T(8,128)S(1)} %add.77), channel_id=1, source_target_pairs={{0,16},{4,20},{8,24},{12,28},{16,0},{20,4},{24,8},{28,12},{1,17},{... | collective-permute-start | bytes 147464 | tf_op jit(solution)/shard_map/ppermute | solution.py:433
  164.1 1.6 collective-permute-start.61
  165.7 3.1 %collective-permute-done.60 = f32[96,128]{1,0:T(8,128)S(1)} collective-permute-done((f32[96,128]{1,0:T(8,128)S(1)}, f32[96,128]{1,0:T(8,128)S(1)}, u32[]{:S(2)}, u32[]{:S(2)}) %collective-permute-start.60) | collective-permute-done | bytes 49184 | tf_op jit(solution)/shard_map/ppermute | solution.py:433
  172.0 1.5 collective-permute-start.64
  175.1 1.9 %collective-permute-done.64 = f32[96,128]{1,0:T(8,128)S(1)} collective-permute-done((f32[96,128]{1,0:T(8,128)S(1)}, f32[96,128]{1,0:T(8,128)S(1)}, u32[]{:S(2)}, u32[]{:S(2)}) %collective-permute-start.64) | collective-permute-done | bytes 49184 | tf_op jit(solution)/shard_map/ppermute | solution.py:430
  177.1 1.2 collective-permute-done.65.other
  178.3 10.3 %finish.1 = (f32[64,768]{1,0:T(8,128)}, f32[64,768]{1,0:T(8,128)}) custom-call(f32[96,128]{1,0:T(8,128)S(1)} %add_add_fusion.mine, f32[96,128]{1,0:T(8,128)S(1)} %collective-permute-done.65.other, s32[2]{0:T(128)S(1)} %pad_add_fusion.pos.refs_9_.refs_10_, f32[192,64]{1,0:T(8,128)S(1)} %get-tuple-element.253.state, ...), custom_call_target="tpu_custom_call" | custom-call | flops 1000000 | bytes 1130504 | tf_op jit(solution)/shard_map/finish/pallas_call | solution.py:399
  (135 shorter events, 27.5 us)
Async XLA Ops:
  2.9 9.0 %collective-permute-start = (bf16[3,64,128]{2,1,0:T(8,128)(2,1)S(1)}, bf16[3,64,128]{2,1,0:T(8,128)(2,1)S(1)}, u32[]{:S(2)}, u32[]{:S(2)}) collective-permute-start(bf16[3,64,128]{2,1,0:T(8,128)(2,1)S(1)} %get-tuple-element.129), channel_id=1, source_target_pairs={{0,8},{4,12},{8,0},{12,4},{16,24},{20,28},{24,16},{28,20},{1,9},{5... | collective-permute-start | bytes 147464 | tf_op jit(solution)/shard_map/ppermute | solution.py:433
  6.0 14.9 %collective-permute-start.8 = (bf16[3,64,128]{2,1,0:T(8,128)(2,1)S(1)}, bf16[3,64,128]{2,1,0:T(8,128)(2,1)S(1)}, u32[]{:S(2)}, u32[]{:S(2)}) collective-permute-start(bf16[3,64,128]{2,1,0:T(8,128)(2,1)S(1)} %get-tuple-element.129), channel_id=1, source_target_pairs={{0,16},{4,20},{8,24},{12,28},{16,0},{20,4},{24,8},{28,12},{1,17},{... | collective-permute-start | bytes 147464 | tf_op jit(solution)/shard_map/ppermute | solution.py:433
  8.6 13.3 %collective-permute-start.9 = (bf16[3,64,128]{2,1,0:T(8,128)(2,1)S(1)}, bf16[3,64,128]{2,1,0:T(8,128)(2,1)S(1)}, u32[]{:S(2)}, u32[]{:S(2)}) collective-permute-start(bf16[3,64,128]{2,1,0:T(8,128)(2,1)S(1)} %get-tuple-element.129), channel_id=1, source_target_pairs={{0,24},{4,28},{8,16},{12,20},{16,8},{20,12},{24,0},{28,4},{1,25},{... | collective-permute-start | bytes 147464 | tf_op jit(solution)/shard_map/ppermute | solution.py:433
  8.6 24.3 %collective-permute-start.10 = (bf16[12,64,128]{2,1,0:T(8,128)(2,1)S(1)}, bf16[12,64,128]{2,1,0:T(8,128)(2,1)S(1)}, u32[]{:S(2)}, u32[]{:S(2)}) collective-permute-start(bf16[12,64,128]{2,1,0:T(8,128)(2,1)S(1)} %get-tuple-element.133.wire.refs_0_), channel_id=1, source_target_pairs={{0,1},{1,0},{2,3},{3,2},{4,5},{5,4},{6,7},{7,6},{8,9},{9,8},{10,11... | collective-permute-start | bytes 589832 | tf_op jit(solution)/shard_map/ppermute | solution.py:430
  10.3 24.2 %collective-permute-start.11 = (bf16[12,64,128]{2,1,0:T(8,128)(2,1)S(1)}, bf16[12,64,128]{2,1,0:T(8,128)(2,1)S(1)}, u32[]{:S(2)}, u32[]{:S(2)}) collective-permute-start(bf16[12,64,128]{2,1,0:T(8,128)(2,1)S(1)} %get-tuple-element.133.wire.refs_0_), channel_id=1, source_target_pairs={{0,2},{1,3},{2,0},{3,1},{4,6},{5,7},{6,4},{7,5},{8,10},{9,11},{10,... | collective-permute-start | bytes 589832 | tf_op jit(solution)/shard_map/ppermute | solution.py:430
  11.9 23.1 %collective-permute-start.12 = (bf16[12,64,128]{2,1,0:T(8,128)(2,1)S(1)}, bf16[12,64,128]{2,1,0:T(8,128)(2,1)S(1)}, u32[]{:S(2)}, u32[]{:S(2)}) collective-permute-start(bf16[12,64,128]{2,1,0:T(8,128)(2,1)S(1)} %get-tuple-element.133.wire.refs_0_), channel_id=1, source_target_pairs={{0,3},{1,2},{2,1},{3,0},{4,7},{5,6},{6,5},{7,4},{8,11},{9,10},{10,... | collective-permute-start | bytes 589832 | tf_op jit(solution)/shard_map/ppermute | solution.py:430
  20.9 4.5 %collective-permute-start.4 = (bf16[3,64,128]{2,1,0:T(8,128)(2,1)S(1)}, bf16[3,64,128]{2,1,0:T(8,128)(2,1)S(1)}, u32[]{:S(2)}, u32[]{:S(2)}) collective-permute-start(bf16[3,64,128]{2,1,0:T(8,128)(2,1)S(1)} %get-tuple-element.145), channel_id=1, source_target_pairs={{0,8},{4,12},{8,0},{12,4},{16,24},{20,28},{24,16},{28,20},{1,9},{5... | collective-permute-start | bytes 147464 | tf_op jit(solution)/shard_map/ppermute | solution.py:433
  21.9 7.0 %collective-permute-start.5 = (bf16[3,64,128]{2,1,0:T(8,128)(2,1)S(1)}, bf16[3,64,128]{2,1,0:T(8,128)(2,1)S(1)}, u32[]{:S(2)}, u32[]{:S(2)}) collective-permute-start(bf16[3,64,128]{2,1,0:T(8,128)(2,1)S(1)} %get-tuple-element.145), channel_id=1, source_target_pairs={{0,16},{4,20},{8,24},{12,28},{16,0},{20,4},{24,8},{28,12},{1,17},{... | collective-permute-start | bytes 147464 | tf_op jit(solution)/shard_map/ppermute | solution.py:433
  25.5 6.0 %collective-permute-start.6 = (bf16[3,64,128]{2,1,0:T(8,128)(2,1)S(1)}, bf16[3,64,128]{2,1,0:T(8,128)(2,1)S(1)}, u32[]{:S(2)}, u32[]{:S(2)}) collective-permute-start(bf16[3,64,128]{2,1,0:T(8,128)(2,1)S(1)} %get-tuple-element.145), channel_id=1, source_target_pairs={{0,24},{4,28},{8,16},{12,20},{16,8},{20,12},{24,0},{28,4},{1,25},{... | collective-permute-start | bytes 147464 | tf_op jit(solution)/shard_map/ppermute | solution.py:433
  28.9 8.5 %collective-permute-start.13 = (bf16[12,64,128]{2,1,0:T(8,128)(2,1)S(1)}, bf16[12,64,128]{2,1,0:T(8,128)(2,1)S(1)}, u32[]{:S(2)}, u32[]{:S(2)}) collective-permute-start(bf16[12,64,128]{2,1,0:T(8,128)(2,1)S(1)} %constant_dynamic-update-slice_fusion.4.refs_4_), channel_id=1, source_target_pairs={{0,4},{4,0},{8,12},{12,8},{16,20},{20,16},{24,28},{28,24},{1,5},{5... | collective-permute-start | bytes 589832 | tf_op jit(solution)/shard_map/ppermute | solution.py:433
  31.4 8.1 %collective-permute-start.1 = (bf16[12,64,128]{2,1,0:T(8,128)(2,1)S(1)}, bf16[12,64,128]{2,1,0:T(8,128)(2,1)S(1)}, u32[]{:S(2)}, u32[]{:S(2)}) collective-permute-start(bf16[12,64,128]{2,1,0:T(8,128)(2,1)S(1)} %get-tuple-element.144.refs_0_.wire), channel_id=1, source_target_pairs={{0,1},{1,0},{2,3},{3,2},{4,5},{5,4},{6,7},{7,6},{8,9},{9,8},{10,11... | collective-permute-start | bytes 589832 | tf_op jit(solution)/shard_map/ppermute | solution.py:430
  32.9 9.3 %collective-permute-start.2 = (bf16[12,64,128]{2,1,0:T(8,128)(2,1)S(1)}, bf16[12,64,128]{2,1,0:T(8,128)(2,1)S(1)}, u32[]{:S(2)}, u32[]{:S(2)}) collective-permute-start(bf16[12,64,128]{2,1,0:T(8,128)(2,1)S(1)} %get-tuple-element.144.refs_0_.wire), channel_id=1, source_target_pairs={{0,2},{1,3},{2,0},{3,1},{4,6},{5,7},{6,4},{7,5},{8,10},{9,11},{10,... | collective-permute-start | bytes 589832 | tf_op jit(solution)/shard_map/ppermute | solution.py:430
  34.5 7.8 %collective-permute-start.3 = (bf16[12,64,128]{2,1,0:T(8,128)(2,1)S(1)}, bf16[12,64,128]{2,1,0:T(8,128)(2,1)S(1)}, u32[]{:S(2)}, u32[]{:S(2)}) collective-permute-start(bf16[12,64,128]{2,1,0:T(8,128)(2,1)S(1)} %get-tuple-element.144.refs_0_.wire), channel_id=1, source_target_pairs={{0,3},{1,2},{2,1},{3,0},{4,7},{5,6},{6,5},{7,4},{8,11},{9,10},{10,... | collective-permute-start | bytes 589832 | tf_op jit(solution)/shard_map/ppermute | solution.py:430
  35.0 7.3 %collective-permute-start.7 = (bf16[12,64,128]{2,1,0:T(8,128)(2,1)S(1)}, bf16[12,64,128]{2,1,0:T(8,128)(2,1)S(1)}, u32[]{:S(2)}, u32[]{:S(2)}) collective-permute-start(bf16[12,64,128]{2,1,0:T(8,128)(2,1)S(1)} %constant_dynamic-update-slice_fusion.refs_4_), channel_id=1, source_target_pairs={{0,4},{4,0},{8,12},{12,8},{16,20},{20,16},{24,28},{28,24},{1,5},{5... | collective-permute-start | bytes 589832 | tf_op jit(solution)/shard_map/ppermute | solution.py:433
  44.2 2.2 %collective-permute-start.15 = (bf16[12,64,128]{2,1,0:T(8,128)(2,1)S(1)}, bf16[12,64,128]{2,1,0:T(8,128)(2,1)S(1)}, u32[]{:S(2)}, u32[]{:S(2)}) collective-permute-start(bf16[12,64,128]{2,1,0:T(8,128)(2,1)S(1)} %get-tuple-element.173), channel_id=1, source_target_pairs={{0,4},{4,0},{8,12},{12,8},{16,20},{20,16},{24,28},{28,24},{1,5},{5... | collective-permute-start | bytes 589832 | tf_op jit(solution)/shard_map/ppermute | solution.py:433
  44.3 8.3 %collective-permute-start.19 = (bf16[12,64,128]{2,1,0:T(8,128)(2,1)S(1)}, bf16[12,64,128]{2,1,0:T(8,128)(2,1)S(1)}, u32[]{:S(2)}, u32[]{:S(2)}) collective-permute-start(bf16[12,64,128]{2,1,0:T(8,128)(2,1)S(1)} %get-tuple-element.178), channel_id=1, source_target_pairs={{0,1},{1,0},{2,3},{3,2},{4,5},{5,4},{6,7},{7,6},{8,9},{9,8},{10,11... | collective-permute-start | bytes 589832 | tf_op jit(solution)/shard_map/ppermute | solution.py:430
  45.1 1.2 collective-permute-start.14
  47.2 7.2 %collective-permute-start.16 = (f32[96,128]{1,0:T(8,128)S(1)}, f32[96,128]{1,0:T(8,128)S(1)}, u32[]{:S(2)}, u32[]{:S(2)}) collective-permute-start(f32[96,128]{1,0:T(8,128)S(1)} %add.63), channel_id=1, source_target_pairs={{0,8},{4,12},{8,0},{12,4},{16,24},{20,28},{24,16},{28,20},{1,9},{5... | collective-permute-start | bytes 147464 | tf_op jit(solution)/shard_map/ppermute | solution.py:433
  47.3 7.1 %collective-permute-start.17 = (f32[96,128]{1,0:T(8,128)S(1)}, f32[96,128]{1,0:T(8,128)S(1)}, u32[]{:S(2)}, u32[]{:S(2)}) collective-permute-start(f32[96,128]{1,0:T(8,128)S(1)} %add.63), channel_id=1, source_target_pairs={{0,16},{4,20},{8,24},{12,28},{16,0},{20,4},{24,8},{28,12},{1,17},{... | collective-permute-start | bytes 147464 | tf_op jit(solution)/shard_map/ppermute | solution.py:433
  49.8 7.3 %collective-permute-start.18 = (f32[96,128]{1,0:T(8,128)S(1)}, f32[96,128]{1,0:T(8,128)S(1)}, u32[]{:S(2)}, u32[]{:S(2)}) collective-permute-start(f32[96,128]{1,0:T(8,128)S(1)} %add.63), channel_id=1, source_target_pairs={{0,24},{4,28},{8,16},{12,20},{16,8},{20,12},{24,0},{28,4},{1,25},{... | collective-permute-start | bytes 147464 | tf_op jit(solution)/shard_map/ppermute | solution.py:433
  51.6 10.3 %collective-permute-start.20 = (bf16[12,64,128]{2,1,0:T(8,128)(2,1)S(1)}, bf16[12,64,128]{2,1,0:T(8,128)(2,1)S(1)}, u32[]{:S(2)}, u32[]{:S(2)}) collective-permute-start(bf16[12,64,128]{2,1,0:T(8,128)(2,1)S(1)} %get-tuple-element.179), channel_id=1, source_target_pairs={{0,2},{1,3},{2,0},{3,1},{4,6},{5,7},{6,4},{7,5},{8,10},{9,11},{10,... | collective-permute-start | bytes 589832 | tf_op jit(solution)/shard_map/ppermute | solution.py:430
  52.6 9.4 %collective-permute-start.21 = (bf16[12,64,128]{2,1,0:T(8,128)(2,1)S(1)}, bf16[12,64,128]{2,1,0:T(8,128)(2,1)S(1)}, u32[]{:S(2)}, u32[]{:S(2)}) collective-permute-start(bf16[12,64,128]{2,1,0:T(8,128)(2,1)S(1)} %get-tuple-element.180), channel_id=1, source_target_pairs={{0,3},{1,2},{2,1},{3,0},{4,7},{5,6},{6,5},{7,4},{8,11},{9,10},{10,... | collective-permute-start | bytes 589832 | tf_op jit(solution)/shard_map/ppermute | solution.py:430
  54.4 7.6 %collective-permute-start.22 = (bf16[3,64,128]{2,1,0:T(8,128)(2,1)S(1)}, bf16[3,64,128]{2,1,0:T(8,128)(2,1)S(1)}, u32[]{:S(2)}, u32[]{:S(2)}) collective-permute-start(bf16[3,64,128]{2,1,0:T(8,128)(2,1)S(1)} %get-tuple-element.181), channel_id=1, source_target_pairs={{0,8},{4,12},{8,0},{12,4},{16,24},{20,28},{24,16},{28,20},{1,9},{5... | collective-permute-start | bytes 147464 | tf_op jit(solution)/shard_map/ppermute | solution.py:433
  54.4 7.6 %collective-permute-start.23 = (bf16[3,64,128]{2,1,0:T(8,128)(2,1)S(1)}, bf16[3,64,128]{2,1,0:T(8,128)(2,1)S(1)}, u32[]{:S(2)}, u32[]{:S(2)}) collective-permute-start(bf16[3,64,128]{2,1,0:T(8,128)(2,1)S(1)} %get-tuple-element.182), channel_id=1, source_target_pairs={{0,16},{4,20},{8,24},{12,28},{16,0},{20,4},{24,8},{28,12},{1,17},{... | collective-permute-start | bytes 147464 | tf_op jit(solution)/shard_map/ppermute | solution.py:433
  57.1 5.9 %collective-permute-start.24 = (bf16[3,64,128]{2,1,0:T(8,128)(2,1)S(1)}, bf16[3,64,128]{2,1,0:T(8,128)(2,1)S(1)}, u32[]{:S(2)}, u32[]{:S(2)}) collective-permute-start(bf16[3,64,128]{2,1,0:T(8,128)(2,1)S(1)} %get-tuple-element.183), channel_id=1, source_target_pairs={{0,24},{4,28},{8,16},{12,20},{16,8},{20,12},{24,0},{28,4},{1,25},{... | collective-permute-start | bytes 147464 | tf_op jit(solution)/shard_map/ppermute | solution.py:433
  63.0 4.1 %collective-permute-start.25 = (f32[96,128]{1,0:T(8,128)S(1)}, f32[96,128]{1,0:T(8,128)S(1)}, u32[]{:S(2)}, u32[]{:S(2)}) collective-permute-start(f32[96,128]{1,0:T(8,128)S(1)} %add_add_fusion.5), channel_id=1, source_target_pairs={{0,1},{1,0},{2,3},{3,2},{4,5},{5,4},{6,7},{7,6},{8,9},{9,8},{10,11... | collective-permute-start | bytes 147464 | tf_op jit(solution)/shard_map/ppermute | solution.py:430
  63.6 4.1 %collective-permute-start.26 = (f32[96,128]{1,0:T(8,128)S(1)}, f32[96,128]{1,0:T(8,128)S(1)}, u32[]{:S(2)}, u32[]{:S(2)}) collective-permute-start(f32[96,128]{1,0:T(8,128)S(1)} %add_add_fusion.5), channel_id=1, source_target_pairs={{0,2},{1,3},{2,0},{3,1},{4,6},{5,7},{6,4},{7,5},{8,10},{9,11},{10,... | collective-permute-start | bytes 147464 | tf_op jit(solution)/shard_map/ppermute | solution.py:430
  65.0 5.0 %collective-permute-start.27 = (f32[96,128]{1,0:T(8,128)S(1)}, f32[96,128]{1,0:T(8,128)S(1)}, u32[]{:S(2)}, u32[]{:S(2)}) collective-permute-start(f32[96,128]{1,0:T(8,128)S(1)} %add_add_fusion.5), channel_id=1, source_target_pairs={{0,3},{1,2},{2,1},{3,0},{4,7},{5,6},{6,5},{7,4},{8,11},{9,10},{10,... | collective-permute-start | bytes 147464 | tf_op jit(solution)/shard_map/ppermute | solution.py:430
  70.0 1.3 collective-permute-start.28
  76.4 6.5 %collective-permute-start.32 = (bf16[3,64,128]{2,1,0:T(8,128)(2,1)S(1)}, bf16[3,64,128]{2,1,0:T(8,128)(2,1)S(1)}, u32[]{:S(2)}, u32[]{:S(2)}) collective-permute-start(bf16[3,64,128]{2,1,0:T(8,128)(2,1)S(1)} %get-tuple-element.194), channel_id=1, source_target_pairs={{0,8},{4,12},{8,0},{12,4},{16,24},{20,28},{24,16},{28,20},{1,9},{5... | collective-permute-start | bytes 147464 | tf_op jit(solution)/shard_map/ppermute | solution.py:433
  76.5 7.9 %collective-permute-start.33 = (bf16[3,64,128]{2,1,0:T(8,128)(2,1)S(1)}, bf16[3,64,128]{2,1,0:T(8,128)(2,1)S(1)}, u32[]{:S(2)}, u32[]{:S(2)}) collective-permute-start(bf16[3,64,128]{2,1,0:T(8,128)(2,1)S(1)} %get-tuple-element.194), channel_id=1, source_target_pairs={{0,16},{4,20},{8,24},{12,28},{16,0},{20,4},{24,8},{28,12},{1,17},{... | collective-permute-start | bytes 147464 | tf_op jit(solution)/shard_map/ppermute | solution.py:433
  78.8 5.9 %collective-permute-start.34 = (bf16[3,64,128]{2,1,0:T(8,128)(2,1)S(1)}, bf16[3,64,128]{2,1,0:T(8,128)(2,1)S(1)}, u32[]{:S(2)}, u32[]{:S(2)}) collective-permute-start(bf16[3,64,128]{2,1,0:T(8,128)(2,1)S(1)} %get-tuple-element.194), channel_id=1, source_target_pairs={{0,24},{4,28},{8,16},{12,20},{16,8},{20,12},{24,0},{28,4},{1,25},{... | collective-permute-start | bytes 147464 | tf_op jit(solution)/shard_map/ppermute | solution.py:433
  80.9 7.8 %collective-permute-start.29 = (bf16[12,64,128]{2,1,0:T(8,128)(2,1)S(1)}, bf16[12,64,128]{2,1,0:T(8,128)(2,1)S(1)}, u32[]{:S(2)}, u32[]{:S(2)}) collective-permute-start(bf16[12,64,128]{2,1,0:T(8,128)(2,1)S(1)} %get-tuple-element.193.refs_0_.wire), channel_id=1, source_target_pairs={{0,1},{1,0},{2,3},{3,2},{4,5},{5,4},{6,7},{7,6},{8,9},{9,8},{10,11... | collective-permute-start | bytes 589832 | tf_op jit(solution)/shard_map/ppermute | solution.py:430
  82.2 10.1 %collective-permute-start.30 = (bf16[12,64,128]{2,1,0:T(8,128)(2,1)S(1)}, bf16[12,64,128]{2,1,0:T(8,128)(2,1)S(1)}, u32[]{:S(2)}, u32[]{:S(2)}) collective-permute-start(bf16[12,64,128]{2,1,0:T(8,128)(2,1)S(1)} %get-tuple-element.193.refs_0_.wire), channel_id=1, source_target_pairs={{0,2},{1,3},{2,0},{3,1},{4,6},{5,7},{6,4},{7,5},{8,10},{9,11},{10,... | collective-permute-start | bytes 589832 | tf_op jit(solution)/shard_map/ppermute | solution.py:430
  83.0 9.3 %collective-permute-start.31 = (bf16[12,64,128]{2,1,0:T(8,128)(2,1)S(1)}, bf16[12,64,128]{2,1,0:T(8,128)(2,1)S(1)}, u32[]{:S(2)}, u32[]{:S(2)}) collective-permute-start(bf16[12,64,128]{2,1,0:T(8,128)(2,1)S(1)} %get-tuple-element.193.refs_0_.wire), channel_id=1, source_target_pairs={{0,3},{1,2},{2,1},{3,0},{4,7},{5,6},{6,5},{7,4},{8,11},{9,10},{10,... | collective-permute-start | bytes 589832 | tf_op jit(solution)/shard_map/ppermute | solution.py:430
  84.7 7.5 %collective-permute-start.35 = (bf16[12,64,128]{2,1,0:T(8,128)(2,1)S(1)}, bf16[12,64,128]{2,1,0:T(8,128)(2,1)S(1)}, u32[]{:S(2)}, u32[]{:S(2)}) collective-permute-start(bf16[12,64,128]{2,1,0:T(8,128)(2,1)S(1)} %constant_dynamic-update-slice_fusion.8.refs_4_), channel_id=1, source_target_pairs={{0,4},{4,0},{8,12},{12,8},{16,20},{20,16},{24,28},{28,24},{1,5},{5... | collective-permute-start | bytes 589832 | tf_op jit(solution)/shard_map/ppermute | solution.py:433
  94.9 4.9 %collective-permute-start.37 = (bf16[24,64,128]{2,1,0:T(8,128)(2,1)S(1)}, bf16[24,64,128]{2,1,0:T(8,128)(2,1)S(1)}, u32[]{:S(2)}, u32[]{:S(2)}) collective-permute-start(bf16[24,64,128]{2,1,0:T(8,128)(2,1)S(1)} %get-tuple-element.216), channel_id=1, source_target_pairs={{0,4},{4,0},{8,12},{12,8},{16,20},{20,16},{24,28},{28,24},{1,5},{5... | collective-permute-start | bytes 1179656 | tf_op jit(solution)/shard_map/ppermute | solution.py:433
  95.0 12.0 %collective-permute-start.41 = (bf16[24,64,128]{2,1,0:T(8,128)(2,1)S(1)}, bf16[24,64,128]{2,1,0:T(8,128)(2,1)S(1)}, u32[]{:S(2)}, u32[]{:S(2)}) collective-permute-start(bf16[24,64,128]{2,1,0:T(8,128)(2,1)S(1)} %get-tuple-element.221), channel_id=1, source_target_pairs={{0,1},{1,0},{2,3},{3,2},{4,5},{5,4},{6,7},{7,6},{8,9},{9,8},{10,11... | collective-permute-start | bytes 1179656 | tf_op jit(solution)/shard_map/ppermute | solution.py:430
  95.8 21.0 %collective-permute-start.42 = (bf16[24,64,128]{2,1,0:T(8,128)(2,1)S(1)}, bf16[24,64,128]{2,1,0:T(8,128)(2,1)S(1)}, u32[]{:S(2)}, u32[]{:S(2)}) collective-permute-start(bf16[24,64,128]{2,1,0:T(8,128)(2,1)S(1)} %get-tuple-element.222), channel_id=1, source_target_pairs={{0,2},{1,3},{2,0},{3,1},{4,6},{5,7},{6,4},{7,5},{8,10},{9,11},{10,... | collective-permute-start | bytes 1179656 | tf_op jit(solution)/shard_map/ppermute | solution.py:430
  96.8 20.1 %collective-permute-start.43 = (bf16[24,64,128]{2,1,0:T(8,128)(2,1)S(1)}, bf16[24,64,128]{2,1,0:T(8,128)(2,1)S(1)}, u32[]{:S(2)}, u32[]{:S(2)}) collective-permute-start(bf16[24,64,128]{2,1,0:T(8,128)(2,1)S(1)} %get-tuple-element.223), channel_id=1, source_target_pairs={{0,3},{1,2},{2,1},{3,0},{4,7},{5,6},{6,5},{7,4},{8,11},{9,10},{10,... | collective-permute-start | bytes 1179656 | tf_op jit(solution)/shard_map/ppermute | solution.py:430
  101.2 11.2 %collective-permute-start.38 = (f32[96,128]{1,0:T(8,128)S(1)}, f32[96,128]{1,0:T(8,128)S(1)}, u32[]{:S(2)}, u32[]{:S(2)}) collective-permute-start(f32[96,128]{1,0:T(8,128)S(1)} %add.70), channel_id=1, source_target_pairs={{0,8},{4,12},{8,0},{12,4},{16,24},{20,28},{24,16},{28,20},{1,9},{5... | collective-permute-start | bytes 147464 | tf_op jit(solution)/shard_map/ppermute | solution.py:433
  101.3 11.2 %collective-permute-start.39 = (f32[96,128]{1,0:T(8,128)S(1)}, f32[96,128]{1,0:T(8,128)S(1)}, u32[]{:S(2)}, u32[]{:S(2)}) collective-permute-start(f32[96,128]{1,0:T(8,128)S(1)} %add.70), channel_id=1, source_target_pairs={{0,16},{4,20},{8,24},{12,28},{16,0},{20,4},{24,8},{28,12},{1,17},{... | collective-permute-start | bytes 147464 | tf_op jit(solution)/shard_map/ppermute | solution.py:433
  107.0 8.3 %collective-permute-start.40 = (f32[96,128]{1,0:T(8,128)S(1)}, f32[96,128]{1,0:T(8,128)S(1)}, u32[]{:S(2)}, u32[]{:S(2)}) collective-permute-start(f32[96,128]{1,0:T(8,128)S(1)} %add.70), channel_id=1, source_target_pairs={{0,24},{4,28},{8,16},{12,20},{16,8},{20,12},{24,0},{28,4},{1,25},{... | collective-permute-start | bytes 147464 | tf_op jit(solution)/shard_map/ppermute | solution.py:433
  112.4 4.8 %collective-permute-start.44 = (bf16[6,64,128]{2,1,0:T(8,128)(2,1)S(1)}, bf16[6,64,128]{2,1,0:T(8,128)(2,1)S(1)}, u32[]{:S(2)}, u32[]{:S(2)}) collective-permute-start(bf16[6,64,128]{2,1,0:T(8,128)(2,1)S(1)} %get-tuple-element.224), channel_id=1, source_target_pairs={{0,8},{4,12},{8,0},{12,4},{16,24},{20,28},{24,16},{28,20},{1,9},{5... | collective-permute-start | bytes 294920 | tf_op jit(solution)/shard_map/ppermute | solution.py:433
  112.5 9.9 %collective-permute-start.45 = (bf16[6,64,128]{2,1,0:T(8,128)(2,1)S(1)}, bf16[6,64,128]{2,1,0:T(8,128)(2,1)S(1)}, u32[]{:S(2)}, u32[]{:S(2)}) collective-permute-start(bf16[6,64,128]{2,1,0:T(8,128)(2,1)S(1)} %get-tuple-element.225), channel_id=1, source_target_pairs={{0,16},{4,20},{8,24},{12,28},{16,0},{20,4},{24,8},{28,12},{1,17},{... | collective-permute-start | bytes 294920 | tf_op jit(solution)/shard_map/ppermute | solution.py:433
  115.3 7.1 %collective-permute-start.46 = (bf16[6,64,128]{2,1,0:T(8,128)(2,1)S(1)}, bf16[6,64,128]{2,1,0:T(8,128)(2,1)S(1)}, u32[]{:S(2)}, u32[]{:S(2)}) collective-permute-start(bf16[6,64,128]{2,1,0:T(8,128)(2,1)S(1)} %get-tuple-element.226), channel_id=1, source_target_pairs={{0,24},{4,28},{8,16},{12,20},{16,8},{20,12},{24,0},{28,4},{1,25},{... | collective-permute-start | bytes 294920 | tf_op jit(solution)/shard_map/ppermute | solution.py:433
  122.4 4.1 %collective-permute-start.47 = (f32[96,128]{1,0:T(8,128)S(1)}, f32[96,128]{1,0:T(8,128)S(1)}, u32[]{:S(2)}, u32[]{:S(2)}) collective-permute-start(f32[96,128]{1,0:T(8,128)S(1)} %add_add_fusion.3), channel_id=1, source_target_pairs={{0,1},{1,0},{2,3},{3,2},{4,5},{5,4},{6,7},{7,6},{8,9},{9,8},{10,11... | collective-permute-start | bytes 147464 | tf_op jit(solution)/shard_map/ppermute | solution.py:430
  123.3 4.1 %collective-permute-start.48 = (f32[96,128]{1,0:T(8,128)S(1)}, f32[96,128]{1,0:T(8,128)S(1)}, u32[]{:S(2)}, u32[]{:S(2)}) collective-permute-start(f32[96,128]{1,0:T(8,128)S(1)} %add_add_fusion.3), channel_id=1, source_target_pairs={{0,2},{1,3},{2,0},{3,1},{4,6},{5,7},{6,4},{7,5},{8,10},{9,11},{10,... | collective-permute-start | bytes 147464 | tf_op jit(solution)/shard_map/ppermute | solution.py:430
  124.1 5.0 %collective-permute-start.49 = (f32[96,128]{1,0:T(8,128)S(1)}, f32[96,128]{1,0:T(8,128)S(1)}, u32[]{:S(2)}, u32[]{:S(2)}) collective-permute-start(f32[96,128]{1,0:T(8,128)S(1)} %add_add_fusion.3), channel_id=1, source_target_pairs={{0,3},{1,2},{2,1},{3,0},{4,7},{5,6},{6,5},{7,4},{8,11},{9,10},{10,... | collective-permute-start | bytes 147464 | tf_op jit(solution)/shard_map/ppermute | solution.py:430
  129.1 1.3 collective-permute-start.50
  141.4 6.8 %collective-permute-start.54 = (bf16[3,64,128]{2,1,0:T(8,128)(2,1)S(1)}, bf16[3,64,128]{2,1,0:T(8,128)(2,1)S(1)}, u32[]{:S(2)}, u32[]{:S(2)}) collective-permute-start(bf16[3,64,128]{2,1,0:T(8,128)(2,1)S(1)} %get-tuple-element.242), channel_id=1, source_target_pairs={{0,8},{4,12},{8,0},{12,4},{16,24},{20,28},{24,16},{28,20},{1,9},{5... | collective-permute-start | bytes 147464 | tf_op jit(solution)/shard_map/ppermute | solution.py:433
  143.1 6.5 %collective-permute-start.55 = (bf16[3,64,128]{2,1,0:T(8,128)(2,1)S(1)}, bf16[3,64,128]{2,1,0:T(8,128)(2,1)S(1)}, u32[]{:S(2)}, u32[]{:S(2)}) collective-permute-start(bf16[3,64,128]{2,1,0:T(8,128)(2,1)S(1)} %get-tuple-element.242), channel_id=1, source_target_pairs={{0,16},{4,20},{8,24},{12,28},{16,0},{20,4},{24,8},{28,12},{1,17},{... | collective-permute-start | bytes 147464 | tf_op jit(solution)/shard_map/ppermute | solution.py:433
  144.3 6.0 %collective-permute-start.56 = (bf16[3,64,128]{2,1,0:T(8,128)(2,1)S(1)}, bf16[3,64,128]{2,1,0:T(8,128)(2,1)S(1)}, u32[]{:S(2)}, u32[]{:S(2)}) collective-permute-start(bf16[3,64,128]{2,1,0:T(8,128)(2,1)S(1)} %get-tuple-element.242), channel_id=1, source_target_pairs={{0,24},{4,28},{8,16},{12,20},{16,8},{20,12},{24,0},{28,4},{1,25},{... | collective-permute-start | bytes 147464 | tf_op jit(solution)/shard_map/ppermute | solution.py:433
  145.9 9.1 %collective-permute-start.51 = (bf16[12,64,128]{2,1,0:T(8,128)(2,1)S(1)}, bf16[12,64,128]{2,1,0:T(8,128)(2,1)S(1)}, u32[]{:S(2)}, u32[]{:S(2)}) collective-permute-start(bf16[12,64,128]{2,1,0:T(8,128)(2,1)S(1)} %get-tuple-element.241.refs_0_), channel_id=1, source_target_pairs={{0,1},{1,0},{2,3},{3,2},{4,5},{5,4},{6,7},{7,6},{8,9},{9,8},{10,11... | collective-permute-start | bytes 589832 | tf_op jit(solution)/shard_map/ppermute | solution.py:430
  147.0 10.1 %collective-permute-start.52 = (bf16[12,64,128]{2,1,0:T(8,128)(2,1)S(1)}, bf16[12,64,128]{2,1,0:T(8,128)(2,1)S(1)}, u32[]{:S(2)}, u32[]{:S(2)}) collective-permute-start(bf16[12,64,128]{2,1,0:T(8,128)(2,1)S(1)} %get-tuple-element.241.refs_0_), channel_id=1, source_target_pairs={{0,2},{1,3},{2,0},{3,1},{4,6},{5,7},{6,4},{7,5},{8,10},{9,11},{10,... | collective-permute-start | bytes 589832 | tf_op jit(solution)/shard_map/ppermute | solution.py:430
  148.2 8.9 %collective-permute-start.53 = (bf16[12,64,128]{2,1,0:T(8,128)(2,1)S(1)}, bf16[12,64,128]{2,1,0:T(8,128)(2,1)S(1)}, u32[]{:S(2)}, u32[]{:S(2)}) collective-permute-start(bf16[12,64,128]{2,1,0:T(8,128)(2,1)S(1)} %get-tuple-element.241.refs_0_), channel_id=1, source_target_pairs={{0,3},{1,2},{2,1},{3,0},{4,7},{5,6},{6,5},{7,4},{8,11},{9,10},{10,... | collective-permute-start | bytes 589832 | tf_op jit(solution)/shard_map/ppermute | solution.py:430
  150.3 6.8 %collective-permute-start.57 = (bf16[12,64,128]{2,1,0:T(8,128)(2,1)S(1)}, bf16[12,64,128]{2,1,0:T(8,128)(2,1)S(1)}, u32[]{:S(2)}, u32[]{:S(2)}) collective-permute-start(bf16[12,64,128]{2,1,0:T(8,128)(2,1)S(1)} %constant_dynamic-update-slice_fusion.12.refs_4_), channel_id=1, source_target_pairs={{0,4},{4,0},{8,12},{12,8},{16,20},{20,16},{24,28},{28,24},{1,5},{5... | collective-permute-start | bytes 589832 | tf_op jit(solution)/shard_map/ppermute | solution.py:433
  161.3 4.5 %collective-permute-start.59 = (f32[96,128]{1,0:T(8,128)S(1)}, f32[96,128]{1,0:T(8,128)S(1)}, u32[]{:S(2)}, u32[]{:S(2)}) collective-permute-start(f32[96,128]{1,0:T(8,128)S(1)} %add.77), channel_id=1, source_target_pairs={{0,8},{4,12},{8,0},{12,4},{16,24},{20,28},{24,16},{28,20},{1,9},{5... | collective-permute-start | bytes 147464 | tf_op jit(solution)/shard_map/ppermute | solution.py:433
  162.0 6.8 %collective-permute-start.60 = (f32[96,128]{1,0:T(8,128)S(1)}, f32[96,128]{1,0:T(8,128)S(1)}, u32[]{:S(2)}, u32[]{:S(2)}) collective-permute-start(f32[96,128]{1,0:T(8,128)S(1)} %add.77), channel_id=1, source_target_pairs={{0,16},{4,20},{8,24},{12,28},{16,0},{20,4},{24,8},{28,12},{1,17},{... | collective-permute-start | bytes 147464 | tf_op jit(solution)/shard_map/ppermute | solution.py:433
  164.1 5.9 %collective-permute-start.61 = (f32[96,128]{1,0:T(8,128)S(1)}, f32[96,128]{1,0:T(8,128)S(1)}, u32[]{:S(2)}, u32[]{:S(2)}) collective-permute-start(f32[96,128]{1,0:T(8,128)S(1)} %add.77), channel_id=1, source_target_pairs={{0,24},{4,28},{8,16},{12,20},{16,8},{20,12},{24,0},{28,4},{1,25},{... | collective-permute-start | bytes 147464 | tf_op jit(solution)/shard_map/ppermute | solution.py:433
  170.0 4.2 %collective-permute-start.62 = (f32[96,128]{1,0:T(8,128)S(1)}, f32[96,128]{1,0:T(8,128)S(1)}, u32[]{:S(2)}, u32[]{:S(2)}) collective-permute-start(f32[96,128]{1,0:T(8,128)S(1)} %add_add_fusion.1), channel_id=1, source_target_pairs={{0,1},{1,0},{2,3},{3,2},{4,5},{5,4},{6,7},{7,6},{8,9},{9,8},{10,11... | collective-permute-start | bytes 147464 | tf_op jit(solution)/shard_map/ppermute | solution.py:430
  171.0 4.1 %collective-permute-start.63 = (f32[96,128]{1,0:T(8,128)S(1)}, f32[96,128]{1,0:T(8,128)S(1)}, u32[]{:S(2)}, u32[]{:S(2)}) collective-permute-start(f32[96,128]{1,0:T(8,128)S(1)} %add_add_fusion.1), channel_id=1, source_target_pairs={{0,2},{1,3},{2,0},{3,1},{4,6},{5,7},{6,4},{7,5},{8,10},{9,11},{10,... | collective-permute-start | bytes 147464 | tf_op jit(solution)/shard_map/ppermute | solution.py:430
  172.0 5.0 %collective-permute-start.64 = (f32[96,128]{1,0:T(8,128)S(1)}, f32[96,128]{1,0:T(8,128)S(1)}, u32[]{:S(2)}, u32[]{:S(2)}) collective-permute-start(f32[96,128]{1,0:T(8,128)S(1)} %add_add_fusion.1), channel_id=1, source_target_pairs={{0,3},{1,2},{2,1},{3,0},{4,7},{5,6},{6,5},{7,4},{8,11},{9,10},{10,... | collective-permute-start | bytes 147464 | tf_op jit(solution)/shard_map/ppermute | solution.py:430
  177.0 1.3 collective-permute-start.65
  (13 other events, 148.9 us)

commit v4 on v3

--- a/solution.py
+++ b/solution.py
@@ -22,31 +22,115 @@
     return lax.dot_general(a, b, (((1,), (1,)), ((), ())), precision=precise_mode, preferred_element_type=f32)
 
 
-def two_parts(block):
-    high = block.astype(bf16).astype(f32)
-    return jnp.concatenate([high, block - high], axis=1).astype(bf16)
-
-
-def write_wire(vector, bnd, wire, edge):
-    blocks, kb = wire.shape[0], wire.shape[2] // 2
-    for i in range(blocks):
-        wire[i] = two_parts(vector[:, i * kb : (i + 1) * kb])
-    for q in range(edge.shape[0]):
-        edge[q] = wire[bnd[q]]
-
-
-def fill_halo(wires, edges, pos, halo):
-    n_row = len(wires)
-    lb = wires[0].shape[0]
+TOP = 32000.0
+LOG_STEP = 0.08664339756999316
+
+
+def low_half(shape):
+    return lax.broadcasted_iota(jnp.int32, shape, 1) < shape[1] // 2
+
+
+def swap(tile):
+    return pltpu.roll(tile, tile.shape[1] // 2, 1)
+
+
+def two_blocks(tile):
+    low = low_half(tile.shape)
+    high = tile.astype(bf16).astype(f32)
+    rest = tile - high
+    one = jnp.where(low, high, swap(rest))
+    two = jnp.where(low, swap(high), rest)
+    return one.astype(bf16), two.astype(bf16)
+
+
+def code(tiles):
+    most = jnp.abs(tiles[0])
+    for tile in tiles[1:]:
+        most = jnp.maximum(most, jnp.abs(tile))
+    most = jnp.maximum(jnp.max(most, axis=1, keepdims=True), 1e-30)
+    power = jnp.broadcast_to(jnp.ceil(jnp.log(most) * (1.0 / LOG_STEP)), tiles[0].shape)
+    factor = TOP * jnp.exp(power * -LOG_STEP)
+    return [jnp.floor(tile * factor + 0.5).astype(jnp.int32) for tile in tiles], power.astype(jnp.int32)
+
+
+def step_of(power):
+    return jnp.exp(power.astype(jnp.int32).astype(f32) * LOG_STEP) * (1.0 / TOP)
+
+
+def decode(tile, step):
+    return tile.astype(jnp.int32).astype(f32) * step
+
+
+def edge_tiles(ifr):
+    return ifr // 2 + 1
+
+
+def code_edge(tiles, ifr):
+    low = low_half(tiles[0].shape)
+    tiles = list(tiles)
+    tiles[-1] = jnp.where(low, tiles[-1], 0.0) if ifr % 2 else jnp.zeros_like(tiles[-1])
+    coded, power = code(tiles)
+    coded[-1] = jnp.where(low, coded[-1], power) if ifr % 2 else power
+    return [tile.astype(jnp.int16) for tile in coded]
+
+
+def decode_edge(ref, start, ifr):
+    tiles = [ref[start + t].astype(jnp.int32) for t in range(edge_tiles(ifr))]
+    low = low_half(tiles[-1].shape)
+    power = jnp.where(low, swap(tiles[-1]), tiles[-1]) if ifr % 2 else tiles[-1]
+    step = step_of(power)
+    return [tile.astype(f32) * step for tile in tiles]
+
+
+def write_wire(vector, bnd, wire, edge, place=0):
+    ifr = bnd.shape[0]
+    width = wire.shape[2]
+    count = vector.shape[1] // width
+    base = place * (count + 1)
+    coded, power = code([vector[:, t * width : (t + 1) * width] for t in range(count)])
+    for t in range(count):
+        wire[base + t] = coded[t].astype(jnp.int16)
+    wire[base + count] = power.astype(jnp.int16)
+    low = low_half(power.shape)
+    slots = []
+    for q in range(ifr):
+        tile = wire[base + bnd[q] // 2].astype(jnp.int32)
+        side = jnp.broadcast_to(bnd[q] % 2, tile.shape)
+        slots.append(jnp.where(side == q % 2, tile, swap(tile)))
+    slots.append(power)
+    if len(slots) % 2:
+        slots.append(power)
+    for t in range(edge_tiles(ifr)):
+        edge[place * edge_tiles(ifr) + t] = jnp.where(low, slots[2 * t], slots[2 * t + 1]).astype(jnp.int16)
+
+
+def fill_halo(vector, wires, edges, pos, halo, ifr, place=0, places=1):
+    width = halo.shape[2]
+    count = vector.shape[1] // width
+    lb = 2 * count
+    n_row = len(wires) + 1
+    for t in range(count):
+        one, two = two_blocks(vector[:, t * width : (t + 1) * width])
+        halo[pos[0] * lb + 2 * t] = one
+        halo[pos[0] * lb + 2 * t + 1] = two
     for k, wire in enumerate(wires):
-        start = (pos[0] ^ k) * lb
-        for i in range(lb):
-            halo[start + i] = wire[i]
-    for k, pair in enumerate(edges):
-        for other, (edge, offset, count) in enumerate(pair):
-            start = n_row * lb + (((pos[1] // 2) ^ k) * 2 + ((pos[1] % 2) ^ other)) * count
-            for q in range(count):
-                halo[start + q] = edge[offset + q]
+        start = (pos[0] ^ (k + 1)) * lb
+        base = place * (count + 1)
+        step = step_of(wire[base + count])
+        for t in range(count):
+            one, two = two_blocks(decode(wire[base + t], step))
+            halo[start + 2 * t] = one
+            halo[start + 2 * t + 1] = two
+    tiles = edge_tiles(ifr)
+    for other, edge in enumerate(edges):
+        for k in range(edge.shape[0] // (places * tiles)):
+            start = n_row * lb + (((pos[1] // 2) ^ k) * 2 + ((pos[1] % 2) ^ other)) * ifr
+            found = decode_edge(edge, (k * places + place) * tiles, ifr)
+            for q in range(0, ifr, 2):
+                blocks = two_blocks(found[q // 2])
+                halo[start + q] = blocks[0]
+                if q + 1 < ifr:
+                    halo[start + q + 1] = blocks[1]
 
 
 def write_halves(table, pos, keep, send):
@@ -63,39 +147,43 @@
     table[pl.ds(pl.multiple_of((1 - core) * height, 8), height), :] = other[...]
 
 
-def forward(halo, wire, stored, diagonal, where, out, diag_out):
-    lb, kb = wire.shape[0], wire.shape[2] // 2
+def forward(halo, pos, stored, diagonal, where, out, diag_out):
+    lb, kb = stored.shape[0], stored.shape[1]
+    own = pos[0] * lb
     groups = stored.shape[2] // (2 * kb)
     for i in range(0, lb, 2):
         sums, diags = [], []
         for m in (i, i + 1):
             row = jnp.concatenate([halo[where[m * groups + g]] for g in range(groups)], axis=1)
             sums.append(lax.dot_general(row, stored[m], (((1,), (1,)), ((), ())), preferred_element_type=f32))
-            diags.append(lax.dot_general(wire[m], diagonal[m], (((1,), (1,)), ((), ())), preferred_element_type=f32))
+            diags.append(lax.dot_general(halo[own + m], diagonal[m], (((1,), (1,)), ((), ())), preferred_element_type=f32))
         out[:, i * kb : (i + 2) * kb] = jnp.concatenate(sums, axis=1)
         diag_out[:, i * kb : (i + 2) * kb] = jnp.concatenate(diags, axis=1)
 
 
-def returned(index, own, rows, edge_own, edges, bnd, back):
-    lb, kb = back.shape[0], back.shape[2]
+def returned(index, own, rows, edge_own, edges, bnd, back, target):
+    count, _, width = back.shape
     ifr = bnd.shape[0]
-    for i in range(lb):
-        total = rows[0][index * lb + i].astype(f32)
-        for row in rows[1:]:
-            total = total + row[index * lb + i].astype(f32)
-        back[i] = own[index * lb + i] + (total[:, :kb] + total[:, kb:])
+    tiles = edge_tiles(ifr)
+    n = target.shape[0]
+    steps = [step_of(row[index * (count + 1) + count]) for row in rows]
+    for t in range(count):
+        total = own[index * n : (index + 1) * n, t * width : (t + 1) * width]
+        for row, step in zip(rows, steps):
+            total = total + decode(row[index * (count + 1) + t], step)
+        back[t] = total
+    found = [edge_own[index * tiles + t] for t in range(tiles)]
+    for edge in edges:
+        found = [a + b for a, b in zip(found, decode_edge(edge, index * tiles, ifr))]
+    low = low_half(back.shape[1:])
     for q in range(ifr):
-        total = edges[0][index * ifr + q].astype(f32)
-        for edge in edges[1:]:
-            total = total + edge[index * ifr + q].astype(f32)
-        back[bnd[q]] = back[bnd[q]] + edge_own[index * ifr + q] + (total[:, :kb] + total[:, kb:])
-
-
-def add_returned(back, target):
-    lb, kb = back.shape[0], back.shape[2]
-    for i in range(0, lb, 2):
-        span = slice(i * kb, (i + 2) * kb)
-        target[:, span] = target[:, span] + jnp.concatenate([back[i], back[i + 1]], axis=1)
+        side = jnp.broadcast_to(bnd[q] % 2, low.shape)
+        block = jnp.where(side == q % 2, found[q // 2], swap(found[q // 2]))
+        spot = bnd[q] // 2
+        back[spot] = back[spot] + jnp.where(low == (side == 0), block, 0.0)
+    for t in range(count):
+        span = slice(t * width, (t + 1) * width)
+        target[:, span] = target[:, span] + back[t]
 
 
 def eliminate(table, full):
@@ -183,99 +271,107 @@
             where[i * groups + g] = target
 
 
-def wire_kernel(vector, bnd, wire, edge):
-    write_wire(vector, bnd, wire, edge)
-
-
-def partial_kernel(n_row, n_z, merge, wire, joined, where, pos, *refs):
+def wire_kernel(x, p, bnd, wire, edge):
+    write_wire(x, bnd, wire, edge, 0)
+    write_wire(p, bnd, wire, edge, 1)
+
+
+def partial_kernel(n_row, n_z, merge, ifr, vector, joined, where, pos, *refs):
     refs = list(refs)
     parts = n_row + 2
     earlier = [refs.pop(0) for _ in range(parts)] if merge else []
     outs, acc = refs[:-1], refs[-1]
     own, core_keep, core_send, *row_outs = outs
-    lb, kb = wire.shape[0], wire.shape[2] // 2
-    ifr = core_keep.shape[0] // (n_z * (2 if merge else 1))
+    width = acc.shape[2]
+    count = vector.shape[1] // width
+    lb, kb, n = 2 * count, joined.shape[1], vector.shape[0]
+    tiles = edge_tiles(ifr)
     groups = joined.shape[2] // kb
-    low = lax.broadcasted_iota(jnp.int32, (kb, 2 * kb), 1) < kb
+    low = low_half(acc.shape[1:])
     core = pos[1] % 2
     for source, target in zip(earlier, outs):
         target[pl.ds(0, source.shape[0])] = source[...]
-    row_base = lb if merge else 0
-    edge_base = n_z * ifr if merge else 0
+    own_base = n if merge else 0
+    row_base = count + 1 if merge else 0
+    edge_base = n_z * tiles if merge else 0
     acc[...] = jnp.zeros(acc.shape, f32)
-    for i in range(lb):
-        blocks = jnp.concatenate([joined[i], joined[i]], axis=0)
-        out = jnp.dot(wire[i], blocks, preferred_element_type=f32)
-        for t in range(groups // 2):
-            tile = out[:, 2 * kb * t : 2 * kb * (t + 1)]
-            one = where[i * groups + 2 * t]
-            two = where[i * groups + 2 * t + 1]
-            acc[one] = acc[one] + jnp.where(low, tile, 0.0)
-            acc[two] = acc[two] + jnp.where(low, 0.0, tile)
-
-    def folded(index):
-        block = acc[index]
-        return block[:, :kb] + block[:, kb:]
+    for pair in range(count):
+        both = two_blocks(vector[:, pair * width : (pair + 1) * width])
+        for m in range(2):
+            i = 2 * pair + m
+            blocks = jnp.concatenate([joined[i], joined[i]], axis=0)
+            out = jnp.dot(both[m], blocks, preferred_element_type=f32)
+            for t in range(groups // 2):
+                tile = out[:, width * t : width * (t + 1)]
+                one = where[i * groups + 2 * t]
+                two = where[i * groups + 2 * t + 1]
+                acc[one] = acc[one] + jnp.where(low, tile, 0.0)
+                acc[two] = acc[two] + jnp.where(low, 0.0, tile)
+
+    def folded(one, two):
+        return jnp.where(low, one, two) + swap(jnp.where(low, two, one))
 
     for k in range(n_row):
         start = (pos[0] ^ k) * lb
-        for i in range(lb):
-            if k == 0:
-                own[row_base + i] = folded(start + i)
+        found = [folded(acc[start + 2 * t], acc[start + 2 * t + 1]) for t in range(count)]
+        if k == 0:
+            for t in range(count):
+                own[own_base : own_base + n, t * width : (t + 1) * width] = found[t]
+        else:
+            coded, power = code(found)
+            for t in range(count):
+                row_outs[k - 1][row_base + t] = coded[t].astype(jnp.int16)
+            row_outs[k - 1][row_base + count] = power.astype(jnp.int16)
+    for z in range(n_z):
+        spot = edge_base + z * tiles
+        for side in range(2):
+            start = n_row * lb + (z * 2 + (core if side == 0 else 1 - core)) * ifr
+            found = []
+            for t in range(tiles):
+                one = acc[start + 2 * t] if 2 * t < ifr else jnp.zeros(acc.shape[1:], f32)
+                two = acc[start + 2 * t + 1] if 2 * t + 1 < ifr else jnp.zeros(acc.shape[1:], f32)
+                found.append(folded(one, two))
+            if side == 0:
+                for t in range(tiles):
+                    core_keep[spot + t] = found[t]
             else:
-                row_outs[k - 1][row_base + i] = two_parts(folded(start + i))
-    for z in range(n_z):
-        for q in range(ifr):
-            spot = edge_base + z * ifr + q
-            core_keep[spot] = folded(n_row * lb + (z * 2 + core) * ifr + q)
-            core_send[spot] = two_parts(folded(n_row * lb + (z * 2 + 1 - core) * ifr + q))
-
-
-def pair_kernel(n_z, count, keep, got, pos, own, *outs):
-    ifr, kb = own.shape[0] // count, own.shape[2]
+                for t, tile in enumerate(code_edge(found, ifr)):
+                    core_send[spot + t] = tile
+
+
+def pair_kernel(n_z, count, ifr, keep, got, pos, own, *outs):
+    tiles = edge_tiles(ifr)
     for k in range(n_z):
         z = (pos[1] // 2) ^ k
         for v in range(count):
-            for q in range(ifr):
-                spot = (v * n_z + z) * ifr + q
-                there = got[spot].astype(f32)
-                total = keep[spot] + (there[:, :kb] + there[:, kb:])
-                if k == 0:
-                    own[v * ifr + q] = total
-                else:
-                    outs[k - 1][v * ifr + q] = two_parts(total)
-
-
-def split_halo(refs, n_row, n_z):
-    wires = [refs.pop(0) for _ in range(n_row)]
-    same, other = refs.pop(0), refs.pop(0)
-    ifr = same.shape[0] // n_z
-    return wires, [((same, k * ifr, ifr), (other, k * ifr, ifr)) for k in range(n_z)]
-
-
-def x_image_kernel(n_row, n_z, *refs):
+            spot = (v * n_z + z) * tiles
+            there = decode_edge(got, spot, ifr)
+            total = [keep[spot + t] + there[t] for t in range(tiles)]
+            if k > 0:
+                total = code_edge(total, ifr)
+            target = own if k == 0 else outs[k - 1]
+            for t in range(tiles):
+                target[v * tiles + t] = total[t]
+
+
+def split_halo(refs, n_row):
+    wires = [refs.pop(0) for _ in range(n_row - 1)]
+    return wires, [refs.pop(0), refs.pop(0)]
+
+
+def start_image_kernel(n_row, ifr, *refs):
     refs = list(refs)
-    wires, edges = split_halo(refs, n_row, n_z)
-    stored, diagonal, where, pos, x, p, half, diag, table, halo = refs
+    wires, edges = split_halo(refs, n_row)
+    stored, diagonal, where, pos, x, p, half_x, diag_x, half_p, diag_p, keep, send, halo_x, halo_p, table = refs
     n = x.shape[0]
-    fill_halo(wires, edges, pos, halo)
-    forward(halo, wires[0], stored, diagonal, where, half, diag)
-    half[...] = half[...] + 0.5 * diag[...]
-    table[0:n, :] = nt(x[...], jnp.concatenate([half[...], x[...]], axis=0))
+    for place, (vector, half, diag, halo) in enumerate(((x, half_x, diag_x, halo_x), (p, half_p, diag_p, halo_p))):
+        fill_halo(vector, wires, edges, pos, halo, ifr, place, 2)
+        forward(halo, pos, stored, diagonal, where, half, diag)
+        half[...] = half[...] + 0.5 * diag[...]
+    table[0:n, :] = nt(x[...], jnp.concatenate([half_x[...], x[...]], axis=0))
     table[n : 2 * n, :] = nt(p[...], jnp.concatenate([x[...], p[...]], axis=0))
-
-
-def p_image_kernel(n_row, n_z, *refs):
-    refs = list(refs)
-    wires, edges = split_halo(refs, n_row, n_z)
-    stored, diagonal, where, pos, x, half_x, p, before, half, diag, keep, send, halo, table = refs
-    n = x.shape[0]
-    fill_halo(wires, edges, pos, halo)
-    forward(halo, wires[0], stored, diagonal, where, half, diag)
-    half[...] = half[...] + 0.5 * diag[...]
-    table[0 : 2 * n, :] = before[...]
-    table[2 * n : 3 * n, :] = nt(p[...], jnp.concatenate([half[...], half_x[...]], axis=0))
-    table[2 * n : 3 * n, n:] = table[2 * n : 3 * n, n:] + nt(half[...], x[...])
+    table[2 * n : 3 * n, :] = nt(p[...], jnp.concatenate([half_p[...], half_x[...]], axis=0))
+    table[2 * n : 3 * n, n:] = table[2 * n : 3 * n, n:] + nt(half_p[...], x[...])
     write_halves(table, pos, keep, send)
 
 
@@ -292,9 +388,8 @@
     mine, other, pos, bnd, x, half, diag, precond, table, ax, energy, w, wire, edge, back = refs
     n = x.shape[0]
     read_halves(mine, other, pos, table)
-    returned(0, *back_parts, bnd, back)
     ax[...] = half[...] + 0.5 * diag[...]
-    add_returned(back, ax)
+    returned(0, *back_parts, bnd, back, ax)
     stored, gram = table[0:n, 0:n], table[0:n, n:]
     total = stored + stored.T
     energy[...] = total
@@ -309,13 +404,13 @@
     solved[...] = inverse(stored + stored.T)
 
 
-def update_image_kernel(n_row, n_z, first, *refs):
+def update_image_kernel(n_row, ifr, first, *refs):
     refs = list(refs)
-    wires, edges = split_halo(refs, n_row, n_z)
+    wires, edges = split_halo(refs, n_row)
     stored, diagonal, where, pos, w, x, p, ax, ap, half, diag, keep, send, halo, table = refs
     n = w.shape[0]
-    fill_halo(wires, edges, pos, halo)
-    forward(halo, wires[0], stored, diagonal, where, half, diag)
+    fill_halo(w, wires, edges, pos, halo, ifr)
+    forward(halo, pos, stored, diagonal, where, half, diag)
     half[...] = half[...] + 0.5 * diag[...]
     here = w[...]
     table[0:n, :] = nt(here, jnp.concatenate([half[...], ap[...]], axis=0))
@@ -330,7 +425,7 @@
     refs = list(refs)
     back_parts = take_returned(refs, n_row, n_z)
     mine, other, pos, bnd, start, energy, pap_inverse, x, p, ax, ap, ap_diag, w, aw, aw_diag, precond = refs[:16]
-    x_out, ax_out, w_out, wire, edge, step_x, step_a, small, table, back = refs[16:]
+    x_out, ax_out, w_out, wire, edge, step_x, step_a, small, table, back, ap_full, aw_full = refs[16:]
     n = x.shape[0]
     read_halves(mine, other, pos, table)
     gram = start[0:n, n:]
@@ -339,17 +434,11 @@
     zw, zp, zwt, zpt, cross, inner, wax, scale = coefficients(
         table, 0.5 * (gram + gram.T), px.T, pp, pax, pap_inverse[...], total_rows
     )
-    step_a[...] = nn(zpt, ap[...] + 0.5 * ap_diag[...]) + nn(zwt, aw[...] + 0.5 * aw_diag[...])
-    returned(0, *back_parts, bnd, back)
-    for i in range(0, back.shape[0], 2):
-        pair = jnp.concatenate([back[i], back[i + 1]], axis=1)
-        span = slice(i * back.shape[2], (i + 2) * back.shape[2])
-        step_a[:, span] = step_a[:, span] + nn(zpt, pair)
-    returned(1, *back_parts, bnd, back)
-    for i in range(0, back.shape[0], 2):
-        pair = jnp.concatenate([back[i], back[i + 1]], axis=1)
-        span = slice(i * back.shape[2], (i + 2) * back.shape[2])
-        step_a[:, span] = step_a[:, span] + nn(zwt, pair)
+    ap_full[...] = ap[...] + 0.5 * ap_diag[...]
+    returned(0, *back_parts, bnd, back, ap_full)
+    aw_full[...] = aw[...] + 0.5 * aw_diag[...]
+    returned(1, *back_parts, bnd, back, aw_full)
+    step_a[...] = nn(zpt, ap_full[...]) + nn(zwt, aw_full[...])
     step_x[...] = nn(zwt, w[...]) + nn(zpt, p[...])
     x_out[...] = nn(scale, x[...] + step_x[...])
     ax_out[...] = nn(scale, ax[...] + step_a[...])
@@ -432,19 +521,22 @@
     def sub_send(value, k):
         return lax.ppermute(value, "sub", [(s, s ^ k) for s in range(n_sub)])
 
-    def wire(*shape):
-        return shaped(*shape, n, 2 * kb, dtype=bf16)
+    tiles = lb // 2
+    edges_in = edge_tiles(ifr)
+
+    def coded(count):
+        return shaped(count, n, 2 * kb, dtype=jnp.int16)
 
     def halo_start(own, edge):
         rows_got = [row_send(own, k) for k in range(1, n_row)]
         return rows_got, [sub_send(edge, 2 * k) for k in range(1, n_z)]
 
-    def halo_end(own, edge, rows_got, edges_got):
+    def halo_end(edge, rows_got, edges_got):
         same = jnp.concatenate([edge] + edges_got, axis=0)
-        return [own] + rows_got + [same, sub_send(same, 1)]
+        return rows_got + [same, sub_send(same, 1)]
 
     def halo_of(own, edge):
-        return halo_end(own, edge, *halo_start(own, edge))
+        return halo_end(edge, *halo_start(own, edge))
 
     def groups_of_four(value, size, send):
         base = 1
@@ -467,10 +559,10 @@
 
     def partials(source, earlier=()):
         m = 2 if earlier else 1
-        outs = [shaped(m * lb, n, kb), shaped(m * n_z * ifr, n, kb), wire(m * n_z * ifr)]
-        outs += [wire(m * lb)] * (n_row - 1)
+        outs = [shaped(m * n, rows), shaped(m * n_z * edges_in, n, 2 * kb), coded(m * n_z * edges_in)]
+        outs += [coded(m * (tiles + 1))] * (n_row - 1)
         return run(
-            functools.partial(partial_kernel, n_row, n_z, m > 1),
+            functools.partial(partial_kernel, n_row, n_z, m > 1, ifr),
             "partials",
             outs,
             [source, joined, where, pos] + list(earlier),
@@ -484,9 +576,9 @@
         edge_got = sub_send(edge_send, 1)
         rows_got = [row_send(row_parts[k - 1], k) for k in range(1, n_row)]
         edge_own, *outs = run(
-            functools.partial(pair_kernel, n_z, m),
+            functools.partial(pair_kernel, n_z, m, ifr),
             "pair",
-            [shaped(m * ifr, n, kb)] + [wire(m * ifr)] * (n_z - 1),
+            [shaped(m * edges_in, n, 2 * kb)] + [coded(m * edges_in)] * (n_z - 1),
             [edge_keep, edge_got, pos],
             smem=(2,),
         )
@@ -499,11 +591,10 @@
 
     x, p = modes.T, search.T
     scaling = precond.reshape(1, rows)
-    wire_shapes = [wire(lb), wire(ifr)]
-    x_wire, x_edge = run(wire_kernel, "wire", wire_shapes, [x, bnd], smem=(1,))
-    x_rows, x_edges = halo_start(x_wire, x_edge)
-    in_val, if_val, p, x_edges[0] = after((in_val, if_val, p, x_edges[0]))
-    p_wire, p_edge = run(wire_kernel, "wire", wire_shapes, [p, bnd], smem=(1,))
+    wire_shapes = [coded(tiles + 1), coded(edges_in)]
+    wire, edge = run(wire_kernel, "wire", [coded(2 * (tiles + 1)), coded(2 * edges_in)], [x, p, bnd], smem=(2,))
+    rows_got, edges_got = halo_start(wire, edge)
+    in_val, if_val, edges_got[0] = after((in_val, if_val, edges_got[0]))
     stored, joined, diagonal, where = run(
         functools.partial(prepare_kernel, groups, n_row * lb),
         "prepare",
@@ -517,35 +608,25 @@
         smem=(2, 3, 4, 5),
         smem_outs=(3,),
     )
-    stored, *x_edges = after((stored, *x_edges))
-    x_halo = halo_end(x_wire, x_edge, x_rows, x_edges)
-    x_parts = partials(x_wire)
-    p_wire, p_edge, *x_parts = after((p_wire, p_edge, *x_parts))
-    p_halo = halo_of(p_wire, p_edge)
-    p_parts = partials(p_wire)
+    stored, *edges_got = after((stored, *edges_got))
+    halo = halo_end(edge, rows_got, edges_got)
+    x_parts = partials(x)
+    p_parts = partials(p)
     blocks = [stored, diagonal, where, pos]
     halo_scratch = VMEM((halo_blocks, n, 2 * kb), bf16)
-    back_scratch = VMEM((lb, n, kb), f32)
+    back_scratch = VMEM((tiles, n, 2 * kb), f32)
     whole = shaped(n, rows)
 
-    count = len(x_halo)
-    half_x, diag_x, table = run(
-        functools.partial(x_image_kernel, n_row, n_z),
-        "x_image",
-        [whole, whole, shaped(2 * n, 2 * n)],
-        x_halo + blocks + [x, p],
-        [halo_scratch],
-        smem=(count + 2, count + 3),
-    )
     table_shape = shaped(3 * n, 2 * n)
     halves_shape = [shaped(3 * n // 2, 2 * n)] * 2
     table_scratch = VMEM((3 * n, 2 * n), f32)
-    half_p, diag_p, keep, send = run(
-        functools.partial(p_image_kernel, n_row, n_z),
-        "p_image",
-        [whole, whole] + halves_shape,
-        p_halo + blocks + [x, half_x, p, table],
-        [halo_scratch, table_scratch],
+    count = len(halo)
+    half_x, diag_x, half_p, diag_p, keep, send = run(
+        functools.partial(start_image_kernel, n_row, ifr),
+        "start_image",
+        [whole] * 4 + halves_shape,
+        halo + blocks + [x, p],
+        [halo_scratch, halo_scratch, table_scratch],
         smem=(count + 2, count + 3),
     )
     keep, send, x_parts, p_parts = after((keep, send, x_parts, p_parts))
@@ -561,12 +642,12 @@
     )
     w_halo = halo_of(w_wire, w_edge)
     (pap_inverse,) = run(inverse_kernel, "pap_inverse", [shaped(n, n)], [table])
-    w_parts = partials(w_wire, p_parts)
+    w_parts = partials(w, p_parts)
 
     def update_image(first, halo, w, x, p, ax, ap):
         count = len(halo)
         return run(
-            functools.partial(update_image_kernel, n_row, n_z, first),
+            functools.partial(update_image_kernel, n_row, ifr, first),
             "update_image",
             [whole, whole] + halves_shape,
             halo + blocks + [w, x, p, ax, ap],
@@ -583,7 +664,7 @@
         "move",
         [whole] * 3 + wire_shapes + [whole, whole, shaped(4 * n, n)],
         w_back + halves + [pos, bnd, table, energy, pap_inverse, x, p, ax, half_p, diag_p, w, half_w, diag_w, scaling],
-        [table_scratch, back_scratch],
+        [table_scratch, back_scratch, VMEM((n, rows), f32), VMEM((n, rows), f32)],
         smem=(count + 2, count + 3),
     )
     w_halo = halo_of(w_wire, w_edge)

time: 189 us -> 187 us (0.989)
  starting transfers between devices: 76.4 us -> 65.8 us
  local copies, waits for them, and re-layouts: 5.07 us -> 10.7 us
    ppermute x39 -> x35, starting transfers between devices: 44.7 us -> 37.5 us  [sub_send(): return lax.ppermute(value, 'sub', [(s, s ^ k) for s in range(n_sub)])]
    unnamed x34 -> x35, local copies, waits for them, and re-layouts: 1.73 us -> 5.75 us
    ppermute x27 -> x24, starting transfers between devices: 31.7 us -> 28.3 us  [row_send(): return lax.ppermute(value, 'row', [(r, r ^ k) for r in range(n_row)])]
    ppermute x39 -> x35, waiting for transfers between devices: 21.5 us -> 23.3 us  [sub_send(): return lax.ppermute(value, 'sub', [(s, s ^ k) for s in range(n_sub)])]
    pallas_call x17 -> x15, Pallas kernels: 58 us -> 59 us  [run(): pl.pallas_call(kernel, name=name, out_shape=outs, in_specs=in_specs, out_...]
    ppermute x27 -> x24, waiting for transfers between devices: 26.4 us -> 26.1 us  [row_send(): return lax.ppermute(value, 'row', [(r, r ^ k) for r in range(n_row)])]
  transfers between devices with their start and end apart: 66 -> 59, of which waited for: 30 -> 32; matrix products, arithmetic and copies ran while one was open for 2% -> 2% of each run, Pallas kernels for 12% -> 10%
where the time goes in v4:
time: 187 us; the launch traced here: 186 us
  starting transfers between devices  65.8 us (35%)
  Pallas kernels  59 us (32%)
  waiting for transfers between devices  49.4 us (26%)
  local copies, waits for them, and re-layouts  10.7 us (6%)
    pallas_call x15, Pallas kernels, run(): pl.pallas_call(kernel, name=name, out_shape=outs, in_specs=in_specs, out_...  59 us
    ppermute x35, starting transfers between devices, sub_send(): return lax.ppermute(value, 'sub', [(s, s ^ k) for s in range(n_sub)])  37.5 us
    ppermute x24, starting transfers between devices, row_send(): return lax.ppermute(value, 'row', [(r, r ^ k) for r in range(n_row)])  28.3 us
    ppermute x24, waiting for transfers between devices, row_send(): return lax.ppermute(value, 'row', [(r, r ^ k) for r in range(n_row)])  26.1 us
    ppermute x35, waiting for transfers between devices, sub_send(): return lax.ppermute(value, 'sub', [(s, s ^ k) for s in range(n_sub)])  23.3 us
    unnamed x35, local copies, waits for them, and re-layouts  5.75 us
    optimization_barrier x1, local copies, waits for them, and re-layouts, local(): in_val, if_val, edges_got[0] = after((in_val, if_val, edges_got[0]))  4.07 us
  transfers between devices with their start and end apart: 59, of which 32 were waited for; matrix products, arithmetic and copies ran while one was open for 2% of the time, Pallas kernels for 10%

profile of v4, /device:TPU:0, one launch (start us, length us, event | category | flops | bytes accessed | tf_op | source)
XLA Modules:
  0.0 186.2 jit_solution(6341369641937010956)
XLA Ops:
  3.2 1.5 wire.1
  4.6 3.0 %collective-permute-start.3 = (s16[4,64,128]{2,1,0:T(8,128)(2,1)S(1)}, s16[4,64,128]{2,1,0:T(8,128)(2,1)}, u32[]{:S(2)}, u32[]{:S(2)}) collective-permute-start(s16[4,64,128]{2,1,0:T(8,128)(2,1)S(1)} %get-tuple-element.118), channel_id=1, source_target_pairs={{0,8},{4,12},{8,0},{12,4},{16,24},{20,28},{24,16},{28,20},{1,9},{5... | collective-permute-start | bytes 196616 | tf_op jit(solution)/shard_map/ppermute | solution.py:522
  7.6 2.6 %collective-permute-start.4 = (s16[4,64,128]{2,1,0:T(8,128)(2,1)S(1)}, s16[4,64,128]{2,1,0:T(8,128)(2,1)}, u32[]{:S(2)}, u32[]{:S(2)}) collective-permute-start(s16[4,64,128]{2,1,0:T(8,128)(2,1)S(1)} %get-tuple-element.118), channel_id=1, source_target_pairs={{0,16},{4,20},{8,24},{12,28},{16,0},{20,4},{24,8},{28,12},{1,17},{... | collective-permute-start | bytes 196616 | tf_op jit(solution)/shard_map/ppermute | solution.py:522
  10.3 4.1 %copy.12 = bf16[1,1,96,64,64]{4,3,2,1,0:T(8,128)(2,1)} copy(bf16[1,1,96,64,64]{2,4,3,1,0:T(8,128)(2,1)} %param.15) | data formatting | bytes 1572864 | tf_op jit(solution)/shard_map/optimization_barrier | solution.py:597
  14.4 1.5 copy-done.2
  15.8 2.2 %prepare.1 = (bf16[12,64,1024]{2,1,0:T(8,128)(2,1)S(1)}, bf16[12,64,512]{2,1,0:T(8,128)(2,1)S(1)}, bf16[12,64,128]{2,1,0:T(8,128)(2,1)S(1)}, s32[96]{0:T(128)S(1)}) custom-call(bf16[96,64,64]{2,1,0:T(8,128)(2,1)S(1)} %bitcast.19, bf16[12,64,64]{2,1,0:T(8,128)(2,1)S(1)} %bitcast.25, s32[96]{0:T(128)S(1)} %bitcast.29, s32[96]{0:T(128)S(1)} %bitcast.30, ...), custom_call_target="tpu_custom_call" | custom-call | flops 1000000 | bytes 3441888 | tf_op jit(solution)/shard_map/prepare/pallas_call | solution.py:488
  20.7 1.8 collective-permute-start
  22.5 1.5 collective-permute-start.1
  24.3 2.2 %partials.3 = (f32[64,768]{1,0:T(8,128)S(1)}, f32[8,64,128]{2,1,0:T(8,128)S(1)}, s16[8,64,128]{2,1,0:T(8,128)(2,1)S(1)}, s16[7,64,128]{2,1,0:T(8,128)(2,1)S(1)},...) custom-call(f32[64,768]{1,0:T(8,128)S(1)} %bitcast.14, ...), custom_call_target="tpu_custom_call" | custom-call | flops 1000000 | bytes 1917320 | tf_op jit(solution)/shard_map/partials/pallas_call | solution.py:488
  26.5 2.2 %partials.4 = (f32[64,768]{1,0:T(8,128)S(1)}, f32[8,64,128]{2,1,0:T(8,128)S(1)}, s16[8,64,128]{2,1,0:T(8,128)(2,1)S(1)}, s16[7,64,128]{2,1,0:T(8,128)(2,1)S(1)},...) custom-call(f32[64,768]{1,0:T(8,128)S(1)} %bitcast.21, ...), custom_call_target="tpu_custom_call" | custom-call | flops 1000000 | bytes 1917320 | tf_op jit(solution)/shard_map/partials/pallas_call | solution.py:488
  29.5 5.9 %collective-permute-done.1.refs_1_ = s16[14,64,128]{2,1,0:T(8,128)(2,1)} collective-permute-done((s16[14,64,128]{2,1,0:T(8,128)(2,1)}, s16[14,64,128]{2,1,0:T(8,128)(2,1)}, u32[]{:S(2)}, u32[]{:S(2)}) %collective-permute-start.1) | collective-permute-done | bytes 229408 | tf_op jit(solution)/shard_map/ppermute | solution.py:519
  35.4 4.9 %start_image.1 = (f32[64,768]{1,0:T(8,128)S(1)}, f32[64,768]{1,0:T(8,128)S(1)}, f32[64,768]{1,0:T(8,128)S(1)}, f32[64,768]{1,0:T(8,128)S(1)}, f32[96,128]{1,0:T(8,128)S(1)}, /*index=5*/f32[96,128]{1,0:T(8,128)S(1)}) custom-call(s16[14,64,128]{2,1,0:T(8,128)(2,1)} %collective-permute-done.refs_0_, s16[14,64,128]{2,1,0:T(8,128)(2,1)} %collective-permute-done.1.refs_1_, ...), custom_call_target="tpu_custom_call" | custom-call | flops 1000000 | bytes 4260232 | tf_op jit(solution)/shard_map/start_image/pallas_call | solution.py:488
  40.4 1.3 collective-permute-start.12
  41.9 1.1 collective-permute-done.7
  43.8 2.9 %collective-permute-start.10 = (f32[96,128]{1,0:T(8,128)S(1)}, f32[96,128]{1,0:T(8,128)S(1)}, u32[]{:S(2)}, u32[]{:S(2)}) collective-permute-start(f32[96,128]{1,0:T(8,128)S(1)} %add.63), channel_id=1, source_target_pairs={{0,16},{4,20},{8,24},{12,28},{16,0},{20,4},{24,8},{28,12},{1,17},{... | collective-permute-start | bytes 147464 | tf_op jit(solution)/shard_map/ppermute | solution.py:522
  46.6 1.5 collective-permute-start.11
  49.4 1.4 collective-permute-start.14
  50.9 1.5 collective-permute-start.15
  52.8 2.4 %collective-permute-start.16 = (s16[2,64,128]{2,1,0:T(8,128)(2,1)S(1)}, s16[2,64,128]{2,1,0:T(8,128)(2,1)S(1)}, u32[]{:S(2)}, u32[]{:S(2)}) collective-permute-start(s16[2,64,128]{2,1,0:T(8,128)(2,1)S(1)} %get-tuple-element.157), channel_id=1, source_target_pairs={{0,16},{4,20},{8,24},{12,28},{16,0},{20,4},{24,8},{28,12},{1,17},{... | collective-permute-start | bytes 98312 | tf_op jit(solution)/shard_map/ppermute | solution.py:522
  55.9 1.7 collective-permute-done.16.refs_6_
  57.6 3.3 %collective-permute-done.17.refs_7_ = s16[2,64,128]{2,1,0:T(8,128)(2,1)S(1)} collective-permute-done((s16[2,64,128]{2,1,0:T(8,128)(2,1)S(1)}, s16[2,64,128]{2,1,0:T(8,128)(2,1)S(1)}, u32[]{:S(2)}, u32[]{:S(2)}) %collective-permute-start.17) | collective-permute-done | bytes 32800 | tf_op jit(solution)/shard_map/ppermute | solution.py:522
  61.7 1.5 collective-permute-start.19
  63.2 1.2 collective-permute-start.20
  65.8 2.4 %collective-permute-done.20 = f32[96,128]{1,0:T(8,128)S(1)} collective-permute-done((f32[96,128]{1,0:T(8,128)S(1)}, f32[96,128]{1,0:T(8,128)S(1)}, u32[]{:S(2)}, u32[]{:S(2)}) %collective-permute-start.20) | collective-permute-done | bytes 49184 | tf_op jit(solution)/shard_map/ppermute | solution.py:519
  68.3 1.2 collective-permute-done.21.refs_9_
  69.5 5.4 %update.1 = (f32[192,128]{1,0:T(8,128)S(1)}, f32[64,768]{1,0:T(8,128)S(1)}, f32[64,64]{1,0:T(8,128)S(1)}, f32[64,768]{1,0:T(8,128)S(1)}, s16[7,64,128]{2,1,0:T(8,128)(2,1)S(1)}, /*index=5*/s16[2,64,128]{2,1,0:T(8,128)(2,1)S(1)}) custom-call(f32[64,768]{1,0:T(8,128)S(1)} %get-tuple-element.144.refs_0_, ...), custom_call_target="tpu_custom_call" | custom-call | flops 1000000 | bytes 2051092 | tf_op jit(solution)/shard_map/update/pallas_call | solution.py:488
  75.9 3.5 %collective-permute-start.27 = (s16[2,64,128]{2,1,0:T(8,128)(2,1)S(1)}, s16[2,64,128]{2,1,0:T(8,128)(2,1)S(1)}, u32[]{:S(2)}, u32[]{:S(2)}) collective-permute-start(s16[2,64,128]{2,1,0:T(8,128)(2,1)S(1)} %get-tuple-element.170), channel_id=1, source_target_pairs={{0,24},{4,28},{8,16},{12,20},{16,8},{20,12},{24,0},{28,4},{1,25},{... | collective-permute-start | bytes 98312 | tf_op jit(solution)/shard_map/ppermute | solution.py:522
  79.9 1.7 collective-permute-done.27
  83.4 1.8 collective-permute-start.24
  85.2 2.4 %partials.5 = (f32[128,768]{1,0:T(8,128)S(1)}, f32[16,64,128]{2,1,0:T(8,128)S(1)}, s16[16,64,128]{2,1,0:T(8,128)(2,1)S(1)}, s16[14,64,128]{2,1,0:T(8,128)(2,1)S(...) custom-call(f32[64,768]{1,0:T(8,128)S(1)} %get-tuple-element.171.refs_9_.vector.refs_20_, ...), custom_call_target="tpu_custom_call" | custom-call | flops 1000000 | bytes 3785096 | tf_op jit(solution)/shard_map/partials/pallas_call | solution.py:488
  87.7 2.6 %collective-permute-done.23.refs_1_ = s16[7,64,128]{2,1,0:T(8,128)(2,1)S(1)} collective-permute-done((s16[7,64,128]{2,1,0:T(8,128)(2,1)S(1)}, s16[7,64,128]{2,1,0:T(8,128)(2,1)S(1)}, u32[]{:S(2)}, u32[]{:S(2)}) %collective-permute-start.23) | collective-permute-done | bytes 114720 | tf_op jit(solution)/shard_map/ppermute | solution.py:519
  90.3 3.3 %update_image.2 = (f32[64,768]{1,0:T(8,128)S(1)}, f32[64,768]{1,0:T(8,128)S(1)}, f32[96,128]{1,0:T(8,128)S(1)}, f32[96,128]{1,0:T(8,128)S(1)}) custom-call(s16[7,64,128]{2,1,0:T(8,128)(2,1)S(1)} %collective-permute-done.22.refs_0_, s16[7,64,128]{2,1,0:T(8,128)(2,1)S(1)} %collective-permute-done.23.refs_1_, ...), custom_call_target="tpu_custom_call" | custom-call | flops 1000000 | bytes 3850632 | tf_op jit(solution)/shard_map/update_image/pallas_call | solution.py:488
  93.6 1.2 collective-permute-start.34
  95.0 1.1 collective-permute-done.29
  96.1 1.0 pair.3
  97.5 3.7 %collective-permute-start.32 = (f32[96,128]{1,0:T(8,128)S(1)}, f32[96,128]{1,0:T(8,128)S(1)}, u32[]{:S(2)}, u32[]{:S(2)}) collective-permute-start(f32[96,128]{1,0:T(8,128)S(1)} %add.70), channel_id=1, source_target_pairs={{0,16},{4,20},{8,24},{12,28},{16,0},{20,4},{24,8},{28,12},{1,17},{... | collective-permute-start | bytes 147464 | tf_op jit(solution)/shard_map/ppermute | solution.py:522
  101.5 3.8 %pap_inverse.1.refs_14_ = f32[64,64]{1,0:T(8,128)S(1)} custom-call(f32[192,128]{1,0:T(8,128)S(1)} %get-tuple-element.203.table.refs_12_), custom_call_target="tpu_custom_call" | custom-call | flops 1000000 | bytes 114688 | tf_op jit(solution)/shard_map/pap_inverse/pallas_call | solution.py:488
  106.0 1.7 collective-permute-start.36
  107.7 3.6 %collective-permute-start.38 = (s16[4,64,128]{2,1,0:T(8,128)(2,1)S(1)}, s16[4,64,128]{2,1,0:T(8,128)(2,1)S(1)}, u32[]{:S(2)}, u32[]{:S(2)}) collective-permute-start(s16[4,64,128]{2,1,0:T(8,128)(2,1)S(1)} %get-tuple-element.201), channel_id=1, source_target_pairs={{0,16},{4,20},{8,24},{12,28},{16,0},{20,4},{24,8},{28,12},{1,17},{... | collective-permute-start | bytes 196616 | tf_op jit(solution)/shard_map/ppermute | solution.py:522
  112.2 5.0 %collective-permute-done.35.refs_2_ = s16[14,64,128]{2,1,0:T(8,128)(2,1)S(1)} collective-permute-done((s16[14,64,128]{2,1,0:T(8,128)(2,1)S(1)}, s16[14,64,128]{2,1,0:T(8,128)(2,1)S(1)}, u32[]{:S(2)}, u32[]{:S(2)}) %collective-permute-start.35) | collective-permute-done | bytes 229408 | tf_op jit(solution)/shard_map/ppermute | solution.py:519
  117.5 1.5 collective-permute-start.40
  119.5 1.5 collective-permute-start.42
  121.6 1.5 collective-permute-done.41
  123.0 1.4 collective-permute-done.42
  124.5 1.2 collective-permute-done.43.refs_9_
  125.8 11.0 %move.1 = (f32[64,768]{1,0:T(8,128)S(1)}, f32[64,768]{1,0:T(8,128)S(1)}, f32[64,768]{1,0:T(8,128)S(1)}, s16[7,64,128]{2,1,0:T(8,128)(2,1)S(1)}, s16[2,64,128]{2,...) custom-call(f32[128,768]{1,0:T(8,128)S(1)} %get-tuple-element.188.refs_0_, ...), custom_call_target="tpu_custom_call" | custom-call | flops 1000000 | bytes 4410388 | tf_op jit(solution)/shard_map/move/pallas_call | solution.py:488
  136.9 3.5 %collective-permute-start.48 = (s16[2,64,128]{2,1,0:T(8,128)(2,1)S(1)}, s16[2,64,128]{2,1,0:T(8,128)(2,1)S(1)}, u32[]{:S(2)}, u32[]{:S(2)}) collective-permute-start(s16[2,64,128]{2,1,0:T(8,128)(2,1)S(1)} %get-tuple-element.218), channel_id=1, source_target_pairs={{0,16},{4,20},{8,24},{12,28},{16,0},{20,4},{24,8},{28,12},{1,17},{... | collective-permute-start | bytes 98312 | tf_op jit(solution)/shard_map/ppermute | solution.py:522
  141.3 1.2 collective-permute-done.48
  142.5 3.6 %collective-permute-done.49 = s16[2,64,128]{2,1,0:T(8,128)(2,1)S(1)} collective-permute-done((s16[2,64,128]{2,1,0:T(8,128)(2,1)S(1)}, s16[2,64,128]{2,1,0:T(8,128)(2,1)S(1)}, u32[]{:S(2)}, u32[]{:S(2)}) %collective-permute-start.49) | collective-permute-done | bytes 32800 | tf_op jit(solution)/shard_map/ppermute | solution.py:522
  147.0 1.5 collective-permute-start.45
  148.5 1.2 collective-permute-start.46
  149.7 4.6 %settle.1 = (f32[64,768]{1,0:T(8,128)S(1)}, f32[64,768]{1,0:T(8,128)S(1)}, f32[192,64]{1,0:T(8,128)S(1)}) custom-call(f32[256,64]{1,0:T(8,128)S(1)} %get-tuple-element.221.small, f32[64,768]{1,0:T(8,128)S(1)} %get-tuple-element.222.step_x, f32[64,768]{1,0:T(8,128)S(1)} %get-tuple-element.223.step_a), custom_call_target="tpu_custom_call" | custom-call | flops 1000000 | bytes 901120 | tf_op jit(solution)/shard_map/settle/pallas_call | solution.py:488
  154.7 3.5 %update_image.3 = (f32[64,768]{1,0:T(8,128)}, f32[64,768]{1,0:T(8,128)}, f32[96,128]{1,0:T(8,128)S(1)}, f32[96,128]{1,0:T(8,128)S(1)}) custom-call(s16[7,64,128]{2,1,0:T(8,128)(2,1)S(1)} %collective-permute-done.44.refs_0_, s16[7,64,128]{2,1,0:T(8,128)(2,1)S(1)} %collective-permute-done.45.refs_1_, s16[7,64,128]{2,1,0:T(8,128)(2,1)S(1)} %collective-permute-done.46.refs_2_, ...), custom_call_target="tpu_custom_call" | custom-call | flops 1000000 | bytes 3850632 | tf_op jit(solution)/shard_map/update_image/pallas_call | solution.py:488
  158.2 1.2 collective-permute-done.51
  159.5 1.9 %collective-permute-start.53 = (f32[96,128]{1,0:T(8,128)S(1)}, f32[96,128]{1,0:T(8,128)S(1)}, u32[]{:S(2)}, u32[]{:S(2)}) collective-permute-start(f32[96,128]{1,0:T(8,128)S(1)} %add.77), channel_id=1, source_target_pairs={{0,16},{4,20},{8,24},{12,28},{16,0},{20,4},{24,8},{28,12},{1,17},{... | collective-permute-start | bytes 147464 | tf_op jit(solution)/shard_map/ppermute | solution.py:522
  161.3 2.5 %collective-permute-start.54 = (f32[96,128]{1,0:T(8,128)S(1)}, f32[96,128]{1,0:T(8,128)S(1)}, u32[]{:S(2)}, u32[]{:S(2)}) collective-permute-start(f32[96,128]{1,0:T(8,128)S(1)} %add.77), channel_id=1, source_target_pairs={{0,24},{4,28},{8,16},{12,20},{16,8},{20,12},{24,0},{28,4},{1,25},{... | collective-permute-start | bytes 147464 | tf_op jit(solution)/shard_map/ppermute | solution.py:522
  164.2 1.1 collective-permute-done.53
  165.2 2.1 %collective-permute-done.54 = f32[96,128]{1,0:T(8,128)S(1)} collective-permute-done((f32[96,128]{1,0:T(8,128)S(1)}, f32[96,128]{1,0:T(8,128)S(1)}, u32[]{:S(2)}, u32[]{:S(2)}) %collective-permute-start.54) | collective-permute-done | bytes 49184 | tf_op jit(solution)/shard_map/ppermute | solution.py:522
  168.1 1.5 collective-permute-start.56
  169.6 1.2 collective-permute-start.57
  171.5 1.1 collective-permute-done.56
  172.6 2.0 %collective-permute-done.57 = f32[96,128]{1,0:T(8,128)S(1)} collective-permute-done((f32[96,128]{1,0:T(8,128)S(1)}, f32[96,128]{1,0:T(8,128)S(1)}, u32[]{:S(2)}, u32[]{:S(2)}) %collective-permute-start.57) | collective-permute-done | bytes 49184 | tf_op jit(solution)/shard_map/ppermute | solution.py:519
  174.7 1.2 collective-permute-done.58.other
  175.9 10.3 %finish.1 = (f32[64,768]{1,0:T(8,128)}, f32[64,768]{1,0:T(8,128)}) custom-call(f32[96,128]{1,0:T(8,128)S(1)} %add_add_fusion.mine, f32[96,128]{1,0:T(8,128)S(1)} %collective-permute-done.58.other, s32[2]{0:T(128)S(1)} %pad_add_fusion.refs_8_.pos.refs_10_, f32[192,64]{1,0:T(8,128)S(1)} %get-tuple-element.229.state, ...), custom_call_target="tpu_custom_call" | custom-call | flops 1000000 | bytes 1130504 | tf_op jit(solution)/shard_map/finish/pallas_call | solution.py:488
  (119 shorter events, 23.4 us)
Async XLA Ops:
  3.1 11.2 %copy-start.9 = (s32[1,1,96]{2,1,0:T(1,128)S(1)}, s32[1,1,96]{2,1,0:T(1,128)}, u32[]{:S(2)}) copy-start(s32[1,1,96]{2,1,0:T(1,128)} %param.14) | copy-start | bytes 1156
  3.2 11.2 %copy-start.10 = (s32[1,1,12]{2,1,0:T(1,128)S(1)}, s32[1,1,12]{2,1,0:T(1,128)}, u32[]{:S(2)}) copy-start(s32[1,1,12]{2,1,0:T(1,128)} %param.17) | copy-start | bytes 148
  3.2 11.2 %copy-start.11 = (s32[1,1,12]{2,1,0:T(1,128)S(1)}, s32[1,1,12]{2,1,0:T(1,128)}, u32[]{:S(2)}) copy-start(s32[1,1,12]{2,1,0:T(1,128)} %param.18) | copy-start | bytes 148
  4.6 5.6 %collective-permute-start.3 = (s16[4,64,128]{2,1,0:T(8,128)(2,1)S(1)}, s16[4,64,128]{2,1,0:T(8,128)(2,1)}, u32[]{:S(2)}, u32[]{:S(2)}) collective-permute-start(s16[4,64,128]{2,1,0:T(8,128)(2,1)S(1)} %get-tuple-element.118), channel_id=1, source_target_pairs={{0,8},{4,12},{8,0},{12,4},{16,24},{20,28},{24,16},{28,20},{1,9},{5... | collective-permute-start | bytes 196616 | tf_op jit(solution)/shard_map/ppermute | solution.py:522
  7.6 10.4 %collective-permute-start.4 = (s16[4,64,128]{2,1,0:T(8,128)(2,1)S(1)}, s16[4,64,128]{2,1,0:T(8,128)(2,1)}, u32[]{:S(2)}, u32[]{:S(2)}) collective-permute-start(s16[4,64,128]{2,1,0:T(8,128)(2,1)S(1)} %get-tuple-element.118), channel_id=1, source_target_pairs={{0,16},{4,20},{8,24},{12,28},{16,0},{20,4},{24,8},{28,12},{1,17},{... | collective-permute-start | bytes 196616 | tf_op jit(solution)/shard_map/ppermute | solution.py:522
  10.2 7.8 %collective-permute-start.5 = (s16[4,64,128]{2,1,0:T(8,128)(2,1)S(1)}, s16[4,64,128]{2,1,0:T(8,128)(2,1)}, u32[]{:S(2)}, u32[]{:S(2)}) collective-permute-start(s16[4,64,128]{2,1,0:T(8,128)(2,1)S(1)} %get-tuple-element.118), channel_id=1, source_target_pairs={{0,24},{4,28},{8,16},{12,20},{16,8},{20,12},{24,0},{28,4},{1,25},{... | collective-permute-start | bytes 196616 | tf_op jit(solution)/shard_map/ppermute | solution.py:522
  20.6 14.8 %collective-permute-start.6 = (s16[16,64,128]{2,1,0:T(8,128)(2,1)S(1)}, s16[16,64,128]{2,1,0:T(8,128)(2,1)S(1)}, u32[]{:S(2)}, u32[]{:S(2)}) collective-permute-start(s16[16,64,128]{2,1,0:T(8,128)(2,1)S(1)} %constant_dynamic-update-slice_fusion.refs_3_), channel_id=1, source_target_pairs={{0,4},{4,0},{8,12},{12,8},{16,20},{20,16},{24,28},{28,24},{1,5},{5... | collective-permute-start | bytes 786440 | tf_op jit(solution)/shard_map/ppermute | solution.py:522
  20.7 8.8 %collective-permute-start = (s16[14,64,128]{2,1,0:T(8,128)(2,1)}, s16[14,64,128]{2,1,0:T(8,128)(2,1)}, u32[]{:S(2)}, u32[]{:S(2)}) collective-permute-start(s16[14,64,128]{2,1,0:T(8,128)(2,1)} %get-tuple-element.117), channel_id=1, source_target_pairs={{0,1},{1,0},{2,3},{3,2},{4,5},{5,4},{6,7},{7,6},{8,9},{9,8},{10,11... | collective-permute-start | bytes 688136 | tf_op jit(solution)/shard_map/ppermute | solution.py:519
  22.5 12.9 %collective-permute-start.1 = (s16[14,64,128]{2,1,0:T(8,128)(2,1)}, s16[14,64,128]{2,1,0:T(8,128)(2,1)}, u32[]{:S(2)}, u32[]{:S(2)}) collective-permute-start(s16[14,64,128]{2,1,0:T(8,128)(2,1)} %get-tuple-element.117), channel_id=1, source_target_pairs={{0,2},{1,3},{2,0},{3,1},{4,6},{5,7},{6,4},{7,5},{8,10},{9,11},{10,... | collective-permute-start | bytes 688136 | tf_op jit(solution)/shard_map/ppermute | solution.py:519
  24.0 11.4 %collective-permute-start.2 = (s16[14,64,128]{2,1,0:T(8,128)(2,1)}, s16[14,64,128]{2,1,0:T(8,128)(2,1)}, u32[]{:S(2)}, u32[]{:S(2)}) collective-permute-start(s16[14,64,128]{2,1,0:T(8,128)(2,1)} %get-tuple-element.117), channel_id=1, source_target_pairs={{0,3},{1,2},{2,1},{3,0},{4,7},{5,6},{6,5},{7,4},{8,11},{9,10},{10,... | collective-permute-start | bytes 688136 | tf_op jit(solution)/shard_map/ppermute | solution.py:519
  35.4 32.9 %copy-start.12 = (f32[768]{0:T(1024)S(1)}, f32[768]{0:T(1024)}, u32[]{:S(2)}) copy-start(f32[768]{0:T(1024)} %param.12) | copy-start | bytes 9220
  35.4 34.2 %copy-start.7 = (s32[1,1,3]{2,1,0:T(1,128)S(1)}, s32[1,1,3]{2,1,0:T(1,128)}, u32[]{:S(2)}) copy-start(s32[1,1,3]{2,1,0:T(1,128)} %param.16) | copy-start | bytes 40
  40.3 2.6 %collective-permute-start.8 = (s16[8,64,128]{2,1,0:T(8,128)(2,1)S(1)}, s16[8,64,128]{2,1,0:T(8,128)(2,1)S(1)}, u32[]{:S(2)}, u32[]{:S(2)}) collective-permute-start(s16[8,64,128]{2,1,0:T(8,128)(2,1)S(1)} %get-tuple-element.148), channel_id=1, source_target_pairs={{0,4},{4,0},{8,12},{12,8},{16,20},{20,16},{24,28},{28,24},{1,5},{5... | collective-permute-start | bytes 393224 | tf_op jit(solution)/shard_map/ppermute | solution.py:522
  40.4 9.0 %collective-permute-start.12 = (s16[7,64,128]{2,1,0:T(8,128)(2,1)S(1)}, s16[7,64,128]{2,1,0:T(8,128)(2,1)S(1)}, u32[]{:S(2)}, u32[]{:S(2)}) collective-permute-start(s16[7,64,128]{2,1,0:T(8,128)(2,1)S(1)} %get-tuple-element.153), channel_id=1, source_target_pairs={{0,1},{1,0},{2,3},{3,2},{4,5},{5,4},{6,7},{7,6},{8,9},{9,8},{10,11... | collective-permute-start | bytes 344072 | tf_op jit(solution)/shard_map/ppermute | solution.py:519
  41.7 1.2 collective-permute-start.7
  43.8 7.1 %collective-permute-start.10 = (f32[96,128]{1,0:T(8,128)S(1)}, f32[96,128]{1,0:T(8,128)S(1)}, u32[]{:S(2)}, u32[]{:S(2)}) collective-permute-start(f32[96,128]{1,0:T(8,128)S(1)} %add.63), channel_id=1, source_target_pairs={{0,16},{4,20},{8,24},{12,28},{16,0},{20,4},{24,8},{28,12},{1,17},{... | collective-permute-start | bytes 147464 | tf_op jit(solution)/shard_map/ppermute | solution.py:522
  46.6 6.1 %collective-permute-start.11 = (f32[96,128]{1,0:T(8,128)S(1)}, f32[96,128]{1,0:T(8,128)S(1)}, u32[]{:S(2)}, u32[]{:S(2)}) collective-permute-start(f32[96,128]{1,0:T(8,128)S(1)} %add.63), channel_id=1, source_target_pairs={{0,24},{4,28},{8,16},{12,20},{16,8},{20,12},{24,0},{28,4},{1,25},{... | collective-permute-start | bytes 147464 | tf_op jit(solution)/shard_map/ppermute | solution.py:522
  48.1 7.1 %collective-permute-start.9 = (f32[96,128]{1,0:T(8,128)S(1)}, f32[96,128]{1,0:T(8,128)S(1)}, u32[]{:S(2)}, u32[]{:S(2)}) collective-permute-start(f32[96,128]{1,0:T(8,128)S(1)} %add.63), channel_id=1, source_target_pairs={{0,8},{4,12},{8,0},{12,4},{16,24},{20,28},{24,16},{28,20},{1,9},{5... | collective-permute-start | bytes 147464 | tf_op jit(solution)/shard_map/ppermute | solution.py:522
  48.6 7.2 %collective-permute-start.13 = (s16[7,64,128]{2,1,0:T(8,128)(2,1)S(1)}, s16[7,64,128]{2,1,0:T(8,128)(2,1)S(1)}, u32[]{:S(2)}, u32[]{:S(2)}) collective-permute-start(s16[7,64,128]{2,1,0:T(8,128)(2,1)S(1)} %get-tuple-element.154), channel_id=1, source_target_pairs={{0,2},{1,3},{2,0},{3,1},{4,6},{5,7},{6,4},{7,5},{8,10},{9,11},{10,... | collective-permute-start | bytes 344072 | tf_op jit(solution)/shard_map/ppermute | solution.py:519
  49.4 6.4 %collective-permute-start.14 = (s16[7,64,128]{2,1,0:T(8,128)(2,1)S(1)}, s16[7,64,128]{2,1,0:T(8,128)(2,1)S(1)}, u32[]{:S(2)}, u32[]{:S(2)}) collective-permute-start(s16[7,64,128]{2,1,0:T(8,128)(2,1)S(1)} %get-tuple-element.155), channel_id=1, source_target_pairs={{0,3},{1,2},{2,1},{3,0},{4,7},{5,6},{6,5},{7,4},{8,11},{9,10},{10,... | collective-permute-start | bytes 344072 | tf_op jit(solution)/shard_map/ppermute | solution.py:519
  50.9 5.0 %collective-permute-start.15 = (s16[2,64,128]{2,1,0:T(8,128)(2,1)S(1)}, s16[2,64,128]{2,1,0:T(8,128)(2,1)S(1)}, u32[]{:S(2)}, u32[]{:S(2)}) collective-permute-start(s16[2,64,128]{2,1,0:T(8,128)(2,1)S(1)} %get-tuple-element.156), channel_id=1, source_target_pairs={{0,8},{4,12},{8,0},{12,4},{16,24},{20,28},{24,16},{28,20},{1,9},{5... | collective-permute-start | bytes 98312 | tf_op jit(solution)/shard_map/ppermute | solution.py:522
  52.8 4.8 %collective-permute-start.16 = (s16[2,64,128]{2,1,0:T(8,128)(2,1)S(1)}, s16[2,64,128]{2,1,0:T(8,128)(2,1)S(1)}, u32[]{:S(2)}, u32[]{:S(2)}) collective-permute-start(s16[2,64,128]{2,1,0:T(8,128)(2,1)S(1)} %get-tuple-element.157), channel_id=1, source_target_pairs={{0,16},{4,20},{8,24},{12,28},{16,0},{20,4},{24,8},{28,12},{1,17},{... | collective-permute-start | bytes 98312 | tf_op jit(solution)/shard_map/ppermute | solution.py:522
  55.2 5.7 %collective-permute-start.17 = (s16[2,64,128]{2,1,0:T(8,128)(2,1)S(1)}, s16[2,64,128]{2,1,0:T(8,128)(2,1)S(1)}, u32[]{:S(2)}, u32[]{:S(2)}) collective-permute-start(s16[2,64,128]{2,1,0:T(8,128)(2,1)S(1)} %get-tuple-element.158), channel_id=1, source_target_pairs={{0,24},{4,28},{8,16},{12,20},{16,8},{20,12},{24,0},{28,4},{1,25},{... | collective-permute-start | bytes 98312 | tf_op jit(solution)/shard_map/ppermute | solution.py:522
  60.9 4.1 %collective-permute-start.18 = (f32[96,128]{1,0:T(8,128)S(1)}, f32[96,128]{1,0:T(8,128)S(1)}, u32[]{:S(2)}, u32[]{:S(2)}) collective-permute-start(f32[96,128]{1,0:T(8,128)S(1)} %add_add_fusion.5), channel_id=1, source_target_pairs={{0,1},{1,0},{2,3},{3,2},{4,5},{5,4},{6,7},{7,6},{8,9},{9,8},{10,11... | collective-permute-start | bytes 147464 | tf_op jit(solution)/shard_map/ppermute | solution.py:519
  61.7 4.1 %collective-permute-start.19 = (f32[96,128]{1,0:T(8,128)S(1)}, f32[96,128]{1,0:T(8,128)S(1)}, u32[]{:S(2)}, u32[]{:S(2)}) collective-permute-start(f32[96,128]{1,0:T(8,128)S(1)} %add_add_fusion.5), channel_id=1, source_target_pairs={{0,2},{1,3},{2,0},{3,1},{4,6},{5,7},{6,4},{7,5},{8,10},{9,11},{10,... | collective-permute-start | bytes 147464 | tf_op jit(solution)/shard_map/ppermute | solution.py:519
  63.2 5.0 %collective-permute-start.20 = (f32[96,128]{1,0:T(8,128)S(1)}, f32[96,128]{1,0:T(8,128)S(1)}, u32[]{:S(2)}, u32[]{:S(2)}) collective-permute-start(f32[96,128]{1,0:T(8,128)S(1)} %add_add_fusion.5), channel_id=1, source_target_pairs={{0,3},{1,2},{2,1},{3,0},{4,7},{5,6},{6,5},{7,4},{8,11},{9,10},{10,... | collective-permute-start | bytes 147464 | tf_op jit(solution)/shard_map/ppermute | solution.py:519
  68.2 1.3 collective-permute-start.21
  74.9 4.5 %collective-permute-start.25 = (s16[2,64,128]{2,1,0:T(8,128)(2,1)S(1)}, s16[2,64,128]{2,1,0:T(8,128)(2,1)S(1)}, u32[]{:S(2)}, u32[]{:S(2)}) collective-permute-start(s16[2,64,128]{2,1,0:T(8,128)(2,1)S(1)} %get-tuple-element.170), channel_id=1, source_target_pairs={{0,8},{4,12},{8,0},{12,4},{16,24},{20,28},{24,16},{28,20},{1,9},{5... | collective-permute-start | bytes 98312 | tf_op jit(solution)/shard_map/ppermute | solution.py:522
  75.0 4.9 %collective-permute-start.26 = (s16[2,64,128]{2,1,0:T(8,128)(2,1)S(1)}, s16[2,64,128]{2,1,0:T(8,128)(2,1)S(1)}, u32[]{:S(2)}, u32[]{:S(2)}) collective-permute-start(s16[2,64,128]{2,1,0:T(8,128)(2,1)S(1)} %get-tuple-element.170), channel_id=1, source_target_pairs={{0,16},{4,20},{8,24},{12,28},{16,0},{20,4},{24,8},{28,12},{1,17},{... | collective-permute-start | bytes 98312 | tf_op jit(solution)/shard_map/ppermute | solution.py:522
  75.9 5.7 %collective-permute-start.27 = (s16[2,64,128]{2,1,0:T(8,128)(2,1)S(1)}, s16[2,64,128]{2,1,0:T(8,128)(2,1)S(1)}, u32[]{:S(2)}, u32[]{:S(2)}) collective-permute-start(s16[2,64,128]{2,1,0:T(8,128)(2,1)S(1)} %get-tuple-element.170), channel_id=1, source_target_pairs={{0,24},{4,28},{8,16},{12,20},{16,8},{20,12},{24,0},{28,4},{1,25},{... | collective-permute-start | bytes 98312 | tf_op jit(solution)/shard_map/ppermute | solution.py:522
  81.6 8.6 %collective-permute-start.28 = (s16[8,64,128]{2,1,0:T(8,128)(2,1)S(1)}, s16[8,64,128]{2,1,0:T(8,128)(2,1)S(1)}, u32[]{:S(2)}, u32[]{:S(2)}) collective-permute-start(s16[8,64,128]{2,1,0:T(8,128)(2,1)S(1)} %constant_dynamic-update-slice_fusion.4.refs_3_), channel_id=1, source_target_pairs={{0,4},{4,0},{8,12},{12,8},{16,20},{20,16},{24,28},{28,24},{1,5},{5... | collective-permute-start | bytes 393224 | tf_op jit(solution)/shard_map/ppermute | solution.py:522
  81.6 6.0 %collective-permute-start.22 = (s16[7,64,128]{2,1,0:T(8,128)(2,1)S(1)}, s16[7,64,128]{2,1,0:T(8,128)(2,1)S(1)}, u32[]{:S(2)}, u32[]{:S(2)}) collective-permute-start(s16[7,64,128]{2,1,0:T(8,128)(2,1)S(1)} %get-tuple-element.169), channel_id=1, source_target_pairs={{0,1},{1,0},{2,3},{3,2},{4,5},{5,4},{6,7},{7,6},{8,9},{9,8},{10,11... | collective-permute-start | bytes 344072 | tf_op jit(solution)/shard_map/ppermute | solution.py:519
  82.6 7.7 %collective-permute-start.23 = (s16[7,64,128]{2,1,0:T(8,128)(2,1)S(1)}, s16[7,64,128]{2,1,0:T(8,128)(2,1)S(1)}, u32[]{:S(2)}, u32[]{:S(2)}) collective-permute-start(s16[7,64,128]{2,1,0:T(8,128)(2,1)S(1)} %get-tuple-element.169), channel_id=1, source_target_pairs={{0,2},{1,3},{2,0},{3,1},{4,6},{5,7},{6,4},{7,5},{8,10},{9,11},{10,... | collective-permute-start | bytes 344072 | tf_op jit(solution)/shard_map/ppermute | solution.py:519
  83.4 6.8 %collective-permute-start.24 = (s16[7,64,128]{2,1,0:T(8,128)(2,1)S(1)}, s16[7,64,128]{2,1,0:T(8,128)(2,1)S(1)}, u32[]{:S(2)}, u32[]{:S(2)}) collective-permute-start(s16[7,64,128]{2,1,0:T(8,128)(2,1)S(1)} %get-tuple-element.169), channel_id=1, source_target_pairs={{0,3},{1,2},{2,1},{3,0},{4,7},{5,6},{6,5},{7,4},{8,11},{9,10},{10,... | collective-permute-start | bytes 344072 | tf_op jit(solution)/shard_map/ppermute | solution.py:519
  93.6 2.5 %collective-permute-start.30 = (s16[16,64,128]{2,1,0:T(8,128)(2,1)S(1)}, s16[16,64,128]{2,1,0:T(8,128)(2,1)S(1)}, u32[]{:S(2)}, u32[]{:S(2)}) collective-permute-start(s16[16,64,128]{2,1,0:T(8,128)(2,1)S(1)} %get-tuple-element.192), channel_id=1, source_target_pairs={{0,4},{4,0},{8,12},{12,8},{16,20},{20,16},{24,28},{28,24},{1,5},{5... | collective-permute-start | bytes 786440 | tf_op jit(solution)/shard_map/ppermute | solution.py:522
  93.6 12.4 %collective-permute-start.34 = (s16[14,64,128]{2,1,0:T(8,128)(2,1)S(1)}, s16[14,64,128]{2,1,0:T(8,128)(2,1)S(1)}, u32[]{:S(2)}, u32[]{:S(2)}) collective-permute-start(s16[14,64,128]{2,1,0:T(8,128)(2,1)S(1)} %get-tuple-element.197), channel_id=1, source_target_pairs={{0,1},{1,0},{2,3},{3,2},{4,5},{5,4},{6,7},{7,6},{8,9},{9,8},{10,11... | collective-permute-start | bytes 688136 | tf_op jit(solution)/shard_map/ppermute | solution.py:519
  94.8 1.2 collective-permute-start.29
  97.1 10.7 %collective-permute-start.31 = (f32[96,128]{1,0:T(8,128)S(1)}, f32[96,128]{1,0:T(8,128)S(1)}, u32[]{:S(2)}, u32[]{:S(2)}) collective-permute-start(f32[96,128]{1,0:T(8,128)S(1)} %add.70), channel_id=1, source_target_pairs={{0,8},{4,12},{8,0},{12,4},{16,24},{20,28},{24,16},{28,20},{1,9},{5... | collective-permute-start | bytes 147464 | tf_op jit(solution)/shard_map/ppermute | solution.py:522
  97.5 10.3 %collective-permute-start.32 = (f32[96,128]{1,0:T(8,128)S(1)}, f32[96,128]{1,0:T(8,128)S(1)}, u32[]{:S(2)}, u32[]{:S(2)}) collective-permute-start(f32[96,128]{1,0:T(8,128)S(1)} %add.70), channel_id=1, source_target_pairs={{0,16},{4,20},{8,24},{12,28},{16,0},{20,4},{24,8},{28,12},{1,17},{... | collective-permute-start | bytes 147464 | tf_op jit(solution)/shard_map/ppermute | solution.py:522
  101.1 10.3 %collective-permute-start.33 = (f32[96,128]{1,0:T(8,128)S(1)}, f32[96,128]{1,0:T(8,128)S(1)}, u32[]{:S(2)}, u32[]{:S(2)}) collective-permute-start(f32[96,128]{1,0:T(8,128)S(1)} %add.70), channel_id=1, source_target_pairs={{0,24},{4,28},{8,16},{12,20},{16,8},{20,12},{24,0},{28,4},{1,25},{... | collective-permute-start | bytes 147464 | tf_op jit(solution)/shard_map/ppermute | solution.py:522
  105.4 11.8 %collective-permute-start.35 = (s16[14,64,128]{2,1,0:T(8,128)(2,1)S(1)}, s16[14,64,128]{2,1,0:T(8,128)(2,1)S(1)}, u32[]{:S(2)}, u32[]{:S(2)}) collective-permute-start(s16[14,64,128]{2,1,0:T(8,128)(2,1)S(1)} %get-tuple-element.198), channel_id=1, source_target_pairs={{0,2},{1,3},{2,0},{3,1},{4,6},{5,7},{6,4},{7,5},{8,10},{9,11},{10,... | collective-permute-start | bytes 688136 | tf_op jit(solution)/shard_map/ppermute | solution.py:519
  106.0 11.1 %collective-permute-start.36 = (s16[14,64,128]{2,1,0:T(8,128)(2,1)S(1)}, s16[14,64,128]{2,1,0:T(8,128)(2,1)S(1)}, u32[]{:S(2)}, u32[]{:S(2)}) collective-permute-start(s16[14,64,128]{2,1,0:T(8,128)(2,1)S(1)} %get-tuple-element.199), channel_id=1, source_target_pairs={{0,3},{1,2},{2,1},{3,0},{4,7},{5,6},{6,5},{7,4},{8,11},{9,10},{10,... | collective-permute-start | bytes 688136 | tf_op jit(solution)/shard_map/ppermute | solution.py:519
  107.7 9.4 %collective-permute-start.37 = (s16[4,64,128]{2,1,0:T(8,128)(2,1)S(1)}, s16[4,64,128]{2,1,0:T(8,128)(2,1)S(1)}, u32[]{:S(2)}, u32[]{:S(2)}) collective-permute-start(s16[4,64,128]{2,1,0:T(8,128)(2,1)S(1)} %get-tuple-element.200), channel_id=1, source_target_pairs={{0,8},{4,12},{8,0},{12,4},{16,24},{20,28},{24,16},{28,20},{1,9},{5... | collective-permute-start | bytes 196616 | tf_op jit(solution)/shard_map/ppermute | solution.py:522
  107.7 9.4 %collective-permute-start.38 = (s16[4,64,128]{2,1,0:T(8,128)(2,1)S(1)}, s16[4,64,128]{2,1,0:T(8,128)(2,1)S(1)}, u32[]{:S(2)}, u32[]{:S(2)}) collective-permute-start(s16[4,64,128]{2,1,0:T(8,128)(2,1)S(1)} %get-tuple-element.201), channel_id=1, source_target_pairs={{0,16},{4,20},{8,24},{12,28},{16,0},{20,4},{24,8},{28,12},{1,17},{... | collective-permute-start | bytes 196616 | tf_op jit(solution)/shard_map/ppermute | solution.py:522
  111.4 6.1 %collective-permute-start.39 = (s16[4,64,128]{2,1,0:T(8,128)(2,1)S(1)}, s16[4,64,128]{2,1,0:T(8,128)(2,1)S(1)}, u32[]{:S(2)}, u32[]{:S(2)}) collective-permute-start(s16[4,64,128]{2,1,0:T(8,128)(2,1)S(1)} %get-tuple-element.202), channel_id=1, source_target_pairs={{0,24},{4,28},{8,16},{12,20},{16,8},{20,12},{24,0},{28,4},{1,25},{... | collective-permute-start | bytes 196616 | tf_op jit(solution)/shard_map/ppermute | solution.py:522
  117.5 4.1 %collective-permute-start.40 = (f32[96,128]{1,0:T(8,128)S(1)}, f32[96,128]{1,0:T(8,128)S(1)}, u32[]{:S(2)}, u32[]{:S(2)}) collective-permute-start(f32[96,128]{1,0:T(8,128)S(1)} %add_add_fusion.3), channel_id=1, source_target_pairs={{0,1},{1,0},{2,3},{3,2},{4,5},{5,4},{6,7},{7,6},{8,9},{9,8},{10,11... | collective-permute-start | bytes 147464 | tf_op jit(solution)/shard_map/ppermute | solution.py:519
  119.0 4.1 %collective-permute-start.41 = (f32[96,128]{1,0:T(8,128)S(1)}, f32[96,128]{1,0:T(8,128)S(1)}, u32[]{:S(2)}, u32[]{:S(2)}) collective-permute-start(f32[96,128]{1,0:T(8,128)S(1)} %add_add_fusion.3), channel_id=1, source_target_pairs={{0,2},{1,3},{2,0},{3,1},{4,6},{5,7},{6,4},{7,5},{8,10},{9,11},{10,... | collective-permute-start | bytes 147464 | tf_op jit(solution)/shard_map/ppermute | solution.py:519
  119.5 5.0 %collective-permute-start.42 = (f32[96,128]{1,0:T(8,128)S(1)}, f32[96,128]{1,0:T(8,128)S(1)}, u32[]{:S(2)}, u32[]{:S(2)}) collective-permute-start(f32[96,128]{1,0:T(8,128)S(1)} %add_add_fusion.3), channel_id=1, source_target_pairs={{0,3},{1,2},{2,1},{3,0},{4,7},{5,6},{6,5},{7,4},{8,11},{9,10},{10,... | collective-permute-start | bytes 147464 | tf_op jit(solution)/shard_map/ppermute | solution.py:519
  124.5 1.3 collective-permute-start.43
  136.8 4.5 %collective-permute-start.47 = (s16[2,64,128]{2,1,0:T(8,128)(2,1)S(1)}, s16[2,64,128]{2,1,0:T(8,128)(2,1)S(1)}, u32[]{:S(2)}, u32[]{:S(2)}) collective-permute-start(s16[2,64,128]{2,1,0:T(8,128)(2,1)S(1)} %get-tuple-element.218), channel_id=1, source_target_pairs={{0,8},{4,12},{8,0},{12,4},{16,24},{20,28},{24,16},{28,20},{1,9},{5... | collective-permute-start | bytes 98312 | tf_op jit(solution)/shard_map/ppermute | solution.py:522
  136.9 5.6 %collective-permute-start.48 = (s16[2,64,128]{2,1,0:T(8,128)(2,1)S(1)}, s16[2,64,128]{2,1,0:T(8,128)(2,1)S(1)}, u32[]{:S(2)}, u32[]{:S(2)}) collective-permute-start(s16[2,64,128]{2,1,0:T(8,128)(2,1)S(1)} %get-tuple-element.218), channel_id=1, source_target_pairs={{0,16},{4,20},{8,24},{12,28},{16,0},{20,4},{24,8},{28,12},{1,17},{... | collective-permute-start | bytes 98312 | tf_op jit(solution)/shard_map/ppermute | solution.py:522
  140.4 5.7 %collective-permute-start.49 = (s16[2,64,128]{2,1,0:T(8,128)(2,1)S(1)}, s16[2,64,128]{2,1,0:T(8,128)(2,1)S(1)}, u32[]{:S(2)}, u32[]{:S(2)}) collective-permute-start(s16[2,64,128]{2,1,0:T(8,128)(2,1)S(1)} %get-tuple-element.218), channel_id=1, source_target_pairs={{0,24},{4,28},{8,16},{12,20},{16,8},{20,12},{24,0},{28,4},{1,25},{... | collective-permute-start | bytes 98312 | tf_op jit(solution)/shard_map/ppermute | solution.py:522
  146.1 8.6 %collective-permute-start.50 = (s16[8,64,128]{2,1,0:T(8,128)(2,1)S(1)}, s16[8,64,128]{2,1,0:T(8,128)(2,1)S(1)}, u32[]{:S(2)}, u32[]{:S(2)}) collective-permute-start(s16[8,64,128]{2,1,0:T(8,128)(2,1)S(1)} %constant_dynamic-update-slice_fusion.8.refs_3_), channel_id=1, source_target_pairs={{0,4},{4,0},{8,12},{12,8},{16,20},{20,16},{24,28},{28,24},{1,5},{5... | collective-permute-start | bytes 393224 | tf_op jit(solution)/shard_map/ppermute | solution.py:522
  146.1 8.2 %collective-permute-start.44 = (s16[7,64,128]{2,1,0:T(8,128)(2,1)S(1)}, s16[7,64,128]{2,1,0:T(8,128)(2,1)S(1)}, u32[]{:S(2)}, u32[]{:S(2)}) collective-permute-start(s16[7,64,128]{2,1,0:T(8,128)(2,1)S(1)} %get-tuple-element.217), channel_id=1, source_target_pairs={{0,1},{1,0},{2,3},{3,2},{4,5},{5,4},{6,7},{7,6},{8,9},{9,8},{10,11... | collective-permute-start | bytes 344072 | tf_op jit(solution)/shard_map/ppermute | solution.py:519
  147.0 7.7 %collective-permute-start.45 = (s16[7,64,128]{2,1,0:T(8,128)(2,1)S(1)}, s16[7,64,128]{2,1,0:T(8,128)(2,1)S(1)}, u32[]{:S(2)}, u32[]{:S(2)}) collective-permute-start(s16[7,64,128]{2,1,0:T(8,128)(2,1)S(1)} %get-tuple-element.217), channel_id=1, source_target_pairs={{0,2},{1,3},{2,0},{3,1},{4,6},{5,7},{6,4},{7,5},{8,10},{9,11},{10,... | collective-permute-start | bytes 344072 | tf_op jit(solution)/shard_map/ppermute | solution.py:519
  148.5 6.2 %collective-permute-start.46 = (s16[7,64,128]{2,1,0:T(8,128)(2,1)S(1)}, s16[7,64,128]{2,1,0:T(8,128)(2,1)S(1)}, u32[]{:S(2)}, u32[]{:S(2)}) collective-permute-start(s16[7,64,128]{2,1,0:T(8,128)(2,1)S(1)} %get-tuple-element.217), channel_id=1, source_target_pairs={{0,3},{1,2},{2,1},{3,0},{4,7},{5,6},{6,5},{7,4},{8,11},{9,10},{10,... | collective-permute-start | bytes 344072 | tf_op jit(solution)/shard_map/ppermute | solution.py:519
  158.1 1.2 collective-permute-start.51
  159.4 4.8 %collective-permute-start.52 = (f32[96,128]{1,0:T(8,128)S(1)}, f32[96,128]{1,0:T(8,128)S(1)}, u32[]{:S(2)}, u32[]{:S(2)}) collective-permute-start(f32[96,128]{1,0:T(8,128)S(1)} %add.77), channel_id=1, source_target_pairs={{0,8},{4,12},{8,0},{12,4},{16,24},{20,28},{24,16},{28,20},{1,9},{5... | collective-permute-start | bytes 147464 | tf_op jit(solution)/shard_map/ppermute | solution.py:522
  159.5 5.8 %collective-permute-start.53 = (f32[96,128]{1,0:T(8,128)S(1)}, f32[96,128]{1,0:T(8,128)S(1)}, u32[]{:S(2)}, u32[]{:S(2)}) collective-permute-start(f32[96,128]{1,0:T(8,128)S(1)} %add.77), channel_id=1, source_target_pairs={{0,16},{4,20},{8,24},{12,28},{16,0},{20,4},{24,8},{28,12},{1,17},{... | collective-permute-start | bytes 147464 | tf_op jit(solution)/shard_map/ppermute | solution.py:522
  161.3 5.9 %collective-permute-start.54 = (f32[96,128]{1,0:T(8,128)S(1)}, f32[96,128]{1,0:T(8,128)S(1)}, u32[]{:S(2)}, u32[]{:S(2)}) collective-permute-start(f32[96,128]{1,0:T(8,128)S(1)} %add.77), channel_id=1, source_target_pairs={{0,24},{4,28},{8,16},{12,20},{16,8},{20,12},{24,0},{28,4},{1,25},{... | collective-permute-start | bytes 147464 | tf_op jit(solution)/shard_map/ppermute | solution.py:522
  167.3 4.2 %collective-permute-start.55 = (f32[96,128]{1,0:T(8,128)S(1)}, f32[96,128]{1,0:T(8,128)S(1)}, u32[]{:S(2)}, u32[]{:S(2)}) collective-permute-start(f32[96,128]{1,0:T(8,128)S(1)} %add_add_fusion.1), channel_id=1, source_target_pairs={{0,1},{1,0},{2,3},{3,2},{4,5},{5,4},{6,7},{7,6},{8,9},{9,8},{10,11... | collective-permute-start | bytes 147464 | tf_op jit(solution)/shard_map/ppermute | solution.py:519
  168.1 4.5 %collective-permute-start.56 = (f32[96,128]{1,0:T(8,128)S(1)}, f32[96,128]{1,0:T(8,128)S(1)}, u32[]{:S(2)}, u32[]{:S(2)}) collective-permute-start(f32[96,128]{1,0:T(8,128)S(1)} %add_add_fusion.1), channel_id=1, source_target_pairs={{0,2},{1,3},{2,0},{3,1},{4,6},{5,7},{6,4},{7,5},{8,10},{9,11},{10,... | collective-permute-start | bytes 147464 | tf_op jit(solution)/shard_map/ppermute | solution.py:519
  169.6 5.0 %collective-permute-start.57 = (f32[96,128]{1,0:T(8,128)S(1)}, f32[96,128]{1,0:T(8,128)S(1)}, u32[]{:S(2)}, u32[]{:S(2)}) collective-permute-start(f32[96,128]{1,0:T(8,128)S(1)} %add_add_fusion.1), channel_id=1, source_target_pairs={{0,3},{1,2},{2,1},{3,0},{4,7},{5,6},{6,5},{7,4},{8,11},{9,10},{10,... | collective-permute-start | bytes 147464 | tf_op jit(solution)/shard_map/ppermute | solution.py:519
  174.6 1.3 collective-permute-start.58
  (8 other events, 47.0 us)

commit v5 on v4

--- a/solution.py
+++ b/solution.py
@@ -122,10 +122,10 @@
             halo[start + 2 * t] = one
             halo[start + 2 * t + 1] = two
     tiles = edge_tiles(ifr)
-    for other, edge in enumerate(edges):
-        for k in range(edge.shape[0] // (places * tiles)):
+    for k, edge in enumerate(edges):
+        for other in range(2):
             start = n_row * lb + (((pos[1] // 2) ^ k) * 2 + ((pos[1] % 2) ^ other)) * ifr
-            found = decode_edge(edge, (k * places + place) * tiles, ifr)
+            found = decode_edge(edge, (other * places + place) * tiles, ifr)
             for q in range(0, ifr, 2):
                 blocks = two_blocks(found[q // 2])
                 halo[start + q] = blocks[0]
@@ -354,14 +354,13 @@
                 target[v * tiles + t] = total[t]
 
 
-def split_halo(refs, n_row):
-    wires = [refs.pop(0) for _ in range(n_row - 1)]
-    return wires, [refs.pop(0), refs.pop(0)]
-
-
-def start_image_kernel(n_row, ifr, *refs):
+def split_halo(refs, n_row, n_z):
+    return [refs.pop(0) for _ in range(n_row - 1)], [refs.pop(0) for _ in range(n_z)]
+
+
+def start_image_kernel(n_row, n_z, ifr, *refs):
     refs = list(refs)
-    wires, edges = split_halo(refs, n_row)
+    wires, edges = split_halo(refs, n_row, n_z)
     stored, diagonal, where, pos, x, p, half_x, diag_x, half_p, diag_p, keep, send, halo_x, halo_p, table = refs
     n = x.shape[0]
     for place, (vector, half, diag, halo) in enumerate(((x, half_x, diag_x, halo_x), (p, half_p, diag_p, halo_p))):
@@ -404,9 +403,9 @@
     solved[...] = inverse(stored + stored.T)
 
 
-def update_image_kernel(n_row, ifr, first, *refs):
+def update_image_kernel(n_row, n_z, ifr, first, *refs):
     refs = list(refs)
-    wires, edges = split_halo(refs, n_row)
+    wires, edges = split_halo(refs, n_row, n_z)
     stored, diagonal, where, pos, w, x, p, ax, ap, half, diag, keep, send, halo, table = refs
     n = w.shape[0]
     fill_halo(w, wires, edges, pos, halo, ifr)
@@ -423,6 +422,7 @@
 
 def move_kernel(n_row, n_z, total_rows, *refs):
     refs = list(refs)
+    start_parts = take_returned(refs, n_row, n_z)
     back_parts = take_returned(refs, n_row, n_z)
     mine, other, pos, bnd, start, energy, pap_inverse, x, p, ax, ap, ap_diag, w, aw, aw_diag, precond = refs[:16]
     x_out, ax_out, w_out, wire, edge, step_x, step_a, small, table, back, ap_full, aw_full = refs[16:]
@@ -435,9 +435,9 @@
         table, 0.5 * (gram + gram.T), px.T, pp, pax, pap_inverse[...], total_rows
     )
     ap_full[...] = ap[...] + 0.5 * ap_diag[...]
-    returned(0, *back_parts, bnd, back, ap_full)
+    returned(1, *start_parts, bnd, back, ap_full)
     aw_full[...] = aw[...] + 0.5 * aw_diag[...]
-    returned(1, *back_parts, bnd, back, aw_full)
+    returned(0, *back_parts, bnd, back, aw_full)
     step_a[...] = nn(zpt, ap_full[...]) + nn(zwt, aw_full[...])
     step_x[...] = nn(zwt, w[...]) + nn(zpt, p[...])
     x_out[...] = nn(scale, x[...] + step_x[...])
@@ -527,16 +527,10 @@
     def coded(count):
         return shaped(count, n, 2 * kb, dtype=jnp.int16)
 
-    def halo_start(own, edge):
+    def halo_of(own, edge):
         rows_got = [row_send(own, k) for k in range(1, n_row)]
-        return rows_got, [sub_send(edge, 2 * k) for k in range(1, n_z)]
-
-    def halo_end(edge, rows_got, edges_got):
-        same = jnp.concatenate([edge] + edges_got, axis=0)
-        return rows_got + [same, sub_send(same, 1)]
-
-    def halo_of(own, edge):
-        return halo_end(edge, *halo_start(own, edge))
+        pair = jnp.concatenate([edge, sub_send(edge, 1)], axis=0)
+        return rows_got + [pair] + [sub_send(pair, 2 * k) for k in range(1, n_z)]
 
     def groups_of_four(value, size, send):
         base = 1
@@ -551,11 +545,12 @@
     def z_send(value, k):
         return sub_send(value, 2 * k)
 
-    def sum_halves(keep, send):
+    def sum_halves(keep, send, meanwhile=()):
         total = keep + sub_send(send, 1)
         total = groups_of_four(total, n_z, z_send)
+        total, *meanwhile = after((total, *meanwhile))
         total = groups_of_four(total, n_row, row_send)
-        return [total, sub_send(total, 1)]
+        return [total, sub_send(total, 1)], meanwhile
 
     def partials(source, earlier=()):
         m = 2 if earlier else 1
@@ -570,9 +565,8 @@
             smem=(2, 3),
         )
 
-    def sum_with_partials(keep, send, parts, m, meanwhile=()):
+    def send_partials(parts, m):
         own, edge_keep, edge_send, *row_parts = parts
-        total = keep + sub_send(send, 1)
         edge_got = sub_send(edge_send, 1)
         rows_got = [row_send(row_parts[k - 1], k) for k in range(1, n_row)]
         edge_own, *outs = run(
@@ -582,19 +576,14 @@
             [edge_keep, edge_got, pos],
             smem=(2,),
         )
-        total, *outs = after((total, *outs))
-        edges_got = [z_send(outs[k - 1], k) for k in range(1, n_z)]
-        total = groups_of_four(total, n_z, z_send)
-        total, rows_got, edges_got, meanwhile = after((total, rows_got, edges_got, list(meanwhile)))
-        total = groups_of_four(total, n_row, row_send)
-        return [total, sub_send(total, 1)], [own] + rows_got + [edge_own] + edges_got, meanwhile
+        return [own] + rows_got + [edge_own] + [z_send(outs[k - 1], k) for k in range(1, n_z)]
 
     x, p = modes.T, search.T
     scaling = precond.reshape(1, rows)
     wire_shapes = [coded(tiles + 1), coded(edges_in)]
     wire, edge = run(wire_kernel, "wire", [coded(2 * (tiles + 1)), coded(2 * edges_in)], [x, p, bnd], smem=(2,))
-    rows_got, edges_got = halo_start(wire, edge)
-    in_val, if_val, edges_got[0] = after((in_val, if_val, edges_got[0]))
+    halo = halo_of(wire, edge)
+    in_val, if_val, halo[0], halo[-1] = after((in_val, if_val, halo[0], halo[-1]))
     stored, joined, diagonal, where = run(
         functools.partial(prepare_kernel, groups, n_row * lb),
         "prepare",
@@ -608,10 +597,7 @@
         smem=(2, 3, 4, 5),
         smem_outs=(3,),
     )
-    stored, *edges_got = after((stored, *edges_got))
-    halo = halo_end(edge, rows_got, edges_got)
-    x_parts = partials(x)
-    p_parts = partials(p)
+    parts = partials(p, partials(x))
     blocks = [stored, diagonal, where, pos]
     halo_scratch = VMEM((halo_blocks, n, 2 * kb), bf16)
     back_scratch = VMEM((tiles, n, 2 * kb), f32)
@@ -622,32 +608,33 @@
     table_scratch = VMEM((3 * n, 2 * n), f32)
     count = len(halo)
     half_x, diag_x, half_p, diag_p, keep, send = run(
-        functools.partial(start_image_kernel, n_row, ifr),
+        functools.partial(start_image_kernel, n_row, n_z, ifr),
         "start_image",
         [whole] * 4 + halves_shape,
         halo + blocks + [x, p],
         [halo_scratch, halo_scratch, table_scratch],
         smem=(count + 2, count + 3),
     )
-    keep, send, x_parts, p_parts = after((keep, send, x_parts, p_parts))
-    halves, x_back, _ = sum_with_partials(keep, send, x_parts, 1)
-    count = len(x_back)
+    start_back = send_partials(parts, 2)
+    keep, send, *start_back = after((keep, send, *start_back))
+    halves, _ = sum_halves(keep, send)
+    count = len(start_back)
     table, ax, energy, w, w_wire, w_edge = run(
         functools.partial(update_kernel, n_row, n_z),
         "update",
         [table_shape, whole, shaped(n, n), whole] + wire_shapes,
-        x_back + halves + [pos, bnd, x, half_x, diag_x, scaling],
+        start_back + halves + [pos, bnd, x, half_x, diag_x, scaling],
         [back_scratch],
         smem=(count + 2, count + 3),
     )
     w_halo = halo_of(w_wire, w_edge)
     (pap_inverse,) = run(inverse_kernel, "pap_inverse", [shaped(n, n)], [table])
-    w_parts = partials(w, p_parts)
+    w_back = send_partials(partials(w), 1)
 
     def update_image(first, halo, w, x, p, ax, ap):
         count = len(halo)
         return run(
-            functools.partial(update_image_kernel, n_row, ifr, first),
+            functools.partial(update_image_kernel, n_row, n_z, ifr, first),
             "update_image",
             [whole, whole] + halves_shape,
             halo + blocks + [w, x, p, ax, ap],
@@ -656,21 +643,21 @@
         )
 
     half_w, diag_w, keep, send = update_image(True, w_halo, w, x, p, ax, half_p)
-    keep, send, w_parts = after((keep, send, w_parts))
-    halves, w_back, (pap_inverse,) = sum_with_partials(keep, send, w_parts, 2, [pap_inverse])
-    count = len(w_back)
+    keep, send, *w_back = after((keep, send, *w_back))
+    halves, (pap_inverse,) = sum_halves(keep, send, [pap_inverse])
+    count = len(start_back) + len(w_back)
     x, ax, w, w_wire, w_edge, step_x, step_a, small = run(
         functools.partial(move_kernel, n_row, n_z, total_rows),
         "move",
         [whole] * 3 + wire_shapes + [whole, whole, shaped(4 * n, n)],
-        w_back + halves + [pos, bnd, table, energy, pap_inverse, x, p, ax, half_p, diag_p, w, half_w, diag_w, scaling],
+        start_back + w_back + halves + [pos, bnd, table, energy, pap_inverse, x, p, ax, half_p, diag_p, w, half_w, diag_w, scaling],
         [table_scratch, back_scratch, VMEM((n, rows), f32), VMEM((n, rows), f32)],
         smem=(count + 2, count + 3),
     )
     w_halo = halo_of(w_wire, w_edge)
     p, ap, state = run(settle_kernel, "settle", [whole, whole, shaped(3 * n, n)], [small, step_x, step_a])
     _, _, keep, send = update_image(False, w_halo, w, x, p, ax, ap)
-    halves = sum_halves(keep, send)
+    halves, _ = sum_halves(keep, send)
     x, p = run(
         functools.partial(finish_kernel, total_rows),
         "finish",

time: 187 us -> 176 us (0.941)
  waiting for transfers between devices: 49.4 us -> 42.4 us
  local copies, waits for them, and re-layouts: 10.7 us -> 5.89 us
  starting transfers between devices: 65.8 us -> 68.4 us
    ppermute x24, waiting for transfers between devices: 26.1 us -> 13.5 us  [row_send(): return lax.ppermute(value, 'row', [(r, r ^ k) for r in range(n_row)])]
    ppermute x35, waiting for transfers between devices: 23.3 us -> 28.8 us  [sub_send(): return lax.ppermute(value, 'sub', [(s, s ^ k) for s in range(n_sub)])]
    unnamed x35 -> x27, local copies, waits for them, and re-layouts: 5.75 us -> 2.55 us
  transfers between devices with their start and end apart: 59 -> 59, of which waited for: 32 -> 30; matrix products, arithmetic and copies ran while one was open for 2% -> 0% of each run, Pallas kernels for 10% -> 12%
where the time goes in v5:
time: 176 us
  starting transfers between devices  68.4 us (39%)
  Pallas kernels  57.9 us (33%)
  waiting for transfers between devices  42.4 us (24%)
  local copies, waits for them, and re-layouts  5.89 us (3%)
    pallas_call x15, Pallas kernels, run(): pl.pallas_call(kernel, name=name, out_shape=outs, in_specs=in_specs, out_...  57.9 us
    ppermute x35, starting transfers between devices, sub_send(): return lax.ppermute(value, 'sub', [(s, s ^ k) for s in range(n_sub)])  38.9 us
    ppermute x24, starting transfers between devices, row_send(): return lax.ppermute(value, 'row', [(r, r ^ k) for r in range(n_row)])  29.5 us
    ppermute x35, waiting for transfers between devices, sub_send(): return lax.ppermute(value, 'sub', [(s, s ^ k) for s in range(n_sub)])  28.8 us
    ppermute x24, waiting for transfers between devices, row_send(): return lax.ppermute(value, 'row', [(r, r ^ k) for r in range(n_row)])  13.5 us
  transfers between devices with their start and end apart: 59, of which 30 were waited for; matrix products, arithmetic and copies ran while one was open for 0% of the time, Pallas kernels for 12%

profile of v5, /device:TPU:0, one launch (start us, length us, event | category | flops | bytes accessed | tf_op | source)
XLA Modules:
  0.0 175.7 jit_solution(7441011933614867612)
XLA Ops:
  4.5 2.6 %collective-permute-start = (s16[14,64,128]{2,1,0:T(8,128)(2,1)S(1)}, s16[14,64,128]{2,1,0:T(8,128)(2,1)S(1)}, u32[]{:S(2)}, u32[]{:S(2)}) collective-permute-start(s16[14,64,128]{2,1,0:T(8,128)(2,1)S(1)} %get-tuple-element.91), channel_id=1, source_target_pairs={{0,1},{1,0},{2,3},{3,2},{4,5},{5,4},{6,7},{7,6},{8,9},{9,8},{10,11... | collective-permute-start | bytes 688136 | tf_op jit(solution)/shard_map/ppermute | solution.py:519
  7.1 3.7 %collective-permute-start.2 = (s16[8,64,128]{2,1,0:T(8,128)(2,1)S(1)}, s16[8,64,128]{2,1,0:T(8,128)(2,1)S(1)}, u32[]{:S(2)}, u32[]{:S(2)}) collective-permute-start(s16[8,64,128]{2,1,0:T(8,128)(2,1)S(1)} %constant_dynamic-update-slice_fusion.refs_3_), channel_id=1, source_target_pairs={{0,24},{4,28},{8,16},{12,20},{16,8},{20,12},{24,0},{28,4},{1,25},{... | collective-permute-start | bytes 393224 | tf_op jit(solution)/shard_map/ppermute | solution.py:522
  10.9 3.9 %collective-permute-done.2.refs_6_ = s16[8,64,128]{2,1,0:T(8,128)(2,1)S(1)} collective-permute-done((s16[8,64,128]{2,1,0:T(8,128)(2,1)S(1)}, s16[8,64,128]{2,1,0:T(8,128)(2,1)S(1)}, u32[]{:S(2)}, u32[]{:S(2)}) %collective-permute-start.2) | collective-permute-done | bytes 131104 | tf_op jit(solution)/shard_map/ppermute | solution.py:522
  14.7 3.3 %copy.12 = bf16[1,1,96,64,64]{4,3,2,1,0:T(8,128)(2,1)S(1)} copy(bf16[1,1,96,64,64]{2,4,3,1,0:T(8,128)(2,1)} %param.15) | data formatting | bytes 1572864 | tf_op jit(solution)/shard_map/optimization_barrier | solution.py:586
  18.1 2.2 %prepare.1 = (bf16[12,64,1024]{2,1,0:T(8,128)(2,1)S(1)}, bf16[12,64,512]{2,1,0:T(8,128)(2,1)S(1)}, bf16[12,64,128]{2,1,0:T(8,128)(2,1)S(1)}, s32[96]{0:T(128)S(1)}) custom-call(bf16[96,64,64]{2,1,0:T(8,128)(2,1)S(1)} %bitcast.19, bf16[12,64,64]{2,1,0:T(8,128)(2,1)S(1)} %bitcast.25, s32[96]{0:T(128)S(1)} %bitcast.29, s32[96]{0:T(128)S(1)} %bitcast.30, ...), custom_call_target="tpu_custom_call" | custom-call | flops 1000000 | bytes 3441888 | tf_op jit(solution)/shard_map/prepare/pallas_call | solution.py:488
  20.3 2.2 %partials.3 = (f32[64,768]{1,0:T(8,128)S(1)}, f32[8,64,128]{2,1,0:T(8,128)S(1)}, s16[8,64,128]{2,1,0:T(8,128)(2,1)S(1)}, s16[7,64,128]{2,1,0:T(8,128)(2,1)S(1)},...) custom-call(f32[64,768]{1,0:T(8,128)S(1)} %bitcast.14, ...), custom_call_target="tpu_custom_call" | custom-call | flops 1000000 | bytes 1917320 | tf_op jit(solution)/shard_map/partials/pallas_call | solution.py:488
  22.5 2.2 %partials.4 = (f32[128,768]{1,0:T(8,128)S(1)}, f32[16,64,128]{2,1,0:T(8,128)S(1)}, s16[16,64,128]{2,1,0:T(8,128)(2,1)S(1)}, s16[14,64,128]{2,1,0:T(8,128)(2,1)S(...) custom-call(f32[64,768]{1,0:T(8,128)S(1)} %bitcast.21, ...), custom_call_target="tpu_custom_call" | custom-call | flops 1000000 | bytes 3785096 | tf_op jit(solution)/shard_map/partials/pallas_call | solution.py:488
  24.8 3.5 %collective-permute-start.6 = (s16[8,64,128]{2,1,0:T(8,128)(2,1)S(1)}, s16[8,64,128]{2,1,0:T(8,128)(2,1)S(1)}, u32[]{:S(2)}, u32[]{:S(2)}) collective-permute-start(s16[8,64,128]{2,1,0:T(8,128)(2,1)S(1)} %constant_dynamic-update-slice_fusion.refs_3_), channel_id=1, source_target_pairs={{0,16},{4,20},{8,24},{12,28},{16,0},{20,4},{24,8},{28,12},{1,17},{... | collective-permute-start | bytes 393224 | tf_op jit(solution)/shard_map/ppermute | solution.py:522
  29.0 2.1 %collective-permute-start.4 = (s16[14,64,128]{2,1,0:T(8,128)(2,1)S(1)}, s16[14,64,128]{2,1,0:T(8,128)(2,1)S(1)}, u32[]{:S(2)}, u32[]{:S(2)}) collective-permute-start(s16[14,64,128]{2,1,0:T(8,128)(2,1)S(1)} %get-tuple-element.91), channel_id=1, source_target_pairs={{0,3},{1,2},{2,1},{3,0},{4,7},{5,6},{6,5},{7,4},{8,11},{9,10},{10,... | collective-permute-start | bytes 688136 | tf_op jit(solution)/shard_map/ppermute | solution.py:519
  31.6 3.7 %collective-permute-done.6.refs_5_ = s16[8,64,128]{2,1,0:T(8,128)(2,1)S(1)} collective-permute-done((s16[8,64,128]{2,1,0:T(8,128)(2,1)S(1)}, s16[8,64,128]{2,1,0:T(8,128)(2,1)S(1)}, u32[]{:S(2)}, u32[]{:S(2)}) %collective-permute-start.6) | collective-permute-done | bytes 131104 | tf_op jit(solution)/shard_map/ppermute | solution.py:522
  35.3 1.2 collective-permute-start.7
  36.5 1.5 collective-permute-start.8
  40.7 1.6 collective-permute-done.3.refs_1_
  42.3 2.8 %collective-permute-start.12 = (s16[4,64,128]{2,1,0:T(8,128)(2,1)S(1)}, s16[4,64,128]{2,1,0:T(8,128)(2,1)S(1)}, u32[]{:S(2)}, u32[]{:S(2)}) collective-permute-start(s16[4,64,128]{2,1,0:T(8,128)(2,1)S(1)} %get-tuple-element.117), channel_id=1, source_target_pairs={{0,16},{4,20},{8,24},{12,28},{16,0},{20,4},{24,8},{28,12},{1,17},{... | collective-permute-start | bytes 196616 | tf_op jit(solution)/shard_map/ppermute | solution.py:522
  45.1 1.9 %collective-permute-start.13 = (s16[4,64,128]{2,1,0:T(8,128)(2,1)S(1)}, s16[4,64,128]{2,1,0:T(8,128)(2,1)S(1)}, u32[]{:S(2)}, u32[]{:S(2)}) collective-permute-start(s16[4,64,128]{2,1,0:T(8,128)(2,1)S(1)} %get-tuple-element.118), channel_id=1, source_target_pairs={{0,24},{4,28},{8,16},{12,20},{16,8},{20,12},{24,0},{28,4},{1,25},{... | collective-permute-start | bytes 196616 | tf_op jit(solution)/shard_map/ppermute | solution.py:522
  47.1 4.4 %start_image.1 = (f32[64,768]{1,0:T(8,128)S(1)}, f32[64,768]{1,0:T(8,128)S(1)}, f32[64,768]{1,0:T(8,128)S(1)}, f32[64,768]{1,0:T(8,128)S(1)}, f32[96,128]{1,0:T(8,128)S(1)}, /*index=5*/f32[96,128]{1,0:T(8,128)S(1)}) custom-call(s16[14,64,128]{2,1,0:T(8,128)(2,1)S(1)} %collective-permute-done.refs_0_, s16[14,64,128]{2,1,0:T(8,128)(2,1)S(1)} %collective-permute-done.3.refs_1_, ...), custom_call_target="tpu_custom_call" | custom-call | flops 1000000 | bytes 4260232 | tf_op jit(solution)/shard_map/start_image/pallas_call | solution.py:488
  52.1 1.2 collective-permute-done.14
  53.4 1.4 collective-permute-start.17
  54.8 1.5 collective-permute-start.16
  56.2 1.6 collective-permute-start.15
  57.8 2.0 %collective-permute-done.17 = f32[96,128]{1,0:T(8,128)S(1)} collective-permute-done((f32[96,128]{1,0:T(8,128)S(1)}, f32[96,128]{1,0:T(8,128)S(1)}, u32[]{:S(2)}, u32[]{:S(2)}) %collective-permute-start.17) | collective-permute-done | bytes 49184 | tf_op jit(solution)/shard_map/ppermute | solution.py:522
  59.8 1.7 collective-permute-done.16
  61.5 1.8 %collective-permute-start.20 = (f32[96,128]{1,0:T(8,128)S(1)}, f32[96,128]{1,0:T(8,128)S(1)}, u32[]{:S(2)}, u32[]{:S(2)}) collective-permute-start(f32[96,128]{1,0:T(8,128)S(1)} %add_add_fusion.5), channel_id=1, source_target_pairs={{0,3},{1,2},{2,1},{3,0},{4,7},{5,6},{6,5},{7,4},{8,11},{9,10},{10,... | collective-permute-start | bytes 147464 | tf_op jit(solution)/shard_map/ppermute | solution.py:519
  65.0 1.5 collective-permute-done.20
  68.4 1.2 collective-permute-done.21.refs_9_
  69.6 5.3 %update.1 = (f32[192,128]{1,0:T(8,128)S(1)}, f32[64,768]{1,0:T(8,128)S(1)}, f32[64,64]{1,0:T(8,128)S(1)}, f32[64,768]{1,0:T(8,128)S(1)}, s16[7,64,128]{2,1,0:T(8,128)(2,1)S(1)}, /*index=5*/s16[2,64,128]{2,1,0:T(8,128)(2,1)S(1)}) custom-call(f32[128,768]{1,0:T(8,128)S(1)} %get-tuple-element.119.refs_0_, ...), custom_call_target="tpu_custom_call" | custom-call | flops 1000000 | bytes 2755604 | tf_op jit(solution)/shard_map/update/pallas_call | solution.py:488
  75.2 1.7 collective-permute-start.24
  76.9 2.3 %partials.5 = (f32[64,768]{1,0:T(8,128)S(1)}, f32[8,64,128]{2,1,0:T(8,128)S(1)}, s16[8,64,128]{2,1,0:T(8,128)(2,1)S(1)}, s16[7,64,128]{2,1,0:T(8,128)(2,1)S(1)},...) custom-call(f32[64,768]{1,0:T(8,128)S(1)} %get-tuple-element.133.refs_11_.vector.refs_28_, ...), custom_call_target="tpu_custom_call" | custom-call | flops 1000000 | bytes 1917320 | tf_op jit(solution)/shard_map/partials/pallas_call | solution.py:488
  79.4 1.4 collective-permute-start.28
  81.3 2.5 %collective-permute-start.26 = (s16[4,64,128]{2,1,0:T(8,128)(2,1)S(1)}, s16[4,64,128]{2,1,0:T(8,128)(2,1)S(1)}, u32[]{:S(2)}, u32[]{:S(2)}) collective-permute-start(s16[4,64,128]{2,1,0:T(8,128)(2,1)S(1)} %constant_dynamic-update-slice_fusion.2.refs_3_), channel_id=1, source_target_pairs={{0,8},{4,12},{8,0},{12,4},{16,24},{20,28},{24,16},{28,20},{1,9},{5... | collective-permute-start | bytes 196616 | tf_op jit(solution)/shard_map/ppermute | solution.py:522
  83.8 2.4 %collective-permute-done.28.refs_6_ = s16[4,64,128]{2,1,0:T(8,128)(2,1)S(1)} collective-permute-done((s16[4,64,128]{2,1,0:T(8,128)(2,1)S(1)}, s16[4,64,128]{2,1,0:T(8,128)(2,1)S(1)}, u32[]{:S(2)}, u32[]{:S(2)}) %collective-permute-start.28) | collective-permute-done | bytes 65568 | tf_op jit(solution)/shard_map/ppermute | solution.py:522
  86.8 1.7 collective-permute-done.27.refs_5_
  89.4 1.1 collective-permute-start.29
  91.1 1.8 collective-permute-start.31
  94.5 1.2 collective-permute-start.34
  95.7 1.2 collective-permute-done.29.refs_9_
  97.0 1.3 collective-permute-start.35
  98.3 3.3 %update_image.2 = (f32[64,768]{1,0:T(8,128)S(1)}, f32[64,768]{1,0:T(8,128)S(1)}, f32[96,128]{1,0:T(8,128)S(1)}, f32[96,128]{1,0:T(8,128)S(1)}) custom-call(s16[7,64,128]{2,1,0:T(8,128)(2,1)S(1)} %collective-permute-done.22.refs_0_, s16[7,64,128]{2,1,0:T(8,128)(2,1)S(1)} %collective-permute-done.23.refs_1_, ...), custom_call_target="tpu_custom_call" | custom-call | flops 1000000 | bytes 3850632 | tf_op jit(solution)/shard_map/update_image/pallas_call | solution.py:488
  102.7 1.2 collective-permute-done.36
  103.9 1.6 collective-permute-start.39
  105.5 2.8 %collective-permute-start.37 = (f32[96,128]{1,0:T(8,128)S(1)}, f32[96,128]{1,0:T(8,128)S(1)}, u32[]{:S(2)}, u32[]{:S(2)}) collective-permute-start(f32[96,128]{1,0:T(8,128)S(1)} %add.70), channel_id=1, source_target_pairs={{0,8},{4,12},{8,0},{12,4},{16,24},{20,28},{24,16},{28,20},{1,9},{5... | collective-permute-start | bytes 147464 | tf_op jit(solution)/shard_map/ppermute | solution.py:522
  108.4 3.8 %pap_inverse.1.refs_22_ = f32[64,64]{1,0:T(8,128)S(1)} custom-call(f32[192,128]{1,0:T(8,128)S(1)} %get-tuple-element.158.table.refs_20_), custom_call_target="tpu_custom_call" | custom-call | flops 1000000 | bytes 114688 | tf_op jit(solution)/shard_map/pap_inverse/pallas_call | solution.py:488
  112.3 1.2 collective-permute-start.42
  113.5 1.2 collective-permute-start.41
  114.7 1.1 collective-permute-start.40
  115.8 1.8 collective-permute-done.42
  118.8 1.2 collective-permute-done.43.refs_17_
  120.1 11.0 %move.1 = (f32[64,768]{1,0:T(8,128)S(1)}, f32[64,768]{1,0:T(8,128)S(1)}, f32[64,768]{1,0:T(8,128)S(1)}, s16[7,64,128]{2,1,0:T(8,128)(2,1)S(1)}, s16[2,64,128]{2,...) custom-call(f32[128,768]{1,0:T(8,128)S(1)} %get-tuple-element.119.refs_0_, ...), custom_call_target="tpu_custom_call" | custom-call | flops 1000000 | bytes 5114900 | tf_op jit(solution)/shard_map/move/pallas_call | solution.py:488
  132.4 1.6 collective-permute-start.50
  134.0 1.2 collective-permute-start.46
  135.1 1.5 collective-permute-start.45
  138.5 1.8 %collective-permute-start.48 = (s16[4,64,128]{2,1,0:T(8,128)(2,1)S(1)}, s16[4,64,128]{2,1,0:T(8,128)(2,1)S(1)}, u32[]{:S(2)}, u32[]{:S(2)}) collective-permute-start(s16[4,64,128]{2,1,0:T(8,128)(2,1)S(1)} %constant_dynamic-update-slice_fusion.4.refs_3_), channel_id=1, source_target_pairs={{0,8},{4,12},{8,0},{12,4},{16,24},{20,28},{24,16},{28,20},{1,9},{5... | collective-permute-start | bytes 196616 | tf_op jit(solution)/shard_map/ppermute | solution.py:522
  140.3 4.6 %settle.1 = (f32[64,768]{1,0:T(8,128)S(1)}, f32[64,768]{1,0:T(8,128)S(1)}, f32[192,64]{1,0:T(8,128)S(1)}) custom-call(f32[256,64]{1,0:T(8,128)S(1)} %get-tuple-element.169.small, f32[64,768]{1,0:T(8,128)S(1)} %get-tuple-element.170.step_x, f32[64,768]{1,0:T(8,128)S(1)} %get-tuple-element.171.step_a), custom_call_target="tpu_custom_call" | custom-call | flops 1000000 | bytes 901120 | tf_op jit(solution)/shard_map/settle/pallas_call | solution.py:488
  144.9 3.5 %update_image.3 = (f32[64,768]{1,0:T(8,128)}, f32[64,768]{1,0:T(8,128)}, f32[96,128]{1,0:T(8,128)S(1)}, f32[96,128]{1,0:T(8,128)S(1)}) custom-call(s16[7,64,128]{2,1,0:T(8,128)(2,1)S(1)} %collective-permute-done.44.refs_0_, s16[7,64,128]{2,1,0:T(8,128)(2,1)S(1)} %collective-permute-done.45.refs_1_, s16[7,64,128]{2,1,0:T(8,128)(2,1)S(1)} %collective-permute-done.46.refs_2_, ...), custom_call_target="tpu_custom_call" | custom-call | flops 1000000 | bytes 3850632 | tf_op jit(solution)/shard_map/update_image/pallas_call | solution.py:488
  148.4 1.2 collective-permute-done.51
  149.7 1.6 collective-permute-start.54
  151.4 2.7 %collective-permute-start.52 = (f32[96,128]{1,0:T(8,128)S(1)}, f32[96,128]{1,0:T(8,128)S(1)}, u32[]{:S(2)}, u32[]{:S(2)}) collective-permute-start(f32[96,128]{1,0:T(8,128)S(1)} %add.77), channel_id=1, source_target_pairs={{0,8},{4,12},{8,0},{12,4},{16,24},{20,28},{24,16},{28,20},{1,9},{5... | collective-permute-start | bytes 147464 | tf_op jit(solution)/shard_map/ppermute | solution.py:522
  154.1 1.8 %collective-permute-done.54 = f32[96,128]{1,0:T(8,128)S(1)} collective-permute-done((f32[96,128]{1,0:T(8,128)S(1)}, f32[96,128]{1,0:T(8,128)S(1)}, u32[]{:S(2)}, u32[]{:S(2)}) %collective-permute-start.54) | collective-permute-done | bytes 49184 | tf_op jit(solution)/shard_map/ppermute | solution.py:522
  155.9 1.5 collective-permute-done.53
  157.4 1.3 collective-permute-start.57
  158.7 1.4 collective-permute-start.56
  161.0 1.8 %collective-permute-done.57 = f32[96,128]{1,0:T(8,128)S(1)} collective-permute-done((f32[96,128]{1,0:T(8,128)S(1)}, f32[96,128]{1,0:T(8,128)S(1)}, u32[]{:S(2)}, u32[]{:S(2)}) %collective-permute-start.57) | collective-permute-done | bytes 49184 | tf_op jit(solution)/shard_map/ppermute | solution.py:519
  164.3 1.2 collective-permute-done.58.other
  165.5 10.2 %finish.1 = (f32[64,768]{1,0:T(8,128)}, f32[64,768]{1,0:T(8,128)}) custom-call(f32[96,128]{1,0:T(8,128)S(1)} %add_add_fusion.mine, f32[96,128]{1,0:T(8,128)S(1)} %collective-permute-done.58.other, s32[2]{0:T(128)S(1)} %pad_add_fusion.refs_10_.pos.refs_18_, f32[192,64]{1,0:T(8,128)S(1)} %get-tuple-element.177.state, ...), custom_call_target="tpu_custom_call" | custom-call | flops 1000000 | bytes 1130504 | tf_op jit(solution)/shard_map/finish/pallas_call | solution.py:488
  (111 shorter events, 24.8 us)
Async XLA Ops:
  3.1 14.9 %copy-start.8 = (s32[1,1,96]{2,1,0:T(1,128)S(1)}, s32[1,1,96]{2,1,0:T(1,128)}, u32[]{:S(2)}) copy-start(s32[1,1,96]{2,1,0:T(1,128)} %param.14) | copy-start | bytes 1156
  3.2 14.9 %copy-start.9 = (s32[1,1,12]{2,1,0:T(1,128)S(1)}, s32[1,1,12]{2,1,0:T(1,128)}, u32[]{:S(2)}) copy-start(s32[1,1,12]{2,1,0:T(1,128)} %param.17) | copy-start | bytes 148
  3.2 14.9 %copy-start.10 = (s32[1,1,12]{2,1,0:T(1,128)S(1)}, s32[1,1,12]{2,1,0:T(1,128)}, u32[]{:S(2)}) copy-start(s32[1,1,12]{2,1,0:T(1,128)} %param.18) | copy-start | bytes 148
  4.0 3.1 %collective-permute-start.1 = (s16[4,64,128]{2,1,0:T(8,128)(2,1)S(1)}, s16[4,64,128]{2,1,0:T(8,128)(2,1)S(1)}, u32[]{:S(2)}, u32[]{:S(2)}) collective-permute-start(s16[4,64,128]{2,1,0:T(8,128)(2,1)S(1)} %get-tuple-element.92), channel_id=1, source_target_pairs={{0,4},{4,0},{8,12},{12,8},{16,20},{20,16},{24,28},{28,24},{1,5},{5... | collective-permute-start | bytes 196616 | tf_op jit(solution)/shard_map/ppermute | solution.py:522
  4.5 10.2 %collective-permute-start = (s16[14,64,128]{2,1,0:T(8,128)(2,1)S(1)}, s16[14,64,128]{2,1,0:T(8,128)(2,1)S(1)}, u32[]{:S(2)}, u32[]{:S(2)}) collective-permute-start(s16[14,64,128]{2,1,0:T(8,128)(2,1)S(1)} %get-tuple-element.91), channel_id=1, source_target_pairs={{0,1},{1,0},{2,3},{3,2},{4,5},{5,4},{6,7},{7,6},{8,9},{9,8},{10,11... | collective-permute-start | bytes 688136 | tf_op jit(solution)/shard_map/ppermute | solution.py:519
  7.1 7.6 %collective-permute-start.2 = (s16[8,64,128]{2,1,0:T(8,128)(2,1)S(1)}, s16[8,64,128]{2,1,0:T(8,128)(2,1)S(1)}, u32[]{:S(2)}, u32[]{:S(2)}) collective-permute-start(s16[8,64,128]{2,1,0:T(8,128)(2,1)S(1)} %constant_dynamic-update-slice_fusion.refs_3_), channel_id=1, source_target_pairs={{0,24},{4,28},{8,16},{12,20},{16,8},{20,12},{24,0},{28,4},{1,25},{... | collective-permute-start | bytes 393224 | tf_op jit(solution)/shard_map/ppermute | solution.py:522
  24.7 13.3 %collective-permute-start.10 = (s16[16,64,128]{2,1,0:T(8,128)(2,1)S(1)}, s16[16,64,128]{2,1,0:T(8,128)(2,1)S(1)}, u32[]{:S(2)}, u32[]{:S(2)}) collective-permute-start(s16[16,64,128]{2,1,0:T(8,128)(2,1)S(1)} %get-tuple-element.114), channel_id=1, source_target_pairs={{0,4},{4,0},{8,12},{12,8},{16,20},{20,16},{24,28},{28,24},{1,5},{5... | collective-permute-start | bytes 786440 | tf_op jit(solution)/shard_map/ppermute | solution.py:522
  24.8 10.5 %collective-permute-start.6 = (s16[8,64,128]{2,1,0:T(8,128)(2,1)S(1)}, s16[8,64,128]{2,1,0:T(8,128)(2,1)S(1)}, u32[]{:S(2)}, u32[]{:S(2)}) collective-permute-start(s16[8,64,128]{2,1,0:T(8,128)(2,1)S(1)} %constant_dynamic-update-slice_fusion.refs_3_), channel_id=1, source_target_pairs={{0,16},{4,20},{8,24},{12,28},{16,0},{20,4},{24,8},{28,12},{1,17},{... | collective-permute-start | bytes 393224 | tf_op jit(solution)/shard_map/ppermute | solution.py:522
  28.3 8.2 %collective-permute-start.5 = (s16[8,64,128]{2,1,0:T(8,128)(2,1)S(1)}, s16[8,64,128]{2,1,0:T(8,128)(2,1)S(1)}, u32[]{:S(2)}, u32[]{:S(2)}) collective-permute-start(s16[8,64,128]{2,1,0:T(8,128)(2,1)S(1)} %constant_dynamic-update-slice_fusion.refs_3_), channel_id=1, source_target_pairs={{0,8},{4,12},{8,0},{12,4},{16,24},{20,28},{24,16},{28,20},{1,9},{5... | collective-permute-start | bytes 393224 | tf_op jit(solution)/shard_map/ppermute | solution.py:522
  29.0 10.8 %collective-permute-start.4 = (s16[14,64,128]{2,1,0:T(8,128)(2,1)S(1)}, s16[14,64,128]{2,1,0:T(8,128)(2,1)S(1)}, u32[]{:S(2)}, u32[]{:S(2)}) collective-permute-start(s16[14,64,128]{2,1,0:T(8,128)(2,1)S(1)} %get-tuple-element.91), channel_id=1, source_target_pairs={{0,3},{1,2},{2,1},{3,0},{4,7},{5,6},{6,5},{7,4},{8,11},{9,10},{10,... | collective-permute-start | bytes 688136 | tf_op jit(solution)/shard_map/ppermute | solution.py:519
  31.1 11.2 %collective-permute-start.3 = (s16[14,64,128]{2,1,0:T(8,128)(2,1)S(1)}, s16[14,64,128]{2,1,0:T(8,128)(2,1)S(1)}, u32[]{:S(2)}, u32[]{:S(2)}) collective-permute-start(s16[14,64,128]{2,1,0:T(8,128)(2,1)S(1)} %get-tuple-element.91), channel_id=1, source_target_pairs={{0,2},{1,3},{2,0},{3,1},{4,6},{5,7},{6,4},{7,5},{8,10},{9,11},{10,... | collective-permute-start | bytes 688136 | tf_op jit(solution)/shard_map/ppermute | solution.py:519
  35.3 9.8 %collective-permute-start.7 = (s16[14,64,128]{2,1,0:T(8,128)(2,1)S(1)}, s16[14,64,128]{2,1,0:T(8,128)(2,1)S(1)}, u32[]{:S(2)}, u32[]{:S(2)}) collective-permute-start(s16[14,64,128]{2,1,0:T(8,128)(2,1)S(1)} %get-tuple-element.110), channel_id=1, source_target_pairs={{0,1},{1,0},{2,3},{3,2},{4,5},{5,4},{6,7},{7,6},{8,9},{9,8},{10,11... | collective-permute-start | bytes 688136 | tf_op jit(solution)/shard_map/ppermute | solution.py:519
  36.5 15.5 %collective-permute-start.8 = (s16[14,64,128]{2,1,0:T(8,128)(2,1)S(1)}, s16[14,64,128]{2,1,0:T(8,128)(2,1)S(1)}, u32[]{:S(2)}, u32[]{:S(2)}) collective-permute-start(s16[14,64,128]{2,1,0:T(8,128)(2,1)S(1)} %get-tuple-element.111), channel_id=1, source_target_pairs={{0,2},{1,3},{2,0},{3,1},{4,6},{5,7},{6,4},{7,5},{8,10},{9,11},{10,... | collective-permute-start | bytes 688136 | tf_op jit(solution)/shard_map/ppermute | solution.py:519
  38.0 14.0 %collective-permute-start.9 = (s16[14,64,128]{2,1,0:T(8,128)(2,1)S(1)}, s16[14,64,128]{2,1,0:T(8,128)(2,1)S(1)}, u32[]{:S(2)}, u32[]{:S(2)}) collective-permute-start(s16[14,64,128]{2,1,0:T(8,128)(2,1)S(1)} %get-tuple-element.112), channel_id=1, source_target_pairs={{0,3},{1,2},{2,1},{3,0},{4,7},{5,6},{6,5},{7,4},{8,11},{9,10},{10,... | collective-permute-start | bytes 688136 | tf_op jit(solution)/shard_map/ppermute | solution.py:519
  39.8 12.2 %collective-permute-start.11 = (s16[4,64,128]{2,1,0:T(8,128)(2,1)S(1)}, s16[4,64,128]{2,1,0:T(8,128)(2,1)S(1)}, u32[]{:S(2)}, u32[]{:S(2)}) collective-permute-start(s16[4,64,128]{2,1,0:T(8,128)(2,1)S(1)} %get-tuple-element.116), channel_id=1, source_target_pairs={{0,8},{4,12},{8,0},{12,4},{16,24},{20,28},{24,16},{28,20},{1,9},{5... | collective-permute-start | bytes 196616 | tf_op jit(solution)/shard_map/ppermute | solution.py:522
  42.3 9.7 %collective-permute-start.12 = (s16[4,64,128]{2,1,0:T(8,128)(2,1)S(1)}, s16[4,64,128]{2,1,0:T(8,128)(2,1)S(1)}, u32[]{:S(2)}, u32[]{:S(2)}) collective-permute-start(s16[4,64,128]{2,1,0:T(8,128)(2,1)S(1)} %get-tuple-element.117), channel_id=1, source_target_pairs={{0,16},{4,20},{8,24},{12,28},{16,0},{20,4},{24,8},{28,12},{1,17},{... | collective-permute-start | bytes 196616 | tf_op jit(solution)/shard_map/ppermute | solution.py:522
  45.1 6.9 %collective-permute-start.13 = (s16[4,64,128]{2,1,0:T(8,128)(2,1)S(1)}, s16[4,64,128]{2,1,0:T(8,128)(2,1)S(1)}, u32[]{:S(2)}, u32[]{:S(2)}) collective-permute-start(s16[4,64,128]{2,1,0:T(8,128)(2,1)S(1)} %get-tuple-element.118), channel_id=1, source_target_pairs={{0,24},{4,28},{8,16},{12,20},{16,8},{20,12},{24,0},{28,4},{1,25},{... | collective-permute-start | bytes 196616 | tf_op jit(solution)/shard_map/ppermute | solution.py:522
  47.1 21.3 %copy-start.11 = (f32[768]{0:T(1024)S(1)}, f32[768]{0:T(1024)}, u32[]{:S(2)}) copy-start(f32[768]{0:T(1024)} %param.12) | copy-start | bytes 9220
  47.1 22.5 %copy-start.6 = (s32[1,1,3]{2,1,0:T(1,128)S(1)}, s32[1,1,3]{2,1,0:T(1,128)}, u32[]{:S(2)}) copy-start(s32[1,1,3]{2,1,0:T(1,128)} %param.16) | copy-start | bytes 40
  52.1 1.3 collective-permute-start.14
  53.4 6.4 %collective-permute-start.17 = (f32[96,128]{1,0:T(8,128)S(1)}, f32[96,128]{1,0:T(8,128)S(1)}, u32[]{:S(2)}, u32[]{:S(2)}) collective-permute-start(f32[96,128]{1,0:T(8,128)S(1)} %add.63), channel_id=1, source_target_pairs={{0,24},{4,28},{8,16},{12,20},{16,8},{20,12},{24,0},{28,4},{1,25},{... | collective-permute-start | bytes 147464 | tf_op jit(solution)/shard_map/ppermute | solution.py:522
  54.8 6.7 %collective-permute-start.16 = (f32[96,128]{1,0:T(8,128)S(1)}, f32[96,128]{1,0:T(8,128)S(1)}, u32[]{:S(2)}, u32[]{:S(2)}) collective-permute-start(f32[96,128]{1,0:T(8,128)S(1)} %add.63), channel_id=1, source_target_pairs={{0,16},{4,20},{8,24},{12,28},{16,0},{20,4},{24,8},{28,12},{1,17},{... | collective-permute-start | bytes 147464 | tf_op jit(solution)/shard_map/ppermute | solution.py:522
  56.2 5.2 %collective-permute-start.15 = (f32[96,128]{1,0:T(8,128)S(1)}, f32[96,128]{1,0:T(8,128)S(1)}, u32[]{:S(2)}, u32[]{:S(2)}) collective-permute-start(f32[96,128]{1,0:T(8,128)S(1)} %add.63), channel_id=1, source_target_pairs={{0,8},{4,12},{8,0},{12,4},{16,24},{20,28},{24,16},{28,20},{1,9},{5... | collective-permute-start | bytes 147464 | tf_op jit(solution)/shard_map/ppermute | solution.py:522
  61.5 5.1 %collective-permute-start.20 = (f32[96,128]{1,0:T(8,128)S(1)}, f32[96,128]{1,0:T(8,128)S(1)}, u32[]{:S(2)}, u32[]{:S(2)}) collective-permute-start(f32[96,128]{1,0:T(8,128)S(1)} %add_add_fusion.5), channel_id=1, source_target_pairs={{0,3},{1,2},{2,1},{3,0},{4,7},{5,6},{6,5},{7,4},{8,11},{9,10},{10,... | collective-permute-start | bytes 147464 | tf_op jit(solution)/shard_map/ppermute | solution.py:519
  63.3 4.1 %collective-permute-start.19 = (f32[96,128]{1,0:T(8,128)S(1)}, f32[96,128]{1,0:T(8,128)S(1)}, u32[]{:S(2)}, u32[]{:S(2)}) collective-permute-start(f32[96,128]{1,0:T(8,128)S(1)} %add_add_fusion.5), channel_id=1, source_target_pairs={{0,2},{1,3},{2,0},{3,1},{4,6},{5,7},{6,4},{7,5},{8,10},{9,11},{10,... | collective-permute-start | bytes 147464 | tf_op jit(solution)/shard_map/ppermute | solution.py:519
  64.2 4.1 %collective-permute-start.18 = (f32[96,128]{1,0:T(8,128)S(1)}, f32[96,128]{1,0:T(8,128)S(1)}, u32[]{:S(2)}, u32[]{:S(2)}) collective-permute-start(f32[96,128]{1,0:T(8,128)S(1)} %add_add_fusion.5), channel_id=1, source_target_pairs={{0,1},{1,0},{2,3},{3,2},{4,5},{5,4},{6,7},{7,6},{8,9},{9,8},{10,11... | collective-permute-start | bytes 147464 | tf_op jit(solution)/shard_map/ppermute | solution.py:519
  68.3 1.3 collective-permute-start.21
  74.9 4.5 %collective-permute-start.25 = (s16[2,64,128]{2,1,0:T(8,128)(2,1)S(1)}, s16[2,64,128]{2,1,0:T(8,128)(2,1)S(1)}, u32[]{:S(2)}, u32[]{:S(2)}) collective-permute-start(s16[2,64,128]{2,1,0:T(8,128)(2,1)S(1)} %get-tuple-element.132), channel_id=1, source_target_pairs={{0,4},{4,0},{8,12},{12,8},{16,20},{20,16},{24,28},{28,24},{1,5},{5... | collective-permute-start | bytes 98312 | tf_op jit(solution)/shard_map/ppermute | solution.py:522
  75.2 15.4 %collective-permute-start.24 = (s16[7,64,128]{2,1,0:T(8,128)(2,1)S(1)}, s16[7,64,128]{2,1,0:T(8,128)(2,1)S(1)}, u32[]{:S(2)}, u32[]{:S(2)}) collective-permute-start(s16[7,64,128]{2,1,0:T(8,128)(2,1)S(1)} %get-tuple-element.131), channel_id=1, source_target_pairs={{0,3},{1,2},{2,1},{3,0},{4,7},{5,6},{6,5},{7,4},{8,11},{9,10},{10,... | collective-permute-start | bytes 344072 | tf_op jit(solution)/shard_map/ppermute | solution.py:519
  79.2 11.9 %collective-permute-start.32 = (s16[8,64,128]{2,1,0:T(8,128)(2,1)S(1)}, s16[8,64,128]{2,1,0:T(8,128)(2,1)S(1)}, u32[]{:S(2)}, u32[]{:S(2)}) collective-permute-start(s16[8,64,128]{2,1,0:T(8,128)(2,1)S(1)} %get-tuple-element.143), channel_id=1, source_target_pairs={{0,4},{4,0},{8,12},{12,8},{16,20},{20,16},{24,28},{28,24},{1,5},{5... | collective-permute-start | bytes 393224 | tf_op jit(solution)/shard_map/ppermute | solution.py:522
  79.4 6.9 %collective-permute-start.28 = (s16[4,64,128]{2,1,0:T(8,128)(2,1)S(1)}, s16[4,64,128]{2,1,0:T(8,128)(2,1)S(1)}, u32[]{:S(2)}, u32[]{:S(2)}) collective-permute-start(s16[4,64,128]{2,1,0:T(8,128)(2,1)S(1)} %constant_dynamic-update-slice_fusion.2.refs_3_), channel_id=1, source_target_pairs={{0,24},{4,28},{8,16},{12,20},{16,8},{20,12},{24,0},{28,4},{1,25},{... | collective-permute-start | bytes 196616 | tf_op jit(solution)/shard_map/ppermute | solution.py:522
  80.8 7.7 %collective-permute-start.27 = (s16[4,64,128]{2,1,0:T(8,128)(2,1)S(1)}, s16[4,64,128]{2,1,0:T(8,128)(2,1)S(1)}, u32[]{:S(2)}, u32[]{:S(2)}) collective-permute-start(s16[4,64,128]{2,1,0:T(8,128)(2,1)S(1)} %constant_dynamic-update-slice_fusion.2.refs_3_), channel_id=1, source_target_pairs={{0,16},{4,20},{8,24},{12,28},{16,0},{20,4},{24,8},{28,12},{1,17},{... | collective-permute-start | bytes 196616 | tf_op jit(solution)/shard_map/ppermute | solution.py:522
  81.3 8.0 %collective-permute-start.26 = (s16[4,64,128]{2,1,0:T(8,128)(2,1)S(1)}, s16[4,64,128]{2,1,0:T(8,128)(2,1)S(1)}, u32[]{:S(2)}, u32[]{:S(2)}) collective-permute-start(s16[4,64,128]{2,1,0:T(8,128)(2,1)S(1)} %constant_dynamic-update-slice_fusion.2.refs_3_), channel_id=1, source_target_pairs={{0,8},{4,12},{8,0},{12,4},{16,24},{20,28},{24,16},{28,20},{1,9},{5... | collective-permute-start | bytes 196616 | tf_op jit(solution)/shard_map/ppermute | solution.py:522
  86.2 7.5 %collective-permute-start.23 = (s16[7,64,128]{2,1,0:T(8,128)(2,1)S(1)}, s16[7,64,128]{2,1,0:T(8,128)(2,1)S(1)}, u32[]{:S(2)}, u32[]{:S(2)}) collective-permute-start(s16[7,64,128]{2,1,0:T(8,128)(2,1)S(1)} %get-tuple-element.131), channel_id=1, source_target_pairs={{0,2},{1,3},{2,0},{3,1},{4,6},{5,7},{6,4},{7,5},{8,10},{9,11},{10,... | collective-permute-start | bytes 344072 | tf_op jit(solution)/shard_map/ppermute | solution.py:519
  88.5 6.0 %collective-permute-start.22 = (s16[7,64,128]{2,1,0:T(8,128)(2,1)S(1)}, s16[7,64,128]{2,1,0:T(8,128)(2,1)S(1)}, u32[]{:S(2)}, u32[]{:S(2)}) collective-permute-start(s16[7,64,128]{2,1,0:T(8,128)(2,1)S(1)} %get-tuple-element.131), channel_id=1, source_target_pairs={{0,1},{1,0},{2,3},{3,2},{4,5},{5,4},{6,7},{7,6},{8,9},{9,8},{10,11... | collective-permute-start | bytes 344072 | tf_op jit(solution)/shard_map/ppermute | solution.py:519
  89.4 7.6 %collective-permute-start.29 = (s16[7,64,128]{2,1,0:T(8,128)(2,1)S(1)}, s16[7,64,128]{2,1,0:T(8,128)(2,1)S(1)}, u32[]{:S(2)}, u32[]{:S(2)}) collective-permute-start(s16[7,64,128]{2,1,0:T(8,128)(2,1)S(1)} %get-tuple-element.139), channel_id=1, source_target_pairs={{0,1},{1,0},{2,3},{3,2},{4,5},{5,4},{6,7},{7,6},{8,9},{9,8},{10,11... | collective-permute-start | bytes 344072 | tf_op jit(solution)/shard_map/ppermute | solution.py:519
  90.5 11.1 %collective-permute-start.30 = (s16[7,64,128]{2,1,0:T(8,128)(2,1)S(1)}, s16[7,64,128]{2,1,0:T(8,128)(2,1)S(1)}, u32[]{:S(2)}, u32[]{:S(2)}) collective-permute-start(s16[7,64,128]{2,1,0:T(8,128)(2,1)S(1)} %get-tuple-element.140), channel_id=1, source_target_pairs={{0,2},{1,3},{2,0},{3,1},{4,6},{5,7},{6,4},{7,5},{8,10},{9,11},{10,... | collective-permute-start | bytes 344072 | tf_op jit(solution)/shard_map/ppermute | solution.py:519
  91.1 10.5 %collective-permute-start.31 = (s16[7,64,128]{2,1,0:T(8,128)(2,1)S(1)}, s16[7,64,128]{2,1,0:T(8,128)(2,1)S(1)}, u32[]{:S(2)}, u32[]{:S(2)}) collective-permute-start(s16[7,64,128]{2,1,0:T(8,128)(2,1)S(1)} %get-tuple-element.141), channel_id=1, source_target_pairs={{0,3},{1,2},{2,1},{3,0},{4,7},{5,6},{6,5},{7,4},{8,11},{9,10},{10,... | collective-permute-start | bytes 344072 | tf_op jit(solution)/shard_map/ppermute | solution.py:519
  93.7 7.9 %collective-permute-start.33 = (s16[2,64,128]{2,1,0:T(8,128)(2,1)S(1)}, s16[2,64,128]{2,1,0:T(8,128)(2,1)S(1)}, u32[]{:S(2)}, u32[]{:S(2)}) collective-permute-start(s16[2,64,128]{2,1,0:T(8,128)(2,1)S(1)} %get-tuple-element.145), channel_id=1, source_target_pairs={{0,8},{4,12},{8,0},{12,4},{16,24},{20,28},{24,16},{28,20},{1,9},{5... | collective-permute-start | bytes 98312 | tf_op jit(solution)/shard_map/ppermute | solution.py:522
  94.5 7.2 %collective-permute-start.34 = (s16[2,64,128]{2,1,0:T(8,128)(2,1)S(1)}, s16[2,64,128]{2,1,0:T(8,128)(2,1)S(1)}, u32[]{:S(2)}, u32[]{:S(2)}) collective-permute-start(s16[2,64,128]{2,1,0:T(8,128)(2,1)S(1)} %get-tuple-element.146), channel_id=1, source_target_pairs={{0,16},{4,20},{8,24},{12,28},{16,0},{20,4},{24,8},{28,12},{1,17},{... | collective-permute-start | bytes 98312 | tf_op jit(solution)/shard_map/ppermute | solution.py:522
  97.0 5.7 %collective-permute-start.35 = (s16[2,64,128]{2,1,0:T(8,128)(2,1)S(1)}, s16[2,64,128]{2,1,0:T(8,128)(2,1)S(1)}, u32[]{:S(2)}, u32[]{:S(2)}) collective-permute-start(s16[2,64,128]{2,1,0:T(8,128)(2,1)S(1)} %get-tuple-element.147), channel_id=1, source_target_pairs={{0,24},{4,28},{8,16},{12,20},{16,8},{20,12},{24,0},{28,4},{1,25},{... | collective-permute-start | bytes 98312 | tf_op jit(solution)/shard_map/ppermute | solution.py:522
  102.7 1.2 collective-permute-start.36
  103.9 8.3 %collective-permute-start.39 = (f32[96,128]{1,0:T(8,128)S(1)}, f32[96,128]{1,0:T(8,128)S(1)}, u32[]{:S(2)}, u32[]{:S(2)}) collective-permute-start(f32[96,128]{1,0:T(8,128)S(1)} %add.70), channel_id=1, source_target_pairs={{0,24},{4,28},{8,16},{12,20},{16,8},{20,12},{24,0},{28,4},{1,25},{... | collective-permute-start | bytes 147464 | tf_op jit(solution)/shard_map/ppermute | solution.py:522
  105.5 6.7 %collective-permute-start.38 = (f32[96,128]{1,0:T(8,128)S(1)}, f32[96,128]{1,0:T(8,128)S(1)}, u32[]{:S(2)}, u32[]{:S(2)}) collective-permute-start(f32[96,128]{1,0:T(8,128)S(1)} %add.70), channel_id=1, source_target_pairs={{0,16},{4,20},{8,24},{12,28},{16,0},{20,4},{24,8},{28,12},{1,17},{... | collective-permute-start | bytes 147464 | tf_op jit(solution)/shard_map/ppermute | solution.py:522
  105.5 6.7 %collective-permute-start.37 = (f32[96,128]{1,0:T(8,128)S(1)}, f32[96,128]{1,0:T(8,128)S(1)}, u32[]{:S(2)}, u32[]{:S(2)}) collective-permute-start(f32[96,128]{1,0:T(8,128)S(1)} %add.70), channel_id=1, source_target_pairs={{0,8},{4,12},{8,0},{12,4},{16,24},{20,28},{24,16},{28,20},{1,9},{5... | collective-permute-start | bytes 147464 | tf_op jit(solution)/shard_map/ppermute | solution.py:522
  112.3 5.3 %collective-permute-start.42 = (f32[96,128]{1,0:T(8,128)S(1)}, f32[96,128]{1,0:T(8,128)S(1)}, u32[]{:S(2)}, u32[]{:S(2)}) collective-permute-start(f32[96,128]{1,0:T(8,128)S(1)} %add_add_fusion.3), channel_id=1, source_target_pairs={{0,3},{1,2},{2,1},{3,0},{4,7},{5,6},{6,5},{7,4},{8,11},{9,10},{10,... | collective-permute-start | bytes 147464 | tf_op jit(solution)/shard_map/ppermute | solution.py:519
  113.5 4.4 %collective-permute-start.41 = (f32[96,128]{1,0:T(8,128)S(1)}, f32[96,128]{1,0:T(8,128)S(1)}, u32[]{:S(2)}, u32[]{:S(2)}) collective-permute-start(f32[96,128]{1,0:T(8,128)S(1)} %add_add_fusion.3), channel_id=1, source_target_pairs={{0,2},{1,3},{2,0},{3,1},{4,6},{5,7},{6,4},{7,5},{8,10},{9,11},{10,... | collective-permute-start | bytes 147464 | tf_op jit(solution)/shard_map/ppermute | solution.py:519
  114.7 4.1 %collective-permute-start.40 = (f32[96,128]{1,0:T(8,128)S(1)}, f32[96,128]{1,0:T(8,128)S(1)}, u32[]{:S(2)}, u32[]{:S(2)}) collective-permute-start(f32[96,128]{1,0:T(8,128)S(1)} %add_add_fusion.3), channel_id=1, source_target_pairs={{0,1},{1,0},{2,3},{3,2},{4,5},{5,4},{6,7},{7,6},{8,9},{9,8},{10,11... | collective-permute-start | bytes 147464 | tf_op jit(solution)/shard_map/ppermute | solution.py:519
  118.8 1.3 collective-permute-start.43
  131.1 1.3 collective-permute-start.47
  132.4 6.1 %collective-permute-start.50 = (s16[4,64,128]{2,1,0:T(8,128)(2,1)S(1)}, s16[4,64,128]{2,1,0:T(8,128)(2,1)S(1)}, u32[]{:S(2)}, u32[]{:S(2)}) collective-permute-start(s16[4,64,128]{2,1,0:T(8,128)(2,1)S(1)} %constant_dynamic-update-slice_fusion.4.refs_3_), channel_id=1, source_target_pairs={{0,24},{4,28},{8,16},{12,20},{16,8},{20,12},{24,0},{28,4},{1,25},{... | collective-permute-start | bytes 196616 | tf_op jit(solution)/shard_map/ppermute | solution.py:522
  134.0 11.0 %collective-permute-start.46 = (s16[7,64,128]{2,1,0:T(8,128)(2,1)S(1)}, s16[7,64,128]{2,1,0:T(8,128)(2,1)S(1)}, u32[]{:S(2)}, u32[]{:S(2)}) collective-permute-start(s16[7,64,128]{2,1,0:T(8,128)(2,1)S(1)} %get-tuple-element.165), channel_id=1, source_target_pairs={{0,3},{1,2},{2,1},{3,0},{4,7},{5,6},{6,5},{7,4},{8,11},{9,10},{10,... | collective-permute-start | bytes 344072 | tf_op jit(solution)/shard_map/ppermute | solution.py:519
  135.1 9.8 %collective-permute-start.45 = (s16[7,64,128]{2,1,0:T(8,128)(2,1)S(1)}, s16[7,64,128]{2,1,0:T(8,128)(2,1)S(1)}, u32[]{:S(2)}, u32[]{:S(2)}) collective-permute-start(s16[7,64,128]{2,1,0:T(8,128)(2,1)S(1)} %get-tuple-element.165), channel_id=1, source_target_pairs={{0,2},{1,3},{2,0},{3,1},{4,6},{5,7},{6,4},{7,5},{8,10},{9,11},{10,... | collective-permute-start | bytes 344072 | tf_op jit(solution)/shard_map/ppermute | solution.py:519
  136.6 8.3 %collective-permute-start.44 = (s16[7,64,128]{2,1,0:T(8,128)(2,1)S(1)}, s16[7,64,128]{2,1,0:T(8,128)(2,1)S(1)}, u32[]{:S(2)}, u32[]{:S(2)}) collective-permute-start(s16[7,64,128]{2,1,0:T(8,128)(2,1)S(1)} %get-tuple-element.165), channel_id=1, source_target_pairs={{0,1},{1,0},{2,3},{3,2},{4,5},{5,4},{6,7},{7,6},{8,9},{9,8},{10,11... | collective-permute-start | bytes 344072 | tf_op jit(solution)/shard_map/ppermute | solution.py:519
  137.4 7.5 %collective-permute-start.49 = (s16[4,64,128]{2,1,0:T(8,128)(2,1)S(1)}, s16[4,64,128]{2,1,0:T(8,128)(2,1)S(1)}, u32[]{:S(2)}, u32[]{:S(2)}) collective-permute-start(s16[4,64,128]{2,1,0:T(8,128)(2,1)S(1)} %constant_dynamic-update-slice_fusion.4.refs_3_), channel_id=1, source_target_pairs={{0,16},{4,20},{8,24},{12,28},{16,0},{20,4},{24,8},{28,12},{1,17},{... | collective-permute-start | bytes 196616 | tf_op jit(solution)/shard_map/ppermute | solution.py:522
  138.5 6.4 %collective-permute-start.48 = (s16[4,64,128]{2,1,0:T(8,128)(2,1)S(1)}, s16[4,64,128]{2,1,0:T(8,128)(2,1)S(1)}, u32[]{:S(2)}, u32[]{:S(2)}) collective-permute-start(s16[4,64,128]{2,1,0:T(8,128)(2,1)S(1)} %constant_dynamic-update-slice_fusion.4.refs_3_), channel_id=1, source_target_pairs={{0,8},{4,12},{8,0},{12,4},{16,24},{20,28},{24,16},{28,20},{1,9},{5... | collective-permute-start | bytes 196616 | tf_op jit(solution)/shard_map/ppermute | solution.py:522
  148.4 1.2 collective-permute-start.51
  149.7 6.3 %collective-permute-start.54 = (f32[96,128]{1,0:T(8,128)S(1)}, f32[96,128]{1,0:T(8,128)S(1)}, u32[]{:S(2)}, u32[]{:S(2)}) collective-permute-start(f32[96,128]{1,0:T(8,128)S(1)} %add.77), channel_id=1, source_target_pairs={{0,24},{4,28},{8,16},{12,20},{16,8},{20,12},{24,0},{28,4},{1,25},{... | collective-permute-start | bytes 147464 | tf_op jit(solution)/shard_map/ppermute | solution.py:522
  151.3 6.1 %collective-permute-start.53 = (f32[96,128]{1,0:T(8,128)S(1)}, f32[96,128]{1,0:T(8,128)S(1)}, u32[]{:S(2)}, u32[]{:S(2)}) collective-permute-start(f32[96,128]{1,0:T(8,128)S(1)} %add.77), channel_id=1, source_target_pairs={{0,16},{4,20},{8,24},{12,28},{16,0},{20,4},{24,8},{28,12},{1,17},{... | collective-permute-start | bytes 147464 | tf_op jit(solution)/shard_map/ppermute | solution.py:522
  151.4 6.0 %collective-permute-start.52 = (f32[96,128]{1,0:T(8,128)S(1)}, f32[96,128]{1,0:T(8,128)S(1)}, u32[]{:S(2)}, u32[]{:S(2)}) collective-permute-start(f32[96,128]{1,0:T(8,128)S(1)} %add.77), channel_id=1, source_target_pairs={{0,8},{4,12},{8,0},{12,4},{16,24},{20,28},{24,16},{28,20},{1,9},{5... | collective-permute-start | bytes 147464 | tf_op jit(solution)/shard_map/ppermute | solution.py:522
  157.4 5.3 %collective-permute-start.57 = (f32[96,128]{1,0:T(8,128)S(1)}, f32[96,128]{1,0:T(8,128)S(1)}, u32[]{:S(2)}, u32[]{:S(2)}) collective-permute-start(f32[96,128]{1,0:T(8,128)S(1)} %add_add_fusion.1), channel_id=1, source_target_pairs={{0,3},{1,2},{2,1},{3,0},{4,7},{5,6},{6,5},{7,4},{8,11},{9,10},{10,... | collective-permute-start | bytes 147464 | tf_op jit(solution)/shard_map/ppermute | solution.py:519
  158.7 4.4 %collective-permute-start.56 = (f32[96,128]{1,0:T(8,128)S(1)}, f32[96,128]{1,0:T(8,128)S(1)}, u32[]{:S(2)}, u32[]{:S(2)}) collective-permute-start(f32[96,128]{1,0:T(8,128)S(1)} %add_add_fusion.1), channel_id=1, source_target_pairs={{0,2},{1,3},{2,0},{3,1},{4,6},{5,7},{6,4},{7,5},{8,10},{9,11},{10,... | collective-permute-start | bytes 147464 | tf_op jit(solution)/shard_map/ppermute | solution.py:519
  160.1 4.1 %collective-permute-start.55 = (f32[96,128]{1,0:T(8,128)S(1)}, f32[96,128]{1,0:T(8,128)S(1)}, u32[]{:S(2)}, u32[]{:S(2)}) collective-permute-start(f32[96,128]{1,0:T(8,128)S(1)} %add_add_fusion.1), channel_id=1, source_target_pairs={{0,1},{1,0},{2,3},{3,2},{4,5},{5,4},{6,7},{7,6},{8,9},{9,8},{10,11... | collective-permute-start | bytes 147464 | tf_op jit(solution)/shard_map/ppermute | solution.py:519
  164.2 1.3 collective-permute-start.58
  (7 other events, 46.3 us)

commit v6 on v5

--- a/solution.py
+++ b/solution.py
@@ -104,7 +104,7 @@
         edge[place * edge_tiles(ifr) + t] = jnp.where(low, slots[2 * t], slots[2 * t + 1]).astype(jnp.int16)
 
 
-def fill_halo(vector, wires, edges, pos, halo, ifr, place=0, places=1):
+def fill_halo(vector, wires, edges, pos, halo, ifr, place=0, base=0):
     width = halo.shape[2]
     count = vector.shape[1] // width
     lb = 2 * count
@@ -115,17 +115,17 @@
         halo[pos[0] * lb + 2 * t + 1] = two
     for k, wire in enumerate(wires):
         start = (pos[0] ^ (k + 1)) * lb
-        base = place * (count + 1)
-        step = step_of(wire[base + count])
+        spot = base + place * (count + 1)
+        step = step_of(wire[spot + count])
         for t in range(count):
-            one, two = two_blocks(decode(wire[base + t], step))
+            one, two = two_blocks(decode(wire[spot + t], step))
             halo[start + 2 * t] = one
             halo[start + 2 * t + 1] = two
     tiles = edge_tiles(ifr)
-    for k, edge in enumerate(edges):
-        for other in range(2):
+    for k, pair in enumerate(edges):
+        for other, (edge, spot) in enumerate(pair):
             start = n_row * lb + (((pos[1] // 2) ^ k) * 2 + ((pos[1] % 2) ^ other)) * ifr
-            found = decode_edge(edge, (other * places + place) * tiles, ifr)
+            found = decode_edge(edge, spot + place * tiles, ifr)
             for q in range(0, ifr, 2):
                 blocks = two_blocks(found[q // 2])
                 halo[start + q] = blocks[0]
@@ -276,10 +276,11 @@
     write_wire(p, bnd, wire, edge, 1)
 
 
-def partial_kernel(n_row, n_z, merge, ifr, vector, joined, where, pos, *refs):
+def partial_kernel(n_row, n_z, merge, extra, ifr, vector, joined, where, pos, *refs):
     refs = list(refs)
     parts = n_row + 2
     earlier = [refs.pop(0) for _ in range(parts)] if merge else []
+    more = [refs.pop(0) for _ in range(2)] if extra else []
     outs, acc = refs[:-1], refs[-1]
     own, core_keep, core_send, *row_outs = outs
     width = acc.shape[2]
@@ -337,11 +338,21 @@
             else:
                 for t, tile in enumerate(code_edge(found, ifr)):
                     core_send[spot + t] = tile
-
-
-def pair_kernel(n_z, count, ifr, keep, got, pos, own, *outs):
+    if extra:
+        for row_out in row_outs:
+            row_out[pl.ds(count + 1, count + 1)] = more[0][...]
+        core_send[pl.ds(n_z * tiles, tiles)] = more[1][...]
+
+
+def pair_kernel(n_z, count, extra, ifr, keep, got, pos, *refs):
+    refs = list(refs)
+    more = refs.pop(0) if extra else None
+    own, outs = refs[0], refs[1:]
     tiles = edge_tiles(ifr)
     for k in range(n_z):
+        if extra and k > 0:
+            outs[k - 1][pl.ds(count * tiles, tiles)] = more[...]
+            outs[k - 1][pl.ds((count + 1) * tiles, tiles)] = got[pl.ds(count * n_z * tiles, tiles)]
         z = (pos[1] // 2) ^ k
         for v in range(count):
             spot = (v * n_z + z) * tiles
@@ -355,7 +366,20 @@
 
 
 def split_halo(refs, n_row, n_z):
-    return [refs.pop(0) for _ in range(n_row - 1)], [refs.pop(0) for _ in range(n_z)]
+    wires = [refs.pop(0) for _ in range(n_row - 1)]
+    edges = [refs.pop(0) for _ in range(n_z)]
+    return wires, [((edge, 0), (edge, edge.shape[0] // 2)) for edge in edges]
+
+
+def split_merged(refs, n_row, n_z, ifr):
+    wires = [refs.pop(0) for _ in range(n_row - 1)]
+    edge, core_got = refs.pop(0), refs.pop(0)
+    tiles = edge_tiles(ifr)
+    edges = [((edge, 0), (core_got, n_z * tiles))]
+    for _ in range(n_z - 1):
+        got = refs.pop(0)
+        edges.append(((got, tiles), (got, 2 * tiles)))
+    return wires, edges
 
 
 def start_image_kernel(n_row, n_z, ifr, *refs):
@@ -364,7 +388,7 @@
     stored, diagonal, where, pos, x, p, half_x, diag_x, half_p, diag_p, keep, send, halo_x, halo_p, table = refs
     n = x.shape[0]
     for place, (vector, half, diag, halo) in enumerate(((x, half_x, diag_x, halo_x), (p, half_p, diag_p, halo_p))):
-        fill_halo(vector, wires, edges, pos, halo, ifr, place, 2)
+        fill_halo(vector, wires, edges, pos, halo, ifr, place)
         forward(halo, pos, stored, diagonal, where, half, diag)
         half[...] = half[...] + 0.5 * diag[...]
     table[0:n, :] = nt(x[...], jnp.concatenate([half_x[...], x[...]], axis=0))
@@ -405,10 +429,10 @@
 
 def update_image_kernel(n_row, n_z, ifr, first, *refs):
     refs = list(refs)
-    wires, edges = split_halo(refs, n_row, n_z)
+    wires, edges = split_merged(refs, n_row, n_z, ifr) if first else split_halo(refs, n_row, n_z)
     stored, diagonal, where, pos, w, x, p, ax, ap, half, diag, keep, send, halo, table = refs
     n = w.shape[0]
-    fill_halo(w, wires, edges, pos, halo, ifr)
+    fill_halo(w, wires, edges, pos, halo, ifr, 0, w.shape[1] // halo.shape[2] + 1 if first else 0)
     forward(halo, pos, stored, diagonal, where, half, diag)
     half[...] = half[...] + 0.5 * diag[...]
     here = w[...]
@@ -552,31 +576,33 @@
         total = groups_of_four(total, n_row, row_send)
         return [total, sub_send(total, 1)], meanwhile
 
-    def partials(source, earlier=()):
+    def partials(source, earlier=(), more=()):
         m = 2 if earlier else 1
-        outs = [shaped(m * n, rows), shaped(m * n_z * edges_in, n, 2 * kb), coded(m * n_z * edges_in)]
-        outs += [coded(m * (tiles + 1))] * (n_row - 1)
+        e = 1 if more else 0
+        outs = [shaped(m * n, rows), shaped(m * n_z * edges_in, n, 2 * kb), coded((m * n_z + e) * edges_in)]
+        outs += [coded((m + e) * (tiles + 1))] * (n_row - 1)
         return run(
-            functools.partial(partial_kernel, n_row, n_z, m > 1, ifr),
+            functools.partial(partial_kernel, n_row, n_z, m > 1, e > 0, ifr),
             "partials",
             outs,
-            [source, joined, where, pos] + list(earlier),
+            [source, joined, where, pos] + list(earlier) + list(more),
             [VMEM((halo_blocks, n, 2 * kb), f32)],
             smem=(2, 3),
         )
 
-    def send_partials(parts, m):
+    def send_partials(parts, m, more=()):
         own, edge_keep, edge_send, *row_parts = parts
+        e = 1 if more else 0
         edge_got = sub_send(edge_send, 1)
         rows_got = [row_send(row_parts[k - 1], k) for k in range(1, n_row)]
         edge_own, *outs = run(
-            functools.partial(pair_kernel, n_z, m, ifr),
+            functools.partial(pair_kernel, n_z, m, e > 0, ifr),
             "pair",
-            [shaped(m * edges_in, n, 2 * kb)] + [coded(m * edges_in)] * (n_z - 1),
-            [edge_keep, edge_got, pos],
+            [shaped(m * edges_in, n, 2 * kb)] + [coded((m + 2 * e) * edges_in)] * (n_z - 1),
+            [edge_keep, edge_got, pos] + list(more),
             smem=(2,),
         )
-        return [own] + rows_got + [edge_own] + [z_send(outs[k - 1], k) for k in range(1, n_z)]
+        return [own] + rows_got + [edge_own] + [z_send(outs[k - 1], k) for k in range(1, n_z)], edge_got
 
     x, p = modes.T, search.T
     scaling = precond.reshape(1, rows)
@@ -597,6 +623,7 @@
         smem=(2, 3, 4, 5),
         smem_outs=(3,),
     )
+    joined, *halo = after((joined, *halo))
     parts = partials(p, partials(x))
     blocks = [stored, diagonal, where, pos]
     halo_scratch = VMEM((halo_blocks, n, 2 * kb), bf16)
@@ -615,7 +642,7 @@
         [halo_scratch, halo_scratch, table_scratch],
         smem=(count + 2, count + 3),
     )
-    start_back = send_partials(parts, 2)
+    start_back, _ = send_partials(parts, 2)
     keep, send, *start_back = after((keep, send, *start_back))
     halves, _ = sum_halves(keep, send)
     count = len(start_back)
@@ -627,9 +654,9 @@
         [back_scratch],
         smem=(count + 2, count + 3),
     )
-    w_halo = halo_of(w_wire, w_edge)
     (pap_inverse,) = run(inverse_kernel, "pap_inverse", [shaped(n, n)], [table])
-    w_back = send_partials(partials(w), 1)
+    w_back, core_got = send_partials(partials(w, more=[w_wire, w_edge]), 1, [w_edge])
+    w_halo = w_back[1:n_row] + [w_edge, core_got] + w_back[n_row + 1 :]
 
     def update_image(first, halo, w, x, p, ax, ap):
         count = len(halo)
@@ -643,7 +670,6 @@
         )
 
     half_w, diag_w, keep, send = update_image(True, w_halo, w, x, p, ax, half_p)
-    keep, send, *w_back = after((keep, send, *w_back))
     halves, (pap_inverse,) = sum_halves(keep, send, [pap_inverse])
     count = len(start_back) + len(w_back)
     x, ax, w, w_wire, w_edge, step_x, step_a, small = run(

time: 176 us -> 164 us (0.932)
  waiting for transfers between devices: 42.4 us -> 34.4 us
  starting transfers between devices: 68.4 us -> 64 us
    ppermute x35 -> x31, waiting for transfers between devices: 28.8 us -> 18.7 us  [sub_send(): return lax.ppermute(value, 'sub', [(s, s ^ k) for s in range(n_sub)])]
    ppermute x24 -> x21, starting transfers between devices: 29.5 us -> 24.7 us  [row_send(): return lax.ppermute(value, 'row', [(r, r ^ k) for r in range(n_row)])]
    ppermute x24 -> x21, waiting for transfers between devices: 13.5 us -> 15.7 us  [row_send(): return lax.ppermute(value, 'row', [(r, r ^ k) for r in range(n_row)])]
    ppermute x35 -> x31, starting transfers between devices: 38.9 us -> 39.3 us  [sub_send(): return lax.ppermute(value, 'sub', [(s, s ^ k) for s in range(n_sub)])]
  transfers between devices with their start and end apart: 59 -> 52, of which waited for: 30 -> 28; matrix products, arithmetic and copies ran while one was open for 0% -> 2% of each run, Pallas kernels for 12% -> 10%
where the time goes in v6:
time: 164 us; the launch traced here: 163 us
  starting transfers between devices  64 us (39%)
  Pallas kernels  57.9 us (35%)
  waiting for transfers between devices  34.4 us (21%)
  local copies, waits for them, and re-layouts  5.87 us (4%)
    pallas_call x15, Pallas kernels, run(): pl.pallas_call(kernel, name=name, out_shape=outs, in_specs=in_specs, out_...  57.9 us
    ppermute x31, starting transfers between devices, sub_send(): return lax.ppermute(value, 'sub', [(s, s ^ k) for s in range(n_sub)])  39.3 us
    ppermute x21, starting transfers between devices, row_send(): return lax.ppermute(value, 'row', [(r, r ^ k) for r in range(n_row)])  24.7 us
    ppermute x31, waiting for transfers between devices, sub_send(): return lax.ppermute(value, 'sub', [(s, s ^ k) for s in range(n_sub)])  18.7 us
    ppermute x21, waiting for transfers between devices, row_send(): return lax.ppermute(value, 'row', [(r, r ^ k) for r in range(n_row)])  15.7 us
    optimization_barrier x1, local copies, waits for them, and re-layouts, local(): after((in_val, if_val, halo[0], halo[-1]))  3.29 us
  transfers between devices with their start and end apart: 52, of which 28 were waited for; matrix products, arithmetic and copies ran while one was open for 2% of the time, Pallas kernels for 10%

profile of v6, /device:TPU:0, one launch (start us, length us, event | category | flops | bytes accessed | tf_op | source)
XLA Modules:
  0.0 163.3 jit_solution(13812149951211376573)
XLA Ops:
  0.6 0.9 copy-done
  1.6 0.9 copy-done.2
  4.5 0.9 collective-permute-done.1
  5.4 5.0 %collective-permute-start.2 = (s16[8,64,128]{2,1,0:T(8,128)(2,1)S(1)}, s16[8,64,128]{2,1,0:T(8,128)(2,1)S(1)}, u32[]{:S(2)}, u32[]{:S(2)}) collective-permute-start(s16[8,64,128]{2,1,0:T(8,128)(2,1)S(1)} %constant_dynamic-update-slice_fusion.refs_3_), channel_id=1, source_target_pairs={{0,24},{4,28},{8,16},{12,20},{16,8},{20,12},{24,0},{28,4},{1,25},{... | collective-permute-start | bytes 393224 | tf_op jit(solution)/shard_map/ppermute | solution.py:546
  10.5 1.5 collective-permute-start
  12.0 1.5 collective-permute-start.4
  14.4 5.8 %collective-permute-start.5 = (s16[8,64,128]{2,1,0:T(8,128)(2,1)S(1)}, s16[8,64,128]{2,1,0:T(8,128)(2,1)S(1)}, u32[]{:S(2)}, u32[]{:S(2)}) collective-permute-start(s16[8,64,128]{2,1,0:T(8,128)(2,1)S(1)} %constant_dynamic-update-slice_fusion.refs_3_), channel_id=1, source_target_pairs={{0,8},{4,12},{8,0},{12,4},{16,24},{20,28},{24,16},{28,20},{1,9},{5... | collective-permute-start | bytes 393224 | tf_op jit(solution)/shard_map/ppermute | solution.py:546
  20.3 3.3 %copy.12 = bf16[1,1,96,64,64]{4,3,2,1,0:T(8,128)(2,1)S(1)} copy(bf16[1,1,96,64,64]{2,4,3,1,0:T(8,128)(2,1)} %param.15) | data formatting | bytes 1572864 | tf_op jit(solution)/shard_map/optimization_barrier | solution.py:612
  23.7 2.2 %prepare.1 = (bf16[12,64,1024]{2,1,0:T(8,128)(2,1)S(1)}, bf16[12,64,512]{2,1,0:T(8,128)(2,1)S(1)}, bf16[12,64,128]{2,1,0:T(8,128)(2,1)S(1)}, s32[96]{0:T(128)S(1)}) custom-call(bf16[96,64,64]{2,1,0:T(8,128)(2,1)S(1)} %bitcast.19, bf16[12,64,64]{2,1,0:T(8,128)(2,1)S(1)} %bitcast.25, s32[96]{0:T(128)S(1)} %bitcast.29, s32[96]{0:T(128)S(1)} %bitcast.30, ...), custom_call_target="tpu_custom_call" | custom-call | flops 1000000 | bytes 3441888 | tf_op jit(solution)/shard_map/prepare/pallas_call | solution.py:512
  25.9 2.2 %partials.3 = (f32[64,768]{1,0:T(8,128)S(1)}, f32[8,64,128]{2,1,0:T(8,128)S(1)}, s16[8,64,128]{2,1,0:T(8,128)(2,1)S(1)}, s16[7,64,128]{2,1,0:T(8,128)(2,1)S(1)},...) custom-call(f32[64,768]{1,0:T(8,128)S(1)} %bitcast.14, ...), custom_call_target="tpu_custom_call" | custom-call | flops 1000000 | bytes 1917320 | tf_op jit(solution)/shard_map/partials/pallas_call | solution.py:512
  28.1 2.2 %partials.4 = (f32[128,768]{1,0:T(8,128)S(1)}, f32[16,64,128]{2,1,0:T(8,128)S(1)}, s16[16,64,128]{2,1,0:T(8,128)(2,1)S(1)}, s16[14,64,128]{2,1,0:T(8,128)(2,1)S(...) custom-call(f32[64,768]{1,0:T(8,128)S(1)} %bitcast.21, ...), custom_call_target="tpu_custom_call" | custom-call | flops 1000000 | bytes 3785096 | tf_op jit(solution)/shard_map/partials/pallas_call | solution.py:512
  30.4 1.5 collective-permute-start.7
  32.0 1.5 collective-permute-start.8
  34.0 1.0 pair.2
  35.0 3.2 %collective-permute-start.12 = (s16[4,64,128]{2,1,0:T(8,128)(2,1)S(1)}, s16[4,64,128]{2,1,0:T(8,128)(2,1)S(1)}, u32[]{:S(2)}, u32[]{:S(2)}) collective-permute-start(s16[4,64,128]{2,1,0:T(8,128)(2,1)S(1)} %get-tuple-element.123), channel_id=1, source_target_pairs={{0,16},{4,20},{8,24},{12,28},{16,0},{20,4},{24,8},{28,12},{1,17},{... | collective-permute-start | bytes 196616 | tf_op jit(solution)/shard_map/ppermute | solution.py:546
  38.9 2.7 %collective-permute-start.13 = (s16[4,64,128]{2,1,0:T(8,128)(2,1)S(1)}, s16[4,64,128]{2,1,0:T(8,128)(2,1)S(1)}, u32[]{:S(2)}, u32[]{:S(2)}) collective-permute-start(s16[4,64,128]{2,1,0:T(8,128)(2,1)S(1)} %get-tuple-element.124), channel_id=1, source_target_pairs={{0,24},{4,28},{8,16},{12,20},{16,8},{20,12},{24,0},{28,4},{1,25},{... | collective-permute-start | bytes 196616 | tf_op jit(solution)/shard_map/ppermute | solution.py:546
  41.6 4.3 %start_image.1 = (f32[64,768]{1,0:T(8,128)S(1)}, f32[64,768]{1,0:T(8,128)S(1)}, f32[64,768]{1,0:T(8,128)S(1)}, f32[64,768]{1,0:T(8,128)S(1)}, f32[96,128]{1,0:T(8,128)S(1)}, /*index=5*/f32[96,128]{1,0:T(8,128)S(1)}) custom-call(s16[14,64,128]{2,1,0:T(8,128)(2,1)S(1)} %collective-permute-done.refs_0_, s16[14,64,128]{2,1,0:T(8,128)(2,1)S(1)} %collective-permute-done.3.refs_1_, ...), custom_call_target="tpu_custom_call" | custom-call | flops 1000000 | bytes 4260232 | tf_op jit(solution)/shard_map/start_image/pallas_call | solution.py:512
  46.0 1.2 collective-permute-done.14
  47.2 1.7 %collective-permute-start.17 = (f32[96,128]{1,0:T(8,128)S(1)}, f32[96,128]{1,0:T(8,128)S(1)}, u32[]{:S(2)}, u32[]{:S(2)}) collective-permute-start(f32[96,128]{1,0:T(8,128)S(1)} %add.63), channel_id=1, source_target_pairs={{0,24},{4,28},{8,16},{12,20},{16,8},{20,12},{24,0},{28,4},{1,25},{... | collective-permute-start | bytes 147464 | tf_op jit(solution)/shard_map/ppermute | solution.py:546
  48.9 2.8 %collective-permute-start.15 = (f32[96,128]{1,0:T(8,128)S(1)}, f32[96,128]{1,0:T(8,128)S(1)}, u32[]{:S(2)}, u32[]{:S(2)}) collective-permute-start(f32[96,128]{1,0:T(8,128)S(1)} %add.63), channel_id=1, source_target_pairs={{0,8},{4,12},{8,0},{12,4},{16,24},{20,28},{24,16},{28,20},{1,9},{5... | collective-permute-start | bytes 147464 | tf_op jit(solution)/shard_map/ppermute | solution.py:546
  51.7 1.8 %collective-permute-done.17 = f32[96,128]{1,0:T(8,128)S(1)} collective-permute-done((f32[96,128]{1,0:T(8,128)S(1)}, f32[96,128]{1,0:T(8,128)S(1)}, u32[]{:S(2)}, u32[]{:S(2)}) %collective-permute-start.17) | collective-permute-done | bytes 49184 | tf_op jit(solution)/shard_map/ppermute | solution.py:546
  53.5 1.5 collective-permute-done.16
  55.0 2.5 %collective-permute-start.20 = (f32[96,128]{1,0:T(8,128)S(1)}, f32[96,128]{1,0:T(8,128)S(1)}, u32[]{:S(2)}, u32[]{:S(2)}) collective-permute-start(f32[96,128]{1,0:T(8,128)S(1)} %add_add_fusion.5), channel_id=1, source_target_pairs={{0,3},{1,2},{2,1},{3,0},{4,7},{5,6},{6,5},{7,4},{8,11},{9,10},{10,... | collective-permute-start | bytes 147464 | tf_op jit(solution)/shard_map/ppermute | solution.py:543
  58.5 1.5 collective-permute-done.20
  60.0 1.5 collective-permute-done.19
  62.2 1.2 collective-permute-done.21.refs_9_
  63.4 5.4 %update.1 = (f32[192,128]{1,0:T(8,128)S(1)}, f32[64,768]{1,0:T(8,128)S(1)}, f32[64,64]{1,0:T(8,128)S(1)}, f32[64,768]{1,0:T(8,128)S(1)}, s16[7,64,128]{2,1,0:T(8,128)(2,1)S(1)}, /*index=5*/s16[2,64,128]{2,1,0:T(8,128)(2,1)S(1)}) custom-call(f32[128,768]{1,0:T(8,128)S(1)} %get-tuple-element.125.refs_0_, ...), custom_call_target="tpu_custom_call" | custom-call | flops 1000000 | bytes 2755604 | tf_op jit(solution)/shard_map/update/pallas_call | solution.py:512
  68.7 2.4 %partials.5 = (f32[64,768]{1,0:T(8,128)S(1)}, f32[8,64,128]{2,1,0:T(8,128)S(1)}, s16[10,64,128]{2,1,0:T(8,128)(2,1)S(1)}, s16[14,64,128]{2,1,0:T(8,128)(2,1)S(1)...) custom-call(f32[64,768]{1,0:T(8,128)S(1)} %get-tuple-element.137.vector.refs_12_.refs_28_, ...), custom_call_target="tpu_custom_call" | custom-call | flops 1000000 | bytes 2441608 | tf_op jit(solution)/shard_map/partials/pallas_call | solution.py:512
  71.7 1.5 collective-permute-start.23
  73.2 1.4 collective-permute-start.24
  75.5 0.9 collective-permute-start.26
  76.4 1.4 collective-permute-start.27
  77.8 1.9 %collective-permute-done.22.refs_0_.refs_9_ = s16[14,64,128]{2,1,0:T(8,128)(2,1)S(1)} collective-permute-done((s16[14,64,128]{2,1,0:T(8,128)(2,1)S(1)}, s16[14,64,128]{2,1,0:T(8,128)(2,1)S(1)}, u32[]{:S(2)}, u32[]{:S(2)}) %collective-permute-start.22) | collective-permute-done | bytes 229408 | tf_op jit(solution)/shard_map/ppermute | solution.py:543
  79.6 1.6 collective-permute-start.28
  81.3 2.4 %collective-permute-done.23.refs_1_.refs_10_ = s16[14,64,128]{2,1,0:T(8,128)(2,1)S(1)} collective-permute-done((s16[14,64,128]{2,1,0:T(8,128)(2,1)S(1)}, s16[14,64,128]{2,1,0:T(8,128)(2,1)S(1)}, u32[]{:S(2)}, u32[]{:S(2)}) %collective-permute-start.23) | collective-permute-done | bytes 229408 | tf_op jit(solution)/shard_map/ppermute | solution.py:543
  83.7 1.0 collective-permute-done.24.refs_2_.refs_11_
  84.7 2.1 %collective-permute-done.27.refs_6_.refs_14_ = s16[6,64,128]{2,1,0:T(8,128)(2,1)S(1)} collective-permute-done((s16[6,64,128]{2,1,0:T(8,128)(2,1)S(1)}, s16[6,64,128]{2,1,0:T(8,128)(2,1)S(1)}, u32[]{:S(2)}, u32[]{:S(2)}) %collective-permute-start.27) | collective-permute-done | bytes 98336 | tf_op jit(solution)/shard_map/ppermute | solution.py:546
  86.9 3.3 %update_image.2 = (f32[64,768]{1,0:T(8,128)S(1)}, f32[64,768]{1,0:T(8,128)S(1)}, f32[96,128]{1,0:T(8,128)S(1)}, f32[96,128]{1,0:T(8,128)S(1)}) custom-call(s16[14,64,128]{2,1,0:T(8,128)(2,1)S(1)} %collective-permute-done.22.refs_0_.refs_9_, s16[14,64,128]{2,1,0:T(8,128)(2,1)S(1)} %collective-permute-done.23.refs_1_.refs_10_, ...), custom_call_target="tpu_custom_call" | custom-call | flops 1000000 | bytes 4424072 | tf_op jit(solution)/shard_map/update_image/pallas_call | solution.py:512
  90.2 1.2 collective-permute-done.29
  91.5 1.7 %collective-permute-start.32 = (f32[96,128]{1,0:T(8,128)S(1)}, f32[96,128]{1,0:T(8,128)S(1)}, u32[]{:S(2)}, u32[]{:S(2)}) collective-permute-start(f32[96,128]{1,0:T(8,128)S(1)} %add.70), channel_id=1, source_target_pairs={{0,24},{4,28},{8,16},{12,20},{16,8},{20,12},{24,0},{28,4},{1,25},{... | collective-permute-start | bytes 147464 | tf_op jit(solution)/shard_map/ppermute | solution.py:546
  93.2 1.5 collective-permute-start.31
  94.7 1.2 collective-permute-start.30
  95.9 3.8 %pap_inverse.1.refs_22_ = f32[64,64]{1,0:T(8,128)S(1)} custom-call(f32[192,128]{1,0:T(8,128)S(1)} %get-tuple-element.154.table.refs_20_), custom_call_target="tpu_custom_call" | custom-call | flops 1000000 | bytes 114688 | tf_op jit(solution)/shard_map/pap_inverse/pallas_call | solution.py:512
  99.8 1.5 collective-permute-start.35
  101.9 1.5 collective-permute-start.33
  103.3 2.0 %collective-permute-done.35 = f32[96,128]{1,0:T(8,128)S(1)} collective-permute-done((f32[96,128]{1,0:T(8,128)S(1)}, f32[96,128]{1,0:T(8,128)S(1)}, u32[]{:S(2)}, u32[]{:S(2)}) %collective-permute-start.35) | collective-permute-done | bytes 49184 | tf_op jit(solution)/shard_map/ppermute | solution.py:543
  106.0 1.2 collective-permute-done.36.refs_17_
  107.3 11.0 %move.1 = (f32[64,768]{1,0:T(8,128)S(1)}, f32[64,768]{1,0:T(8,128)S(1)}, f32[64,768]{1,0:T(8,128)S(1)}, s16[7,64,128]{2,1,0:T(8,128)(2,1)S(1)}, s16[2,64,128]{2,...) custom-call(f32[128,768]{1,0:T(8,128)S(1)} %get-tuple-element.125.refs_0_, ...), custom_call_target="tpu_custom_call" | custom-call | flops 1000000 | bytes 5655572 | tf_op jit(solution)/shard_map/move/pallas_call | solution.py:512
  118.6 1.0 collective-permute-done.40
  119.6 1.7 %collective-permute-start.43 = (s16[4,64,128]{2,1,0:T(8,128)(2,1)S(1)}, s16[4,64,128]{2,1,0:T(8,128)(2,1)S(1)}, u32[]{:S(2)}, u32[]{:S(2)}) collective-permute-start(s16[4,64,128]{2,1,0:T(8,128)(2,1)S(1)} %constant_dynamic-update-slice_fusion.2.refs_3_), channel_id=1, source_target_pairs={{0,24},{4,28},{8,16},{12,20},{16,8},{20,12},{24,0},{28,4},{1,25},{... | collective-permute-start | bytes 196616 | tf_op jit(solution)/shard_map/ppermute | solution.py:546
  121.2 2.5 %collective-permute-start.39 = (s16[7,64,128]{2,1,0:T(8,128)(2,1)S(1)}, s16[7,64,128]{2,1,0:T(8,128)(2,1)S(1)}, u32[]{:S(2)}, u32[]{:S(2)}) collective-permute-start(s16[7,64,128]{2,1,0:T(8,128)(2,1)S(1)} %get-tuple-element.161), channel_id=1, source_target_pairs={{0,3},{1,2},{2,1},{3,0},{4,7},{5,6},{6,5},{7,4},{8,11},{9,10},{10,... | collective-permute-start | bytes 344072 | tf_op jit(solution)/shard_map/ppermute | solution.py:543
  125.7 1.8 %collective-permute-start.41 = (s16[4,64,128]{2,1,0:T(8,128)(2,1)S(1)}, s16[4,64,128]{2,1,0:T(8,128)(2,1)S(1)}, u32[]{:S(2)}, u32[]{:S(2)}) collective-permute-start(s16[4,64,128]{2,1,0:T(8,128)(2,1)S(1)} %constant_dynamic-update-slice_fusion.2.refs_3_), channel_id=1, source_target_pairs={{0,8},{4,12},{8,0},{12,4},{16,24},{20,28},{24,16},{28,20},{1,9},{5... | collective-permute-start | bytes 196616 | tf_op jit(solution)/shard_map/ppermute | solution.py:546
  127.5 4.7 %settle.1 = (f32[64,768]{1,0:T(8,128)S(1)}, f32[64,768]{1,0:T(8,128)S(1)}, f32[192,64]{1,0:T(8,128)S(1)}) custom-call(f32[256,64]{1,0:T(8,128)S(1)} %get-tuple-element.165.small, f32[64,768]{1,0:T(8,128)S(1)} %get-tuple-element.166.step_x, f32[64,768]{1,0:T(8,128)S(1)} %get-tuple-element.167.step_a), custom_call_target="tpu_custom_call" | custom-call | flops 1000000 | bytes 901120 | tf_op jit(solution)/shard_map/settle/pallas_call | solution.py:512
  132.2 3.5 %update_image.3 = (f32[64,768]{1,0:T(8,128)}, f32[64,768]{1,0:T(8,128)}, f32[96,128]{1,0:T(8,128)S(1)}, f32[96,128]{1,0:T(8,128)S(1)}) custom-call(s16[7,64,128]{2,1,0:T(8,128)(2,1)S(1)} %collective-permute-done.37.refs_0_, s16[7,64,128]{2,1,0:T(8,128)(2,1)S(1)} %collective-permute-done.38.refs_1_, s16[7,64,128]{2,1,0:T(8,128)(2,1)S(1)} %collective-permute-done.39.refs_2_, ...), custom_call_target="tpu_custom_call" | custom-call | flops 1000000 | bytes 3850632 | tf_op jit(solution)/shard_map/update_image/pallas_call | solution.py:512
  135.7 1.2 collective-permute-done.44
  136.9 1.7 %collective-permute-start.47 = (f32[96,128]{1,0:T(8,128)S(1)}, f32[96,128]{1,0:T(8,128)S(1)}, u32[]{:S(2)}, u32[]{:S(2)}) collective-permute-start(f32[96,128]{1,0:T(8,128)S(1)} %add.77), channel_id=1, source_target_pairs={{0,24},{4,28},{8,16},{12,20},{16,8},{20,12},{24,0},{28,4},{1,25},{... | collective-permute-start | bytes 147464 | tf_op jit(solution)/shard_map/ppermute | solution.py:546
  138.6 2.7 %collective-permute-start.45 = (f32[96,128]{1,0:T(8,128)S(1)}, f32[96,128]{1,0:T(8,128)S(1)}, u32[]{:S(2)}, u32[]{:S(2)}) collective-permute-start(f32[96,128]{1,0:T(8,128)S(1)} %add.77), channel_id=1, source_target_pairs={{0,8},{4,12},{8,0},{12,4},{16,24},{20,28},{24,16},{28,20},{1,9},{5... | collective-permute-start | bytes 147464 | tf_op jit(solution)/shard_map/ppermute | solution.py:546
  141.4 1.8 %collective-permute-done.47 = f32[96,128]{1,0:T(8,128)S(1)} collective-permute-done((f32[96,128]{1,0:T(8,128)S(1)}, f32[96,128]{1,0:T(8,128)S(1)}, u32[]{:S(2)}, u32[]{:S(2)}) %collective-permute-start.47) | collective-permute-done | bytes 49184 | tf_op jit(solution)/shard_map/ppermute | solution.py:546
  143.2 1.5 collective-permute-done.46
  144.6 2.5 %collective-permute-start.50 = (f32[96,128]{1,0:T(8,128)S(1)}, f32[96,128]{1,0:T(8,128)S(1)}, u32[]{:S(2)}, u32[]{:S(2)}) collective-permute-start(f32[96,128]{1,0:T(8,128)S(1)} %add_add_fusion.1), channel_id=1, source_target_pairs={{0,3},{1,2},{2,1},{3,0},{4,7},{5,6},{6,5},{7,4},{8,11},{9,10},{10,... | collective-permute-start | bytes 147464 | tf_op jit(solution)/shard_map/ppermute | solution.py:543
  148.2 1.5 collective-permute-done.50
  149.7 1.5 collective-permute-done.49
  151.8 1.2 collective-permute-done.51.other
  153.1 10.3 %finish.1 = (f32[64,768]{1,0:T(8,128)}, f32[64,768]{1,0:T(8,128)}) custom-call(f32[96,128]{1,0:T(8,128)S(1)} %add_add_fusion.mine, f32[96,128]{1,0:T(8,128)S(1)} %collective-permute-done.51.other, s32[2]{0:T(128)S(1)} %pad_add_fusion.refs_10_.pos.refs_11_.refs_18_, f32[192,64]{1,0:T(8,128)S(1)} %get-tuple-element.173.state, ...), custom_call_target="tpu_custom_call" | custom-call | flops 1000000 | bytes 1130504 | tf_op jit(solution)/shard_map/finish/pallas_call | solution.py:512
  (95 shorter events, 12.8 us)
Async XLA Ops:
  0.6 0.9 copy-start
  1.6 0.9 copy-start.2
  2.5 0.7 copy-start.5
  3.1 20.5 %copy-start.4 = (bf16[1,1,12,64,64]{4,3,2,1,0:T(8,128)(2,1)S(1)}, bf16[1,1,12,64,64]{4,3,2,1,0:T(8,128)(2,1)}, u32[]{:S(2)}) copy-start(bf16[1,1,12,64,64]{4,3,2,1,0:T(8,128)(2,1)} %param.19) | copy-start | bytes 294916
  3.1 20.5 %copy-start.7 = (s32[1,1,96]{2,1,0:T(1,128)S(1)}, s32[1,1,96]{2,1,0:T(1,128)}, u32[]{:S(2)}) copy-start(s32[1,1,96]{2,1,0:T(1,128)} %param.13) | copy-start | bytes 1156
  3.1 20.5 %copy-start.8 = (s32[1,1,96]{2,1,0:T(1,128)S(1)}, s32[1,1,96]{2,1,0:T(1,128)}, u32[]{:S(2)}) copy-start(s32[1,1,96]{2,1,0:T(1,128)} %param.14) | copy-start | bytes 1156
  3.2 20.5 %copy-start.9 = (s32[1,1,12]{2,1,0:T(1,128)S(1)}, s32[1,1,12]{2,1,0:T(1,128)}, u32[]{:S(2)}) copy-start(s32[1,1,12]{2,1,0:T(1,128)} %param.17) | copy-start | bytes 148
  3.2 20.5 %copy-start.10 = (s32[1,1,12]{2,1,0:T(1,128)S(1)}, s32[1,1,12]{2,1,0:T(1,128)}, u32[]{:S(2)}) copy-start(s32[1,1,12]{2,1,0:T(1,128)} %param.18) | copy-start | bytes 148
  4.0 1.4 collective-permute-start.1
  5.4 8.9 %collective-permute-start.2 = (s16[8,64,128]{2,1,0:T(8,128)(2,1)S(1)}, s16[8,64,128]{2,1,0:T(8,128)(2,1)S(1)}, u32[]{:S(2)}, u32[]{:S(2)}) collective-permute-start(s16[8,64,128]{2,1,0:T(8,128)(2,1)S(1)} %constant_dynamic-update-slice_fusion.refs_3_), channel_id=1, source_target_pairs={{0,24},{4,28},{8,16},{12,20},{16,8},{20,12},{24,0},{28,4},{1,25},{... | collective-permute-start | bytes 393224 | tf_op jit(solution)/shard_map/ppermute | solution.py:546
  10.5 9.8 %collective-permute-start = (s16[14,64,128]{2,1,0:T(8,128)(2,1)S(1)}, s16[14,64,128]{2,1,0:T(8,128)(2,1)S(1)}, u32[]{:S(2)}, u32[]{:S(2)}) collective-permute-start(s16[14,64,128]{2,1,0:T(8,128)(2,1)S(1)} %get-tuple-element.89), channel_id=1, source_target_pairs={{0,1},{1,0},{2,3},{3,2},{4,5},{5,4},{6,7},{7,6},{8,9},{9,8},{10,11... | collective-permute-start | bytes 688136 | tf_op jit(solution)/shard_map/ppermute | solution.py:543
  12.0 14.0 %collective-permute-start.4 = (s16[14,64,128]{2,1,0:T(8,128)(2,1)S(1)}, s16[14,64,128]{2,1,0:T(8,128)(2,1)S(1)}, u32[]{:S(2)}, u32[]{:S(2)}) collective-permute-start(s16[14,64,128]{2,1,0:T(8,128)(2,1)S(1)} %get-tuple-element.89), channel_id=1, source_target_pairs={{0,3},{1,2},{2,1},{3,0},{4,7},{5,6},{6,5},{7,4},{8,11},{9,10},{10,... | collective-permute-start | bytes 688136 | tf_op jit(solution)/shard_map/ppermute | solution.py:543
  13.4 12.5 %collective-permute-start.3 = (s16[14,64,128]{2,1,0:T(8,128)(2,1)S(1)}, s16[14,64,128]{2,1,0:T(8,128)(2,1)S(1)}, u32[]{:S(2)}, u32[]{:S(2)}) collective-permute-start(s16[14,64,128]{2,1,0:T(8,128)(2,1)S(1)} %get-tuple-element.89), channel_id=1, source_target_pairs={{0,2},{1,3},{2,0},{3,1},{4,6},{5,7},{6,4},{7,5},{8,10},{9,11},{10,... | collective-permute-start | bytes 688136 | tf_op jit(solution)/shard_map/ppermute | solution.py:543
  13.9 11.9 %collective-permute-start.6 = (s16[8,64,128]{2,1,0:T(8,128)(2,1)S(1)}, s16[8,64,128]{2,1,0:T(8,128)(2,1)S(1)}, u32[]{:S(2)}, u32[]{:S(2)}) collective-permute-start(s16[8,64,128]{2,1,0:T(8,128)(2,1)S(1)} %constant_dynamic-update-slice_fusion.refs_3_), channel_id=1, source_target_pairs={{0,16},{4,20},{8,24},{12,28},{16,0},{20,4},{24,8},{28,12},{1,17},{... | collective-permute-start | bytes 393224 | tf_op jit(solution)/shard_map/ppermute | solution.py:546
  14.4 11.5 %collective-permute-start.5 = (s16[8,64,128]{2,1,0:T(8,128)(2,1)S(1)}, s16[8,64,128]{2,1,0:T(8,128)(2,1)S(1)}, u32[]{:S(2)}, u32[]{:S(2)}) collective-permute-start(s16[8,64,128]{2,1,0:T(8,128)(2,1)S(1)} %constant_dynamic-update-slice_fusion.refs_3_), channel_id=1, source_target_pairs={{0,8},{4,12},{8,0},{12,4},{16,24},{20,28},{24,16},{28,20},{1,9},{5... | collective-permute-start | bytes 393224 | tf_op jit(solution)/shard_map/ppermute | solution.py:546
  20.3 5.6 %copy-start.1 = (f32[768,64]{0,1:T(8,128)S(1)}, f32[768,64]{0,1:T(8,128)}, u32[]{:S(2)}) copy-start(f32[768,64]{0,1:T(8,128)} %param.10) | copy-start | bytes 589828
  23.6 4.5 %copy-start.3 = (f32[768,64]{0,1:T(8,128)S(1)}, f32[768,64]{0,1:T(8,128)}, u32[]{:S(2)}) copy-start(f32[768,64]{0,1:T(8,128)} %param.11) | copy-start | bytes 589828
  30.3 3.6 %collective-permute-start.10 = (s16[16,64,128]{2,1,0:T(8,128)(2,1)S(1)}, s16[16,64,128]{2,1,0:T(8,128)(2,1)S(1)}, u32[]{:S(2)}, u32[]{:S(2)}) collective-permute-start(s16[16,64,128]{2,1,0:T(8,128)(2,1)S(1)} %get-tuple-element.120), channel_id=1, source_target_pairs={{0,4},{4,0},{8,12},{12,8},{16,20},{20,16},{24,28},{28,24},{1,5},{5... | collective-permute-start | bytes 786440 | tf_op jit(solution)/shard_map/ppermute | solution.py:546
  30.4 8.5 %collective-permute-start.7 = (s16[14,64,128]{2,1,0:T(8,128)(2,1)S(1)}, s16[14,64,128]{2,1,0:T(8,128)(2,1)S(1)}, u32[]{:S(2)}, u32[]{:S(2)}) collective-permute-start(s16[14,64,128]{2,1,0:T(8,128)(2,1)S(1)} %get-tuple-element.116), channel_id=1, source_target_pairs={{0,1},{1,0},{2,3},{3,2},{4,5},{5,4},{6,7},{7,6},{8,9},{9,8},{10,11... | collective-permute-start | bytes 688136 | tf_op jit(solution)/shard_map/ppermute | solution.py:543
  32.0 13.9 %collective-permute-start.8 = (s16[14,64,128]{2,1,0:T(8,128)(2,1)S(1)}, s16[14,64,128]{2,1,0:T(8,128)(2,1)S(1)}, u32[]{:S(2)}, u32[]{:S(2)}) collective-permute-start(s16[14,64,128]{2,1,0:T(8,128)(2,1)S(1)} %get-tuple-element.117), channel_id=1, source_target_pairs={{0,2},{1,3},{2,0},{3,1},{4,6},{5,7},{6,4},{7,5},{8,10},{9,11},{10,... | collective-permute-start | bytes 688136 | tf_op jit(solution)/shard_map/ppermute | solution.py:543
  33.5 12.4 %collective-permute-start.9 = (s16[14,64,128]{2,1,0:T(8,128)(2,1)S(1)}, s16[14,64,128]{2,1,0:T(8,128)(2,1)S(1)}, u32[]{:S(2)}, u32[]{:S(2)}) collective-permute-start(s16[14,64,128]{2,1,0:T(8,128)(2,1)S(1)} %get-tuple-element.118), channel_id=1, source_target_pairs={{0,3},{1,2},{2,1},{3,0},{4,7},{5,6},{6,5},{7,4},{8,11},{9,10},{10,... | collective-permute-start | bytes 688136 | tf_op jit(solution)/shard_map/ppermute | solution.py:543
  35.0 10.9 %collective-permute-start.11 = (s16[4,64,128]{2,1,0:T(8,128)(2,1)S(1)}, s16[4,64,128]{2,1,0:T(8,128)(2,1)S(1)}, u32[]{:S(2)}, u32[]{:S(2)}) collective-permute-start(s16[4,64,128]{2,1,0:T(8,128)(2,1)S(1)} %get-tuple-element.122), channel_id=1, source_target_pairs={{0,8},{4,12},{8,0},{12,4},{16,24},{20,28},{24,16},{28,20},{1,9},{5... | collective-permute-start | bytes 196616 | tf_op jit(solution)/shard_map/ppermute | solution.py:546
  35.0 10.8 %collective-permute-start.12 = (s16[4,64,128]{2,1,0:T(8,128)(2,1)S(1)}, s16[4,64,128]{2,1,0:T(8,128)(2,1)S(1)}, u32[]{:S(2)}, u32[]{:S(2)}) collective-permute-start(s16[4,64,128]{2,1,0:T(8,128)(2,1)S(1)} %get-tuple-element.123), channel_id=1, source_target_pairs={{0,16},{4,20},{8,24},{12,28},{16,0},{20,4},{24,8},{28,12},{1,17},{... | collective-permute-start | bytes 196616 | tf_op jit(solution)/shard_map/ppermute | solution.py:546
  38.9 7.0 %collective-permute-start.13 = (s16[4,64,128]{2,1,0:T(8,128)(2,1)S(1)}, s16[4,64,128]{2,1,0:T(8,128)(2,1)S(1)}, u32[]{:S(2)}, u32[]{:S(2)}) collective-permute-start(s16[4,64,128]{2,1,0:T(8,128)(2,1)S(1)} %get-tuple-element.124), channel_id=1, source_target_pairs={{0,24},{4,28},{8,16},{12,20},{16,8},{20,12},{24,0},{28,4},{1,25},{... | collective-permute-start | bytes 196616 | tf_op jit(solution)/shard_map/ppermute | solution.py:546
  41.5 20.6 %copy-start.11 = (f32[768]{0:T(1024)S(1)}, f32[768]{0:T(1024)}, u32[]{:S(2)}) copy-start(f32[768]{0:T(1024)} %param.12) | copy-start | bytes 9220
  41.6 21.8 %copy-start.6 = (s32[1,1,3]{2,1,0:T(1,128)S(1)}, s32[1,1,3]{2,1,0:T(1,128)}, u32[]{:S(2)}) copy-start(s32[1,1,3]{2,1,0:T(1,128)} %param.16) | copy-start | bytes 40
  45.9 1.3 collective-permute-start.14
  47.2 6.3 %collective-permute-start.17 = (f32[96,128]{1,0:T(8,128)S(1)}, f32[96,128]{1,0:T(8,128)S(1)}, u32[]{:S(2)}, u32[]{:S(2)}) collective-permute-start(f32[96,128]{1,0:T(8,128)S(1)} %add.63), channel_id=1, source_target_pairs={{0,24},{4,28},{8,16},{12,20},{16,8},{20,12},{24,0},{28,4},{1,25},{... | collective-permute-start | bytes 147464 | tf_op jit(solution)/shard_map/ppermute | solution.py:546
  48.9 6.0 %collective-permute-start.16 = (f32[96,128]{1,0:T(8,128)S(1)}, f32[96,128]{1,0:T(8,128)S(1)}, u32[]{:S(2)}, u32[]{:S(2)}) collective-permute-start(f32[96,128]{1,0:T(8,128)S(1)} %add.63), channel_id=1, source_target_pairs={{0,16},{4,20},{8,24},{12,28},{16,0},{20,4},{24,8},{28,12},{1,17},{... | collective-permute-start | bytes 147464 | tf_op jit(solution)/shard_map/ppermute | solution.py:546
  48.9 6.0 %collective-permute-start.15 = (f32[96,128]{1,0:T(8,128)S(1)}, f32[96,128]{1,0:T(8,128)S(1)}, u32[]{:S(2)}, u32[]{:S(2)}) collective-permute-start(f32[96,128]{1,0:T(8,128)S(1)} %add.63), channel_id=1, source_target_pairs={{0,8},{4,12},{8,0},{12,4},{16,24},{20,28},{24,16},{28,20},{1,9},{5... | collective-permute-start | bytes 147464 | tf_op jit(solution)/shard_map/ppermute | solution.py:546
  55.0 5.1 %collective-permute-start.20 = (f32[96,128]{1,0:T(8,128)S(1)}, f32[96,128]{1,0:T(8,128)S(1)}, u32[]{:S(2)}, u32[]{:S(2)}) collective-permute-start(f32[96,128]{1,0:T(8,128)S(1)} %add_add_fusion.5), channel_id=1, source_target_pairs={{0,3},{1,2},{2,1},{3,0},{4,7},{5,6},{6,5},{7,4},{8,11},{9,10},{10,... | collective-permute-start | bytes 147464 | tf_op jit(solution)/shard_map/ppermute | solution.py:543
  57.5 4.1 %collective-permute-start.19 = (f32[96,128]{1,0:T(8,128)S(1)}, f32[96,128]{1,0:T(8,128)S(1)}, u32[]{:S(2)}, u32[]{:S(2)}) collective-permute-start(f32[96,128]{1,0:T(8,128)S(1)} %add_add_fusion.5), channel_id=1, source_target_pairs={{0,2},{1,3},{2,0},{3,1},{4,6},{5,7},{6,4},{7,5},{8,10},{9,11},{10,... | collective-permute-start | bytes 147464 | tf_op jit(solution)/shard_map/ppermute | solution.py:543
  58.0 4.1 %collective-permute-start.18 = (f32[96,128]{1,0:T(8,128)S(1)}, f32[96,128]{1,0:T(8,128)S(1)}, u32[]{:S(2)}, u32[]{:S(2)}) collective-permute-start(f32[96,128]{1,0:T(8,128)S(1)} %add_add_fusion.5), channel_id=1, source_target_pairs={{0,1},{1,0},{2,3},{3,2},{4,5},{5,4},{6,7},{7,6},{8,9},{9,8},{10,11... | collective-permute-start | bytes 147464 | tf_op jit(solution)/shard_map/ppermute | solution.py:543
  62.1 1.3 collective-permute-start.21
  71.1 8.5 %collective-permute-start.22 = (s16[14,64,128]{2,1,0:T(8,128)(2,1)S(1)}, s16[14,64,128]{2,1,0:T(8,128)(2,1)S(1)}, u32[]{:S(2)}, u32[]{:S(2)}) collective-permute-start(s16[14,64,128]{2,1,0:T(8,128)(2,1)S(1)} %get-tuple-element.141), channel_id=1, source_target_pairs={{0,1},{1,0},{2,3},{3,2},{4,5},{5,4},{6,7},{7,6},{8,9},{9,8},{10,11... | collective-permute-start | bytes 688136 | tf_op jit(solution)/shard_map/ppermute | solution.py:543
  71.7 3.0 %collective-permute-start.25 = (s16[10,64,128]{2,1,0:T(8,128)(2,1)S(1)}, s16[10,64,128]{2,1,0:T(8,128)(2,1)S(1)}, u32[]{:S(2)}, u32[]{:S(2)}) collective-permute-start(s16[10,64,128]{2,1,0:T(8,128)(2,1)S(1)} %get-tuple-element.145), channel_id=1, source_target_pairs={{0,4},{4,0},{8,12},{12,8},{16,20},{20,16},{24,28},{28,24},{1,5},{5... | collective-permute-start | bytes 491528 | tf_op jit(solution)/shard_map/ppermute | solution.py:546
  71.7 12.0 %collective-permute-start.23 = (s16[14,64,128]{2,1,0:T(8,128)(2,1)S(1)}, s16[14,64,128]{2,1,0:T(8,128)(2,1)S(1)}, u32[]{:S(2)}, u32[]{:S(2)}) collective-permute-start(s16[14,64,128]{2,1,0:T(8,128)(2,1)S(1)} %get-tuple-element.142), channel_id=1, source_target_pairs={{0,2},{1,3},{2,0},{3,1},{4,6},{5,7},{6,4},{7,5},{8,10},{9,11},{10,... | collective-permute-start | bytes 688136 | tf_op jit(solution)/shard_map/ppermute | solution.py:543
  73.2 11.5 %collective-permute-start.24 = (s16[14,64,128]{2,1,0:T(8,128)(2,1)S(1)}, s16[14,64,128]{2,1,0:T(8,128)(2,1)S(1)}, u32[]{:S(2)}, u32[]{:S(2)}) collective-permute-start(s16[14,64,128]{2,1,0:T(8,128)(2,1)S(1)} %get-tuple-element.143), channel_id=1, source_target_pairs={{0,3},{1,2},{2,1},{3,0},{4,7},{5,6},{6,5},{7,4},{8,11},{9,10},{10,... | collective-permute-start | bytes 688136 | tf_op jit(solution)/shard_map/ppermute | solution.py:543
  75.5 9.2 %collective-permute-start.26 = (s16[6,64,128]{2,1,0:T(8,128)(2,1)S(1)}, s16[6,64,128]{2,1,0:T(8,128)(2,1)S(1)}, u32[]{:S(2)}, u32[]{:S(2)}) collective-permute-start(s16[6,64,128]{2,1,0:T(8,128)(2,1)S(1)} %get-tuple-element.147), channel_id=1, source_target_pairs={{0,8},{4,12},{8,0},{12,4},{16,24},{20,28},{24,16},{28,20},{1,9},{5... | collective-permute-start | bytes 294920 | tf_op jit(solution)/shard_map/ppermute | solution.py:546
  76.4 10.5 %collective-permute-start.27 = (s16[6,64,128]{2,1,0:T(8,128)(2,1)S(1)}, s16[6,64,128]{2,1,0:T(8,128)(2,1)S(1)}, u32[]{:S(2)}, u32[]{:S(2)}) collective-permute-start(s16[6,64,128]{2,1,0:T(8,128)(2,1)S(1)} %get-tuple-element.148), channel_id=1, source_target_pairs={{0,16},{4,20},{8,24},{12,28},{16,0},{20,4},{24,8},{28,12},{1,17},{... | collective-permute-start | bytes 294920 | tf_op jit(solution)/shard_map/ppermute | solution.py:546
  79.6 7.2 %collective-permute-start.28 = (s16[6,64,128]{2,1,0:T(8,128)(2,1)S(1)}, s16[6,64,128]{2,1,0:T(8,128)(2,1)S(1)}, u32[]{:S(2)}, u32[]{:S(2)}) collective-permute-start(s16[6,64,128]{2,1,0:T(8,128)(2,1)S(1)} %get-tuple-element.149), channel_id=1, source_target_pairs={{0,24},{4,28},{8,16},{12,20},{16,8},{20,12},{24,0},{28,4},{1,25},{... | collective-permute-start | bytes 294920 | tf_op jit(solution)/shard_map/ppermute | solution.py:546
  90.2 1.3 collective-permute-start.29
  91.5 8.3 %collective-permute-start.32 = (f32[96,128]{1,0:T(8,128)S(1)}, f32[96,128]{1,0:T(8,128)S(1)}, u32[]{:S(2)}, u32[]{:S(2)}) collective-permute-start(f32[96,128]{1,0:T(8,128)S(1)} %add.70), channel_id=1, source_target_pairs={{0,24},{4,28},{8,16},{12,20},{16,8},{20,12},{24,0},{28,4},{1,25},{... | collective-permute-start | bytes 147464 | tf_op jit(solution)/shard_map/ppermute | solution.py:546
  93.2 6.6 %collective-permute-start.31 = (f32[96,128]{1,0:T(8,128)S(1)}, f32[96,128]{1,0:T(8,128)S(1)}, u32[]{:S(2)}, u32[]{:S(2)}) collective-permute-start(f32[96,128]{1,0:T(8,128)S(1)} %add.70), channel_id=1, source_target_pairs={{0,16},{4,20},{8,24},{12,28},{16,0},{20,4},{24,8},{28,12},{1,17},{... | collective-permute-start | bytes 147464 | tf_op jit(solution)/shard_map/ppermute | solution.py:546
  94.7 5.1 %collective-permute-start.30 = (f32[96,128]{1,0:T(8,128)S(1)}, f32[96,128]{1,0:T(8,128)S(1)}, u32[]{:S(2)}, u32[]{:S(2)}) collective-permute-start(f32[96,128]{1,0:T(8,128)S(1)} %add.70), channel_id=1, source_target_pairs={{0,8},{4,12},{8,0},{12,4},{16,24},{20,28},{24,16},{28,20},{1,9},{5... | collective-permute-start | bytes 147464 | tf_op jit(solution)/shard_map/ppermute | solution.py:546
  99.8 5.5 %collective-permute-start.35 = (f32[96,128]{1,0:T(8,128)S(1)}, f32[96,128]{1,0:T(8,128)S(1)}, u32[]{:S(2)}, u32[]{:S(2)}) collective-permute-start(f32[96,128]{1,0:T(8,128)S(1)} %add_add_fusion.3), channel_id=1, source_target_pairs={{0,3},{1,2},{2,1},{3,0},{4,7},{5,6},{6,5},{7,4},{8,11},{9,10},{10,... | collective-permute-start | bytes 147464 | tf_op jit(solution)/shard_map/ppermute | solution.py:543
  101.3 4.3 %collective-permute-start.34 = (f32[96,128]{1,0:T(8,128)S(1)}, f32[96,128]{1,0:T(8,128)S(1)}, u32[]{:S(2)}, u32[]{:S(2)}) collective-permute-start(f32[96,128]{1,0:T(8,128)S(1)} %add_add_fusion.3), channel_id=1, source_target_pairs={{0,2},{1,3},{2,0},{3,1},{4,6},{5,7},{6,4},{7,5},{8,10},{9,11},{10,... | collective-permute-start | bytes 147464 | tf_op jit(solution)/shard_map/ppermute | solution.py:543
  101.9 4.1 %collective-permute-start.33 = (f32[96,128]{1,0:T(8,128)S(1)}, f32[96,128]{1,0:T(8,128)S(1)}, u32[]{:S(2)}, u32[]{:S(2)}) collective-permute-start(f32[96,128]{1,0:T(8,128)S(1)} %add_add_fusion.3), channel_id=1, source_target_pairs={{0,1},{1,0},{2,3},{3,2},{4,5},{5,4},{6,7},{7,6},{8,9},{9,8},{10,11... | collective-permute-start | bytes 147464 | tf_op jit(solution)/shard_map/ppermute | solution.py:543
  106.0 1.3 collective-permute-start.36
  118.3 1.3 collective-permute-start.40
  119.6 6.1 %collective-permute-start.43 = (s16[4,64,128]{2,1,0:T(8,128)(2,1)S(1)}, s16[4,64,128]{2,1,0:T(8,128)(2,1)S(1)}, u32[]{:S(2)}, u32[]{:S(2)}) collective-permute-start(s16[4,64,128]{2,1,0:T(8,128)(2,1)S(1)} %constant_dynamic-update-slice_fusion.2.refs_3_), channel_id=1, source_target_pairs={{0,24},{4,28},{8,16},{12,20},{16,8},{20,12},{24,0},{28,4},{1,25},{... | collective-permute-start | bytes 196616 | tf_op jit(solution)/shard_map/ppermute | solution.py:546
  121.2 10.9 %collective-permute-start.39 = (s16[7,64,128]{2,1,0:T(8,128)(2,1)S(1)}, s16[7,64,128]{2,1,0:T(8,128)(2,1)S(1)}, u32[]{:S(2)}, u32[]{:S(2)}) collective-permute-start(s16[7,64,128]{2,1,0:T(8,128)(2,1)S(1)} %get-tuple-element.161), channel_id=1, source_target_pairs={{0,3},{1,2},{2,1},{3,0},{4,7},{5,6},{6,5},{7,4},{8,11},{9,10},{10,... | collective-permute-start | bytes 344072 | tf_op jit(solution)/shard_map/ppermute | solution.py:543
  123.7 8.4 %collective-permute-start.38 = (s16[7,64,128]{2,1,0:T(8,128)(2,1)S(1)}, s16[7,64,128]{2,1,0:T(8,128)(2,1)S(1)}, u32[]{:S(2)}, u32[]{:S(2)}) collective-permute-start(s16[7,64,128]{2,1,0:T(8,128)(2,1)S(1)} %get-tuple-element.161), channel_id=1, source_target_pairs={{0,2},{1,3},{2,0},{3,1},{4,6},{5,7},{6,4},{7,5},{8,10},{9,11},{10,... | collective-permute-start | bytes 344072 | tf_op jit(solution)/shard_map/ppermute | solution.py:543
  124.2 8.0 %collective-permute-start.37 = (s16[7,64,128]{2,1,0:T(8,128)(2,1)S(1)}, s16[7,64,128]{2,1,0:T(8,128)(2,1)S(1)}, u32[]{:S(2)}, u32[]{:S(2)}) collective-permute-start(s16[7,64,128]{2,1,0:T(8,128)(2,1)S(1)} %get-tuple-element.161), channel_id=1, source_target_pairs={{0,1},{1,0},{2,3},{3,2},{4,5},{5,4},{6,7},{7,6},{8,9},{9,8},{10,11... | collective-permute-start | bytes 344072 | tf_op jit(solution)/shard_map/ppermute | solution.py:543
  124.7 7.4 %collective-permute-start.42 = (s16[4,64,128]{2,1,0:T(8,128)(2,1)S(1)}, s16[4,64,128]{2,1,0:T(8,128)(2,1)S(1)}, u32[]{:S(2)}, u32[]{:S(2)}) collective-permute-start(s16[4,64,128]{2,1,0:T(8,128)(2,1)S(1)} %constant_dynamic-update-slice_fusion.2.refs_3_), channel_id=1, source_target_pairs={{0,16},{4,20},{8,24},{12,28},{16,0},{20,4},{24,8},{28,12},{1,17},{... | collective-permute-start | bytes 196616 | tf_op jit(solution)/shard_map/ppermute | solution.py:546
  125.7 6.5 %collective-permute-start.41 = (s16[4,64,128]{2,1,0:T(8,128)(2,1)S(1)}, s16[4,64,128]{2,1,0:T(8,128)(2,1)S(1)}, u32[]{:S(2)}, u32[]{:S(2)}) collective-permute-start(s16[4,64,128]{2,1,0:T(8,128)(2,1)S(1)} %constant_dynamic-update-slice_fusion.2.refs_3_), channel_id=1, source_target_pairs={{0,8},{4,12},{8,0},{12,4},{16,24},{20,28},{24,16},{28,20},{1,9},{5... | collective-permute-start | bytes 196616 | tf_op jit(solution)/shard_map/ppermute | solution.py:546
  135.7 1.2 collective-permute-start.44
  136.9 6.3 %collective-permute-start.47 = (f32[96,128]{1,0:T(8,128)S(1)}, f32[96,128]{1,0:T(8,128)S(1)}, u32[]{:S(2)}, u32[]{:S(2)}) collective-permute-start(f32[96,128]{1,0:T(8,128)S(1)} %add.77), channel_id=1, source_target_pairs={{0,24},{4,28},{8,16},{12,20},{16,8},{20,12},{24,0},{28,4},{1,25},{... | collective-permute-start | bytes 147464 | tf_op jit(solution)/shard_map/ppermute | solution.py:546
  138.6 6.0 %collective-permute-start.46 = (f32[96,128]{1,0:T(8,128)S(1)}, f32[96,128]{1,0:T(8,128)S(1)}, u32[]{:S(2)}, u32[]{:S(2)}) collective-permute-start(f32[96,128]{1,0:T(8,128)S(1)} %add.77), channel_id=1, source_target_pairs={{0,16},{4,20},{8,24},{12,28},{16,0},{20,4},{24,8},{28,12},{1,17},{... | collective-permute-start | bytes 147464 | tf_op jit(solution)/shard_map/ppermute | solution.py:546
  138.6 6.0 %collective-permute-start.45 = (f32[96,128]{1,0:T(8,128)S(1)}, f32[96,128]{1,0:T(8,128)S(1)}, u32[]{:S(2)}, u32[]{:S(2)}) collective-permute-start(f32[96,128]{1,0:T(8,128)S(1)} %add.77), channel_id=1, source_target_pairs={{0,8},{4,12},{8,0},{12,4},{16,24},{20,28},{24,16},{28,20},{1,9},{5... | collective-permute-start | bytes 147464 | tf_op jit(solution)/shard_map/ppermute | solution.py:546
  144.6 5.1 %collective-permute-start.50 = (f32[96,128]{1,0:T(8,128)S(1)}, f32[96,128]{1,0:T(8,128)S(1)}, u32[]{:S(2)}, u32[]{:S(2)}) collective-permute-start(f32[96,128]{1,0:T(8,128)S(1)} %add_add_fusion.1), channel_id=1, source_target_pairs={{0,3},{1,2},{2,1},{3,0},{4,7},{5,6},{6,5},{7,4},{8,11},{9,10},{10,... | collective-permute-start | bytes 147464 | tf_op jit(solution)/shard_map/ppermute | solution.py:543
  147.1 4.1 %collective-permute-start.49 = (f32[96,128]{1,0:T(8,128)S(1)}, f32[96,128]{1,0:T(8,128)S(1)}, u32[]{:S(2)}, u32[]{:S(2)}) collective-permute-start(f32[96,128]{1,0:T(8,128)S(1)} %add_add_fusion.1), channel_id=1, source_target_pairs={{0,2},{1,3},{2,0},{3,1},{4,6},{5,7},{6,4},{7,5},{8,10},{9,11},{10,... | collective-permute-start | bytes 147464 | tf_op jit(solution)/shard_map/ppermute | solution.py:543
  147.7 4.1 %collective-permute-start.48 = (f32[96,128]{1,0:T(8,128)S(1)}, f32[96,128]{1,0:T(8,128)S(1)}, u32[]{:S(2)}, u32[]{:S(2)}) collective-permute-start(f32[96,128]{1,0:T(8,128)S(1)} %add_add_fusion.1), channel_id=1, source_target_pairs={{0,1},{1,0},{2,3},{3,2},{4,5},{5,4},{6,7},{7,6},{8,9},{9,8},{10,11... | collective-permute-start | bytes 147464 | tf_op jit(solution)/shard_map/ppermute | solution.py:543
  151.8 1.3 collective-permute-start.51

commit v7 on v6

--- a/solution.py
+++ b/solution.py
@@ -186,43 +186,45 @@
         target[:, span] = target[:, span] + back[t]
 
 
-def eliminate(table, full):
-    order = table.shape[0]
-    rows = lax.broadcasted_iota(jnp.int32, table.shape, 0)
-    for j in range(0, order, 2):
-        left = jnp.broadcast_to(table[:, j : j + 1], table.shape)
-        right = jnp.broadcast_to(table[:, j + 1 : j + 2], table.shape)
-        one, two = table[j : j + 1, :], table[j + 1 : j + 2, :]
-        over = 1.0 / left[j : j + 1, :]
-        ratio = left[j + 1 : j + 2, :] * over
-        beside = right[j : j + 1, :]
-        two = two - ratio * one
-        second = two * (1.0 / (right[j + 1 : j + 2, :] - ratio * beside))
-        first = (one - beside * second) * over
-        moved = table - left * first - right * second
-        if full:
-            table = jnp.where(rows == j, first, jnp.where(rows == j + 1, second, moved))
-        else:
-            table = jnp.where(rows > j + 1, moved, jnp.where(rows == j + 1, two, table))
-    return table
-
-
 def unit(order):
     return (
         lax.broadcasted_iota(jnp.int32, (order, order), 0) == lax.broadcasted_iota(jnp.int32, (order, order), 1)
     ).astype(f32)
 
 
+def eliminate(matrix, right, full):
+    order = matrix.shape[0]
+    held = matrix * unit(order)
+    down = 1.0 / jnp.sqrt(jnp.sum(held, axis=1, keepdims=True))
+    across = 1.0 / jnp.sqrt(jnp.sum(held, axis=0, keepdims=True))
+    table = jnp.concatenate([matrix * across, right], axis=1) * down
+    rows = lax.broadcasted_iota(jnp.int32, table.shape, 0)
+    for j in range(0, order, 2):
+        left = jnp.broadcast_to(table[:, j : j + 1], table.shape)
+        beside = jnp.broadcast_to(table[:, j + 1 : j + 2], table.shape)
+        one, two = table[j : j + 1, :], table[j + 1 : j + 2, :]
+        a, b = left[j : j + 1, :], beside[j : j + 1, :]
+        c, d = left[j + 1 : j + 2, :], beside[j + 1 : j + 2, :]
+        scale = 1.0 / (a * d - b * c)
+        first = (d * one - b * two) * scale
+        second = (a * two - c * one) * scale
+        moved = table - left * first - beside * second
+        if full:
+            table = jnp.where(rows == j, first, jnp.where(rows == j + 1, second, moved))
+        else:
+            table = jnp.where(rows > j + 1, moved, jnp.where(rows == j + 1, two - (c / a) * one, table))
+    if full:
+        return table[:, order:] * down
+    pivots = jnp.sum(table[:, :order] * unit(order), axis=1, keepdims=True)
+    return table[:, order:] * (1.0 / jnp.sqrt(pivots))
+
+
 def inverse(matrix):
-    order = matrix.shape[0]
-    return eliminate(jnp.concatenate([matrix, unit(order)], axis=1), True)[:, order:]
+    return eliminate(matrix, unit(matrix.shape[0]), True)
 
 
 def cholesky_inverse(matrix):
-    order = matrix.shape[0]
-    done = eliminate(jnp.concatenate([matrix, unit(order)], axis=1), False)
-    pivots = jnp.sum(done[:, :order] * unit(order), axis=1, keepdims=True)
-    return done[:, order:] * (1.0 / jnp.sqrt(pivots))
+    return eliminate(matrix, unit(matrix.shape[0]), False)
 
 
 def coefficients(table, gram, xp, pp, pax, pap_inverse, total_rows):
@@ -238,7 +240,7 @@
         second = nn(pap_inverse, pax)
         rhs = nn(wap, second) - wax
     schur = waw - nn(wap, first)
-    zw = eliminate(jnp.concatenate([schur, rhs], axis=1), True)[:, n:]
+    zw = eliminate(schur, rhs, True)
     zp = -nn(first, zw)
     if pax is not None:
         zp = zp - second

time: 164 us -> 161 us (0.982)
  Pallas kernels: 57.9 us -> 55.2 us
    pallas_call x15, Pallas kernels: 57.9 us -> 55.2 us  [run(): pl.pallas_call(kernel, name=name, out_shape=outs, in_specs=in_specs, out_...]
  transfers between devices with their start and end apart: 52 -> 52, of which waited for: 28 -> 29; matrix products, arithmetic and copies ran while one was open for 2% -> 2% of each run, Pallas kernels for 10% -> 10%
where the time goes in v7:
time: 161 us
  starting transfers between devices  63.4 us (39%)
  Pallas kernels  55.2 us (34%)
  waiting for transfers between devices  35.3 us (22%)
  local copies, waits for them, and re-layouts  5.87 us (4%)
    pallas_call x15, Pallas kernels, run(): pl.pallas_call(kernel, name=name, out_shape=outs, in_specs=in_specs, out_...  55.2 us
    ppermute x31, starting transfers between devices, sub_send(): return lax.ppermute(value, 'sub', [(s, s ^ k) for s in range(n_sub)])  38.7 us
    ppermute x21, starting transfers between devices, row_send(): return lax.ppermute(value, 'row', [(r, r ^ k) for r in range(n_row)])  24.7 us
    ppermute x31, waiting for transfers between devices, sub_send(): return lax.ppermute(value, 'sub', [(s, s ^ k) for s in range(n_sub)])  19.4 us
    ppermute x21, waiting for transfers between devices, row_send(): return lax.ppermute(value, 'row', [(r, r ^ k) for r in range(n_row)])  15.9 us
    optimization_barrier x1, local copies, waits for them, and re-layouts, local(): after((in_val, if_val, halo[0], halo[-1]))  3.29 us
  transfers between devices with their start and end apart: 52, of which 29 were waited for; matrix products, arithmetic and copies ran while one was open for 2% of the time, Pallas kernels for 10%

profile of v7, /device:TPU:0, one launch (start us, length us, event | category | flops | bytes accessed | tf_op | source)
XLA Modules:
  0.0 160.9 jit_solution(125710205430775549)
XLA Ops:
  0.6 0.9 copy-done
  1.6 0.9 copy-done.2
  4.5 0.9 collective-permute-done.1
  5.4 5.0 %collective-permute-start.2 = (s16[8,64,128]{2,1,0:T(8,128)(2,1)S(1)}, s16[8,64,128]{2,1,0:T(8,128)(2,1)S(1)}, u32[]{:S(2)}, u32[]{:S(2)}) collective-permute-start(s16[8,64,128]{2,1,0:T(8,128)(2,1)S(1)} %constant_dynamic-update-slice_fusion.refs_3_), channel_id=1, source_target_pairs={{0,24},{4,28},{8,16},{12,20},{16,8},{20,12},{24,0},{28,4},{1,25},{... | collective-permute-start | bytes 393224 | tf_op jit(solution)/shard_map/ppermute | solution.py:548
  10.5 1.5 collective-permute-start
  11.9 1.5 collective-permute-start.4
  14.4 5.8 %collective-permute-start.5 = (s16[8,64,128]{2,1,0:T(8,128)(2,1)S(1)}, s16[8,64,128]{2,1,0:T(8,128)(2,1)S(1)}, u32[]{:S(2)}, u32[]{:S(2)}) collective-permute-start(s16[8,64,128]{2,1,0:T(8,128)(2,1)S(1)} %constant_dynamic-update-slice_fusion.refs_3_), channel_id=1, source_target_pairs={{0,8},{4,12},{8,0},{12,4},{16,24},{20,28},{24,16},{28,20},{1,9},{5... | collective-permute-start | bytes 393224 | tf_op jit(solution)/shard_map/ppermute | solution.py:548
  20.3 3.3 %copy.12 = bf16[1,1,96,64,64]{4,3,2,1,0:T(8,128)(2,1)S(1)} copy(bf16[1,1,96,64,64]{2,4,3,1,0:T(8,128)(2,1)} %param.15) | data formatting | bytes 1572864 | tf_op jit(solution)/shard_map/optimization_barrier | solution.py:614
  23.7 2.2 %prepare.1 = (bf16[12,64,1024]{2,1,0:T(8,128)(2,1)S(1)}, bf16[12,64,512]{2,1,0:T(8,128)(2,1)S(1)}, bf16[12,64,128]{2,1,0:T(8,128)(2,1)S(1)}, s32[96]{0:T(128)S(1)}) custom-call(bf16[96,64,64]{2,1,0:T(8,128)(2,1)S(1)} %bitcast.19, bf16[12,64,64]{2,1,0:T(8,128)(2,1)S(1)} %bitcast.25, s32[96]{0:T(128)S(1)} %bitcast.29, s32[96]{0:T(128)S(1)} %bitcast.30, ...), custom_call_target="tpu_custom_call" | custom-call | flops 1000000 | bytes 3441888 | tf_op jit(solution)/shard_map/prepare/pallas_call | solution.py:514
  25.9 2.2 %partials.3 = (f32[64,768]{1,0:T(8,128)S(1)}, f32[8,64,128]{2,1,0:T(8,128)S(1)}, s16[8,64,128]{2,1,0:T(8,128)(2,1)S(1)}, s16[7,64,128]{2,1,0:T(8,128)(2,1)S(1)},...) custom-call(f32[64,768]{1,0:T(8,128)S(1)} %bitcast.14, ...), custom_call_target="tpu_custom_call" | custom-call | flops 1000000 | bytes 1917320 | tf_op jit(solution)/shard_map/partials/pallas_call | solution.py:514
  28.1 2.2 %partials.4 = (f32[128,768]{1,0:T(8,128)S(1)}, f32[16,64,128]{2,1,0:T(8,128)S(1)}, s16[16,64,128]{2,1,0:T(8,128)(2,1)S(1)}, s16[14,64,128]{2,1,0:T(8,128)(2,1)S(...) custom-call(f32[64,768]{1,0:T(8,128)S(1)} %bitcast.21, ...), custom_call_target="tpu_custom_call" | custom-call | flops 1000000 | bytes 3785096 | tf_op jit(solution)/shard_map/partials/pallas_call | solution.py:514
  30.5 1.6 collective-permute-start.7
  32.0 1.5 collective-permute-start.8
  34.0 1.0 pair.2
  35.1 3.1 %collective-permute-start.12 = (s16[4,64,128]{2,1,0:T(8,128)(2,1)S(1)}, s16[4,64,128]{2,1,0:T(8,128)(2,1)S(1)}, u32[]{:S(2)}, u32[]{:S(2)}) collective-permute-start(s16[4,64,128]{2,1,0:T(8,128)(2,1)S(1)} %get-tuple-element.123), channel_id=1, source_target_pairs={{0,16},{4,20},{8,24},{12,28},{16,0},{20,4},{24,8},{28,12},{1,17},{... | collective-permute-start | bytes 196616 | tf_op jit(solution)/shard_map/ppermute | solution.py:548
  38.9 2.6 %collective-permute-start.13 = (s16[4,64,128]{2,1,0:T(8,128)(2,1)S(1)}, s16[4,64,128]{2,1,0:T(8,128)(2,1)S(1)}, u32[]{:S(2)}, u32[]{:S(2)}) collective-permute-start(s16[4,64,128]{2,1,0:T(8,128)(2,1)S(1)} %get-tuple-element.124), channel_id=1, source_target_pairs={{0,24},{4,28},{8,16},{12,20},{16,8},{20,12},{24,0},{28,4},{1,25},{... | collective-permute-start | bytes 196616 | tf_op jit(solution)/shard_map/ppermute | solution.py:548
  41.5 4.3 %start_image.1 = (f32[64,768]{1,0:T(8,128)S(1)}, f32[64,768]{1,0:T(8,128)S(1)}, f32[64,768]{1,0:T(8,128)S(1)}, f32[64,768]{1,0:T(8,128)S(1)}, f32[96,128]{1,0:T(8,128)S(1)}, /*index=5*/f32[96,128]{1,0:T(8,128)S(1)}) custom-call(s16[14,64,128]{2,1,0:T(8,128)(2,1)S(1)} %collective-permute-done.refs_0_, s16[14,64,128]{2,1,0:T(8,128)(2,1)S(1)} %collective-permute-done.3.refs_1_, ...), custom_call_target="tpu_custom_call" | custom-call | flops 1000000 | bytes 4260232 | tf_op jit(solution)/shard_map/start_image/pallas_call | solution.py:514
  45.9 1.2 collective-permute-done.14
  47.2 1.7 %collective-permute-start.17 = (f32[96,128]{1,0:T(8,128)S(1)}, f32[96,128]{1,0:T(8,128)S(1)}, u32[]{:S(2)}, u32[]{:S(2)}) collective-permute-start(f32[96,128]{1,0:T(8,128)S(1)} %add.63), channel_id=1, source_target_pairs={{0,24},{4,28},{8,16},{12,20},{16,8},{20,12},{24,0},{28,4},{1,25},{... | collective-permute-start | bytes 147464 | tf_op jit(solution)/shard_map/ppermute | solution.py:548
  48.9 2.8 %collective-permute-start.15 = (f32[96,128]{1,0:T(8,128)S(1)}, f32[96,128]{1,0:T(8,128)S(1)}, u32[]{:S(2)}, u32[]{:S(2)}) collective-permute-start(f32[96,128]{1,0:T(8,128)S(1)} %add.63), channel_id=1, source_target_pairs={{0,8},{4,12},{8,0},{12,4},{16,24},{20,28},{24,16},{28,20},{1,9},{5... | collective-permute-start | bytes 147464 | tf_op jit(solution)/shard_map/ppermute | solution.py:548
  51.6 1.8 %collective-permute-done.17 = f32[96,128]{1,0:T(8,128)S(1)} collective-permute-done((f32[96,128]{1,0:T(8,128)S(1)}, f32[96,128]{1,0:T(8,128)S(1)}, u32[]{:S(2)}, u32[]{:S(2)}) %collective-permute-start.17) | collective-permute-done | bytes 49184 | tf_op jit(solution)/shard_map/ppermute | solution.py:548
  53.4 1.5 collective-permute-done.16
  54.9 2.6 %collective-permute-start.20 = (f32[96,128]{1,0:T(8,128)S(1)}, f32[96,128]{1,0:T(8,128)S(1)}, u32[]{:S(2)}, u32[]{:S(2)}) collective-permute-start(f32[96,128]{1,0:T(8,128)S(1)} %add_add_fusion.5), channel_id=1, source_target_pairs={{0,3},{1,2},{2,1},{3,0},{4,7},{5,6},{6,5},{7,4},{8,11},{9,10},{10,... | collective-permute-start | bytes 147464 | tf_op jit(solution)/shard_map/ppermute | solution.py:545
  58.4 1.5 collective-permute-done.20
  60.0 1.6 collective-permute-done.19
  62.2 1.2 collective-permute-done.21.refs_9_
  63.4 4.9 %update.1 = (f32[192,128]{1,0:T(8,128)S(1)}, f32[64,768]{1,0:T(8,128)S(1)}, f32[64,64]{1,0:T(8,128)S(1)}, f32[64,768]{1,0:T(8,128)S(1)}, s16[7,64,128]{2,1,0:T(8,128)(2,1)S(1)}, /*index=5*/s16[2,64,128]{2,1,0:T(8,128)(2,1)S(1)}) custom-call(f32[128,768]{1,0:T(8,128)S(1)} %get-tuple-element.125.refs_0_, ...), custom_call_target="tpu_custom_call" | custom-call | flops 1000000 | bytes 2755604 | tf_op jit(solution)/shard_map/update/pallas_call | solution.py:514
  68.3 2.4 %partials.5 = (f32[64,768]{1,0:T(8,128)S(1)}, f32[8,64,128]{2,1,0:T(8,128)S(1)}, s16[10,64,128]{2,1,0:T(8,128)(2,1)S(1)}, s16[14,64,128]{2,1,0:T(8,128)(2,1)S(1)...) custom-call(f32[64,768]{1,0:T(8,128)S(1)} %get-tuple-element.137.vector.refs_12_.refs_28_, ...), custom_call_target="tpu_custom_call" | custom-call | flops 1000000 | bytes 2441608 | tf_op jit(solution)/shard_map/partials/pallas_call | solution.py:514
  71.2 1.6 collective-permute-start.23
  72.8 1.4 collective-permute-start.24
  75.1 0.9 collective-permute-start.26
  75.9 1.4 collective-permute-start.27
  77.3 1.9 %collective-permute-done.22.refs_0_.refs_9_ = s16[14,64,128]{2,1,0:T(8,128)(2,1)S(1)} collective-permute-done((s16[14,64,128]{2,1,0:T(8,128)(2,1)S(1)}, s16[14,64,128]{2,1,0:T(8,128)(2,1)S(1)}, u32[]{:S(2)}, u32[]{:S(2)}) %collective-permute-start.22) | collective-permute-done | bytes 229408 | tf_op jit(solution)/shard_map/ppermute | solution.py:545
  79.2 1.6 %collective-permute-start.28 = (s16[6,64,128]{2,1,0:T(8,128)(2,1)S(1)}, s16[6,64,128]{2,1,0:T(8,128)(2,1)S(1)}, u32[]{:S(2)}, u32[]{:S(2)}) collective-permute-start(s16[6,64,128]{2,1,0:T(8,128)(2,1)S(1)} %get-tuple-element.149), channel_id=1, source_target_pairs={{0,24},{4,28},{8,16},{12,20},{16,8},{20,12},{24,0},{28,4},{1,25},{... | collective-permute-start | bytes 294920 | tf_op jit(solution)/shard_map/ppermute | solution.py:548
  80.8 2.4 %collective-permute-done.23.refs_1_.refs_10_ = s16[14,64,128]{2,1,0:T(8,128)(2,1)S(1)} collective-permute-done((s16[14,64,128]{2,1,0:T(8,128)(2,1)S(1)}, s16[14,64,128]{2,1,0:T(8,128)(2,1)S(1)}, u32[]{:S(2)}, u32[]{:S(2)}) %collective-permute-start.23) | collective-permute-done | bytes 229408 | tf_op jit(solution)/shard_map/ppermute | solution.py:545
  83.3 1.0 collective-permute-done.24.refs_2_.refs_11_
  84.3 2.1 %collective-permute-done.27.refs_6_.refs_14_ = s16[6,64,128]{2,1,0:T(8,128)(2,1)S(1)} collective-permute-done((s16[6,64,128]{2,1,0:T(8,128)(2,1)S(1)}, s16[6,64,128]{2,1,0:T(8,128)(2,1)S(1)}, u32[]{:S(2)}, u32[]{:S(2)}) %collective-permute-start.27) | collective-permute-done | bytes 98336 | tf_op jit(solution)/shard_map/ppermute | solution.py:548
  86.4 3.3 %update_image.2 = (f32[64,768]{1,0:T(8,128)S(1)}, f32[64,768]{1,0:T(8,128)S(1)}, f32[96,128]{1,0:T(8,128)S(1)}, f32[96,128]{1,0:T(8,128)S(1)}) custom-call(s16[14,64,128]{2,1,0:T(8,128)(2,1)S(1)} %collective-permute-done.22.refs_0_.refs_9_, s16[14,64,128]{2,1,0:T(8,128)(2,1)S(1)} %collective-permute-done.23.refs_1_.refs_10_, ...), custom_call_target="tpu_custom_call" | custom-call | flops 1000000 | bytes 4424072 | tf_op jit(solution)/shard_map/update_image/pallas_call | solution.py:514
  89.8 1.2 collective-permute-done.29
  91.0 1.7 %collective-permute-start.32 = (f32[96,128]{1,0:T(8,128)S(1)}, f32[96,128]{1,0:T(8,128)S(1)}, u32[]{:S(2)}, u32[]{:S(2)}) collective-permute-start(f32[96,128]{1,0:T(8,128)S(1)} %add.70), channel_id=1, source_target_pairs={{0,24},{4,28},{8,16},{12,20},{16,8},{20,12},{24,0},{28,4},{1,25},{... | collective-permute-start | bytes 147464 | tf_op jit(solution)/shard_map/ppermute | solution.py:548
  92.7 1.5 collective-permute-start.31
  94.2 1.3 collective-permute-start.30
  95.5 3.4 %pap_inverse.1.refs_22_ = f32[64,64]{1,0:T(8,128)S(1)} custom-call(f32[192,128]{1,0:T(8,128)S(1)} %get-tuple-element.154.table.refs_20_), custom_call_target="tpu_custom_call" | custom-call | flops 1000000 | bytes 114688 | tf_op jit(solution)/shard_map/pap_inverse/pallas_call | solution.py:514
  99.3 1.5 collective-permute-start.35
  101.3 1.5 collective-permute-start.33
  102.8 1.9 %collective-permute-done.35 = f32[96,128]{1,0:T(8,128)S(1)} collective-permute-done((f32[96,128]{1,0:T(8,128)S(1)}, f32[96,128]{1,0:T(8,128)S(1)}, u32[]{:S(2)}, u32[]{:S(2)}) %collective-permute-start.35) | collective-permute-done | bytes 49184 | tf_op jit(solution)/shard_map/ppermute | solution.py:545
  105.5 1.2 collective-permute-done.36.refs_17_
  106.7 10.3 %move.1 = (f32[64,768]{1,0:T(8,128)S(1)}, f32[64,768]{1,0:T(8,128)S(1)}, f32[64,768]{1,0:T(8,128)S(1)}, s16[7,64,128]{2,1,0:T(8,128)(2,1)S(1)}, s16[2,64,128]{2,...) custom-call(f32[128,768]{1,0:T(8,128)S(1)} %get-tuple-element.125.refs_0_, ...), custom_call_target="tpu_custom_call" | custom-call | flops 1000000 | bytes 5655572 | tf_op jit(solution)/shard_map/move/pallas_call | solution.py:514
  117.2 1.0 collective-permute-done.40
  118.2 1.7 %collective-permute-start.43 = (s16[4,64,128]{2,1,0:T(8,128)(2,1)S(1)}, s16[4,64,128]{2,1,0:T(8,128)(2,1)S(1)}, u32[]{:S(2)}, u32[]{:S(2)}) collective-permute-start(s16[4,64,128]{2,1,0:T(8,128)(2,1)S(1)} %constant_dynamic-update-slice_fusion.2.refs_3_), channel_id=1, source_target_pairs={{0,24},{4,28},{8,16},{12,20},{16,8},{20,12},{24,0},{28,4},{1,25},{... | collective-permute-start | bytes 196616 | tf_op jit(solution)/shard_map/ppermute | solution.py:548
  119.9 2.5 %collective-permute-start.39 = (s16[7,64,128]{2,1,0:T(8,128)(2,1)S(1)}, s16[7,64,128]{2,1,0:T(8,128)(2,1)S(1)}, u32[]{:S(2)}, u32[]{:S(2)}) collective-permute-start(s16[7,64,128]{2,1,0:T(8,128)(2,1)S(1)} %get-tuple-element.161), channel_id=1, source_target_pairs={{0,3},{1,2},{2,1},{3,0},{4,7},{5,6},{6,5},{7,4},{8,11},{9,10},{10,... | collective-permute-start | bytes 344072 | tf_op jit(solution)/shard_map/ppermute | solution.py:545
  124.3 1.8 %collective-permute-start.41 = (s16[4,64,128]{2,1,0:T(8,128)(2,1)S(1)}, s16[4,64,128]{2,1,0:T(8,128)(2,1)S(1)}, u32[]{:S(2)}, u32[]{:S(2)}) collective-permute-start(s16[4,64,128]{2,1,0:T(8,128)(2,1)S(1)} %constant_dynamic-update-slice_fusion.2.refs_3_), channel_id=1, source_target_pairs={{0,8},{4,12},{8,0},{12,4},{16,24},{20,28},{24,16},{28,20},{1,9},{5... | collective-permute-start | bytes 196616 | tf_op jit(solution)/shard_map/ppermute | solution.py:548
  126.1 4.3 %settle.1 = (f32[64,768]{1,0:T(8,128)S(1)}, f32[64,768]{1,0:T(8,128)S(1)}, f32[192,64]{1,0:T(8,128)S(1)}) custom-call(f32[256,64]{1,0:T(8,128)S(1)} %get-tuple-element.165.small, f32[64,768]{1,0:T(8,128)S(1)} %get-tuple-element.166.step_x, f32[64,768]{1,0:T(8,128)S(1)} %get-tuple-element.167.step_a), custom_call_target="tpu_custom_call" | custom-call | flops 1000000 | bytes 901120 | tf_op jit(solution)/shard_map/settle/pallas_call | solution.py:514
  130.4 3.5 %update_image.3 = (f32[64,768]{1,0:T(8,128)}, f32[64,768]{1,0:T(8,128)}, f32[96,128]{1,0:T(8,128)S(1)}, f32[96,128]{1,0:T(8,128)S(1)}) custom-call(s16[7,64,128]{2,1,0:T(8,128)(2,1)S(1)} %collective-permute-done.37.refs_0_, s16[7,64,128]{2,1,0:T(8,128)(2,1)S(1)} %collective-permute-done.38.refs_1_, s16[7,64,128]{2,1,0:T(8,128)(2,1)S(1)} %collective-permute-done.39.refs_2_, ...), custom_call_target="tpu_custom_call" | custom-call | flops 1000000 | bytes 3850632 | tf_op jit(solution)/shard_map/update_image/pallas_call | solution.py:514
  133.9 1.2 collective-permute-done.44
  135.2 1.7 %collective-permute-start.47 = (f32[96,128]{1,0:T(8,128)S(1)}, f32[96,128]{1,0:T(8,128)S(1)}, u32[]{:S(2)}, u32[]{:S(2)}) collective-permute-start(f32[96,128]{1,0:T(8,128)S(1)} %add.77), channel_id=1, source_target_pairs={{0,24},{4,28},{8,16},{12,20},{16,8},{20,12},{24,0},{28,4},{1,25},{... | collective-permute-start | bytes 147464 | tf_op jit(solution)/shard_map/ppermute | solution.py:548
  136.9 2.7 %collective-permute-start.45 = (f32[96,128]{1,0:T(8,128)S(1)}, f32[96,128]{1,0:T(8,128)S(1)}, u32[]{:S(2)}, u32[]{:S(2)}) collective-permute-start(f32[96,128]{1,0:T(8,128)S(1)} %add.77), channel_id=1, source_target_pairs={{0,8},{4,12},{8,0},{12,4},{16,24},{20,28},{24,16},{28,20},{1,9},{5... | collective-permute-start | bytes 147464 | tf_op jit(solution)/shard_map/ppermute | solution.py:548
  139.6 1.8 %collective-permute-done.47 = f32[96,128]{1,0:T(8,128)S(1)} collective-permute-done((f32[96,128]{1,0:T(8,128)S(1)}, f32[96,128]{1,0:T(8,128)S(1)}, u32[]{:S(2)}, u32[]{:S(2)}) %collective-permute-start.47) | collective-permute-done | bytes 49184 | tf_op jit(solution)/shard_map/ppermute | solution.py:548
  141.4 1.5 collective-permute-done.46
  142.9 2.6 %collective-permute-start.50 = (f32[96,128]{1,0:T(8,128)S(1)}, f32[96,128]{1,0:T(8,128)S(1)}, u32[]{:S(2)}, u32[]{:S(2)}) collective-permute-start(f32[96,128]{1,0:T(8,128)S(1)} %add_add_fusion.1), channel_id=1, source_target_pairs={{0,3},{1,2},{2,1},{3,0},{4,7},{5,6},{6,5},{7,4},{8,11},{9,10},{10,... | collective-permute-start | bytes 147464 | tf_op jit(solution)/shard_map/ppermute | solution.py:545
  146.5 1.5 collective-permute-done.50
  148.0 1.6 %collective-permute-done.49 = f32[96,128]{1,0:T(8,128)S(1)} collective-permute-done((f32[96,128]{1,0:T(8,128)S(1)}, f32[96,128]{1,0:T(8,128)S(1)}, u32[]{:S(2)}, u32[]{:S(2)}) %collective-permute-start.49) | collective-permute-done | bytes 49184 | tf_op jit(solution)/shard_map/ppermute | solution.py:545
  150.2 1.2 collective-permute-done.51.other
  151.4 9.5 %finish.1 = (f32[64,768]{1,0:T(8,128)}, f32[64,768]{1,0:T(8,128)}) custom-call(f32[96,128]{1,0:T(8,128)S(1)} %add_add_fusion.mine, f32[96,128]{1,0:T(8,128)S(1)} %collective-permute-done.51.other, s32[2]{0:T(128)S(1)} %pad_add_fusion.refs_10_.pos.refs_11_.refs_18_, f32[192,64]{1,0:T(8,128)S(1)} %get-tuple-element.173.state, ...), custom_call_target="tpu_custom_call" | custom-call | flops 1000000 | bytes 1130504 | tf_op jit(solution)/shard_map/finish/pallas_call | solution.py:514
  (95 shorter events, 12.9 us)
Async XLA Ops:
  0.6 0.9 copy-start
  1.6 0.9 copy-start.2
  2.5 0.7 copy-start.5
  3.1 20.5 %copy-start.4 = (bf16[1,1,12,64,64]{4,3,2,1,0:T(8,128)(2,1)S(1)}, bf16[1,1,12,64,64]{4,3,2,1,0:T(8,128)(2,1)}, u32[]{:S(2)}) copy-start(bf16[1,1,12,64,64]{4,3,2,1,0:T(8,128)(2,1)} %param.19) | copy-start | bytes 294916
  3.1 20.5 %copy-start.7 = (s32[1,1,96]{2,1,0:T(1,128)S(1)}, s32[1,1,96]{2,1,0:T(1,128)}, u32[]{:S(2)}) copy-start(s32[1,1,96]{2,1,0:T(1,128)} %param.13) | copy-start | bytes 1156
  3.1 20.5 %copy-start.8 = (s32[1,1,96]{2,1,0:T(1,128)S(1)}, s32[1,1,96]{2,1,0:T(1,128)}, u32[]{:S(2)}) copy-start(s32[1,1,96]{2,1,0:T(1,128)} %param.14) | copy-start | bytes 1156
  3.2 20.5 %copy-start.9 = (s32[1,1,12]{2,1,0:T(1,128)S(1)}, s32[1,1,12]{2,1,0:T(1,128)}, u32[]{:S(2)}) copy-start(s32[1,1,12]{2,1,0:T(1,128)} %param.17) | copy-start | bytes 148
  3.2 20.5 %copy-start.10 = (s32[1,1,12]{2,1,0:T(1,128)S(1)}, s32[1,1,12]{2,1,0:T(1,128)}, u32[]{:S(2)}) copy-start(s32[1,1,12]{2,1,0:T(1,128)} %param.18) | copy-start | bytes 148
  4.0 1.4 collective-permute-start.1
  5.4 8.9 %collective-permute-start.2 = (s16[8,64,128]{2,1,0:T(8,128)(2,1)S(1)}, s16[8,64,128]{2,1,0:T(8,128)(2,1)S(1)}, u32[]{:S(2)}, u32[]{:S(2)}) collective-permute-start(s16[8,64,128]{2,1,0:T(8,128)(2,1)S(1)} %constant_dynamic-update-slice_fusion.refs_3_), channel_id=1, source_target_pairs={{0,24},{4,28},{8,16},{12,20},{16,8},{20,12},{24,0},{28,4},{1,25},{... | collective-permute-start | bytes 393224 | tf_op jit(solution)/shard_map/ppermute | solution.py:548
  10.5 9.8 %collective-permute-start = (s16[14,64,128]{2,1,0:T(8,128)(2,1)S(1)}, s16[14,64,128]{2,1,0:T(8,128)(2,1)S(1)}, u32[]{:S(2)}, u32[]{:S(2)}) collective-permute-start(s16[14,64,128]{2,1,0:T(8,128)(2,1)S(1)} %get-tuple-element.89), channel_id=1, source_target_pairs={{0,1},{1,0},{2,3},{3,2},{4,5},{5,4},{6,7},{7,6},{8,9},{9,8},{10,11... | collective-permute-start | bytes 688136 | tf_op jit(solution)/shard_map/ppermute | solution.py:545
  11.9 14.0 %collective-permute-start.4 = (s16[14,64,128]{2,1,0:T(8,128)(2,1)S(1)}, s16[14,64,128]{2,1,0:T(8,128)(2,1)S(1)}, u32[]{:S(2)}, u32[]{:S(2)}) collective-permute-start(s16[14,64,128]{2,1,0:T(8,128)(2,1)S(1)} %get-tuple-element.89), channel_id=1, source_target_pairs={{0,3},{1,2},{2,1},{3,0},{4,7},{5,6},{6,5},{7,4},{8,11},{9,10},{10,... | collective-permute-start | bytes 688136 | tf_op jit(solution)/shard_map/ppermute | solution.py:545
  13.4 12.5 %collective-permute-start.3 = (s16[14,64,128]{2,1,0:T(8,128)(2,1)S(1)}, s16[14,64,128]{2,1,0:T(8,128)(2,1)S(1)}, u32[]{:S(2)}, u32[]{:S(2)}) collective-permute-start(s16[14,64,128]{2,1,0:T(8,128)(2,1)S(1)} %get-tuple-element.89), channel_id=1, source_target_pairs={{0,2},{1,3},{2,0},{3,1},{4,6},{5,7},{6,4},{7,5},{8,10},{9,11},{10,... | collective-permute-start | bytes 688136 | tf_op jit(solution)/shard_map/ppermute | solution.py:545
  14.0 11.9 %collective-permute-start.6 = (s16[8,64,128]{2,1,0:T(8,128)(2,1)S(1)}, s16[8,64,128]{2,1,0:T(8,128)(2,1)S(1)}, u32[]{:S(2)}, u32[]{:S(2)}) collective-permute-start(s16[8,64,128]{2,1,0:T(8,128)(2,1)S(1)} %constant_dynamic-update-slice_fusion.refs_3_), channel_id=1, source_target_pairs={{0,16},{4,20},{8,24},{12,28},{16,0},{20,4},{24,8},{28,12},{1,17},{... | collective-permute-start | bytes 393224 | tf_op jit(solution)/shard_map/ppermute | solution.py:548
  14.4 11.5 %collective-permute-start.5 = (s16[8,64,128]{2,1,0:T(8,128)(2,1)S(1)}, s16[8,64,128]{2,1,0:T(8,128)(2,1)S(1)}, u32[]{:S(2)}, u32[]{:S(2)}) collective-permute-start(s16[8,64,128]{2,1,0:T(8,128)(2,1)S(1)} %constant_dynamic-update-slice_fusion.refs_3_), channel_id=1, source_target_pairs={{0,8},{4,12},{8,0},{12,4},{16,24},{20,28},{24,16},{28,20},{1,9},{5... | collective-permute-start | bytes 393224 | tf_op jit(solution)/shard_map/ppermute | solution.py:548
  20.3 5.6 %copy-start.1 = (f32[768,64]{0,1:T(8,128)S(1)}, f32[768,64]{0,1:T(8,128)}, u32[]{:S(2)}) copy-start(f32[768,64]{0,1:T(8,128)} %param.10) | copy-start | bytes 589828
  23.6 4.5 %copy-start.3 = (f32[768,64]{0,1:T(8,128)S(1)}, f32[768,64]{0,1:T(8,128)}, u32[]{:S(2)}) copy-start(f32[768,64]{0,1:T(8,128)} %param.11) | copy-start | bytes 589828
  30.4 3.6 %collective-permute-start.10 = (s16[16,64,128]{2,1,0:T(8,128)(2,1)S(1)}, s16[16,64,128]{2,1,0:T(8,128)(2,1)S(1)}, u32[]{:S(2)}, u32[]{:S(2)}) collective-permute-start(s16[16,64,128]{2,1,0:T(8,128)(2,1)S(1)} %get-tuple-element.120), channel_id=1, source_target_pairs={{0,4},{4,0},{8,12},{12,8},{16,20},{20,16},{24,28},{28,24},{1,5},{5... | collective-permute-start | bytes 786440 | tf_op jit(solution)/shard_map/ppermute | solution.py:548
  30.5 8.5 %collective-permute-start.7 = (s16[14,64,128]{2,1,0:T(8,128)(2,1)S(1)}, s16[14,64,128]{2,1,0:T(8,128)(2,1)S(1)}, u32[]{:S(2)}, u32[]{:S(2)}) collective-permute-start(s16[14,64,128]{2,1,0:T(8,128)(2,1)S(1)} %get-tuple-element.116), channel_id=1, source_target_pairs={{0,1},{1,0},{2,3},{3,2},{4,5},{5,4},{6,7},{7,6},{8,9},{9,8},{10,11... | collective-permute-start | bytes 688136 | tf_op jit(solution)/shard_map/ppermute | solution.py:545
  32.0 13.8 %collective-permute-start.8 = (s16[14,64,128]{2,1,0:T(8,128)(2,1)S(1)}, s16[14,64,128]{2,1,0:T(8,128)(2,1)S(1)}, u32[]{:S(2)}, u32[]{:S(2)}) collective-permute-start(s16[14,64,128]{2,1,0:T(8,128)(2,1)S(1)} %get-tuple-element.117), channel_id=1, source_target_pairs={{0,2},{1,3},{2,0},{3,1},{4,6},{5,7},{6,4},{7,5},{8,10},{9,11},{10,... | collective-permute-start | bytes 688136 | tf_op jit(solution)/shard_map/ppermute | solution.py:545
  33.5 12.3 %collective-permute-start.9 = (s16[14,64,128]{2,1,0:T(8,128)(2,1)S(1)}, s16[14,64,128]{2,1,0:T(8,128)(2,1)S(1)}, u32[]{:S(2)}, u32[]{:S(2)}) collective-permute-start(s16[14,64,128]{2,1,0:T(8,128)(2,1)S(1)} %get-tuple-element.118), channel_id=1, source_target_pairs={{0,3},{1,2},{2,1},{3,0},{4,7},{5,6},{6,5},{7,4},{8,11},{9,10},{10,... | collective-permute-start | bytes 688136 | tf_op jit(solution)/shard_map/ppermute | solution.py:545
  35.0 10.8 %collective-permute-start.11 = (s16[4,64,128]{2,1,0:T(8,128)(2,1)S(1)}, s16[4,64,128]{2,1,0:T(8,128)(2,1)S(1)}, u32[]{:S(2)}, u32[]{:S(2)}) collective-permute-start(s16[4,64,128]{2,1,0:T(8,128)(2,1)S(1)} %get-tuple-element.122), channel_id=1, source_target_pairs={{0,8},{4,12},{8,0},{12,4},{16,24},{20,28},{24,16},{28,20},{1,9},{5... | collective-permute-start | bytes 196616 | tf_op jit(solution)/shard_map/ppermute | solution.py:548
  35.1 10.8 %collective-permute-start.12 = (s16[4,64,128]{2,1,0:T(8,128)(2,1)S(1)}, s16[4,64,128]{2,1,0:T(8,128)(2,1)S(1)}, u32[]{:S(2)}, u32[]{:S(2)}) collective-permute-start(s16[4,64,128]{2,1,0:T(8,128)(2,1)S(1)} %get-tuple-element.123), channel_id=1, source_target_pairs={{0,16},{4,20},{8,24},{12,28},{16,0},{20,4},{24,8},{28,12},{1,17},{... | collective-permute-start | bytes 196616 | tf_op jit(solution)/shard_map/ppermute | solution.py:548
  38.9 6.9 %collective-permute-start.13 = (s16[4,64,128]{2,1,0:T(8,128)(2,1)S(1)}, s16[4,64,128]{2,1,0:T(8,128)(2,1)S(1)}, u32[]{:S(2)}, u32[]{:S(2)}) collective-permute-start(s16[4,64,128]{2,1,0:T(8,128)(2,1)S(1)} %get-tuple-element.124), channel_id=1, source_target_pairs={{0,24},{4,28},{8,16},{12,20},{16,8},{20,12},{24,0},{28,4},{1,25},{... | collective-permute-start | bytes 196616 | tf_op jit(solution)/shard_map/ppermute | solution.py:548
  41.5 20.7 %copy-start.11 = (f32[768]{0:T(1024)S(1)}, f32[768]{0:T(1024)}, u32[]{:S(2)}) copy-start(f32[768]{0:T(1024)} %param.12) | copy-start | bytes 9220
  41.5 21.9 %copy-start.6 = (s32[1,1,3]{2,1,0:T(1,128)S(1)}, s32[1,1,3]{2,1,0:T(1,128)}, u32[]{:S(2)}) copy-start(s32[1,1,3]{2,1,0:T(1,128)} %param.16) | copy-start | bytes 40
  45.9 1.3 collective-permute-start.14
  47.2 6.3 %collective-permute-start.17 = (f32[96,128]{1,0:T(8,128)S(1)}, f32[96,128]{1,0:T(8,128)S(1)}, u32[]{:S(2)}, u32[]{:S(2)}) collective-permute-start(f32[96,128]{1,0:T(8,128)S(1)} %add.63), channel_id=1, source_target_pairs={{0,24},{4,28},{8,16},{12,20},{16,8},{20,12},{24,0},{28,4},{1,25},{... | collective-permute-start | bytes 147464 | tf_op jit(solution)/shard_map/ppermute | solution.py:548
  48.9 6.0 %collective-permute-start.16 = (f32[96,128]{1,0:T(8,128)S(1)}, f32[96,128]{1,0:T(8,128)S(1)}, u32[]{:S(2)}, u32[]{:S(2)}) collective-permute-start(f32[96,128]{1,0:T(8,128)S(1)} %add.63), channel_id=1, source_target_pairs={{0,16},{4,20},{8,24},{12,28},{16,0},{20,4},{24,8},{28,12},{1,17},{... | collective-permute-start | bytes 147464 | tf_op jit(solution)/shard_map/ppermute | solution.py:548
  48.9 6.0 %collective-permute-start.15 = (f32[96,128]{1,0:T(8,128)S(1)}, f32[96,128]{1,0:T(8,128)S(1)}, u32[]{:S(2)}, u32[]{:S(2)}) collective-permute-start(f32[96,128]{1,0:T(8,128)S(1)} %add.63), channel_id=1, source_target_pairs={{0,8},{4,12},{8,0},{12,4},{16,24},{20,28},{24,16},{28,20},{1,9},{5... | collective-permute-start | bytes 147464 | tf_op jit(solution)/shard_map/ppermute | solution.py:548
  54.9 5.1 %collective-permute-start.20 = (f32[96,128]{1,0:T(8,128)S(1)}, f32[96,128]{1,0:T(8,128)S(1)}, u32[]{:S(2)}, u32[]{:S(2)}) collective-permute-start(f32[96,128]{1,0:T(8,128)S(1)} %add_add_fusion.5), channel_id=1, source_target_pairs={{0,3},{1,2},{2,1},{3,0},{4,7},{5,6},{6,5},{7,4},{8,11},{9,10},{10,... | collective-permute-start | bytes 147464 | tf_op jit(solution)/shard_map/ppermute | solution.py:545
  57.5 4.1 %collective-permute-start.19 = (f32[96,128]{1,0:T(8,128)S(1)}, f32[96,128]{1,0:T(8,128)S(1)}, u32[]{:S(2)}, u32[]{:S(2)}) collective-permute-start(f32[96,128]{1,0:T(8,128)S(1)} %add_add_fusion.5), channel_id=1, source_target_pairs={{0,2},{1,3},{2,0},{3,1},{4,6},{5,7},{6,4},{7,5},{8,10},{9,11},{10,... | collective-permute-start | bytes 147464 | tf_op jit(solution)/shard_map/ppermute | solution.py:545
  58.0 4.1 %collective-permute-start.18 = (f32[96,128]{1,0:T(8,128)S(1)}, f32[96,128]{1,0:T(8,128)S(1)}, u32[]{:S(2)}, u32[]{:S(2)}) collective-permute-start(f32[96,128]{1,0:T(8,128)S(1)} %add_add_fusion.5), channel_id=1, source_target_pairs={{0,1},{1,0},{2,3},{3,2},{4,5},{5,4},{6,7},{7,6},{8,9},{9,8},{10,11... | collective-permute-start | bytes 147464 | tf_op jit(solution)/shard_map/ppermute | solution.py:545
  62.1 1.3 collective-permute-start.21
  70.7 8.5 %collective-permute-start.22 = (s16[14,64,128]{2,1,0:T(8,128)(2,1)S(1)}, s16[14,64,128]{2,1,0:T(8,128)(2,1)S(1)}, u32[]{:S(2)}, u32[]{:S(2)}) collective-permute-start(s16[14,64,128]{2,1,0:T(8,128)(2,1)S(1)} %get-tuple-element.141), channel_id=1, source_target_pairs={{0,1},{1,0},{2,3},{3,2},{4,5},{5,4},{6,7},{7,6},{8,9},{9,8},{10,11... | collective-permute-start | bytes 688136 | tf_op jit(solution)/shard_map/ppermute | solution.py:545
  71.2 3.0 %collective-permute-start.25 = (s16[10,64,128]{2,1,0:T(8,128)(2,1)S(1)}, s16[10,64,128]{2,1,0:T(8,128)(2,1)S(1)}, u32[]{:S(2)}, u32[]{:S(2)}) collective-permute-start(s16[10,64,128]{2,1,0:T(8,128)(2,1)S(1)} %get-tuple-element.145), channel_id=1, source_target_pairs={{0,4},{4,0},{8,12},{12,8},{16,20},{20,16},{24,28},{28,24},{1,5},{5... | collective-permute-start | bytes 491528 | tf_op jit(solution)/shard_map/ppermute | solution.py:548
  71.2 12.0 %collective-permute-start.23 = (s16[14,64,128]{2,1,0:T(8,128)(2,1)S(1)}, s16[14,64,128]{2,1,0:T(8,128)(2,1)S(1)}, u32[]{:S(2)}, u32[]{:S(2)}) collective-permute-start(s16[14,64,128]{2,1,0:T(8,128)(2,1)S(1)} %get-tuple-element.142), channel_id=1, source_target_pairs={{0,2},{1,3},{2,0},{3,1},{4,6},{5,7},{6,4},{7,5},{8,10},{9,11},{10,... | collective-permute-start | bytes 688136 | tf_op jit(solution)/shard_map/ppermute | solution.py:545
  72.8 11.5 %collective-permute-start.24 = (s16[14,64,128]{2,1,0:T(8,128)(2,1)S(1)}, s16[14,64,128]{2,1,0:T(8,128)(2,1)S(1)}, u32[]{:S(2)}, u32[]{:S(2)}) collective-permute-start(s16[14,64,128]{2,1,0:T(8,128)(2,1)S(1)} %get-tuple-element.143), channel_id=1, source_target_pairs={{0,3},{1,2},{2,1},{3,0},{4,7},{5,6},{6,5},{7,4},{8,11},{9,10},{10,... | collective-permute-start | bytes 688136 | tf_op jit(solution)/shard_map/ppermute | solution.py:545
  75.1 9.2 %collective-permute-start.26 = (s16[6,64,128]{2,1,0:T(8,128)(2,1)S(1)}, s16[6,64,128]{2,1,0:T(8,128)(2,1)S(1)}, u32[]{:S(2)}, u32[]{:S(2)}) collective-permute-start(s16[6,64,128]{2,1,0:T(8,128)(2,1)S(1)} %get-tuple-element.147), channel_id=1, source_target_pairs={{0,8},{4,12},{8,0},{12,4},{16,24},{20,28},{24,16},{28,20},{1,9},{5... | collective-permute-start | bytes 294920 | tf_op jit(solution)/shard_map/ppermute | solution.py:548
  75.9 10.5 %collective-permute-start.27 = (s16[6,64,128]{2,1,0:T(8,128)(2,1)S(1)}, s16[6,64,128]{2,1,0:T(8,128)(2,1)S(1)}, u32[]{:S(2)}, u32[]{:S(2)}) collective-permute-start(s16[6,64,128]{2,1,0:T(8,128)(2,1)S(1)} %get-tuple-element.148), channel_id=1, source_target_pairs={{0,16},{4,20},{8,24},{12,28},{16,0},{20,4},{24,8},{28,12},{1,17},{... | collective-permute-start | bytes 294920 | tf_op jit(solution)/shard_map/ppermute | solution.py:548
  79.2 7.2 %collective-permute-start.28 = (s16[6,64,128]{2,1,0:T(8,128)(2,1)S(1)}, s16[6,64,128]{2,1,0:T(8,128)(2,1)S(1)}, u32[]{:S(2)}, u32[]{:S(2)}) collective-permute-start(s16[6,64,128]{2,1,0:T(8,128)(2,1)S(1)} %get-tuple-element.149), channel_id=1, source_target_pairs={{0,24},{4,28},{8,16},{12,20},{16,8},{20,12},{24,0},{28,4},{1,25},{... | collective-permute-start | bytes 294920 | tf_op jit(solution)/shard_map/ppermute | solution.py:548
  89.7 1.3 collective-permute-start.29
  91.0 7.9 %collective-permute-start.32 = (f32[96,128]{1,0:T(8,128)S(1)}, f32[96,128]{1,0:T(8,128)S(1)}, u32[]{:S(2)}, u32[]{:S(2)}) collective-permute-start(f32[96,128]{1,0:T(8,128)S(1)} %add.70), channel_id=1, source_target_pairs={{0,24},{4,28},{8,16},{12,20},{16,8},{20,12},{24,0},{28,4},{1,25},{... | collective-permute-start | bytes 147464 | tf_op jit(solution)/shard_map/ppermute | solution.py:548
  92.7 6.5 %collective-permute-start.31 = (f32[96,128]{1,0:T(8,128)S(1)}, f32[96,128]{1,0:T(8,128)S(1)}, u32[]{:S(2)}, u32[]{:S(2)}) collective-permute-start(f32[96,128]{1,0:T(8,128)S(1)} %add.70), channel_id=1, source_target_pairs={{0,16},{4,20},{8,24},{12,28},{16,0},{20,4},{24,8},{28,12},{1,17},{... | collective-permute-start | bytes 147464 | tf_op jit(solution)/shard_map/ppermute | solution.py:548
  94.2 5.0 %collective-permute-start.30 = (f32[96,128]{1,0:T(8,128)S(1)}, f32[96,128]{1,0:T(8,128)S(1)}, u32[]{:S(2)}, u32[]{:S(2)}) collective-permute-start(f32[96,128]{1,0:T(8,128)S(1)} %add.70), channel_id=1, source_target_pairs={{0,8},{4,12},{8,0},{12,4},{16,24},{20,28},{24,16},{28,20},{1,9},{5... | collective-permute-start | bytes 147464 | tf_op jit(solution)/shard_map/ppermute | solution.py:548
  99.3 5.5 %collective-permute-start.35 = (f32[96,128]{1,0:T(8,128)S(1)}, f32[96,128]{1,0:T(8,128)S(1)}, u32[]{:S(2)}, u32[]{:S(2)}) collective-permute-start(f32[96,128]{1,0:T(8,128)S(1)} %add_add_fusion.3), channel_id=1, source_target_pairs={{0,3},{1,2},{2,1},{3,0},{4,7},{5,6},{6,5},{7,4},{8,11},{9,10},{10,... | collective-permute-start | bytes 147464 | tf_op jit(solution)/shard_map/ppermute | solution.py:545
  100.8 4.3 %collective-permute-start.34 = (f32[96,128]{1,0:T(8,128)S(1)}, f32[96,128]{1,0:T(8,128)S(1)}, u32[]{:S(2)}, u32[]{:S(2)}) collective-permute-start(f32[96,128]{1,0:T(8,128)S(1)} %add_add_fusion.3), channel_id=1, source_target_pairs={{0,2},{1,3},{2,0},{3,1},{4,6},{5,7},{6,4},{7,5},{8,10},{9,11},{10,... | collective-permute-start | bytes 147464 | tf_op jit(solution)/shard_map/ppermute | solution.py:545
  101.3 4.1 %collective-permute-start.33 = (f32[96,128]{1,0:T(8,128)S(1)}, f32[96,128]{1,0:T(8,128)S(1)}, u32[]{:S(2)}, u32[]{:S(2)}) collective-permute-start(f32[96,128]{1,0:T(8,128)S(1)} %add_add_fusion.3), channel_id=1, source_target_pairs={{0,1},{1,0},{2,3},{3,2},{4,5},{5,4},{6,7},{7,6},{8,9},{9,8},{10,11... | collective-permute-start | bytes 147464 | tf_op jit(solution)/shard_map/ppermute | solution.py:545
  105.4 1.3 collective-permute-start.36
  117.0 1.3 collective-permute-start.40
  118.2 6.1 %collective-permute-start.43 = (s16[4,64,128]{2,1,0:T(8,128)(2,1)S(1)}, s16[4,64,128]{2,1,0:T(8,128)(2,1)S(1)}, u32[]{:S(2)}, u32[]{:S(2)}) collective-permute-start(s16[4,64,128]{2,1,0:T(8,128)(2,1)S(1)} %constant_dynamic-update-slice_fusion.2.refs_3_), channel_id=1, source_target_pairs={{0,24},{4,28},{8,16},{12,20},{16,8},{20,12},{24,0},{28,4},{1,25},{... | collective-permute-start | bytes 196616 | tf_op jit(solution)/shard_map/ppermute | solution.py:548
  119.9 10.5 %collective-permute-start.39 = (s16[7,64,128]{2,1,0:T(8,128)(2,1)S(1)}, s16[7,64,128]{2,1,0:T(8,128)(2,1)S(1)}, u32[]{:S(2)}, u32[]{:S(2)}) collective-permute-start(s16[7,64,128]{2,1,0:T(8,128)(2,1)S(1)} %get-tuple-element.161), channel_id=1, source_target_pairs={{0,3},{1,2},{2,1},{3,0},{4,7},{5,6},{6,5},{7,4},{8,11},{9,10},{10,... | collective-permute-start | bytes 344072 | tf_op jit(solution)/shard_map/ppermute | solution.py:545
  122.4 8.0 %collective-permute-start.38 = (s16[7,64,128]{2,1,0:T(8,128)(2,1)S(1)}, s16[7,64,128]{2,1,0:T(8,128)(2,1)S(1)}, u32[]{:S(2)}, u32[]{:S(2)}) collective-permute-start(s16[7,64,128]{2,1,0:T(8,128)(2,1)S(1)} %get-tuple-element.161), channel_id=1, source_target_pairs={{0,2},{1,3},{2,0},{3,1},{4,6},{5,7},{6,4},{7,5},{8,10},{9,11},{10,... | collective-permute-start | bytes 344072 | tf_op jit(solution)/shard_map/ppermute | solution.py:545
  122.9 7.5 %collective-permute-start.37 = (s16[7,64,128]{2,1,0:T(8,128)(2,1)S(1)}, s16[7,64,128]{2,1,0:T(8,128)(2,1)S(1)}, u32[]{:S(2)}, u32[]{:S(2)}) collective-permute-start(s16[7,64,128]{2,1,0:T(8,128)(2,1)S(1)} %get-tuple-element.161), channel_id=1, source_target_pairs={{0,1},{1,0},{2,3},{3,2},{4,5},{5,4},{6,7},{7,6},{8,9},{9,8},{10,11... | collective-permute-start | bytes 344072 | tf_op jit(solution)/shard_map/ppermute | solution.py:545
  123.4 7.0 %collective-permute-start.42 = (s16[4,64,128]{2,1,0:T(8,128)(2,1)S(1)}, s16[4,64,128]{2,1,0:T(8,128)(2,1)S(1)}, u32[]{:S(2)}, u32[]{:S(2)}) collective-permute-start(s16[4,64,128]{2,1,0:T(8,128)(2,1)S(1)} %constant_dynamic-update-slice_fusion.2.refs_3_), channel_id=1, source_target_pairs={{0,16},{4,20},{8,24},{12,28},{16,0},{20,4},{24,8},{28,12},{1,17},{... | collective-permute-start | bytes 196616 | tf_op jit(solution)/shard_map/ppermute | solution.py:548
  124.3 6.1 %collective-permute-start.41 = (s16[4,64,128]{2,1,0:T(8,128)(2,1)S(1)}, s16[4,64,128]{2,1,0:T(8,128)(2,1)S(1)}, u32[]{:S(2)}, u32[]{:S(2)}) collective-permute-start(s16[4,64,128]{2,1,0:T(8,128)(2,1)S(1)} %constant_dynamic-update-slice_fusion.2.refs_3_), channel_id=1, source_target_pairs={{0,8},{4,12},{8,0},{12,4},{16,24},{20,28},{24,16},{28,20},{1,9},{5... | collective-permute-start | bytes 196616 | tf_op jit(solution)/shard_map/ppermute | solution.py:548
  133.9 1.2 collective-permute-start.44
  135.2 6.3 %collective-permute-start.47 = (f32[96,128]{1,0:T(8,128)S(1)}, f32[96,128]{1,0:T(8,128)S(1)}, u32[]{:S(2)}, u32[]{:S(2)}) collective-permute-start(f32[96,128]{1,0:T(8,128)S(1)} %add.77), channel_id=1, source_target_pairs={{0,24},{4,28},{8,16},{12,20},{16,8},{20,12},{24,0},{28,4},{1,25},{... | collective-permute-start | bytes 147464 | tf_op jit(solution)/shard_map/ppermute | solution.py:548
  136.9 6.0 %collective-permute-start.46 = (f32[96,128]{1,0:T(8,128)S(1)}, f32[96,128]{1,0:T(8,128)S(1)}, u32[]{:S(2)}, u32[]{:S(2)}) collective-permute-start(f32[96,128]{1,0:T(8,128)S(1)} %add.77), channel_id=1, source_target_pairs={{0,16},{4,20},{8,24},{12,28},{16,0},{20,4},{24,8},{28,12},{1,17},{... | collective-permute-start | bytes 147464 | tf_op jit(solution)/shard_map/ppermute | solution.py:548
  136.9 6.0 %collective-permute-start.45 = (f32[96,128]{1,0:T(8,128)S(1)}, f32[96,128]{1,0:T(8,128)S(1)}, u32[]{:S(2)}, u32[]{:S(2)}) collective-permute-start(f32[96,128]{1,0:T(8,128)S(1)} %add.77), channel_id=1, source_target_pairs={{0,8},{4,12},{8,0},{12,4},{16,24},{20,28},{24,16},{28,20},{1,9},{5... | collective-permute-start | bytes 147464 | tf_op jit(solution)/shard_map/ppermute | solution.py:548
  142.9 5.1 %collective-permute-start.50 = (f32[96,128]{1,0:T(8,128)S(1)}, f32[96,128]{1,0:T(8,128)S(1)}, u32[]{:S(2)}, u32[]{:S(2)}) collective-permute-start(f32[96,128]{1,0:T(8,128)S(1)} %add_add_fusion.1), channel_id=1, source_target_pairs={{0,3},{1,2},{2,1},{3,0},{4,7},{5,6},{6,5},{7,4},{8,11},{9,10},{10,... | collective-permute-start | bytes 147464 | tf_op jit(solution)/shard_map/ppermute | solution.py:545
  145.5 4.1 %collective-permute-start.49 = (f32[96,128]{1,0:T(8,128)S(1)}, f32[96,128]{1,0:T(8,128)S(1)}, u32[]{:S(2)}, u32[]{:S(2)}) collective-permute-start(f32[96,128]{1,0:T(8,128)S(1)} %add_add_fusion.1), channel_id=1, source_target_pairs={{0,2},{1,3},{2,0},{3,1},{4,6},{5,7},{6,4},{7,5},{8,10},{9,11},{10,... | collective-permute-start | bytes 147464 | tf_op jit(solution)/shard_map/ppermute | solution.py:545
  146.0 4.1 %collective-permute-start.48 = (f32[96,128]{1,0:T(8,128)S(1)}, f32[96,128]{1,0:T(8,128)S(1)}, u32[]{:S(2)}, u32[]{:S(2)}) collective-permute-start(f32[96,128]{1,0:T(8,128)S(1)} %add_add_fusion.1), channel_id=1, source_target_pairs={{0,1},{1,0},{2,3},{3,2},{4,5},{5,4},{6,7},{7,6},{8,9},{9,8},{10,11... | collective-permute-start | bytes 147464 | tf_op jit(solution)/shard_map/ppermute | solution.py:545
  150.1 1.3 collective-permute-start.51
